TPU v7x, 32 devices: a whole 2x2x4 slice. The times are simulated.
32 devices in a mesh: wide: 16 (over z, y, core), narrow: 2 (over x).
Axes of the slice: x: 2, y: 2, z: 4, core: 2. Of those that a mesh axis runs over, the one named last changes fastest.
Arguments:
- tokens_in: bfloat16 [32768, 512], P(('wide', 'narrow')), may hold values from -6 to 6
- ln1_gain: float32 [512], replicated, may hold values from 0.1 to 1.9
- ln1_bias: float32 [512], replicated, may hold values from -4 to 4
- w_qkv: bfloat16 [512, 1536], replicated, may hold values from -0.25 to 0.25
- w_out: bfloat16 [512, 512], replicated, may hold values from -0.75 to 0.75
- ln2_gain: float32 [512], replicated, may hold values from 0.1 to 1.9
- ln2_bias: float32 [512], replicated, may hold values from -4 to 4
- w_up: bfloat16 [512, 2048], P(None, 'narrow'), may hold values from -0.25 to 0.25
- b_up: bfloat16 [2048], P('narrow'), may hold values from -4 to 4
- w_down: bfloat16 [2048, 512], P('narrow'), may hold values from -0.1875 to 0.1875
- b_down: float32 [512], replicated, may hold values from -4 to 4
- segment_ids: int32 [256, 128], P(('wide', 'narrow')), may hold values from 0 to 2, as said below
- step_ids: int32 [256, 128], P(('wide', 'narrow')), may hold values from 0 to 20, as said below
- pad_mask: int32 [256, 128], P(('wide', 'narrow')), may hold values from 0 to 1, as said below
- cotangent: bfloat16 [32768, 512], P(('wide', 'narrow')), may hold values from -6 to 6
Outputs:
- block_out: bfloat16 [32768, 512], P(('wide', 'narrow'))
- grad_tokens: float32 [32768, 512], P(('wide', 'narrow'))
- grad_ln1_gain: float32 [512], replicated
- grad_ln1_bias: float32 [512], replicated
- grad_w_qkv: float32 [512, 1536], replicated
- grad_w_out: float32 [512, 512], replicated
- grad_ln2_gain: float32 [512], replicated
- grad_ln2_bias: float32 [512], replicated
- grad_w_up: float32 [512, 2048], P(None, 'narrow')
- grad_b_up: float32 [2048], P('narrow')
- grad_w_down: float32 [2048, 512], P('narrow')
- grad_b_down: float32 [512], replicated
Inputs may be any that keep to these rules, and one draw needn't show every extreme that they name: `segment_ids`: fragment numbers never fall along a row; padding slots carry the number of the row's last fragment. `step_ids`: step numbers never fall within a fragment; padding slots carry 0. `pad_mask`: padding slots stand at the end of a row.
All inputs are finite; a program needn't handle non-finite values.
Results may differ from a plain program's by a relative error of at most 0.019.
Values may be sent and summed in bfloat16 or wider, within the bound.
No kernel may reach another device: no remote copies, remote signals or barrier semaphores. Data moves between devices by JAX's collectives and lax.ppermute only.
A program may use at most 192 MiB of HBM per device.

v0:
```python
import jax
import jax.numpy as jnp
from jax import lax
from jax.sharding import PartitionSpec as P

HEAD = 64


NORM_EPS = 1e-05


def dot_last(left_mat, right_mat):
    return lax.dot_general(
        left_mat, right_mat, (((1,), (1,)), ((), ())), preferred_element_type=jnp.float32
    )


def dot_first(left_mat, right_mat):
    return lax.dot_general(
        left_mat, right_mat, (((0,), (0,)), ((), ())), preferred_element_type=jnp.float32
    )


def norm_parts(inputs, gain_vec, shift_vec):
    row_mean = jnp.mean(inputs, axis=-1, keepdims=True)
    centered = inputs - row_mean
    inv_std = lax.rsqrt(jnp.mean(centered * centered, axis=-1, keepdims=True) + NORM_EPS)
    unit_rows = centered * inv_std
    return (unit_rows * gain_vec + shift_vec, unit_rows, inv_std)


def norm_back(incoming, unit_rows, inv_std, gain_vec):
    scaled = incoming * gain_vec
    return inv_std * (
        scaled
        - jnp.mean(scaled, axis=-1, keepdims=True)
        - unit_rows * jnp.mean(scaled * unit_rows, axis=-1, keepdims=True)
    )


def gelu_slope(act_value):
    normal_cdf = 0.5 * (1.0 + lax.erf(act_value * 0.7071067811865476))
    return normal_cdf + act_value * jnp.exp(-0.5 * act_value * act_value) * 0.3989422804014327


def visible_keys(frag_ids, step_nums, pad_flags):
    same_frag = frag_ids[:, :, None] == frag_ids[:, None, :]
    earlier = step_nums[:, None, :] <= step_nums[:, :, None]
    live_keys = (pad_flags == 0)[:, None, :]
    itself = jnp.eye(frag_ids.shape[1], dtype=bool)[None]
    return same_frag & earlier & live_keys | itself


def local(
    tokens_in,
    ln1_gain,
    ln1_bias,
    w_qkv,
    w_out,
    ln2_gain,
    ln2_bias,
    w_up,
    b_up,
    w_down,
    b_down,
    segment_ids,
    step_ids,
    pad_mask,
    cotangent,
):
    row_count, slot_count = segment_ids.shape
    model_width = tokens_in.shape[1]
    head_count = model_width // HEAD
    tok_count = row_count * slot_count
    score_scale = HEAD ** (-0.5)
    visible = visible_keys(segment_ids, step_ids, pad_mask)[:, None]
    head_shape = (row_count, slot_count, head_count, HEAD)
    residual_in = tokens_in.astype(jnp.float32)
    normed, unit_one, inv_one = norm_parts(residual_in, ln1_gain, ln1_bias)
    normed = normed.astype(jnp.bfloat16)
    qkv = jnp.dot(normed, w_qkv, preferred_element_type=jnp.float32).astype(jnp.bfloat16)
    queries = qkv[:, :model_width].reshape(head_shape)
    key_rows = qkv[:, model_width : 2 * model_width].reshape(head_shape)
    value_rows = qkv[:, 2 * model_width :].reshape(head_shape)

    def masked_scores():
        raw_scores = (
            jnp.einsum("rqhd,rkhd->rhqk", queries, key_rows, preferred_element_type=jnp.float32)
            * score_scale
        )
        return jnp.where(visible, raw_scores, -1e30)

    scores = masked_scores()
    row_top = jnp.max(scores, axis=-1, keepdims=True)
    weight = jnp.exp(scores - row_top)
    row_total = jnp.sum(weight, axis=-1, keepdims=True)
    log_total = row_top + jnp.log(row_total)
    head_mixed = jnp.einsum(
        "rhqk,rkhd->rqhd",
        (weight / row_total).astype(jnp.bfloat16),
        value_rows,
        preferred_element_type=jnp.float32,
    )
    head_mixed = head_mixed.reshape(tok_count, model_width).astype(jnp.bfloat16)
    residual = residual_in + jnp.dot(head_mixed, w_out, preferred_element_type=jnp.float32)
    second, unit_two, inv_two = norm_parts(residual, ln2_gain, ln2_bias)
    second = second.astype(jnp.bfloat16)
    grad_top = cotangent.astype(jnp.float32)
    second_all = lax.all_gather(second, "narrow", axis=0, tiled=True)
    pre_act = jnp.dot(second_all, w_up, preferred_element_type=jnp.float32) + b_up.astype(
        jnp.float32
    )
    hidden = jax.nn.gelu(pre_act, approximate=False).astype(jnp.bfloat16)
    down_out = lax.psum_scatter(
        jnp.dot(hidden, w_down, preferred_element_type=jnp.float32).astype(jnp.bfloat16),
        "narrow",
        scatter_dimension=0,
        tiled=True,
    ).astype(jnp.float32)
    grad_all = lax.all_gather(cotangent, "narrow", axis=0, tiled=True)
    grad_hidden = dot_last(grad_all, w_down)
    grad_w_down = dot_first(hidden, grad_all)
    grad_pre = (grad_hidden * gelu_slope(pre_act)).astype(jnp.bfloat16)
    grad_b_up = jnp.sum(grad_pre.astype(jnp.float32), axis=0)
    second_all = lax.all_gather(second, "narrow", axis=0, tiled=True)
    grad_w_up = dot_first(second_all, grad_pre)
    grad_second = lax.psum_scatter(
        dot_last(grad_pre, w_up), "narrow", scatter_dimension=0, tiled=True
    )
    block_out = (residual + (down_out + b_down)).astype(jnp.bfloat16)
    grad_w_up, grad_b_up, grad_w_down = (
        lax.psum(grad_w_up.astype(jnp.bfloat16), "wide").astype(jnp.float32),
        lax.psum(grad_b_up.astype(jnp.bfloat16), "wide").astype(jnp.float32),
        lax.psum(grad_w_down.astype(jnp.bfloat16), "wide").astype(jnp.float32),
    )
    grad_residual = grad_top + norm_back(grad_second, unit_two, inv_two, ln2_gain)
    grad_branch = grad_residual.astype(jnp.bfloat16)
    grad_w_out = dot_first(head_mixed, grad_branch)
    grad_mixed = dot_last(grad_branch, w_out).astype(jnp.bfloat16).reshape(head_shape)
    attn_prob = jnp.exp(masked_scores() - log_total)
    grad_values = jnp.einsum(
        "rhqk,rqhd->rkhd",
        attn_prob.astype(jnp.bfloat16),
        grad_mixed,
        preferred_element_type=jnp.float32,
    )
    grad_prob = jnp.einsum(
        "rqhd,rkhd->rhqk", grad_mixed, value_rows, preferred_element_type=jnp.float32
    )
    grad_scores = (
        attn_prob * (grad_prob - jnp.sum(attn_prob * grad_prob, axis=-1, keepdims=True))
    ).astype(jnp.bfloat16)
    grad_queries = (
        jnp.einsum("rhqk,rkhd->rqhd", grad_scores, key_rows, preferred_element_type=jnp.float32)
        * score_scale
    )
    grad_keys = (
        jnp.einsum("rhqk,rqhd->rkhd", grad_scores, queries, preferred_element_type=jnp.float32)
        * score_scale
    )
    grad_qkv = jnp.concatenate(
        [
            grad_queries.reshape(tok_count, model_width),
            grad_keys.reshape(tok_count, model_width),
            grad_values.reshape(tok_count, model_width),
        ],
        axis=1,
    ).astype(jnp.bfloat16)
    grad_w_qkv = dot_first(normed, grad_qkv)
    grad_normed = dot_last(grad_qkv, w_qkv)
    grad_tokens = grad_residual + norm_back(grad_normed, unit_one, inv_one, ln1_gain)
    shared = lax.psum(
        (
            grad_w_qkv,
            grad_w_out,
            jnp.sum(grad_normed * unit_one, axis=0),
            jnp.sum(grad_normed, axis=0),
            jnp.sum(grad_second * unit_two, axis=0),
            jnp.sum(grad_second, axis=0),
            jnp.sum(grad_top, axis=0),
        ),
        ("wide", "narrow"),
    )
    return (
        block_out,
        grad_tokens,
        shared[2],
        shared[3],
        shared[0],
        shared[1],
        shared[4],
        shared[5],
        grad_w_up,
        grad_b_up,
        grad_w_down,
        shared[6],
    )


def solution(mesh):
    in_specs = (
        P(("wide", "narrow"), None),
        P(),
        P(),
        P(),
        P(),
        P(),
        P(),
        P(None, "narrow"),
        P("narrow"),
        P("narrow", None),
        P(),
        P(("wide", "narrow"), None),
        P(("wide", "narrow"), None),
        P(("wide", "narrow"), None),
        P(("wide", "narrow"), None),
    )
    out_specs = (
        P(("wide", "narrow"), None),
        P(("wide", "narrow"), None),
        P(),
        P(),
        P(),
        P(),
        P(),
        P(),
        P(None, "narrow"),
        P("narrow"),
        P("narrow", None),
        P(),
    )
    return jax.shard_map(local, mesh=mesh, in_specs=in_specs, out_specs=out_specs, check_vma=False)
```

profile of v0, /device:TPU:0, one launch (start us, length us, event | category | flops | bytes accessed | tf_op | source)
XLA Modules:
  0.0 481.2 jit_solution(1577409980523828646)
XLA Ops:
  7.3 1.6 copy.47
  10.3 2.0 convolution_convert_fusion
  12.2 1.7 fusion.56
  14.0 3.9 reshape.132
  17.9 3.0 copy.51
  20.8 3.9 reshape.133
  24.7 3.0 copy.52
  27.8 3.9 reshape.131
  31.6 3.0 copy.53
  35.4 2.5 fusion.57
  43.8 1.3 add_convert_fusion.1
  46.0 35.1 %all-gather.3.cloned.1.call-done = bf16[2048,512]{0,1:T(8,128)(2,1)} async-done(((bf16[1024,512]{0,1:T(8,128)(2,1)}), bf16[2048,512]{0,1:T(8,128)(2,1)}) %all-gather.3.cloned.1.call-update) | async-done | bytes 2097168 | tf_op jit(solution)/shard_map/all_gather | solution.py:109
  81.1 23.1 %fusion.2 = (bf16[2048,1024]{1,0:T(8,128)(2,1)}, f32[2048,1024]{1,0:T(8,128)}) fusion(f32[1024]{0:T(1024)S(1)} %convert_element_type.83, bf16[2048,512]{0,1:T(8,128)(2,1)} %all-gather.3.cloned.1.call-done, bf16[512,1024]{1,0:T(8,128)(2,1)} %param.22), kind=kOutput, calls=%fused_computation.4 | convolution fusion | flops 2285895680 | bytes 15732736 | tf_op jit(solution)/shard_map/dot_general | solution.py:110
  104.2 11.6 %all-gather.5.cloned.1.call-done = bf16[2048,512]{1,0:T(8,128)(2,1)} async-done(((bf16[1024,512]{1,0:T(8,128)(2,1)}), bf16[2048,512]{1,0:T(8,128)(2,1)}) %all-gather.5.cloned.1.call-update) | async-done | bytes 2097168 | tf_op jit(solution)/shard_map/all_gather | solution.py:120
  115.8 8.1 %fusion.60 = (bf16[1024]{0:T(1024)(128)(2,1)S(1)}, bf16[2048,1024]{1,0:T(8,128)(2,1)S(1)}) fusion(f32[2048,1024]{1,0:T(8,128)} %get-tuple-element.63, f32[1024]{0:T(1024)S(1)} %convert_element_type.83, bf16[2048,512]{1,0:T(8,128)(2,1)} %all-gather.5.cloned.1.call-done, bf16[1024,512]{1,0:T(8,128)(2,1)} %param.24), kind=kOutput, calls=%fused_computation.104 | convolution fusion | flops 2172648448 | bytes 15734784 | tf_op jit(solution)/shard_map/dot_general | solution.py:13
  124.0 2.0 copy-done.38
  125.9 4.3 fusion.61
  130.3 6.2 %convolution_convert_fusion.1 = bf16[2048,512]{0,1:T(8,128)(2,1)} fusion(bf16[2048,1024]{1,0:T(8,128)(2,1)} %get-tuple-element.62, bf16[1024,512]{1,0:T(8,128)(2,1)} %param.24), kind=kOutput, calls=%fused_computation.38 | convolution fusion | flops 2148532224 | bytes 7340032 | tf_op jit(solution)/shard_map/dot_general | solution.py:115
  136.6 2.7 copy.57
  139.3 6.3 %convolution_convert_fusion.4 = bf16[512,1024]{1,0:T(8,128)(2,1)} fusion(bf16[2048,512]{0,1:T(8,128)(2,1)} %all-gather.3.cloned.1.call-done, bf16[2048,1024]{1,0:T(8,128)(2,1)} %copy-done.38), kind=kOutput, calls=%fused_computation.72 | convolution fusion | flops 2148007936 | bytes 7340032 | tf_op jit(solution)/shard_map/dot_general | solution.py:19
  145.7 3.3 convolution_convert_fusion.3
  149.1 35.6 %reduce-scatter.5.cloned.1.call-done = f32[1024,512]{0,1:T(8,128)} async-done(((f32[2048,512]{0,1:T(8,128)}), f32[1024,512]{0,1:T(8,128)}) %reduce-scatter.5.cloned.1.call-update) | async-done | bytes 2097168 | tf_op jit(solution)/shard_map/reduce_scatter | solution.py:127
  184.7 3.0 multiply_reduce_fusion.1
  187.8 31.6 %reduce-scatter.3.cloned.1.call-done = bf16[1024,512]{0,1:T(8,128)(2,1)} async-done(((bf16[2048,512]{0,1:T(8,128)(2,1)}), bf16[1024,512]{0,1:T(8,128)(2,1)}) %reduce-scatter.3.cloned.1.call-update) | async-done | bytes 1048592 | tf_op jit(solution)/shard_map/reduce_scatter | solution.py:114
  219.3 5.0 %convert_add_fusion.1 = (f32[1024,512]{0,1:T(8,128)S(1)}, bf16[1024,512]{0,1:T(8,128)(2,1)}, f32[512]{0:T(512)S(1)}) fusion(bf16[1024,512]{0,1:T(8,128)(2,1)} %copy.57, f32[1024,512]{0,1:T(8,128)} %reduce-scatter.5.cloned.1.call-done, f32[1024,512]{0,1:T(8,128)} %copy-done.3, f32[1024]{0:T(1024)S(1)} %get-tuple-element.70, f32[1024]{0:T(1024)S(1)} %get-tuple-element.71, ...), kind=kLoop, calls=%fused_computation.40 | loop fusion | flops 7339520 | bytes 9459712 | tf_op jit(solution)/shard_map/add | solution.py:136
  224.3 1.3 copy-done.4
  225.6 1.7 convolution_convert_fusion.2
  227.4 4.1 reshape.134
  231.5 3.0 copy.60
  234.5 4.2 fusion.41
  238.9 1.2 multiply_reduce_fusion
  240.1 1.3 multiply_convert_fusion
  241.5 1.5 fusion.45
  247.7 2.0 fusion.46
  249.7 3.6 fusion.53
  253.4 33.7 %psum.77 = bf16[1024]{0:T(1024)(128)(2,1)S(1)} all-reduce(bf16[1024]{0:T(1024)(128)(2,1)S(1)} %get-tuple-element.68), channel_id=1, replica_groups=mesh['wide'=16,'narrow'=2] {'wide'}, use_global_device_ids=true, to_apply=%region_25.26 | all-reduce | flops 1024 | bytes 4096 | tf_op jit(solution)/shard_map/psum | solution.py:133
  287.7 33.2 %all-reduce.8.cloned.1.call-done = (bf16[512,1024]{1,0:T(8,128)(2,1)}, bf16[1024,512]{1,0:T(8,128)(2,1)}) async-done(((bf16[512,1024]{1,0:T(8,128)(2,1)}, bf16[1024,512]{1,0:T(8,128)(2,1)}), (bf16[512,1024]{1,0:T(8,128)(2,1)}, bf16[1024,512]{1,0:T(8,128)(2,1)})) %all-reduce.8.cloned.1.call-update) | async-done | bytes 2097168 | tf_op jit(solution)/shard_map/psum | solution.py:132
  320.9 2.9 convert_element_type.95
  323.9 1.6 convert_element_type.98
  325.5 3.2 fusion.59
  328.6 2.9 copy.71
  331.5 2.9 fusion.30
  334.5 3.6 fusion.29
  338.1 3.0 copy.74
  341.1 1.3 copy.73
  342.4 39.7 %all-reduce = (f32[512]{0:T(512)}, f32[512]{0:T(512)}, f32[512]{0:T(512)}, f32[512]{0:T(512)}, f32[512]{0:T(512)}) all-reduce(f32[512]{0:T(512)S(1)} %get-tuple-element.38, f32[512]{0:T(512)S(1)} %get-tuple-element.66, f32[512]{0:T(512)S(1)} %get-tuple-element.36, ...), channel_id=1, replica_groups=mesh['wide'=16,'narrow'=2] {'wide','narrow'}, use_global_device_ids=true, to_apply=%region_14.15 | all-reduce | flops 2560 | bytes 20480 | tf_op jit(solution)/shard_map/psum | solution.py:172
  382.1 87.2 %all-reduce.6.cloned.1.call-done = (f32[512,1536]{1,0:T(8,128)}, f32[512,512]{1,0:T(8,128)}) async-done(((f32[512,1536]{1,0:T(8,128)}, f32[512,512]{1,0:T(8,128)}), (f32[512,1536]{1,0:T(8,128)}, f32[512,512]{1,0:T(8,128)})) %all-reduce.6.cloned.1.call-update) | async-done | bytes 4194320 | tf_op jit(solution)/shard_map/psum | solution.py:172
  469.3 3.8 copy.112
  (116 shorter events, 15.4 us)
Async XLA Ops:
  7.2 3.1 copy-start
  7.2 3.1 copy-start.27
  7.2 3.1 copy-start.35
  7.2 73.9 %all-gather.3.cloned.1.call-start = ((), (), s32[]{:S(2)}) async-start(), calls=%async_computation.2 | async-start | bytes 3145728 | tf_op jit(solution)/shard_map/all_gather | solution.py:109
  9.1 0.6 copy-start.20
  9.7 0.6 copy-start.22
  20.8 6.9 %copy-start.29 = (s32[8,128]{1,0:T(8,128)S(1)}, s32[8,128]{1,0:T(8,128)}, u32[]{:S(2)}) copy-start(s32[8,128]{1,0:T(8,128)} %param.28) | copy-start | bytes 12292
  27.7 6.9 %copy-start.25 = (s32[8,128]{1,0:T(8,128)S(1)}, s32[8,128]{1,0:T(8,128)}, u32[]{:S(2)}) copy-start(s32[8,128]{1,0:T(8,128)} %param.27) | copy-start | bytes 12292
  27.7 6.9 %copy-start.26 = (s32[8,128]{1,0:T(8,128)S(1)}, s32[8,128]{1,0:T(8,128)}, u32[]{:S(2)}) copy-start(s32[8,128]{1,0:T(8,128)} %param.26) | copy-start | bytes 12292
  38.0 2.8 copy-start.1
  38.0 2.0 copy-start.12
  40.0 1.5 copy-start.15
  41.5 1.0 copy-start.7
  41.5 2.3 copy-start.24
  41.5 2.3 copy-start.30
  42.5 1.3 copy-start.3
  42.8 3.2 copy-start.32
  45.2 70.7 %all-gather.5.cloned.1.call-start = ((), (), s32[]{:S(2)}) async-start(), calls=%async_computation.4 | async-start | bytes 3145728 | tf_op jit(solution)/shard_map/all_gather | solution.py:120
  45.9 138.8 %reduce-scatter.5.cloned.1.call-start = ((), (), s32[]{:S(2)}) async-start(), calls=%async_computation.5 | async-start | bytes 6291456 | tf_op jit(solution)/shard_map/reduce_scatter | solution.py:127
  115.8 10.1 %copy-start.34 = (bf16[512,1024]{1,0:T(8,128)(2,1)S(1)}, bf16[512,1024]{1,0:T(8,128)(2,1)}, u32[]{:S(2)}) copy-start(bf16[512,1024]{1,0:T(8,128)(2,1)} %param.22) | copy-start | bytes 3145732
  123.9 2.0 copy-start.38
  130.3 89.1 %reduce-scatter.3.cloned.1.call-start = ((), (), s32[]{:S(2)}) async-start(), calls=%async_computation.3 | async-start | bytes 3145728 | tf_op jit(solution)/shard_map/reduce_scatter | solution.py:114
  136.5 184.4 %all-reduce.8.cloned.1.call-start = ((), (), s32[]{:S(2)}) async-start(), calls=%async_computation.7 | async-start | bytes 4194304 | tf_op jit(solution)/shard_map/psum | solution.py:132
  139.3 6.4 %copy-start.33 = (bf16[2048,512]{1,0:T(8,128)(2,1)S(1)}, bf16[2048,512]{1,0:T(8,128)(2,1)}, u32[]{:S(2)}) copy-start(bf16[2048,512]{1,0:T(8,128)(2,1)} %all-gather.5.cloned.1.call-done) | copy-start | bytes 6291460
  139.3 6.4 %copy-start.37 = (bf16[2048,1024]{1,0:T(8,128)(2,1)S(1)}, bf16[2048,1024]{1,0:T(8,128)(2,1)}, u32[]{:S(2)}) copy-start(bf16[2048,1024]{1,0:T(8,128)(2,1)} %get-tuple-element.62) | copy-start | bytes 12582916
  149.0 70.3 %copy-start.31 = (f32[512]{0:T(512)S(1)}, f32[512]{0:T(512)}, u32[]{:S(2)}) copy-start(f32[512]{0:T(512)} %param.25) | copy-start | bytes 6148
  149.1 320.2 %all-reduce.6.cloned.1.call-start = ((), (), s32[]{:S(2)}) async-start(), calls=%async_computation.6 | async-start | bytes 8388608 | tf_op jit(solution)/shard_map/psum | solution.py:172
  224.3 1.3 copy-start.4
  234.5 4.2 copy-start.2
  234.5 4.3 copy-start.11
  234.5 4.5 copy-start.13
  240.1 1.3 copy-start.9
  241.4 1.5 copy-start.10
  245.8 1.6 copy-start.5
  245.8 1.9 copy-start.8
  246.3 3.5 copy-start.21
  246.3 3.5 copy-start.23
  246.3 3.4 copy-start.28
  246.3 3.4 copy-start.36
  247.7 2.0 copy-start.18
  320.9 2.9 copy-start.16
  320.9 4.6 copy-start.19
  331.5 2.9 copy-start.6
  338.1 3.0 copy-start.14
  469.3 3.8 copy-start.17
Sparse Core Ops, SparseCore 0:
  45.3 35.8 all-gather.2
  82.7 33.1 all-gather.4
  130.4 54.3 reduce-scatter.4
  187.5 31.8 reduce-scatter.2
  222.8 98.0 all-reduce.7
  327.4 141.8 all-reduce.5
where the time goes:
time: 488 us; the launch traced here: 481 us
  waiting for transfers between devices  235 us (48%)
  matrix products  75.7 us (16%)
  blocking collectives  73.4 us (15%)
  local copies, waits for them, and re-layouts  57 us (12%)
  other arithmetic  24.9 us (5%)
  between operations  14.8 us (3%)
    psum x1, waiting for transfers between devices, local(): lax.psum((grad_w_qkv, grad_w_out, jnp.sum(grad_normed * unit_one, axis=0)...  87.2 us
    psum x1, blocking collectives, local(): lax.psum((grad_w_qkv, grad_w_out, jnp.sum(grad_normed * unit_one, axis=0)...  39.7 us
    reduce_scatter x1, waiting for transfers between devices, local(): lax.psum_scatter(dot_last(grad_pre, w_up), 'narrow', scatter_dimension=0,...  35.6 us
    all_gather x1, waiting for transfers between devices, local(): second_all = lax.all_gather(second, 'narrow', axis=0, tiled=True)  35.1 us
    psum x1, blocking collectives, local(): lax.psum(grad_b_up.astype(jnp.bfloat16), 'wide').astype(jnp.float32)  33.7 us
    psum x1, waiting for transfers between devices, local(): lax.psum(grad_w_up.astype(jnp.bfloat16), 'wide').astype(jnp.float32)  33.2 us
    reduce_scatter x1, waiting for transfers between devices, local(): lax.psum_scatter(jnp.dot(hidden, w_down, preferred_element_type=jnp.float...  31.6 us
    dot_general x1, matrix products, local(): jnp.dot(second_all, w_up, preferred_element_type=jnp.float32)  23.1 us
  transfers between devices with their start and end apart: 6, of which 6 were waited for; matrix products, arithmetic and copies ran while one was open for 20% of the time, Pallas kernels for 0%

commit v1 on v0

v1 whole, which is shorter than its diff:
```python
import functools

import jax
import jax.numpy as jnp
import numpy as np
from jax import lax
from jax.experimental import pallas as pl
from jax.experimental.pallas import tpu as pltpu
from jax.sharding import PartitionSpec as P

HEAD = 64
PAIR = 2 * HEAD
NORM_EPS = 1e-05
BF = jnp.bfloat16
F32 = jnp.float32
AXES = ("wide", "narrow")
TILE = 16
TOKS = 256
VMEM_LIMIT = 50 * 1024 * 1024


def mm(a, b):
    return lax.dot_general(a, b, (((1,), (0,)), ((), ())), preferred_element_type=F32)


def mm_nt(a, b):
    return lax.dot_general(a, b, (((1,), (1,)), ((), ())), preferred_element_type=F32)


def mm_tn(a, b):
    return lax.dot_general(a, b, (((0,), (0,)), ((), ())), preferred_element_type=F32)


def whole(*shape):
    return pl.BlockSpec(shape, lambda *_: (0,) * len(shape))


def rows_of(width, toks=TOKS):
    return pl.BlockSpec((toks, width), lambda i, *_: (i, 0))


def call(kernel, name, grid, in_specs, out_specs, out_shape, scratch, info, args):
    return pl.pallas_call(
        kernel,
        grid_spec=pltpu.PrefetchScalarGridSpec(
            num_scalar_prefetch=1, grid=grid, in_specs=in_specs, out_specs=out_specs, scratch_shapes=scratch
        ),
        out_shape=out_shape,
        compiler_params=pltpu.CompilerParams(vmem_limit_bytes=VMEM_LIMIT),
        name=name,
    )(info, *args)


def unit_parts(rows):
    mean = jnp.mean(rows, axis=-1, keepdims=True)
    centered = rows - mean
    inv = lax.rsqrt(jnp.mean(centered * centered, axis=-1, keepdims=True) + NORM_EPS)
    return centered * inv, inv


def norm_back(incoming, unit, inv, gain):
    scaled = incoming * gain
    return inv * (
        scaled
        - jnp.mean(scaled, axis=-1, keepdims=True)
        - unit * jnp.mean(scaled * unit, axis=-1, keepdims=True)
    )


def gelu_pair(x):
    cdf = 0.5 * (1.0 + lax.erf(x * 0.7071067811865476))
    return x * cdf, cdf + x * jnp.exp(-0.5 * x * x) * 0.3989422804014327


def by_head(block):
    lane = lax.broadcasted_iota(jnp.int32, block.shape, 1)
    zero = jnp.zeros_like(block)
    first = lane < HEAD
    return jnp.concatenate([jnp.where(first, block, zero), jnp.where(first, zero, block)], axis=0)


def places(order, blocks):
    bits = blocks.bit_length() - 1
    table = []
    for place in range(blocks):
        owner = 0
        for step in range(bits):
            if place >> (bits - 1 - step) & 1:
                owner ^= order[step]
        table.append(owner)
    return table


def block_at(place, tables, core, own):
    first, second = tables[0][place], tables[1][place]
    if first == second:
        return own ^ first
    return own ^ jnp.where(core == 0, first, second)


def permuted(dst_ref, acc_ref, tables, core, own):
    blocks = len(tables[0])
    size = acc_ref.shape[0] // blocks
    for place in range(blocks):
        block = block_at(place, tables, core, own)
        rows = pl.ds(pl.multiple_of(block * size, size), size)
        dst_ref[place * size : (place + 1) * size, :] = acc_ref[rows, :].astype(dst_ref.dtype)


def attend_kernel(
    info_ref, tok_ref, g1_ref, c1_ref, wqkv_ref, wout_ref, g2_ref, c2_ref, seg_ref, step_ref, pad_ref,
    qkv_ref, prob_ref, mixed_ref, res_ref, second_ref,
):
    slots = seg_ref.shape[1]
    toks, width = tok_ref.shape
    rows = toks // slots
    at = pl.program_id(0)
    tokens = tok_ref[...].astype(F32)
    unit, _ = unit_parts(tokens)
    normed = (unit * g1_ref[...] + c1_ref[...]).astype(BF)
    qkv_ref[...] = mm(normed, wqkv_ref[...]).astype(BF)
    q_id = lax.broadcasted_iota(jnp.int32, (slots, slots), 0)
    k_id = lax.broadcasted_iota(jnp.int32, (slots, slots), 1)
    eye = q_id == k_id
    for r in range(rows):
        here = pl.ds(at * rows + r, 1)
        seg = jnp.broadcast_to(seg_ref[here, :].astype(F32), (slots, slots))
        step = jnp.broadcast_to(step_ref[here, :].astype(F32), (slots, slots))
        live = jnp.broadcast_to(pad_ref[here, :], (slots, slots)) == 0
        visible = ((seg == seg.T) & (step <= step.T) & live) | eye
        span = slice(r * slots, (r + 1) * slots)
        for p in range(width // PAIR):
            cols = slice(p * PAIR, (p + 1) * PAIR)
            q = qkv_ref[span, p * PAIR : (p + 1) * PAIR]
            k = qkv_ref[span, width + p * PAIR : width + (p + 1) * PAIR]
            v = qkv_ref[span, 2 * width + p * PAIR : 2 * width + (p + 1) * PAIR]
            scores = mm_nt(q, by_head(k * HEAD ** (-0.5)))
            halves = []
            for half in (scores[:, :slots], scores[:, slots:]):
                half = jnp.where(visible, half, -1e30)
                weight = jnp.exp(half - jnp.max(half, axis=-1, keepdims=True))
                total = jnp.sum(weight, axis=-1, keepdims=True)
                halves.append((weight * (1.0 / total)).astype(BF))
            prob = jnp.concatenate(halves, axis=1)
            prob_ref[r, p] = prob
            mixed_ref[span, cols] = mm(prob, by_head(v)).astype(BF)
    residual = tokens + mm(mixed_ref[...], wout_ref[...])
    res_ref[...] = residual
    unit, _ = unit_parts(residual)
    second_ref[...] = (unit * g2_ref[...] + c2_ref[...]).astype(BF)


def attend(info, tokens, g1, c1, wqkv, wout, g2, c2, seg, step, pad):
    n, width = tokens.shape
    rows, slots = seg.shape
    per, pairs = TOKS // slots, width // PAIR
    return call(
        attend_kernel,
        "attend",
        (n // TOKS,),
        [rows_of(width), whole(1, width), whole(1, width), whole(*wqkv.shape), whole(*wout.shape)]
        + [whole(1, width)] * 2
        + [whole(rows, slots)] * 3,
        [
            rows_of(3 * width),
            pl.BlockSpec((per, pairs, slots, 2 * slots), lambda i, *_: (i, 0, 0, 0)),
            rows_of(width),
            rows_of(width),
            rows_of(width),
        ],
        [
            jax.ShapeDtypeStruct((n, 3 * width), BF),
            jax.ShapeDtypeStruct((rows, pairs, slots, 2 * slots), BF),
            jax.ShapeDtypeStruct((n, width), BF),
            jax.ShapeDtypeStruct((n, width), F32),
            jax.ShapeDtypeStruct((n, width), BF),
        ],
        [],
        info,
        (tokens, g1, c1, wqkv, wout, g2, c2, seg, step, pad),
    )


def ffn_block(sec, sec_t, dy, dy_t, up, bias, down, acc_ref, bacc_ref, out, dsec):
    units = up.shape[1]
    pre = mm(sec, up) + bias
    hid, slope = gelu_pair(pre)
    hid = hid.astype(BF)
    dpre = (mm_nt(dy, down) * slope).astype(BF)
    acc_ref[:, :units] += mm(sec_t, dpre)
    acc_ref[:, units:] += mm(dy_t, hid)
    bacc_ref[...] += jnp.sum(dpre.astype(F32), axis=0, keepdims=True)
    o = mm(hid, down)
    d = mm_nt(dpre, up)
    return (o if out is None else out + o), (d if dsec is None else dsec + d)


def ffn_own_kernel(tables, info_ref, sec_ref, dy_ref, *refs):
    ups, biases, downs = refs[:2], refs[2:4], refs[4:6]
    out_ref, dsec_ref = refs[6:8]
    grads, bgrads, accs, baccs = refs[8:10], refs[10:12], refs[12:14], refs[14:16]
    at, last = pl.program_id(0), pl.num_programs(0) - 1

    @pl.when(at == 0)
    def _():
        for ref in accs + baccs:
            ref[...] = jnp.zeros_like(ref)

    sec, dy = sec_ref[...], dy_ref[...]
    sec_t, dy_t = sec.T, dy.T
    out = dsec = None
    for i in range(2):
        out, dsec = ffn_block(
            sec, sec_t, dy, dy_t, ups[i][...], biases[i][...].astype(F32), downs[i][...], accs[i], baccs[i], out, dsec
        )
    out_ref[...] = out
    dsec_ref[...] = dsec

    @pl.when(at == last)
    def _():
        core, own = info_ref[0], info_ref[1]
        for i in range(2):
            permuted(grads[i], accs[i], tables, core ^ i, own)
            bgrads[i][...] = baccs[i][...]


def ffn_own(info, tables, second, dy, up, bias, down):
    n, width = second.shape
    units = up.shape[1] // 2
    chunk = lambda i: (lambda t, info: (0, info[0] ^ i))
    return call(
        functools.partial(ffn_own_kernel, tables),
        "ffn_own",
        (n // TOKS,),
        [rows_of(width), rows_of(width)]
        + [pl.BlockSpec((width, units), chunk(i)) for i in range(2)]
        + [pl.BlockSpec((1, units), chunk(i)) for i in range(2)]
        + [pl.BlockSpec((units, width), lambda t, info, i=i: (info[0] ^ i, 0)) for i in range(2)],
        [rows_of(width)] * 2 + [whole(width, 2 * units)] * 2 + [whole(1, units)] * 2,
        [jax.ShapeDtypeStruct((n, width), F32)] * 2
        + [jax.ShapeDtypeStruct((width, 2 * units), BF)] * 2
        + [jax.ShapeDtypeStruct((1, units), F32)] * 2,
        [pltpu.VMEM((width, 2 * units), F32)] * 2 + [pltpu.VMEM((1, units), F32)] * 2,
        info,
        (second, dy, up, up, bias, bias, down, down),
    )


def ffn_rest_kernel(
    tables, count, info_ref, sec_ref, dy_ref, out_part_ref, dsec_part_ref, res_ref, mixed_ref, bdown_ref, g2_ref, wout_ref, *refs
):
    ups, downs = refs[:count], refs[count : 2 * count]
    block_ref, gres_ref, gmix_ref, vec_ref, dwout_ref = refs[2 * count : 2 * count + 5]
    rest = refs[2 * count + 5 :]
    grads, bgrads = rest[:count], rest[count : 2 * count]
    accs, baccs = rest[2 * count : 3 * count], rest[3 * count : 4 * count]
    wacc_ref = rest[4 * count]
    at, last = pl.program_id(0), pl.num_programs(0) - 1
    width = sec_ref.shape[1]

    @pl.when(at == 0)
    def _():
        for ref in accs + baccs + (wacc_ref, vec_ref):
            ref[...] = jnp.zeros_like(ref)

    sec, dy = sec_ref[...], dy_ref[...]
    sec_t, dy_t = sec.T, dy.T
    out, dsec = out_part_ref[...], dsec_part_ref[...]
    for i in range(count):
        bias = ups[i][width : width + TILE, :].astype(F32)[:1]
        out, dsec = ffn_block(sec, sec_t, dy, dy_t, ups[i][:width, :], bias, downs[i][...], accs[i], baccs[i], out, dsec)
    residual = res_ref[...]
    block_ref[...] = (residual + (out + bdown_ref[...])).astype(BF)
    dy32 = dy.astype(F32)
    unit, inv = unit_parts(residual)
    vec_ref[0:1, :] += jnp.sum(dsec * unit, axis=0, keepdims=True)
    vec_ref[1:2, :] += jnp.sum(dsec, axis=0, keepdims=True)
    vec_ref[2:3, :] += jnp.sum(dy32, axis=0, keepdims=True)
    gres = dy32 + norm_back(dsec, unit, inv, g2_ref[...])
    gres_ref[...] = gres
    branch = gres.astype(BF)
    gmix_ref[...] = mm_nt(branch, wout_ref[...]).astype(BF)
    wacc_ref[...] += mm_tn(mixed_ref[...], branch)

    @pl.when(at == last)
    def _():
        core, own = info_ref[0], info_ref[1]
        for i in range(count):
            permuted(grads[i], accs[i], tables, core ^ (i % 2), own)
            bgrads[i][...] = baccs[i][...]
        dwout_ref[...] = wacc_ref[...]


def ffn_rest(info, tables, second, dy, out_part, dsec_part, residual, mixed, bdown, g2, wout, chunks):
    n, width = second.shape
    count = len(chunks)
    units = chunks[0][0].shape[1]
    return call(
        functools.partial(ffn_rest_kernel, tables, count),
        "ffn_rest",
        (n // TOKS,),
        [rows_of(width)] * 6
        + [whole(1, width)] * 2
        + [whole(width, width)]
        + [whole(width + TILE, units)] * count
        + [whole(units, width)] * count,
        [rows_of(width)] * 3
        + [whole(8, width), whole(width, width)]
        + [whole(width, 2 * units)] * count
        + [whole(1, units)] * count,
        [
            jax.ShapeDtypeStruct((n, width), BF),
            jax.ShapeDtypeStruct((n, width), F32),
            jax.ShapeDtypeStruct((n, width), BF),
            jax.ShapeDtypeStruct((8, width), F32),
            jax.ShapeDtypeStruct((width, width), F32),
        ]
        + [jax.ShapeDtypeStruct((width, 2 * units), BF)] * count
        + [jax.ShapeDtypeStruct((1, units), F32)] * count,
        [pltpu.VMEM((width, 2 * units), F32)] * count
        + [pltpu.VMEM((1, units), F32)] * count
        + [pltpu.VMEM((width, width), F32)],
        info,
        (second, dy, out_part, dsec_part, residual, mixed, bdown, g2, wout)
        + tuple(c[0] for c in chunks)
        + tuple(c[1] for c in chunks),
    )


def attend_back_kernel(
    tables, info_ref, qkv_ref, prob_ref, gmix_ref, tok_ref, g1_ref, c1_ref, dwout_ref, grad_ref, dw_keep_ref, dw_send_ref,
    dqkv_ref, acc_ref,
):
    at, last = pl.program_id(0), pl.num_programs(0) - 1
    toks, width = tok_ref.shape
    rows, pairs, slots, _ = prob_ref.shape

    @pl.when(at == 0)
    def _():
        acc_ref[:, : 3 * width] = jnp.zeros((width, 3 * width), F32)
        acc_ref[:, 3 * width :] = dwout_ref[...]

    scale = HEAD ** (-0.5)
    for r in range(rows):
        span = slice(r * slots, (r + 1) * slots)
        for p in range(pairs):
            cols = slice(p * PAIR, (p + 1) * PAIR)
            kcols = slice(width + p * PAIR, width + (p + 1) * PAIR)
            vcols = slice(2 * width + p * PAIR, 2 * width + (p + 1) * PAIR)
            q = qkv_ref[span, cols]
            k = qkv_ref[span, kcols]
            v = qkv_ref[span, vcols]
            g = gmix_ref[span, cols]
            prob = prob_ref[r, p]
            dprob = mm_nt(g, by_head(v))
            p32 = prob.astype(F32)
            prod = p32 * dprob
            first = jnp.sum(prod[:, :slots], axis=-1, keepdims=True)
            second = jnp.sum(prod[:, slots:], axis=-1, keepdims=True)
            ds_a = (p32[:, :slots] * (dprob[:, :slots] - first)).astype(BF)
            ds_b = (p32[:, slots:] * (dprob[:, slots:] - second)).astype(BF)
            dqkv_ref[span, cols] = mm(jnp.concatenate([ds_a, ds_b], axis=1), by_head(k * scale)).astype(BF)
            dqkv_ref[span, kcols] = mm_tn(jnp.concatenate([ds_a, ds_b], axis=0), by_head(q * scale)).astype(BF)
            dqkv_ref[span, vcols] = mm_tn(
                jnp.concatenate([prob[:, :slots], prob[:, slots:]], axis=0), by_head(g)
            ).astype(BF)
    unit, _ = unit_parts(tok_ref[...].astype(F32))
    normed = (unit * g1_ref[...] + c1_ref[...]).astype(BF)
    acc_ref[:, : 3 * width] += mm_tn(normed, dqkv_ref[...])
    grad_ref[...] = dqkv_ref[...]

    @pl.when(at == last)
    def _():
        core, own = info_ref[0], info_ref[2]
        half = width // 2
        size = width // len(tables[0])
        for place in range(len(tables[0])):
            dst = dw_keep_ref if place * size < half else dw_send_ref
            block = block_at(place, tables, core, own)
            rows_at = pl.ds(pl.multiple_of(block * size, size), size)
            to = place * size % half
            dst[to : to + size, :] = acc_ref[rows_at, :].astype(BF)


def attend_back(info, tables, qkv, prob, gmix, tokens, g1, c1, dwout):
    n, width = tokens.shape
    rows, pairs, slots, _ = prob.shape
    per = TOKS // slots
    return call(
        functools.partial(attend_back_kernel, tables),
        "attend_back",
        (n // TOKS,),
        [
            rows_of(3 * width),
            pl.BlockSpec((per, pairs, slots, 2 * slots), lambda i, *_: (i, 0, 0, 0)),
            rows_of(width),
            rows_of(width),
            whole(1, width),
            whole(1, width),
            whole(width, width),
        ],
        [rows_of(3 * width)] + [whole(width // 2, 4 * width)] * 2,
        [jax.ShapeDtypeStruct((n, 3 * width), BF)] + [jax.ShapeDtypeStruct((width // 2, 4 * width), BF)] * 2,
        [pltpu.VMEM((TOKS, 3 * width), BF), pltpu.VMEM((width, 4 * width), F32)],
        info,
        (qkv, prob, gmix, tokens, g1, c1, dwout),
    )


def first_back_kernel(info_ref, dqkv_ref, wqkv_ref, tok_ref, gres_ref, g1_ref, vec_in_ref, out_ref, vec_ref):
    @pl.when(pl.program_id(0) == 0)
    def _():
        vec_ref[...] = vec_in_ref[...]

    dnormed = mm_nt(dqkv_ref[...], wqkv_ref[...])
    unit, inv = unit_parts(tok_ref[...].astype(F32))
    vec_ref[3:4, :] += jnp.sum(dnormed * unit, axis=0, keepdims=True)
    vec_ref[4:5, :] += jnp.sum(dnormed, axis=0, keepdims=True)
    out_ref[...] = gres_ref[...] + norm_back(dnormed, unit, inv, g1_ref[...])


def first_back(info, dqkv, wqkv, tokens, gres, g1, vec):
    n, width = tokens.shape
    return call(
        first_back_kernel,
        "first_back",
        (n // TOKS,),
        [rows_of(3 * width), whole(*wqkv.shape), rows_of(width), rows_of(width), whole(1, width), whole(*vec.shape)],
        [rows_of(width), whole(*vec.shape)],
        [jax.ShapeDtypeStruct((n, width), F32), jax.ShapeDtypeStruct(vec.shape, F32)],
        [],
        info,
        (dqkv, wqkv, tokens, gres, g1, vec),
    )


def ffn_end_kernel(tables, info_ref, keep_ref, other_ref, up_ref, down_ref, full_ref):
    core, own = info_ref[0], info_ref[1]
    units = up_ref.shape[1]
    blocks = len(tables[0])
    size = keep_ref.shape[0] // blocks

    def lay(src_ref, whose):
        for place in range(blocks):
            block = block_at(place, tables, whose, own)
            rows = pl.ds(pl.multiple_of(block * size, size), size)
            part = src_ref[place * size : (place + 1) * size, :].astype(F32)
            up_ref[rows, :] = part[:, :units]
            full_ref[rows, :] = part[:, units:]
        down_ref[...] = full_ref[...].T

    @pl.when(pl.program_id(0) == 0)
    def _():
        lay(keep_ref, core)

    @pl.when(pl.program_id(0) == 1)
    def _():
        lay(other_ref, core ^ 1)


def ffn_end(info, tables, keep, other):
    width, double = keep.shape
    units = double // 2
    return call(
        functools.partial(ffn_end_kernel, tables),
        "ffn_end",
        (2,),
        [whole(width, double)] * 2,
        [
            pl.BlockSpec((width, units), lambda i, info: (0, info[0] ^ i)),
            pl.BlockSpec((units, width), lambda i, info: (info[0] ^ i, 0)),
        ],
        [jax.ShapeDtypeStruct((width, double), F32), jax.ShapeDtypeStruct((double, width), F32)],
        [pltpu.VMEM((width, units), F32)],
        info,
        (keep, other),
    )


def attend_end_kernel(tables, info_ref, keep_ref, other_ref, qkv_ref, out_ref):
    core, own = info_ref[0], info_ref[2]
    width = out_ref.shape[1]
    blocks = len(tables[0])
    size = out_ref.shape[0] // blocks
    half = out_ref.shape[0] // 2
    for place in range(blocks):
        src = keep_ref if place * size < half else other_ref
        at = place * size % half
        block = block_at(place, tables, core, own)
        rows = pl.ds(pl.multiple_of(block * size, size), size)
        part = src[at : at + size, :].astype(F32)
        qkv_ref[rows, :] = part[:, : 3 * width]
        out_ref[rows, :] = part[:, 3 * width :]


def attend_end(info, tables, keep, other):
    rows, width = 2 * keep.shape[0], keep.shape[1] // 4
    return call(
        functools.partial(attend_end_kernel, tables),
        "attend_end",
        (1,),
        [whole(*keep.shape)] * 2,
        [whole(rows, 3 * width), whole(rows, width)],
        [jax.ShapeDtypeStruct((rows, 3 * width), F32), jax.ShapeDtypeStruct((rows, width), F32)],
        [],
        info,
        (keep, other),
    )


def local(
    wide, narrow, tokens_in, ln1_gain, ln1_bias, w_qkv, w_out, ln2_gain, ln2_bias, w_up, b_up, w_down, b_down, segment_ids,
    step_ids, pad_mask, cotangent,
):
    width = tokens_in.shape[1]
    units = w_up.shape[1] // 2
    core_mask = narrow
    narrow_masks = [1 << b for b in range(narrow.bit_length() - 1)]
    wide_masks = [narrow << b for b in range(1, wide.bit_length() - 1)]

    def swap(value, first, second=None):
        masks = (first, first if second is None else second)
        pairs = [(i, i ^ masks[i // narrow & 1]) for i in range(wide * narrow)]
        return lax.ppermute(value, AXES, pairs)

    def add(a, b):
        return (a.astype(F32) + b.astype(F32)).astype(a.dtype)

    def orders(masks):
        if len(masks) < 2:
            return (masks, masks)
        return (masks, [masks[1], masks[0]] + masks[2:])

    def scatter(value, order):
        for first, second in zip(*order):
            half = value.shape[0] // 2
            value = add(value[:half], swap(value[half:], first, second))
        return value

    def gather(value, order):
        for first, second in reversed(list(zip(*order))):
            value = jnp.concatenate([value, swap(value, first, second)], axis=0)
        return value

    wide_at, narrow_at = lax.axis_index("wide"), lax.axis_index("narrow")
    core = wide_at & 1
    flat = wide_at * narrow + narrow_at

    ff_order = orders(wide_masks)
    ff_tables = tuple([owner // (2 * narrow) for owner in places(o, wide // 2)] for o in ff_order)
    masks = narrow_masks + wide_masks
    split = min(len(masks), (width // TILE).bit_length() - 2)
    at_order = orders(masks[:split])
    at_rest = masks[split:]
    blocks = 1 << split
    near = [places(o, blocks) for o in at_order]
    used = [core_mask] + masks[:split]

    def named(owner):
        return sum((1 << b) for b, m in enumerate(used) if owner & m)

    at_tables = tuple(
        [named(o) for o in near[c]] + [named(o ^ core_mask) for o in near[1 - c]] for c in range(2)
    )
    own_block = sum((flat // m & 1) << b for b, m in enumerate(used))
    info = jnp.stack([core, wide_at // 2, own_block]).astype(jnp.int32)

    up_chunk = lax.dynamic_slice(w_up, (0, core * units), (width, units))
    bias_chunk = lax.dynamic_slice(b_up, (core * units,), (units,))
    up_chunk = jnp.concatenate([up_chunk, jnp.broadcast_to(bias_chunk[None], (TILE, units))], axis=0)
    down_chunk = lax.dynamic_slice(w_down, (core * units, 0), (units, width))
    fetched = [(up_chunk, down_chunk)]
    for mask in narrow_masks:
        fetched = fetched + [(swap(u, mask), swap(d, mask)) for u, d in fetched]
    chunks = []
    for up, down in fetched[1:]:
        chunks += [(up, down), (swap(up, core_mask), swap(down, core_mask))]

    row = lambda v: v[None].astype(F32)
    qkv, prob, mixed, residual, second = attend(
        info, tokens_in, row(ln1_gain), row(ln1_bias), w_qkv, w_out, row(ln2_gain), row(ln2_bias), segment_ids, step_ids, pad_mask
    )
    out_part, dsec_part, own_keep, own_send, bown_keep, bown_send = ffn_own(
        info, ff_tables, second, cotangent, w_up, b_up[None], w_down
    )
    rest = ffn_rest(
        info, ff_tables, second, cotangent, out_part, dsec_part, residual, mixed, row(b_down), row(ln2_gain), w_out, chunks
    )
    block_out, gres, gmix, vec, dwout = rest[:5]
    count = len(chunks)
    grads, bgrads = rest[5 : 5 + count], rest[5 + count :]

    held = [add(own_keep, swap(own_send, core_mask))]
    held += [add(grads[2 * j], swap(grads[2 * j + 1], core_mask)) for j in range(narrow - 1)]
    for mask in reversed(narrow_masks):
        held = [add(held[j], swap(held[j + mask], mask)) for j in range(mask)]
    ff_keep = gather(scatter(held[0], ff_order), ff_order)
    ff_other = swap(ff_keep, core_mask)
    grad_w_up, grad_w_down = ffn_end(info, ff_tables, ff_keep, ff_other)

    dqkv, keep, send = attend_back(
        info, at_tables, qkv, prob, gmix, tokens_in, row(ln1_gain), row(ln1_bias), dwout
    )
    keep = scatter(add(keep, swap(send, core_mask)), at_order)
    for mask in at_rest:
        keep = add(keep, swap(keep, mask))
    keep = gather(keep, at_order)
    grad_w_qkv, grad_w_out = attend_end(info, at_tables, keep, swap(keep, core_mask))

    grad_tokens, vec = first_back(info, dqkv, w_qkv, tokens_in, gres, row(ln1_gain), vec)

    b_parts = [(0, bown_keep, bown_send)] + [(j, bgrads[2 * j - 2], bgrads[2 * j - 1]) for j in range(1, narrow)]
    b_all = jnp.zeros((narrow, 2, units), F32)
    for j, mine, other in b_parts:
        both = jnp.where(core == 0, jnp.concatenate([mine, other], 0), jnp.concatenate([other, mine], 0))
        b_all = lax.dynamic_update_slice(b_all, both[None], (narrow_at ^ j, 0, 0))
    vec = jnp.concatenate([vec, b_all.reshape(-1, width)], axis=0)
    for mask in [core_mask] + masks:
        vec = vec + swap(vec, mask)
    b_sum = vec[8:].reshape(narrow, 2 * units)
    grad_b_up = lax.dynamic_slice(b_sum, (narrow_at, 0), (1, 2 * units))[0]
    return (
        block_out,
        grad_tokens,
        vec[3],
        vec[4],
        grad_w_qkv,
        grad_w_out,
        vec[0],
        vec[1],
        grad_w_up,
        grad_b_up,
        grad_w_down,
        vec[2],
    )


def solution(mesh):
    rows = P(("wide", "narrow"), None)
    in_specs = (
        rows, P(), P(), P(), P(), P(), P(), P(None, "narrow"), P("narrow"), P("narrow", None), P(), rows, rows, rows, rows,
    )
    out_specs = (
        rows, rows, P(), P(), P(), P(), P(), P(), P(None, "narrow"), P("narrow"), P("narrow", None), P(),
    )
    wide, narrow = mesh.shape["wide"], mesh.shape["narrow"]
    return jax.shard_map(
        functools.partial(local, wide, narrow), mesh=mesh, in_specs=in_specs, out_specs=out_specs, check_vma=False
    )
```

time: 488 us -> 211 us (0.43); the launches traced: 481 us -> 211 us
  waiting for transfers between devices: 235 us -> 93.1 us
  matrix products: 75.7 us -> 0 us
  blocking collectives: 73.4 us -> 0 us
  Pallas kernels: 0 us -> 72.6 us
  local copies, waits for them, and re-layouts: 57 us -> 6.38 us
  starting transfers between devices: 0.24 us -> 33.5 us
  other arithmetic: 24.9 us -> 3.94 us
  between operations: 14.8 us -> 1.14 us
    psum x2 -> x0, waiting for transfers between devices: 120 us -> none  [the longest x1 87.2 us: local(): lax.psum((grad_w_qkv, grad_w_out, jnp.sum(grad_normed * unit_one, axis=0)...]
    ppermute x0 -> x29, waiting for transfers between devices: none -> 93.1 us  [swap(): return lax.ppermute(value, AXES, pairs)]
    dot_general x18 -> x0, matrix products: 75.7 us -> none  [the longest x1 23.1 us: local(): jnp.dot(second_all, w_up, preferred_element_type=jnp.float32)]
    psum x2 -> x0, blocking collectives: 73.4 us -> none  [the longest x1 39.7 us: local(): lax.psum((grad_w_qkv, grad_w_out, jnp.sum(grad_normed * unit_one, axis=0)...]
    pallas_call x0 -> x7, Pallas kernels: none -> 72.6 us  [call(): pl.pallas_call(kernel, grid_spec=pltpu.PrefetchScalarGridSpec(num_scalar_...]
    reduce_scatter x2 -> x0, waiting for transfers between devices: 67.2 us -> none  [the longest x1 35.6 us: local(): lax.psum_scatter(dot_last(grad_pre, w_up), 'narrow', scatter_dimension=0,...]
    all_gather x2 -> x0, waiting for transfers between devices: 46.7 us -> none  [the longest x1 35.1 us: local(): second_all = lax.all_gather(second, 'narrow', axis=0, tiled=True)]
    ppermute x0 -> x29, starting transfers between devices: none -> 33.5 us  [swap(): return lax.ppermute(value, AXES, pairs)]
  transfers between devices with their start and end apart: 6 -> 29, of which waited for: 6 -> 18; matrix products, arithmetic and copies ran while one was open for 20% -> 4% of each run, Pallas kernels for 0% -> 16%
where the time goes in v1:
time: 211 us
  waiting for transfers between devices  93.1 us (44%)
  Pallas kernels  72.6 us (34%)
  starting transfers between devices  33.5 us (16%)
  local copies, waits for them, and re-layouts  6.38 us (3%)
  other arithmetic  3.94 us (2%)
    ppermute x29, waiting for transfers between devices, swap(): return lax.ppermute(value, AXES, pairs)  93.1 us
    pallas_call x7, Pallas kernels, call(): pl.pallas_call(kernel, grid_spec=pltpu.PrefetchScalarGridSpec(num_scalar_...  72.6 us
    ppermute x29, starting transfers between devices, swap(): return lax.ppermute(value, AXES, pairs)  33.5 us
  transfers between devices with their start and end apart: 29, of which 18 were waited for; matrix products, arithmetic and copies ran while one was open for 4% of the time, Pallas kernels for 16%

profile of v1, /device:TPU:0, one launch (start us, length us, event | category | flops | bytes accessed | tf_op | source)
XLA Modules:
  0.0 210.7 jit_solution(6743357181630567209)
XLA Ops:
  0.8 1.2 constant_dynamic-slice_fusion.2
  2.0 0.8 dynamic_slice.13
  2.8 3.0 %collective-permute-start = (bf16[528,512]{1,0:T(8,128)(2,1)S(1)}, bf16[528,512]{1,0:T(8,128)(2,1)S(1)}, u32[]{:S(2)}, u32[]{:S(2)}) collective-permute-start(bf16[528,512]{1,0:T(8,128)(2,1)S(1)} %pad_maximum_fusion.1), channel_id=1, source_target_pairs={{0,1},{1,0},{2,3},{3,2},{4,5},{5,4},{6,7},{7,6},{8,9},{9,8},{10,11... | collective-permute-start | bytes 1622024 | tf_op jit(solution)/shard_map/ppermute | solution.py:524
  6.0 13.0 %collective-permute-done.refs_0_ = bf16[528,512]{1,0:T(8,128)(2,1)S(1)} collective-permute-done((bf16[528,512]{1,0:T(8,128)(2,1)S(1)}, bf16[528,512]{1,0:T(8,128)(2,1)S(1)}, u32[]{:S(2)}, u32[]{:S(2)}) %collective-permute-start) | collective-permute-done | bytes 540704 | tf_op jit(solution)/shard_map/ppermute | solution.py:524
  18.9 10.4 %collective-permute-done.2.refs_2_ = bf16[512,512]{1,0:T(8,128)(2,1)S(1)} collective-permute-done((bf16[512,512]{1,0:T(8,128)(2,1)S(1)}, bf16[512,512]{1,0:T(8,128)(2,1)S(1)}, u32[]{:S(2)}, u32[]{:S(2)}) %collective-permute-start.2) | collective-permute-done | bytes 524320 | tf_op jit(solution)/shard_map/ppermute | solution.py:524
  29.5 10.7 %attend.1 = (bf16[1024,1536]{1,0:T(8,128)(2,1)}, bf16[8,4,128,256]{3,2,1,0:T(8,128)(2,1)}, bf16[1024,512]{1,0:T(8,128)(2,1)S(1)}, f32[1024,512]{1,0:T(8,128)}, bf16[1024,512]{1,0:T(8,128)(2,1)S(1)}) custom-call(s32[3]{0:T(128)S(1)} %pad_add_fusion.info_ref, bf16[1024,512]{1,0:T(8,128)(2,1)S(1)} %copy-done, f32[1,512]{1,0:T(1,128)S(1)} %bitcast.18, ...), custom_call_target="tpu_custom_call" | custom-call | tf_op jit(solution)/shard_map/attend/pallas_call | solution.py:43
  40.2 12.8 %ffn_own.1 = (f32[1024,512]{1,0:T(8,128)}, f32[1024,512]{1,0:T(8,128)}, bf16[512,1024]{1,0:T(8,128)(2,1)S(1)}, bf16[512,1024]{1,0:T(8,128)(2,1)S(1)}, f32[1,512]{1,0:T(1,128)S(1)}, /*index=5*/f32[1,512]{1,0:T(1,128)S(1)}) custom-call(s32[3]{0:T(128)S(1)} %pad_add_fusion.info_ref, bf16[1024,512]{1,0:T(8,128)(2,1)S(1)} %get-tuple-element.41.sec_ref, ...), custom_call_target="tpu_custom_call" | custom-call | tf_op jit(solution)/shard_map/ffn_own/pallas_call | solution.py:43
  53.1 16.6 %ffn_rest.1 = (bf16[1024,512]{1,0:T(8,128)(2,1)}, f32[1024,512]{1,0:T(8,128)}, bf16[1024,512]{1,0:T(8,128)(2,1)S(1)}, f32[8,512]{1,0:T(8,128)S(1)}, f32[512,512]...) custom-call(s32[3]{0:T(128)S(1)} %pad_add_fusion.info_ref, ...), custom_call_target="tpu_custom_call" | custom-call | tf_op jit(solution)/shard_map/ffn_rest/pallas_call | solution.py:43
  69.7 17.0 %attend_back.1 = (bf16[1024,1536]{1,0:T(8,128)(2,1)}, bf16[256,2048]{1,0:T(8,128)(2,1)S(1)}, bf16[256,2048]{1,0:T(8,128)(2,1)S(1)}) custom-call(s32[3]{0:T(128)S(1)} %pad_add_fusion.info_ref, bf16[1024,1536]{1,0:T(8,128)(2,1)} %get-tuple-element.47.qkv_ref, bf16[8,4,128,256]{3,2,1,0:T(8,128)(2,1)} %get-tuple-element.48.prob_ref, ...), custom_call_target="tpu_custom_call" | custom-call | tf_op jit(solution)/shard_map/attend_back/pallas_call | solution.py:43
  87.3 2.2 %collective-permute-done.9 = bf16[256,2048]{1,0:T(8,128)(2,1)S(1)} collective-permute-done((bf16[256,2048]{1,0:T(8,128)(2,1)S(1)}, bf16[256,2048]{1,0:T(8,128)(2,1)S(1)}, u32[]{:S(2)}, u32[]{:S(2)}) %collective-permute-start.9) | collective-permute-done | bytes 1048608 | tf_op jit(solution)/shard_map/ppermute | solution.py:524
  89.9 1.8 collective-permute-start.10
  92.3 1.6 collective-permute-start.21
  93.8 9.1 %collective-permute-done.10 = bf16[128,2048]{1,0:T(8,128)(2,1)S(1)} collective-permute-done((bf16[128,2048]{1,0:T(8,128)(2,1)S(1)}, bf16[128,2048]{1,0:T(8,128)(2,1)S(1)}, u32[]{:S(2)}, u32[]{:S(2)}) %collective-permute-start.10) | collective-permute-done | bytes 524320 | tf_op jit(solution)/shard_map/ppermute | solution.py:524
  103.1 2.1 collective-permute-start.11
  105.2 4.4 %collective-permute-done.11 = bf16[64,2048]{1,0:T(8,128)(2,1)S(1)} collective-permute-done((bf16[64,2048]{1,0:T(8,128)(2,1)S(1)}, bf16[64,2048]{1,0:T(8,128)(2,1)S(1)}, u32[]{:S(2)}, u32[]{:S(2)}) %collective-permute-start.11) | collective-permute-done | bytes 262176 | tf_op jit(solution)/shard_map/ppermute | solution.py:524
  109.6 2.1 collective-permute-start.12
  111.7 12.7 %collective-permute-done.21 = bf16[512,1024]{1,0:T(8,128)(2,1)S(1)} collective-permute-done((bf16[512,1024]{1,0:T(8,128)(2,1)S(1)}, bf16[512,1024]{1,0:T(8,128)(2,1)S(1)}, u32[]{:S(2)}, u32[]{:S(2)}) %collective-permute-start.21) | collective-permute-done | bytes 1048608 | tf_op jit(solution)/shard_map/ppermute | solution.py:524
  125.1 1.8 collective-permute-start.22
  127.0 2.6 %collective-permute-start.13 = (bf16[16,2048]{1,0:T(8,128)(2,1)S(1)}, bf16[16,2048]{1,0:T(8,128)(2,1)S(1)}, u32[]{:S(2)}, u32[]{:S(2)}) collective-permute-start(bf16[16,2048]{1,0:T(8,128)(2,1)S(1)} %slice.89), channel_id=1, source_target_pairs={{0,16},{1,17},{2,18},{3,19},{4,20},{5,21},{6,22},{7,23},{8,24},{9,... | collective-permute-start | bytes 196616 | tf_op jit(solution)/shard_map/ppermute | solution.py:524
  129.7 4.7 %collective-permute-done.22 = bf16[256,1024]{1,0:T(8,128)(2,1)S(1)} collective-permute-done((bf16[256,1024]{1,0:T(8,128)(2,1)S(1)}, bf16[256,1024]{1,0:T(8,128)(2,1)S(1)}, u32[]{:S(2)}, u32[]{:S(2)}) %collective-permute-start.22) | collective-permute-done | bytes 524320 | tf_op jit(solution)/shard_map/ppermute | solution.py:524
  134.6 1.9 collective-permute-start.23
  137.1 2.6 %collective-permute-start.14 = (bf16[16,2048]{1,0:T(8,128)(2,1)S(1)}, bf16[16,2048]{1,0:T(8,128)(2,1)S(1)}, u32[]{:S(2)}, u32[]{:S(2)}) collective-permute-start(bf16[16,2048]{1,0:T(8,128)(2,1)S(1)} %get-tuple-element.71), channel_id=1, source_target_pairs={{0,16},{1,17},{2,18},{3,19},{4,20},{5,21},{6,22},{7,23},{8,24},{9,... | collective-permute-start | bytes 196616 | tf_op jit(solution)/shard_map/ppermute | solution.py:524
  139.7 1.9 collective-permute-done.23
  141.7 3.0 %collective-permute-start.24 = (bf16[64,1024]{1,0:T(8,128)(2,1)S(1)}, bf16[64,1024]{1,0:T(8,128)(2,1)S(1)}, u32[]{:S(2)}, u32[]{:S(2)}) collective-permute-start(bf16[64,1024]{1,0:T(8,128)(2,1)S(1)} %slice.97), channel_id=1, source_target_pairs={{0,16},{1,17},{2,18},{3,19},{4,20},{5,21},{6,22},{7,23},{8,24},{9,... | collective-permute-start | bytes 393224 | tf_op jit(solution)/shard_map/ppermute | solution.py:524
  144.8 1.7 collective-permute-start.15
  146.5 3.9 %collective-permute-done.24 = bf16[64,1024]{1,0:T(8,128)(2,1)S(1)} collective-permute-done((bf16[64,1024]{1,0:T(8,128)(2,1)S(1)}, bf16[64,1024]{1,0:T(8,128)(2,1)S(1)}, u32[]{:S(2)}, u32[]{:S(2)}) %collective-permute-start.24) | collective-permute-done | bytes 131104 | tf_op jit(solution)/shard_map/ppermute | solution.py:524
  150.4 0.8 collective-permute-start.25
  151.2 1.6 collective-permute-start.16
  152.8 5.8 %collective-permute-done.25 = bf16[64,1024]{1,0:T(8,128)(2,1)S(1)} collective-permute-done((bf16[64,1024]{1,0:T(8,128)(2,1)S(1)}, bf16[64,1024]{1,0:T(8,128)(2,1)S(1)}, u32[]{:S(2)}, u32[]{:S(2)}) %collective-permute-start.25) | collective-permute-done | bytes 131104 | tf_op jit(solution)/shard_map/ppermute | solution.py:524
  159.4 0.8 collective-permute-start.17
  160.2 4.8 %collective-permute-done.26 = bf16[128,1024]{1,0:T(8,128)(2,1)S(1)} collective-permute-done((bf16[128,1024]{1,0:T(8,128)(2,1)S(1)}, bf16[128,1024]{1,0:T(8,128)(2,1)S(1)}, u32[]{:S(2)}, u32[]{:S(2)}) %collective-permute-start.26) | collective-permute-done | bytes 262176 | tf_op jit(solution)/shard_map/ppermute | solution.py:524
  165.1 0.9 collective-permute-start.27
  166.6 0.7 constant_dynamic-update-slice_fusion.3
  167.4 1.3 collective-permute-done.17
  168.6 0.8 constant_dynamic-update-slice_fusion.2.keep_ref
  169.5 1.1 collective-permute-start.18
  170.5 4.3 %collective-permute-done.27 = bf16[256,1024]{1,0:T(8,128)(2,1)S(1)} collective-permute-done((bf16[256,1024]{1,0:T(8,128)(2,1)S(1)}, bf16[256,1024]{1,0:T(8,128)(2,1)S(1)}, u32[]{:S(2)}, u32[]{:S(2)}) %collective-permute-start.27) | collective-permute-done | bytes 524320 | tf_op jit(solution)/shard_map/ppermute | solution.py:524
  174.8 1.0 pad_maximum_fusion.keep_ref
  175.9 6.5 %first_back.1 = (f32[1024,512]{1,0:T(8,128)}, f32[8,512]{1,0:T(8,128)S(1)}) custom-call(s32[3]{0:T(128)S(1)} %pad_add_fusion.info_ref, bf16[1024,1536]{1,0:T(8,128)(2,1)} %get-tuple-element.51.dqkv_ref, bf16[512,1536]{1,0:T(8,128)(2,1)S(1)} %copy-done.2, bf16[1024,512]{1,0:T(8,128)(2,1)S(1)} %copy-done.1, f32[1024,512]{1,0:T(8,128)} %get-tuple-element.52.gres_ref, ...), custom_call_target="tpu_custom_call" | custom-call | tf_op jit(solution)/shard_map/first_back/pallas_call | solution.py:43
  183.0 0.9 collective-permute-done.4
  183.9 1.9 collective-permute-start.5
  185.8 2.0 collective-permute-done.5
  187.8 0.8 collective-permute-start.6
  188.6 3.1 %collective-permute-done.6 = f32[12,512]{1,0:T(8,128)S(1)} collective-permute-done((f32[12,512]{1,0:T(8,128)S(1)}, f32[12,512]{1,0:T(8,128)S(1)}, u32[]{:S(2)}, u32[]{:S(2)}) %collective-permute-start.6) | collective-permute-done | bytes 24608 | tf_op jit(solution)/shard_map/ppermute | solution.py:524
  191.7 3.9 %collective-permute-done.7 = f32[12,512]{1,0:T(8,128)S(1)} collective-permute-done((f32[12,512]{1,0:T(8,128)S(1)}, f32[12,512]{1,0:T(8,128)S(1)}, u32[]{:S(2)}, u32[]{:S(2)}) %collective-permute-start.7) | collective-permute-done | bytes 24608 | tf_op jit(solution)/shard_map/ppermute | solution.py:524
  195.7 4.8 %collective-permute-done.8 = f32[12,512]{1,0:T(8,128)S(1)} collective-permute-done((f32[12,512]{1,0:T(8,128)S(1)}, f32[12,512]{1,0:T(8,128)S(1)}, u32[]{:S(2)}, u32[]{:S(2)}) %collective-permute-start.8) | collective-permute-done | bytes 24608 | tf_op jit(solution)/shard_map/ppermute | solution.py:524
  201.7 4.4 %attend_end.1 = (f32[512,1536]{1,0:T(8,128)}, f32[512,512]{1,0:T(8,128)}) custom-call(s32[3]{0:T(128)S(1)} %pad_add_fusion.info_ref, bf16[256,2048]{1,0:T(8,128)(2,1)} %constant_dynamic-update-slice_fusion.2.keep_ref, bf16[256,2048]{1,0:T(8,128)(2,1)} %collective-permute-done.18.other_ref), custom_call_target="tpu_custom_call" | custom-call | tf_op jit(solution)/shard_map/attend_end/pallas_call | solution.py:43
  206.1 4.6 %ffn_end.1 = (f32[512,1024]{1,0:T(8,128)}, f32[1024,512]{1,0:T(8,128)}) custom-call(s32[3]{0:T(128)S(1)} %pad_add_fusion.info_ref, bf16[512,1024]{1,0:T(8,128)(2,1)} %pad_maximum_fusion.keep_ref, bf16[512,1024]{1,0:T(8,128)(2,1)} %collective-permute-done.28.other_ref), custom_call_target="tpu_custom_call" | custom-call | tf_op jit(solution)/shard_map/ffn_end/pallas_call | solution.py:43
  (102 shorter events, 7.1 us)
Async XLA Ops:
  0.6 28.7 %copy-start.16 = (bf16[1024]{0:T(1024)(128)(2,1)S(1)}, bf16[1024]{0:T(1024)(128)(2,1)}, u32[]{:S(2)}) copy-start(bf16[1024]{0:T(1024)(128)(2,1)} %param.23) | copy-start | bytes 6148
  0.7 5.2 %copy-start.14 = (bf16[1024,512]{1,0:T(8,128)(2,1)S(1)}, bf16[1024,512]{1,0:T(8,128)(2,1)}, u32[]{:S(2)}) copy-start(bf16[1024,512]{1,0:T(8,128)(2,1)} %refs_5_.1) | copy-start | bytes 3145732
  0.7 28.8 %copy-start.6 = (f32[512]{0:T(512)S(1)}, f32[512]{0:T(512)}, u32[]{:S(2)}) copy-start(f32[512]{0:T(512)} %param.16) | copy-start | bytes 6148
  0.7 28.8 %copy-start.8 = (f32[512]{0:T(512)S(1)}, f32[512]{0:T(512)}, u32[]{:S(2)}) copy-start(f32[512]{0:T(512)} %param.17) | copy-start | bytes 6148
  0.7 28.8 %copy-start.7 = (f32[512]{0:T(512)S(1)}, f32[512]{0:T(512)}, u32[]{:S(2)}) copy-start(f32[512]{0:T(512)} %param.20) | copy-start | bytes 6148
  0.7 28.8 %copy-start.12 = (f32[512]{0:T(512)S(1)}, f32[512]{0:T(512)}, u32[]{:S(2)}) copy-start(f32[512]{0:T(512)} %param.21) | copy-start | bytes 6148
  0.7 28.8 %copy-start = (bf16[1024,512]{1,0:T(8,128)(2,1)S(1)}, bf16[1024,512]{1,0:T(8,128)(2,1)}, u32[]{:S(2)}) copy-start(bf16[1024,512]{1,0:T(8,128)(2,1)} %tok_ref.5) | copy-start | bytes 3145732
  0.7 28.8 %copy-start.4 = (bf16[512,512]{1,0:T(8,128)(2,1)S(1)}, bf16[512,512]{1,0:T(8,128)(2,1)}, u32[]{:S(2)}) copy-start(bf16[512,512]{1,0:T(8,128)(2,1)} %wout_ref.3) | copy-start | bytes 1572868
  0.7 28.8 %copy-start.9 = (s32[8,128]{1,0:T(8,128)S(1)}, s32[8,128]{1,0:T(8,128)}, u32[]{:S(2)}) copy-start(s32[8,128]{1,0:T(8,128)} %seg_ref.1) | copy-start | bytes 12292
  0.7 28.8 %copy-start.10 = (s32[8,128]{1,0:T(8,128)S(1)}, s32[8,128]{1,0:T(8,128)}, u32[]{:S(2)}) copy-start(s32[8,128]{1,0:T(8,128)} %step_ref.1) | copy-start | bytes 12292
  0.8 28.8 %copy-start.11 = (s32[8,128]{1,0:T(8,128)S(1)}, s32[8,128]{1,0:T(8,128)}, u32[]{:S(2)}) copy-start(s32[8,128]{1,0:T(8,128)} %pad_ref.1) | copy-start | bytes 12292
  2.8 16.1 %collective-permute-start = (bf16[528,512]{1,0:T(8,128)(2,1)S(1)}, bf16[528,512]{1,0:T(8,128)(2,1)S(1)}, u32[]{:S(2)}, u32[]{:S(2)}) collective-permute-start(bf16[528,512]{1,0:T(8,128)(2,1)S(1)} %pad_maximum_fusion.1), channel_id=1, source_target_pairs={{0,1},{1,0},{2,3},{3,2},{4,5},{5,4},{6,7},{7,6},{8,9},{9,8},{10,11... | collective-permute-start | bytes 1622024 | tf_op jit(solution)/shard_map/ppermute | solution.py:524
  5.9 23.5 %collective-permute-start.2 = (bf16[512,512]{1,0:T(8,128)(2,1)S(1)}, bf16[512,512]{1,0:T(8,128)(2,1)S(1)}, u32[]{:S(2)}, u32[]{:S(2)}) collective-permute-start(bf16[512,512]{1,0:T(8,128)(2,1)S(1)} %constant_dynamic-slice_fusion.1), channel_id=1, source_target_pairs={{0,1},{1,0},{2,3},{3,2},{4,5},{5,4},{6,7},{7,6},{8,9},{9,8},{10,11... | collective-permute-start | bytes 1572872 | tf_op jit(solution)/shard_map/ppermute | solution.py:524
  18.9 34.1 %collective-permute-start.1 = (bf16[528,512]{1,0:T(8,128)(2,1)S(1)}, bf16[528,512]{1,0:T(8,128)(2,1)S(1)}, u32[]{:S(2)}, u32[]{:S(2)}) collective-permute-start(bf16[528,512]{1,0:T(8,128)(2,1)S(1)} %collective-permute-done.refs_0_), channel_id=1, source_target_pairs={{0,2},{1,3},{2,0},{3,1},{4,6},{5,7},{6,4},{7,5},{8,10},{9,11},{10,... | collective-permute-start | bytes 1622024 | tf_op jit(solution)/shard_map/ppermute | solution.py:524
  29.3 23.7 %collective-permute-start.3 = (bf16[512,512]{1,0:T(8,128)(2,1)S(1)}, bf16[512,512]{1,0:T(8,128)(2,1)}, u32[]{:S(2)}, u32[]{:S(2)}) collective-permute-start(bf16[512,512]{1,0:T(8,128)(2,1)S(1)} %collective-permute-done.2.refs_2_), channel_id=1, source_target_pairs={{0,2},{1,3},{2,0},{3,1},{4,6},{5,7},{6,4},{7,5},{8,10},{9,11},{10,... | collective-permute-start | bytes 1572872 | tf_op jit(solution)/shard_map/ppermute | solution.py:524
  40.2 12.8 %copy-start.3 = (bf16[1024,512]{1,0:T(8,128)(2,1)}, bf16[1024,512]{1,0:T(8,128)(2,1)S(1)}, u32[]{:S(2)}) copy-start(bf16[1024,512]{1,0:T(8,128)(2,1)S(1)} %get-tuple-element.41.sec_ref) | copy-start | bytes 3145732
  40.2 12.8 %copy-start.5 = (bf16[1024,512]{1,0:T(8,128)(2,1)}, bf16[1024,512]{1,0:T(8,128)(2,1)S(1)}, u32[]{:S(2)}) copy-start(bf16[1024,512]{1,0:T(8,128)(2,1)S(1)} %get-tuple-element.45.mixed_ref) | copy-start | bytes 3145732
  40.2 12.8 %copy-start.13 = (f32[512]{0:T(512)S(1)}, f32[512]{0:T(512)}, u32[]{:S(2)}) copy-start(f32[512]{0:T(512)} %param.25) | copy-start | bytes 6148
  69.7 17.5 %copy-start.17 = (bf16[512,1024]{1,0:T(8,128)(2,1)S(1)}, bf16[512,1024]{1,0:T(8,128)(2,1)}, u32[]{:S(2)}) copy-start(bf16[512,1024]{1,0:T(8,128)(2,1)} %get-tuple-element.67) | copy-start | bytes 3145732
  86.7 2.7 %collective-permute-start.9 = (bf16[256,2048]{1,0:T(8,128)(2,1)S(1)}, bf16[256,2048]{1,0:T(8,128)(2,1)S(1)}, u32[]{:S(2)}, u32[]{:S(2)}) collective-permute-start(bf16[256,2048]{1,0:T(8,128)(2,1)S(1)} %get-tuple-element.61), channel_id=1, source_target_pairs={{0,2},{1,3},{2,0},{3,1},{4,6},{5,7},{6,4},{7,5},{8,10},{9,11},{10,... | collective-permute-start | bytes 3145736 | tf_op jit(solution)/shard_map/ppermute | solution.py:524
  87.2 4.6 %collective-permute-start.20 = (bf16[512,1024]{1,0:T(8,128)(2,1)S(1)}, bf16[512,1024]{1,0:T(8,128)(2,1)S(1)}, u32[]{:S(2)}, u32[]{:S(2)}) collective-permute-start(bf16[512,1024]{1,0:T(8,128)(2,1)S(1)} %copy-done.17), channel_id=1, source_target_pairs={{0,2},{1,3},{2,0},{3,1},{4,6},{5,7},{6,4},{7,5},{8,10},{9,11},{10,... | collective-permute-start | bytes 3145736 | tf_op jit(solution)/shard_map/ppermute | solution.py:524
  89.5 2.4 %copy-start.15 = (bf16[512,1024]{1,0:T(8,128)(2,1)S(1)}, bf16[512,1024]{1,0:T(8,128)(2,1)}, u32[]{:S(2)}) copy-start(bf16[512,1024]{1,0:T(8,128)(2,1)} %get-tuple-element.66) | copy-start | bytes 3145732
  89.9 13.0 %collective-permute-start.10 = (bf16[128,2048]{1,0:T(8,128)(2,1)S(1)}, bf16[128,2048]{1,0:T(8,128)(2,1)S(1)}, u32[]{:S(2)}, u32[]{:S(2)}) collective-permute-start(bf16[128,2048]{1,0:T(8,128)(2,1)S(1)} %slice.83), channel_id=1, source_target_pairs={{0,1},{1,0},{2,6},{3,7},{4,5},{5,4},{6,2},{7,3},{8,9},{9,8},{10,14... | collective-permute-start | bytes 1572872 | tf_op jit(solution)/shard_map/ppermute | solution.py:524
  91.7 20.0 %collective-permute-start.19 = (bf16[512,1024]{1,0:T(8,128)(2,1)S(1)}, bf16[512,1024]{1,0:T(8,128)(2,1)S(1)}, u32[]{:S(2)}, u32[]{:S(2)}) collective-permute-start(bf16[512,1024]{1,0:T(8,128)(2,1)S(1)} %get-tuple-element.65), channel_id=1, source_target_pairs={{0,2},{1,3},{2,0},{3,1},{4,6},{5,7},{6,4},{7,5},{8,10},{9,11},{10,... | collective-permute-start | bytes 3145736 | tf_op jit(solution)/shard_map/ppermute | solution.py:524
  92.3 32.2 %collective-permute-start.21 = (bf16[512,1024]{1,0:T(8,128)(2,1)S(1)}, bf16[512,1024]{1,0:T(8,128)(2,1)S(1)}, u32[]{:S(2)}, u32[]{:S(2)}) collective-permute-start(bf16[512,1024]{1,0:T(8,128)(2,1)S(1)} %add_convert_fusion.1), channel_id=1, source_target_pairs={{0,1},{1,0},{2,3},{3,2},{4,5},{5,4},{6,7},{7,6},{8,9},{9,8},{10,11... | collective-permute-start | bytes 3145736 | tf_op jit(solution)/shard_map/ppermute | solution.py:524
  103.1 6.4 %collective-permute-start.11 = (bf16[64,2048]{1,0:T(8,128)(2,1)S(1)}, bf16[64,2048]{1,0:T(8,128)(2,1)S(1)}, u32[]{:S(2)}, u32[]{:S(2)}) collective-permute-start(bf16[64,2048]{1,0:T(8,128)(2,1)S(1)} %slice.85), channel_id=1, source_target_pairs={{0,4},{1,5},{2,3},{3,2},{4,0},{5,1},{6,7},{7,6},{8,12},{9,13},{10,... | collective-permute-start | bytes 786440 | tf_op jit(solution)/shard_map/ppermute | solution.py:524
  109.6 17.3 %collective-permute-start.12 = (bf16[32,2048]{1,0:T(8,128)(2,1)S(1)}, bf16[32,2048]{1,0:T(8,128)(2,1)S(1)}, u32[]{:S(2)}, u32[]{:S(2)}) collective-permute-start(bf16[32,2048]{1,0:T(8,128)(2,1)S(1)} %slice.87), channel_id=1, source_target_pairs={{0,8},{1,9},{2,10},{3,11},{4,12},{5,13},{6,14},{7,15},{8,0},{9,1},... | collective-permute-start | bytes 393224 | tf_op jit(solution)/shard_map/ppermute | solution.py:524
  125.1 9.2 %collective-permute-start.22 = (bf16[256,1024]{1,0:T(8,128)(2,1)S(1)}, bf16[256,1024]{1,0:T(8,128)(2,1)S(1)}, u32[]{:S(2)}, u32[]{:S(2)}) collective-permute-start(bf16[256,1024]{1,0:T(8,128)(2,1)S(1)} %slice.93), channel_id=1, source_target_pairs={{0,4},{1,5},{2,10},{3,11},{4,0},{5,1},{6,14},{7,15},{8,12},{9,13},... | collective-permute-start | bytes 1572872 | tf_op jit(solution)/shard_map/ppermute | solution.py:524
  127.0 9.5 %collective-permute-start.13 = (bf16[16,2048]{1,0:T(8,128)(2,1)S(1)}, bf16[16,2048]{1,0:T(8,128)(2,1)S(1)}, u32[]{:S(2)}, u32[]{:S(2)}) collective-permute-start(bf16[16,2048]{1,0:T(8,128)(2,1)S(1)} %slice.89), channel_id=1, source_target_pairs={{0,16},{1,17},{2,18},{3,19},{4,20},{5,21},{6,22},{7,23},{8,24},{9,... | collective-permute-start | bytes 196616 | tf_op jit(solution)/shard_map/ppermute | solution.py:524
  134.6 7.0 %collective-permute-start.23 = (bf16[128,1024]{1,0:T(8,128)(2,1)S(1)}, bf16[128,1024]{1,0:T(8,128)(2,1)S(1)}, u32[]{:S(2)}, u32[]{:S(2)}) collective-permute-start(bf16[128,1024]{1,0:T(8,128)(2,1)S(1)} %slice.95), channel_id=1, source_target_pairs={{0,8},{1,9},{2,6},{3,7},{4,12},{5,13},{6,2},{7,3},{8,0},{9,1},{10,... | collective-permute-start | bytes 786440 | tf_op jit(solution)/shard_map/ppermute | solution.py:524
  137.1 7.6 %collective-permute-start.14 = (bf16[16,2048]{1,0:T(8,128)(2,1)S(1)}, bf16[16,2048]{1,0:T(8,128)(2,1)S(1)}, u32[]{:S(2)}, u32[]{:S(2)}) collective-permute-start(bf16[16,2048]{1,0:T(8,128)(2,1)S(1)} %get-tuple-element.71), channel_id=1, source_target_pairs={{0,16},{1,17},{2,18},{3,19},{4,20},{5,21},{6,22},{7,23},{8,24},{9,... | collective-permute-start | bytes 196616 | tf_op jit(solution)/shard_map/ppermute | solution.py:524
  141.7 8.6 %collective-permute-start.24 = (bf16[64,1024]{1,0:T(8,128)(2,1)S(1)}, bf16[64,1024]{1,0:T(8,128)(2,1)S(1)}, u32[]{:S(2)}, u32[]{:S(2)}) collective-permute-start(bf16[64,1024]{1,0:T(8,128)(2,1)S(1)} %slice.97), channel_id=1, source_target_pairs={{0,16},{1,17},{2,18},{3,19},{4,20},{5,21},{6,22},{7,23},{8,24},{9,... | collective-permute-start | bytes 393224 | tf_op jit(solution)/shard_map/ppermute | solution.py:524
  144.8 6.5 %collective-permute-start.15 = (bf16[32,2048]{1,0:T(8,128)(2,1)S(1)}, bf16[32,2048]{1,0:T(8,128)(2,1)S(1)}, u32[]{:S(2)}, u32[]{:S(2)}) collective-permute-start(bf16[32,2048]{1,0:T(8,128)(2,1)S(1)} %pad_maximum_fusion.6), channel_id=1, source_target_pairs={{0,8},{1,9},{2,10},{3,11},{4,12},{5,13},{6,14},{7,15},{8,0},{9,1},... | collective-permute-start | bytes 393224 | tf_op jit(solution)/shard_map/ppermute | solution.py:524
  150.4 8.2 %collective-permute-start.25 = (bf16[64,1024]{1,0:T(8,128)(2,1)S(1)}, bf16[64,1024]{1,0:T(8,128)(2,1)S(1)}, u32[]{:S(2)}, u32[]{:S(2)}) collective-permute-start(bf16[64,1024]{1,0:T(8,128)(2,1)S(1)} %add_convert_fusion.8), channel_id=1, source_target_pairs={{0,16},{1,17},{2,18},{3,19},{4,20},{5,21},{6,22},{7,23},{8,24},{9,... | collective-permute-start | bytes 393224 | tf_op jit(solution)/shard_map/ppermute | solution.py:524
  151.2 8.1 %collective-permute-start.16 = (bf16[64,2048]{1,0:T(8,128)(2,1)S(1)}, bf16[64,2048]{1,0:T(8,128)(2,1)S(1)}, u32[]{:S(2)}, u32[]{:S(2)}) collective-permute-start(bf16[64,2048]{1,0:T(8,128)(2,1)S(1)} %pad_maximum_fusion.4), channel_id=1, source_target_pairs={{0,4},{1,5},{2,3},{3,2},{4,0},{5,1},{6,7},{7,6},{8,12},{9,13},{10,... | collective-permute-start | bytes 786440 | tf_op jit(solution)/shard_map/ppermute | solution.py:524
  158.6 6.4 %collective-permute-start.26 = (bf16[128,1024]{1,0:T(8,128)(2,1)S(1)}, bf16[128,1024]{1,0:T(8,128)(2,1)S(1)}, u32[]{:S(2)}, u32[]{:S(2)}) collective-permute-start(bf16[128,1024]{1,0:T(8,128)(2,1)S(1)} %pad_maximum_fusion.5), channel_id=1, source_target_pairs={{0,8},{1,9},{2,6},{3,7},{4,12},{5,13},{6,2},{7,3},{8,0},{9,1},{10,... | collective-permute-start | bytes 786440 | tf_op jit(solution)/shard_map/ppermute | solution.py:524
  159.4 9.2 %collective-permute-start.17 = (bf16[128,2048]{1,0:T(8,128)(2,1)S(1)}, bf16[128,2048]{1,0:T(8,128)(2,1)S(1)}, u32[]{:S(2)}, u32[]{:S(2)}) collective-permute-start(bf16[128,2048]{1,0:T(8,128)(2,1)S(1)} %pad_maximum_fusion.2), channel_id=1, source_target_pairs={{0,1},{1,0},{2,6},{3,7},{4,5},{5,4},{6,2},{7,3},{8,9},{9,8},{10,14... | collective-permute-start | bytes 1572872 | tf_op jit(solution)/shard_map/ppermute | solution.py:524
  165.1 10.8 %copy-start.1 = (bf16[1024,512]{1,0:T(8,128)(2,1)S(1)}, bf16[1024,512]{1,0:T(8,128)(2,1)}, u32[]{:S(2)}) copy-start(bf16[1024,512]{1,0:T(8,128)(2,1)} %tok_ref.5) | copy-start | bytes 3145732
  165.1 10.8 %copy-start.2 = (bf16[512,1536]{1,0:T(8,128)(2,1)S(1)}, bf16[512,1536]{1,0:T(8,128)(2,1)}, u32[]{:S(2)}) copy-start(bf16[512,1536]{1,0:T(8,128)(2,1)} %wqkv_ref.3) | copy-start | bytes 4718596
  165.1 9.7 %collective-permute-start.27 = (bf16[256,1024]{1,0:T(8,128)(2,1)S(1)}, bf16[256,1024]{1,0:T(8,128)(2,1)S(1)}, u32[]{:S(2)}, u32[]{:S(2)}) collective-permute-start(bf16[256,1024]{1,0:T(8,128)(2,1)S(1)} %pad_maximum_fusion.3), channel_id=1, source_target_pairs={{0,4},{1,5},{2,10},{3,11},{4,0},{5,1},{6,14},{7,15},{8,12},{9,13},... | collective-permute-start | bytes 1572872 | tf_op jit(solution)/shard_map/ppermute | solution.py:524
  169.5 32.3 %collective-permute-start.18 = (bf16[256,2048]{1,0:T(8,128)(2,1)}, bf16[256,2048]{1,0:T(8,128)(2,1)}, u32[]{:S(2)}, u32[]{:S(2)}) collective-permute-start(bf16[256,2048]{1,0:T(8,128)(2,1)} %constant_dynamic-update-slice_fusion.2.keep_ref), channel_id=1, source_target_pairs={{0,2},{1,3},{2,0},{3,1},{4,6},{5,7},{6,4},{7,5},{8,10},{9,11},{10,... | collective-permute-start | bytes 3145736 | tf_op jit(solution)/shard_map/ppermute | solution.py:524
  175.8 30.2 %collective-permute-start.28 = (bf16[512,1024]{1,0:T(8,128)(2,1)}, bf16[512,1024]{1,0:T(8,128)(2,1)}, u32[]{:S(2)}, u32[]{:S(2)}) collective-permute-start(bf16[512,1024]{1,0:T(8,128)(2,1)} %pad_maximum_fusion.keep_ref), channel_id=1, source_target_pairs={{0,2},{1,3},{2,0},{3,1},{4,6},{5,7},{6,4},{7,5},{8,10},{9,11},{10,... | collective-permute-start | bytes 3145736 | tf_op jit(solution)/shard_map/ppermute | solution.py:524
  182.4 1.4 collective-permute-start.4
  183.9 3.9 %collective-permute-start.5 = (f32[12,512]{1,0:T(8,128)S(1)}, f32[12,512]{1,0:T(8,128)S(1)}, u32[]{:S(2)}, u32[]{:S(2)}) collective-permute-start(f32[12,512]{1,0:T(8,128)S(1)} %add.89), channel_id=1, source_target_pairs={{0,1},{1,0},{2,3},{3,2},{4,5},{5,4},{6,7},{7,6},{8,9},{9,8},{10,11... | collective-permute-start | bytes 73736 | tf_op jit(solution)/shard_map/ppermute | solution.py:524
  187.8 3.9 %collective-permute-start.6 = (f32[12,512]{1,0:T(8,128)S(1)}, f32[12,512]{1,0:T(8,128)S(1)}, u32[]{:S(2)}, u32[]{:S(2)}) collective-permute-start(f32[12,512]{1,0:T(8,128)S(1)} %add.90), channel_id=1, source_target_pairs={{0,4},{1,5},{2,6},{3,7},{4,0},{5,1},{6,2},{7,3},{8,12},{9,13},{10,... | collective-permute-start | bytes 73736 | tf_op jit(solution)/shard_map/ppermute | solution.py:524
  191.7 3.9 %collective-permute-start.7 = (f32[12,512]{1,0:T(8,128)S(1)}, f32[12,512]{1,0:T(8,128)S(1)}, u32[]{:S(2)}, u32[]{:S(2)}) collective-permute-start(f32[12,512]{1,0:T(8,128)S(1)} %add.91), channel_id=1, source_target_pairs={{0,8},{1,9},{2,10},{3,11},{4,12},{5,13},{6,14},{7,15},{8,0},{9,1},... | collective-permute-start | bytes 73736 | tf_op jit(solution)/shard_map/ppermute | solution.py:524
  195.7 4.8 %collective-permute-start.8 = (f32[12,512]{1,0:T(8,128)S(1)}, f32[12,512]{1,0:T(8,128)S(1)}, u32[]{:S(2)}, u32[]{:S(2)}) collective-permute-start(f32[12,512]{1,0:T(8,128)S(1)} %add.92), channel_id=1, source_target_pairs={{0,16},{1,17},{2,18},{3,19},{4,20},{5,21},{6,22},{7,23},{8,24},{9,... | collective-permute-start | bytes 73736 | tf_op jit(solution)/shard_map/ppermute | solution.py:524

commit v2 on v1

--- a/solution.py
+++ b/solution.py
@@ -14,6 +14,8 @@
 BF = jnp.bfloat16
 F32 = jnp.float32
 AXES = ("wide", "narrow")
+LANES = 128
+SUMS = 8
 TILE = 16
 TOKS = 256
 VMEM_LIMIT = 50 * 1024 * 1024
@@ -47,6 +49,7 @@
         ),
         out_shape=out_shape,
         compiler_params=pltpu.CompilerParams(vmem_limit_bytes=VMEM_LIMIT),
+        cost_estimate=pl.CostEstimate(flops=1000, bytes_accessed=1000, transcendentals=0),
         name=name,
     )(info, *args)
 
@@ -328,8 +331,8 @@
 
 
 def attend_back_kernel(
-    tables, info_ref, qkv_ref, prob_ref, gmix_ref, tok_ref, g1_ref, c1_ref, dwout_ref, grad_ref, dw_keep_ref, dw_send_ref,
-    dqkv_ref, acc_ref,
+    tables, info_ref, qkv_ref, prob_ref, gmix_ref, tok_ref, vec_ref, dwout_ref, grad_ref, dw_keep_ref, dw_send_ref,
+    dqkv_ref, acc_ref, row_ref,
 ):
     at, last = pl.program_id(0), pl.num_programs(0) - 1
     toks, width = tok_ref.shape
@@ -338,7 +341,9 @@
     @pl.when(at == 0)
     def _():
         acc_ref[:, : 3 * width] = jnp.zeros((width, 3 * width), F32)
-        acc_ref[:, 3 * width :] = dwout_ref[...]
+        acc_ref[:, 3 * width : 4 * width] = dwout_ref[...]
+        row_ref[...] = jnp.zeros_like(row_ref)
+        row_ref[SUMS : SUMS + vec_ref.shape[0], :] = vec_ref[...]
 
     scale = HEAD ** (-0.5)
     for r in range(rows):
@@ -365,13 +370,16 @@
                 jnp.concatenate([prob[:, :slots], prob[:, slots:]], axis=0), by_head(g)
             ).astype(BF)
     unit, _ = unit_parts(tok_ref[...].astype(F32))
-    normed = (unit * g1_ref[...] + c1_ref[...]).astype(BF)
-    acc_ref[:, : 3 * width] += mm_tn(normed, dqkv_ref[...])
+    acc_ref[:, : 3 * width] += mm_tn(unit.astype(BF), dqkv_ref[...])
     grad_ref[...] = dqkv_ref[...]
+    for i in range(3):
+        part = dqkv_ref[:, i * width : (i + 1) * width].astype(F32)
+        row_ref[i : i + 1, :] += jnp.sum(part, axis=0, keepdims=True)
 
     @pl.when(at == last)
     def _():
         core, own = info_ref[0], info_ref[2]
+        acc_ref[:, 4 * width :] = row_ref[...].T
         half = width // 2
         size = width // len(tables[0])
         for place in range(len(tables[0])):
@@ -382,7 +390,7 @@
             dst[to : to + size, :] = acc_ref[rows_at, :].astype(BF)
 
 
-def attend_back(info, tables, qkv, prob, gmix, tokens, g1, c1, dwout):
+def attend_back(info, tables, qkv, prob, gmix, tokens, vec, dwout):
     n, width = tokens.shape
     rows, pairs, slots, _ = prob.shape
     per = TOKS // slots
@@ -395,42 +403,39 @@
             pl.BlockSpec((per, pairs, slots, 2 * slots), lambda i, *_: (i, 0, 0, 0)),
             rows_of(width),
             rows_of(width),
-            whole(1, width),
-            whole(1, width),
+            whole(*vec.shape),
             whole(width, width),
         ],
-        [rows_of(3 * width)] + [whole(width // 2, 4 * width)] * 2,
-        [jax.ShapeDtypeStruct((n, 3 * width), BF)] + [jax.ShapeDtypeStruct((width // 2, 4 * width), BF)] * 2,
-        [pltpu.VMEM((TOKS, 3 * width), BF), pltpu.VMEM((width, 4 * width), F32)],
+        [rows_of(3 * width)] + [whole(width // 2, 4 * width + LANES)] * 2,
+        [jax.ShapeDtypeStruct((n, 3 * width), BF)] + [jax.ShapeDtypeStruct((width // 2, 4 * width + LANES), BF)] * 2,
+        [
+            pltpu.VMEM((TOKS, 3 * width), BF),
+            pltpu.VMEM((width, 4 * width + LANES), F32),
+            pltpu.VMEM((LANES, width), F32),
+        ],
         info,
-        (qkv, prob, gmix, tokens, g1, c1, dwout),
-    )
-
-
-def first_back_kernel(info_ref, dqkv_ref, wqkv_ref, tok_ref, gres_ref, g1_ref, vec_in_ref, out_ref, vec_ref):
-    @pl.when(pl.program_id(0) == 0)
-    def _():
-        vec_ref[...] = vec_in_ref[...]
-
+        (qkv, prob, gmix, tokens, vec, dwout),
+    )
+
+
+def first_back_kernel(info_ref, dqkv_ref, wqkv_ref, tok_ref, gres_ref, g1_ref, out_ref):
     dnormed = mm_nt(dqkv_ref[...], wqkv_ref[...])
     unit, inv = unit_parts(tok_ref[...].astype(F32))
-    vec_ref[3:4, :] += jnp.sum(dnormed * unit, axis=0, keepdims=True)
-    vec_ref[4:5, :] += jnp.sum(dnormed, axis=0, keepdims=True)
     out_ref[...] = gres_ref[...] + norm_back(dnormed, unit, inv, g1_ref[...])
 
 
-def first_back(info, dqkv, wqkv, tokens, gres, g1, vec):
+def first_back(info, dqkv, wqkv, tokens, gres, g1):
     n, width = tokens.shape
     return call(
         first_back_kernel,
         "first_back",
         (n // TOKS,),
-        [rows_of(3 * width), whole(*wqkv.shape), rows_of(width), rows_of(width), whole(1, width), whole(*vec.shape)],
-        [rows_of(width), whole(*vec.shape)],
-        [jax.ShapeDtypeStruct((n, width), F32), jax.ShapeDtypeStruct(vec.shape, F32)],
+        [rows_of(3 * width), whole(*wqkv.shape), rows_of(width), rows_of(width), whole(1, width)],
+        rows_of(width),
+        jax.ShapeDtypeStruct((n, width), F32),
         [],
         info,
-        (dqkv, wqkv, tokens, gres, g1, vec),
+        (dqkv, wqkv, tokens, gres, g1),
     )
 
 
@@ -477,7 +482,7 @@
     )
 
 
-def attend_end_kernel(tables, info_ref, keep_ref, other_ref, qkv_ref, out_ref):
+def attend_end_kernel(tables, info_ref, keep_ref, other_ref, w_ref, g1_ref, c1_ref, qkv_ref, out_ref, vec_ref, sum_ref, col_ref):
     core, own = info_ref[0], info_ref[2]
     width = out_ref.shape[1]
     blocks = len(tables[0])
@@ -489,22 +494,40 @@
         block = block_at(place, tables, core, own)
         rows = pl.ds(pl.multiple_of(block * size, size), size)
         part = src[at : at + size, :].astype(F32)
-        qkv_ref[rows, :] = part[:, : 3 * width]
-        out_ref[rows, :] = part[:, 3 * width :]
-
-
-def attend_end(info, tables, keep, other):
-    rows, width = 2 * keep.shape[0], keep.shape[1] // 4
+        sum_ref[rows, :] = part[:, : 3 * width]
+        out_ref[rows, :] = part[:, 3 * width : 4 * width]
+        col_ref[rows, :] = part[:, 4 * width :]
+    vec = col_ref[...].T
+    wide_row = jnp.concatenate([vec[i : i + 1, :] for i in range(3)], axis=1)
+    pair = jnp.concatenate([g1_ref[...], c1_ref[...], jnp.zeros((LANES - 2, width), F32)], axis=0).T
+    gain, bias = pair[:, 0:1], pair[:, 1:2]
+    w = w_ref[...].astype(F32)
+    sums = sum_ref[...]
+    qkv_ref[...] = gain * sums + bias * wide_row
+    lane = lax.broadcasted_iota(jnp.int32, (width, LANES), 1)
+    d_gain = jnp.sum(w * sums, axis=1, keepdims=True)
+    d_bias = jnp.sum(w * wide_row, axis=1, keepdims=True)
+    both = jnp.where(lane == 0, d_gain, jnp.where(lane == 1, d_bias, 0.0)).T
+    vec_ref[...] = vec[: vec_ref.shape[0], :]
+    vec_ref[0:2, :] = both[0:2, :]
+
+
+def attend_end(info, tables, keep, other, w_qkv, g1, c1, count):
+    rows, width = 2 * keep.shape[0], w_qkv.shape[0]
     return call(
         functools.partial(attend_end_kernel, tables),
         "attend_end",
         (1,),
-        [whole(*keep.shape)] * 2,
-        [whole(rows, 3 * width), whole(rows, width)],
-        [jax.ShapeDtypeStruct((rows, 3 * width), F32), jax.ShapeDtypeStruct((rows, width), F32)],
-        [],
+        [whole(*keep.shape)] * 2 + [whole(*w_qkv.shape)] + [whole(1, width)] * 2,
+        [whole(rows, 3 * width), whole(rows, width), whole(count, width)],
+        [
+            jax.ShapeDtypeStruct((rows, 3 * width), F32),
+            jax.ShapeDtypeStruct((rows, width), F32),
+            jax.ShapeDtypeStruct((count, width), F32),
+        ],
+        [pltpu.VMEM((rows, 3 * width), F32), pltpu.VMEM((rows, LANES), F32)],
         info,
-        (keep, other),
+        (keep, other, w_qkv, g1, c1),
     )
 
 
@@ -531,11 +554,16 @@
             return (masks, masks)
         return (masks, [masks[1], masks[0]] + masks[2:])
 
-    def scatter(value, order):
-        for first, second in zip(*order):
+    def after(*values):
+        return lax.optimization_barrier(values)
+
+    def scatter(value, order, beside=None):
+        for step, (first, second) in enumerate(zip(*order)):
             half = value.shape[0] // 2
             value = add(value[:half], swap(value[half:], first, second))
-        return value
+            if beside is not None and step == 0:
+                value, beside = after(value, beside)
+        return value if beside is None else (value, beside)
 
     def gather(value, order):
         for first, second in reversed(list(zip(*order))):
@@ -572,66 +600,68 @@
     fetched = [(up_chunk, down_chunk)]
     for mask in narrow_masks:
         fetched = fetched + [(swap(u, mask), swap(d, mask)) for u, d in fetched]
+
+    row = lambda v: v[None].astype(F32)
+    g1, c1, g2 = row(ln1_gain), row(ln1_bias), row(ln2_gain)
+    qkv, prob, mixed, residual, second = attend(
+        info, tokens_in, g1, c1, w_qkv, w_out, g2, row(ln2_bias), segment_ids, step_ids, pad_mask
+    )
+    second, fetched = after(second, fetched)
     chunks = []
     for up, down in fetched[1:]:
         chunks += [(up, down), (swap(up, core_mask), swap(down, core_mask))]
-
-    row = lambda v: v[None].astype(F32)
-    qkv, prob, mixed, residual, second = attend(
-        info, tokens_in, row(ln1_gain), row(ln1_bias), w_qkv, w_out, row(ln2_gain), row(ln2_bias), segment_ids, step_ids, pad_mask
-    )
     out_part, dsec_part, own_keep, own_send, bown_keep, bown_send = ffn_own(
         info, ff_tables, second, cotangent, w_up, b_up[None], w_down
     )
     rest = ffn_rest(
-        info, ff_tables, second, cotangent, out_part, dsec_part, residual, mixed, row(b_down), row(ln2_gain), w_out, chunks
+        info, ff_tables, second, cotangent, out_part, dsec_part, residual, mixed, row(b_down), g2, w_out, chunks
     )
     block_out, gres, gmix, vec, dwout = rest[:5]
     count = len(chunks)
     grads, bgrads = rest[5 : 5 + count], rest[5 + count :]
 
+    b_all = jnp.concatenate([bown_keep, bown_send, *bgrads], axis=0)
+    for bit in range(narrow.bit_length()):
+        flipped = jnp.flip(b_all.reshape(-1, 2, 1 << bit, units), axis=1).reshape(b_all.shape)
+        b_all = jnp.where((narrow_at * 2 + core) >> bit & 1, flipped, b_all)
+    vec = jnp.concatenate([vec, b_all.reshape(-1, width)], axis=0)
+
     held = [add(own_keep, swap(own_send, core_mask))]
     held += [add(grads[2 * j], swap(grads[2 * j + 1], core_mask)) for j in range(narrow - 1)]
+    gmix, held = after(gmix, held)
     for mask in reversed(narrow_masks):
         held = [add(held[j], swap(held[j + mask], mask)) for j in range(mask)]
+
+    dqkv, keep, send = attend_back(info, at_tables, qkv, prob, gmix, tokens_in, vec, dwout)
+    keep = add(keep, swap(send, core_mask))
+    keep, held = after(keep, held)
+    grad_tokens = first_back(info, dqkv, w_qkv, tokens_in, gres, g1)
     ff_keep = gather(scatter(held[0], ff_order), ff_order)
     ff_other = swap(ff_keep, core_mask)
     grad_w_up, grad_w_down = ffn_end(info, ff_tables, ff_keep, ff_other)
 
-    dqkv, keep, send = attend_back(
-        info, at_tables, qkv, prob, gmix, tokens_in, row(ln1_gain), row(ln1_bias), dwout
-    )
-    keep = scatter(add(keep, swap(send, core_mask)), at_order)
+    keep, grad_tokens = scatter(keep, at_order, grad_tokens)
     for mask in at_rest:
         keep = add(keep, swap(keep, mask))
     keep = gather(keep, at_order)
-    grad_w_qkv, grad_w_out = attend_end(info, at_tables, keep, swap(keep, core_mask))
-
-    grad_tokens, vec = first_back(info, dqkv, w_qkv, tokens_in, gres, row(ln1_gain), vec)
-
-    b_parts = [(0, bown_keep, bown_send)] + [(j, bgrads[2 * j - 2], bgrads[2 * j - 1]) for j in range(1, narrow)]
-    b_all = jnp.zeros((narrow, 2, units), F32)
-    for j, mine, other in b_parts:
-        both = jnp.where(core == 0, jnp.concatenate([mine, other], 0), jnp.concatenate([other, mine], 0))
-        b_all = lax.dynamic_update_slice(b_all, both[None], (narrow_at ^ j, 0, 0))
-    vec = jnp.concatenate([vec, b_all.reshape(-1, width)], axis=0)
-    for mask in [core_mask] + masks:
-        vec = vec + swap(vec, mask)
-    b_sum = vec[8:].reshape(narrow, 2 * units)
+    grad_w_qkv, grad_w_out, vec = attend_end(
+        info, at_tables, keep, swap(keep, core_mask), w_qkv, g1, c1, SUMS + vec.shape[0]
+    )
+    b_sum = vec[SUMS + 8 :].reshape(narrow, 2 * units)
     grad_b_up = lax.dynamic_slice(b_sum, (narrow_at, 0), (1, 2 * units))[0]
     return (
         block_out,
         grad_tokens,
-        vec[3],
-        vec[4],
+        vec[0],
+        vec[1],
         grad_w_qkv,
         grad_w_out,
-        vec[0],
-        vec[1],
+        vec[SUMS],
+        vec[SUMS + 1],
         grad_w_up,
         grad_b_up,
         grad_w_down,
-        vec[2],
+        vec[SUMS + 2],
     )
 
 

time: 211 us -> 177 us (0.84)
  waiting for transfers between devices: 93.1 us -> 57.6 us
  starting transfers between devices: 33.5 us -> 28.1 us
  local copies, waits for them, and re-layouts: 6.38 us -> 10.3 us
  other arithmetic: 3.94 us -> 6.72 us
    ppermute x29 -> x24, waiting for transfers between devices: 93.1 us -> 57.6 us  [swap(): return lax.ppermute(value, AXES, pairs)]
    ppermute x29 -> x24, starting transfers between devices: 33.5 us -> 28.1 us  [swap(): return lax.ppermute(value, AXES, pairs)]
    unnamed x40 -> x45, local copies, waits for them, and re-layouts: 2.11 us -> 5.08 us
    convert_element_type x9 -> x10, other arithmetic: 1.95 us -> 4.91 us  [add(): return (a.astype(F32) + b.astype(F32)).astype(a.dtype)]
  transfers between devices with their start and end apart: 29 -> 24, of which waited for: 18 -> 14; matrix products, arithmetic and copies ran while one was open for 4% -> 4% of each run, Pallas kernels for 16% -> 38%
where the time goes in v2:
time: 177 us
  Pallas kernels  72.8 us (41%)
  waiting for transfers between devices  57.6 us (33%)
  starting transfers between devices  28.1 us (16%)
  local copies, waits for them, and re-layouts  10.3 us (6%)
  other arithmetic  6.72 us (4%)
    pallas_call x7, Pallas kernels, call(): pl.pallas_call(kernel, grid_spec=pltpu.PrefetchScalarGridSpec(num_scalar_...  72.8 us
    ppermute x24, waiting for transfers between devices, swap(): return lax.ppermute(value, AXES, pairs)  57.6 us
    ppermute x24, starting transfers between devices, swap(): return lax.ppermute(value, AXES, pairs)  28.1 us
    unnamed x45, local copies, waits for them, and re-layouts  5.08 us
    convert_element_type x10, other arithmetic, add(): return (a.astype(F32) + b.astype(F32)).astype(a.dtype)  4.91 us
  transfers between devices with their start and end apart: 24, of which 14 were waited for; matrix products, arithmetic and copies ran while one was open for 4% of the time, Pallas kernels for 38%

profile of v2, /device:TPU:0, one launch (start us, length us, event | category | flops | bytes accessed | tf_op | source)
XLA Modules:
  0.0 176.6 jit_solution(3960634484865707874)
XLA Ops:
  0.7 1.2 constant_dynamic-slice_fusion.2
  1.8 0.8 dynamic_slice.13
  2.7 0.8 pad_maximum_fusion.2
  3.5 2.9 %collective-permute-start = (bf16[528,512]{1,0:T(8,128)(2,1)}, bf16[528,512]{1,0:T(8,128)(2,1)S(1)}, u32[]{:S(2)}, u32[]{:S(2)}) collective-permute-start(bf16[528,512]{1,0:T(8,128)(2,1)} %pad_maximum_fusion.2), channel_id=1, source_target_pairs={{0,1},{1,0},{2,3},{3,2},{4,5},{5,4},{6,7},{7,6},{8,9},{9,8},{10,11... | collective-permute-start | bytes 1622024 | tf_op jit(solution)/shard_map/ppermute | solution.py:547
  6.5 0.8 constant_dynamic-slice_fusion.1
  7.5 10.7 %attend.1 = (bf16[1024,1536]{1,0:T(8,128)(2,1)}, bf16[8,4,128,256]{3,2,1,0:T(8,128)(2,1)}, bf16[1024,512]{1,0:T(8,128)(2,1)S(1)}, f32[1024,512]{1,0:T(8,128)}, bf16[1024,512]{1,0:T(8,128)(2,1)S(1)}) custom-call(s32[3]{0:T(128)S(1)} %pad_add_fusion.info_ref, bf16[1024,512]{1,0:T(8,128)(2,1)S(1)} %copy-done.1, f32[1,512]{1,0:T(1,128)S(1)} %bitcast.18, ...), custom_call_target="tpu_custom_call" | custom-call | flops 1000 | bytes 1000 | tf_op jit(solution)/shard_map/attend/pallas_call | solution.py:45
  18.1 1.0 copy-done.6
  19.1 11.1 %collective-permute-done.1.refs_2_ = bf16[512,512]{1,0:T(8,128)(2,1)S(1)} collective-permute-done((bf16[512,512]{1,0:T(8,128)(2,1)}, bf16[512,512]{1,0:T(8,128)(2,1)S(1)}, u32[]{:S(2)}, u32[]{:S(2)}) %collective-permute-start.1) | collective-permute-done | bytes 524320 | tf_op jit(solution)/shard_map/ppermute | solution.py:547
  30.2 0.5 collective-permute-start.3
  30.7 13.0 %ffn_own.1 = (f32[1024,512]{1,0:T(8,128)}, f32[1024,512]{1,0:T(8,128)}, bf16[512,1024]{1,0:T(8,128)(2,1)S(1)}, bf16[512,1024]{1,0:T(8,128)(2,1)}, f32[1,512]{1,0:T(1,128)S(1)}, /*index=5*/f32[1,512]{1,0:T(1,128)S(1)}) custom-call(s32[3]{0:T(128)S(1)} %pad_add_fusion.info_ref, bf16[1024,512]{1,0:T(8,128)(2,1)S(1)} %get-tuple-element.51.sec_ref, ...), custom_call_target="tpu_custom_call" | custom-call | flops 1000 | bytes 1000 | tf_op jit(solution)/shard_map/ffn_own/pallas_call | solution.py:45
  43.8 0.9 copy-done.5
  44.8 1.0 copy-done.8
  45.8 16.2 %ffn_rest.1 = (bf16[1024,512]{1,0:T(8,128)(2,1)}, f32[1024,512]{1,0:T(8,128)}, bf16[1024,512]{1,0:T(8,128)(2,1)S(1)}, f32[8,512]{1,0:T(8,128)S(1)}, f32[512,512]...) custom-call(s32[3]{0:T(128)S(1)} %pad_add_fusion.info_ref, ...), custom_call_target="tpu_custom_call" | custom-call | flops 1000 | bytes 1000 | tf_op jit(solution)/shard_map/ffn_rest/pallas_call | solution.py:45
  62.8 2.0 %add_convert_fusion.3 = bf16[512,1024]{1,0:T(8,128)(2,1)S(1)} fusion(bf16[512,1024]{1,0:T(8,128)(2,1)} %collective-permute-done.4, bf16[512,1024]{1,0:T(8,128)(2,1)} %copy-done.5), kind=kLoop, calls=%fused_computation.3 | loop fusion | flops 2097152 | bytes 3145728 | tf_op jit(solution)/shard_map/convert_element_type | solution.py:550
  65.1 1.7 add_convert_fusion.2
  66.9 1.8 %collective-permute-start.7 = (bf16[512,1024]{1,0:T(8,128)(2,1)S(1)}, bf16[512,1024]{1,0:T(8,128)(2,1)S(1)}, u32[]{:S(2)}, u32[]{:S(2)}) collective-permute-start(bf16[512,1024]{1,0:T(8,128)(2,1)S(1)} %add_convert_fusion.2), channel_id=1, source_target_pairs={{0,1},{1,0},{2,3},{3,2},{4,5},{5,4},{6,7},{7,6},{8,9},{9,8},{10,11... | collective-permute-start | bytes 3145736 | tf_op jit(solution)/shard_map/ppermute | solution.py:547
  68.7 17.3 %attend_back.1 = (bf16[1024,1536]{1,0:T(8,128)(2,1)}, bf16[256,2176]{1,0:T(8,128)(2,1)}, bf16[256,2176]{1,0:T(8,128)(2,1)}) custom-call(s32[3]{0:T(128)S(1)} %pad_add_fusion.info_ref, bf16[1024,1536]{1,0:T(8,128)(2,1)} %get-tuple-element.59.qkv_ref, bf16[8,4,128,256]{3,2,1,0:T(8,128)(2,1)} %get-tuple-element.60.prob_ref, ...), custom_call_target="tpu_custom_call" | custom-call | flops 1000 | bytes 1000 | tf_op jit(solution)/shard_map/attend_back/pallas_call | solution.py:45
  86.2 6.2 %collective-permute-done.7 = bf16[512,1024]{1,0:T(8,128)(2,1)S(1)} collective-permute-done((bf16[512,1024]{1,0:T(8,128)(2,1)S(1)}, bf16[512,1024]{1,0:T(8,128)(2,1)S(1)}, u32[]{:S(2)}, u32[]{:S(2)}) %collective-permute-start.7) | collective-permute-done | bytes 1048608 | tf_op jit(solution)/shard_map/ppermute | solution.py:547
  93.1 1.8 %collective-permute-start.8 = (bf16[128,2176]{1,0:T(8,128)(2,1)S(1)}, bf16[128,2176]{1,0:T(8,128)(2,1)S(1)}, u32[]{:S(2)}, u32[]{:S(2)}) collective-permute-start(bf16[128,2176]{1,0:T(8,128)(2,1)S(1)} %slice.61), channel_id=1, source_target_pairs={{0,1},{1,0},{2,6},{3,7},{4,5},{5,4},{6,2},{7,3},{8,9},{9,8},{10,14... | collective-permute-start | bytes 1671176 | tf_op jit(solution)/shard_map/ppermute | solution.py:547
  94.9 6.4 %first_back.1 = f32[1024,512]{1,0:T(8,128)} custom-call(s32[3]{0:T(128)S(1)} %pad_add_fusion.info_ref, bf16[1024,1536]{1,0:T(8,128)(2,1)} %get-tuple-element.78.dqkv_ref, bf16[512,1536]{1,0:T(8,128)(2,1)S(1)} %copy-done, bf16[1024,512]{1,0:T(8,128)(2,1)S(1)} %copy-done.1, f32[1024,512]{1,0:T(8,128)} %get-tuple-element.79.gres_ref, f32[1,512]{1,0:T(1,128)S(1)} %bitcast.19), custom_call_target="tpu_custom_call" | custom-call | flops 1000 | bytes 1000 | tf_op jit(solution)/shard_map/first_back/pallas_call | solution.py:45
  101.3 1.4 collective-permute-done.8
  102.9 1.8 %collective-permute-start.9 = (bf16[64,2176]{1,0:T(8,128)(2,1)S(1)}, bf16[64,2176]{1,0:T(8,128)(2,1)S(1)}, u32[]{:S(2)}, u32[]{:S(2)}) collective-permute-start(bf16[64,2176]{1,0:T(8,128)(2,1)S(1)} %slice.63), channel_id=1, source_target_pairs={{0,4},{1,5},{2,3},{3,2},{4,0},{5,1},{6,7},{7,6},{8,12},{9,13},{10,... | collective-permute-start | bytes 835592 | tf_op jit(solution)/shard_map/ppermute | solution.py:547
  105.1 4.4 %collective-permute-done.9 = bf16[64,2176]{1,0:T(8,128)(2,1)S(1)} collective-permute-done((bf16[64,2176]{1,0:T(8,128)(2,1)S(1)}, bf16[64,2176]{1,0:T(8,128)(2,1)S(1)}, u32[]{:S(2)}, u32[]{:S(2)}) %collective-permute-start.9) | collective-permute-done | bytes 278560 | tf_op jit(solution)/shard_map/ppermute | solution.py:547
  109.6 1.9 %collective-permute-start.10 = (bf16[32,2176]{1,0:T(8,128)(2,1)S(1)}, bf16[32,2176]{1,0:T(8,128)(2,1)S(1)}, u32[]{:S(2)}, u32[]{:S(2)}) collective-permute-start(bf16[32,2176]{1,0:T(8,128)(2,1)S(1)} %slice.81), channel_id=1, source_target_pairs={{0,8},{1,9},{2,10},{3,11},{4,12},{5,13},{6,14},{7,15},{8,0},{9,1},... | collective-permute-start | bytes 417800 | tf_op jit(solution)/shard_map/ppermute | solution.py:547
  111.5 4.3 %collective-permute-done.17 = bf16[256,1024]{1,0:T(8,128)(2,1)S(1)} collective-permute-done((bf16[256,1024]{1,0:T(8,128)(2,1)S(1)}, bf16[256,1024]{1,0:T(8,128)(2,1)S(1)}, u32[]{:S(2)}, u32[]{:S(2)}) %collective-permute-start.17) | collective-permute-done | bytes 524320 | tf_op jit(solution)/shard_map/ppermute | solution.py:547
  116.0 2.1 %collective-permute-start.18 = (bf16[128,1024]{1,0:T(8,128)(2,1)S(1)}, bf16[128,1024]{1,0:T(8,128)(2,1)S(1)}, u32[]{:S(2)}, u32[]{:S(2)}) collective-permute-start(bf16[128,1024]{1,0:T(8,128)(2,1)S(1)} %slice.85), channel_id=1, source_target_pairs={{0,8},{1,9},{2,6},{3,7},{4,12},{5,13},{6,2},{7,3},{8,0},{9,1},{10,... | collective-permute-start | bytes 786440 | tf_op jit(solution)/shard_map/ppermute | solution.py:547
  118.2 2.7 %collective-permute-start.11 = (bf16[16,2176]{1,0:T(8,128)(2,1)S(1)}, bf16[16,2176]{1,0:T(8,128)(2,1)S(1)}, u32[]{:S(2)}, u32[]{:S(2)}) collective-permute-start(bf16[16,2176]{1,0:T(8,128)(2,1)S(1)} %slice.83), channel_id=1, source_target_pairs={{0,16},{1,17},{2,18},{3,19},{4,20},{5,21},{6,22},{7,23},{8,24},{9,... | collective-permute-start | bytes 208904 | tf_op jit(solution)/shard_map/ppermute | solution.py:547
  120.8 3.4 %collective-permute-done.18 = bf16[128,1024]{1,0:T(8,128)(2,1)S(1)} collective-permute-done((bf16[128,1024]{1,0:T(8,128)(2,1)S(1)}, bf16[128,1024]{1,0:T(8,128)(2,1)S(1)}, u32[]{:S(2)}, u32[]{:S(2)}) %collective-permute-start.18) | collective-permute-done | bytes 262176 | tf_op jit(solution)/shard_map/ppermute | solution.py:547
  124.3 3.4 %collective-permute-start.19 = (bf16[64,1024]{1,0:T(8,128)(2,1)S(1)}, bf16[64,1024]{1,0:T(8,128)(2,1)S(1)}, u32[]{:S(2)}, u32[]{:S(2)}) collective-permute-start(bf16[64,1024]{1,0:T(8,128)(2,1)S(1)} %slice.87), channel_id=1, source_target_pairs={{0,16},{1,17},{2,18},{3,19},{4,20},{5,21},{6,22},{7,23},{8,24},{9,... | collective-permute-start | bytes 393224 | tf_op jit(solution)/shard_map/ppermute | solution.py:547
  127.7 0.6 constant_dynamic-update-slice_fusion.4
  128.7 5.8 %collective-permute-done.19 = bf16[64,1024]{1,0:T(8,128)(2,1)S(1)} collective-permute-done((bf16[64,1024]{1,0:T(8,128)(2,1)S(1)}, bf16[64,1024]{1,0:T(8,128)(2,1)S(1)}, u32[]{:S(2)}, u32[]{:S(2)}) %collective-permute-start.19) | collective-permute-done | bytes 131104 | tf_op jit(solution)/shard_map/ppermute | solution.py:547
  134.7 0.6 collective-permute-done.12
  135.3 3.4 %collective-permute-start.13 = (bf16[32,2176]{1,0:T(8,128)(2,1)S(1)}, bf16[32,2176]{1,0:T(8,128)(2,1)S(1)}, u32[]{:S(2)}, u32[]{:S(2)}) collective-permute-start(bf16[32,2176]{1,0:T(8,128)(2,1)S(1)} %pad_maximum_fusion.6), channel_id=1, source_target_pairs={{0,8},{1,9},{2,10},{3,11},{4,12},{5,13},{6,14},{7,15},{8,0},{9,1},... | collective-permute-start | bytes 417800 | tf_op jit(solution)/shard_map/ppermute | solution.py:547
  138.7 3.3 %collective-permute-done.20 = bf16[64,1024]{1,0:T(8,128)(2,1)S(1)} collective-permute-done((bf16[64,1024]{1,0:T(8,128)(2,1)S(1)}, bf16[64,1024]{1,0:T(8,128)(2,1)S(1)}, u32[]{:S(2)}, u32[]{:S(2)}) %collective-permute-start.20) | collective-permute-done | bytes 131104 | tf_op jit(solution)/shard_map/ppermute | solution.py:547
  142.6 1.6 collective-permute-start.14
  144.2 0.6 constant_dynamic-update-slice_fusion.3
  144.8 6.5 %collective-permute-done.14 = bf16[64,2176]{1,0:T(8,128)(2,1)S(1)} collective-permute-done((bf16[64,2176]{1,0:T(8,128)(2,1)S(1)}, bf16[64,2176]{1,0:T(8,128)(2,1)S(1)}, u32[]{:S(2)}, u32[]{:S(2)}) %collective-permute-start.14) | collective-permute-done | bytes 278560 | tf_op jit(solution)/shard_map/ppermute | solution.py:547
  151.7 0.7 constant_dynamic-update-slice_fusion.2
  152.4 1.7 collective-permute-start.22
  154.1 0.7 constant_dynamic-update-slice_fusion.1
  154.8 6.1 %collective-permute-done.15 = bf16[128,2176]{1,0:T(8,128)(2,1)S(1)} collective-permute-done((bf16[128,2176]{1,0:T(8,128)(2,1)S(1)}, bf16[128,2176]{1,0:T(8,128)(2,1)S(1)}, u32[]{:S(2)}, u32[]{:S(2)}) %collective-permute-start.15) | collective-permute-done | bytes 557088 | tf_op jit(solution)/shard_map/ppermute | solution.py:547
  160.9 0.9 constant_dynamic-update-slice_fusion.keep_ref
  161.9 0.6 collective-permute-start.23
  162.4 3.7 %collective-permute-done.23.other_ref = bf16[512,1024]{1,0:T(8,128)(2,1)} collective-permute-done((bf16[512,1024]{1,0:T(8,128)(2,1)S(1)}, bf16[512,1024]{1,0:T(8,128)(2,1)}, u32[]{:S(2)}, u32[]{:S(2)}) %collective-permute-start.23) | collective-permute-done | bytes 1048608 | tf_op jit(solution)/shard_map/ppermute | solution.py:547
  166.2 4.3 %ffn_end.1 = (f32[512,1024]{1,0:T(8,128)}, f32[1024,512]{1,0:T(8,128)}) custom-call(s32[3]{0:T(128)S(1)} %pad_add_fusion.info_ref, bf16[512,1024]{1,0:T(8,128)(2,1)S(1)} %pad_maximum_fusion.keep_ref, bf16[512,1024]{1,0:T(8,128)(2,1)} %collective-permute-done.23.other_ref), custom_call_target="tpu_custom_call" | custom-call | flops 1000 | bytes 1000 | tf_op jit(solution)/shard_map/ffn_end/pallas_call | solution.py:45
  170.5 4.9 %attend_end.1 = (f32[512,1536]{1,0:T(8,128)}, f32[512,512]{1,0:T(8,128)}, f32[20,512]{1,0:T(8,128)S(1)}) custom-call(s32[3]{0:T(128)S(1)} %pad_add_fusion.info_ref, bf16[256,2176]{1,0:T(8,128)(2,1)} %constant_dynamic-update-slice_fusion.keep_ref, bf16[256,2176]{1,0:T(8,128)(2,1)} %collective-permute-done.16.other_ref, bf16[512,1536]{1,0:T(8,128)(2,1)S(1)} %copy-done, ...), custom_call_target="tpu_custom_call" | custom-call | flops 1000 | bytes 1000 | tf_op jit(solution)/shard_map/attend_end/pallas_call | solution.py:45
  175.4 0.6 fusion
  176.0 0.6 constant_dynamic-slice_fusion
  (98 shorter events, 4.6 us)
Async XLA Ops:
  0.6 5.8 %copy-start.17 = (bf16[1024,512]{1,0:T(8,128)(2,1)S(1)}, bf16[1024,512]{1,0:T(8,128)(2,1)}, u32[]{:S(2)}) copy-start(bf16[1024,512]{1,0:T(8,128)(2,1)} %refs_5_.1) | copy-start | bytes 3145732
  2.6 4.8 %copy-start.1 = (bf16[1024,512]{1,0:T(8,128)(2,1)S(1)}, bf16[1024,512]{1,0:T(8,128)(2,1)}, u32[]{:S(2)}) copy-start(bf16[1024,512]{1,0:T(8,128)(2,1)} %tok_ref.5) | copy-start | bytes 3145732
  2.6 4.8 %copy-start.3 = (bf16[512,512]{1,0:T(8,128)(2,1)S(1)}, bf16[512,512]{1,0:T(8,128)(2,1)}, u32[]{:S(2)}) copy-start(bf16[512,512]{1,0:T(8,128)(2,1)} %wout_ref.3) | copy-start | bytes 1572868
  2.6 4.8 %copy-start.9 = (f32[512]{0:T(512)S(1)}, f32[512]{0:T(512)}, u32[]{:S(2)}) copy-start(f32[512]{0:T(512)} %param.16) | copy-start | bytes 6148
  2.6 4.8 %copy-start.10 = (f32[512]{0:T(512)S(1)}, f32[512]{0:T(512)}, u32[]{:S(2)}) copy-start(f32[512]{0:T(512)} %param.17) | copy-start | bytes 6148
  2.6 4.8 %copy-start.11 = (f32[512]{0:T(512)S(1)}, f32[512]{0:T(512)}, u32[]{:S(2)}) copy-start(f32[512]{0:T(512)} %param.20) | copy-start | bytes 6148
  2.6 4.8 %copy-start.12 = (s32[8,128]{1,0:T(8,128)S(1)}, s32[8,128]{1,0:T(8,128)}, u32[]{:S(2)}) copy-start(s32[8,128]{1,0:T(8,128)} %seg_ref.1) | copy-start | bytes 12292
  2.7 4.8 %copy-start.13 = (s32[8,128]{1,0:T(8,128)S(1)}, s32[8,128]{1,0:T(8,128)}, u32[]{:S(2)}) copy-start(s32[8,128]{1,0:T(8,128)} %step_ref.1) | copy-start | bytes 12292
  2.7 4.8 %copy-start.14 = (s32[8,128]{1,0:T(8,128)S(1)}, s32[8,128]{1,0:T(8,128)}, u32[]{:S(2)}) copy-start(s32[8,128]{1,0:T(8,128)} %pad_ref.1) | copy-start | bytes 12292
  2.7 4.8 %copy-start.15 = (f32[512]{0:T(512)S(1)}, f32[512]{0:T(512)}, u32[]{:S(2)}) copy-start(f32[512]{0:T(512)} %param.21) | copy-start | bytes 6148
  3.5 26.7 %collective-permute-start = (bf16[528,512]{1,0:T(8,128)(2,1)}, bf16[528,512]{1,0:T(8,128)(2,1)S(1)}, u32[]{:S(2)}, u32[]{:S(2)}) collective-permute-start(bf16[528,512]{1,0:T(8,128)(2,1)} %pad_maximum_fusion.2), channel_id=1, source_target_pairs={{0,1},{1,0},{2,3},{3,2},{4,5},{5,4},{6,7},{7,6},{8,9},{9,8},{10,11... | collective-permute-start | bytes 1622024 | tf_op jit(solution)/shard_map/ppermute | solution.py:547
  7.3 22.9 %collective-permute-start.1 = (bf16[512,512]{1,0:T(8,128)(2,1)}, bf16[512,512]{1,0:T(8,128)(2,1)S(1)}, u32[]{:S(2)}, u32[]{:S(2)}) collective-permute-start(bf16[512,512]{1,0:T(8,128)(2,1)} %constant_dynamic-slice_fusion.1), channel_id=1, source_target_pairs={{0,1},{1,0},{2,3},{3,2},{4,5},{5,4},{6,7},{7,6},{8,9},{9,8},{10,11... | collective-permute-start | bytes 1572872 | tf_op jit(solution)/shard_map/ppermute | solution.py:547
  7.4 23.3 %copy-start.20 = (bf16[1024]{0:T(1024)(128)(2,1)S(1)}, bf16[1024]{0:T(1024)(128)(2,1)}, u32[]{:S(2)}) copy-start(bf16[1024]{0:T(1024)(128)(2,1)} %param.23) | copy-start | bytes 6148
  18.1 1.0 copy-start.6
  19.1 24.6 %copy-start.2 = (bf16[1024,512]{1,0:T(8,128)(2,1)}, bf16[1024,512]{1,0:T(8,128)(2,1)S(1)}, u32[]{:S(2)}) copy-start(bf16[1024,512]{1,0:T(8,128)(2,1)S(1)} %get-tuple-element.51.sec_ref) | copy-start | bytes 3145732
  30.2 13.6 %copy-start.7 = (bf16[512,512]{1,0:T(8,128)(2,1)}, bf16[512,512]{1,0:T(8,128)(2,1)S(1)}, u32[]{:S(2)}) copy-start(bf16[512,512]{1,0:T(8,128)(2,1)S(1)} %collective-permute-done.1.refs_2_) | copy-start | bytes 1572868
  30.2 14.6 %collective-permute-start.2 = (bf16[528,512]{1,0:T(8,128)(2,1)S(1)}, bf16[528,512]{1,0:T(8,128)(2,1)S(1)}, u32[]{:S(2)}, u32[]{:S(2)}) collective-permute-start(bf16[528,512]{1,0:T(8,128)(2,1)S(1)} %collective-permute-done.refs_0_), channel_id=1, source_target_pairs={{0,2},{1,3},{2,0},{3,1},{4,6},{5,7},{6,4},{7,5},{8,10},{9,11},{10,... | collective-permute-start | bytes 1622024 | tf_op jit(solution)/shard_map/ppermute | solution.py:547
  30.2 14.6 %collective-permute-start.3 = (bf16[512,512]{1,0:T(8,128)(2,1)S(1)}, bf16[512,512]{1,0:T(8,128)(2,1)S(1)}, u32[]{:S(2)}, u32[]{:S(2)}) collective-permute-start(bf16[512,512]{1,0:T(8,128)(2,1)S(1)} %collective-permute-done.1.refs_2_), channel_id=1, source_target_pairs={{0,2},{1,3},{2,0},{3,1},{4,6},{5,7},{6,4},{7,5},{8,10},{9,11},{10,... | collective-permute-start | bytes 1572872 | tf_op jit(solution)/shard_map/ppermute | solution.py:547
  30.7 14.1 %copy-start.16 = (f32[512]{0:T(512)S(1)}, f32[512]{0:T(512)}, u32[]{:S(2)}) copy-start(f32[512]{0:T(512)} %param.25) | copy-start | bytes 6148
  43.7 1.0 copy-start.5
  44.7 18.1 %collective-permute-start.4 = (bf16[512,1024]{1,0:T(8,128)(2,1)}, bf16[512,1024]{1,0:T(8,128)(2,1)}, u32[]{:S(2)}, u32[]{:S(2)}) collective-permute-start(bf16[512,1024]{1,0:T(8,128)(2,1)} %get-tuple-element.63), channel_id=1, source_target_pairs={{0,2},{1,3},{2,0},{3,1},{4,6},{5,7},{6,4},{7,5},{8,10},{9,11},{10,... | collective-permute-start | bytes 3145736 | tf_op jit(solution)/shard_map/ppermute | solution.py:547
  44.8 1.0 copy-start.8
  62.0 3.1 %collective-permute-start.5 = (bf16[512,1024]{1,0:T(8,128)(2,1)}, bf16[512,1024]{1,0:T(8,128)(2,1)}, u32[]{:S(2)}, u32[]{:S(2)}) collective-permute-start(bf16[512,1024]{1,0:T(8,128)(2,1)} %get-tuple-element.65), channel_id=1, source_target_pairs={{0,2},{1,3},{2,0},{3,1},{4,6},{5,7},{6,4},{7,5},{8,10},{9,11},{10,... | collective-permute-start | bytes 3145736 | tf_op jit(solution)/shard_map/ppermute | solution.py:547
  62.8 2.4 %copy-start.19 = (bf16[512,1024]{1,0:T(8,128)(2,1)S(1)}, bf16[512,1024]{1,0:T(8,128)(2,1)}, u32[]{:S(2)}) copy-start(bf16[512,1024]{1,0:T(8,128)(2,1)} %get-tuple-element.64) | copy-start | bytes 3145732
  65.1 3.6 %copy-start.4 = (f32[512,512]{1,0:T(8,128)S(1)}, f32[512,512]{1,0:T(8,128)}, u32[]{:S(2)}) copy-start(f32[512,512]{1,0:T(8,128)} %get-tuple-element.72.dwout_ref) | copy-start | bytes 3145732
  66.9 25.5 %collective-permute-start.7 = (bf16[512,1024]{1,0:T(8,128)(2,1)S(1)}, bf16[512,1024]{1,0:T(8,128)(2,1)S(1)}, u32[]{:S(2)}, u32[]{:S(2)}) collective-permute-start(bf16[512,1024]{1,0:T(8,128)(2,1)S(1)} %add_convert_fusion.2), channel_id=1, source_target_pairs={{0,1},{1,0},{2,3},{3,2},{4,5},{5,4},{6,7},{7,6},{8,9},{9,8},{10,11... | collective-permute-start | bytes 3145736 | tf_op jit(solution)/shard_map/ppermute | solution.py:547
  86.0 6.8 %copy-start.18 = (bf16[256,2176]{1,0:T(8,128)(2,1)S(1)}, bf16[256,2176]{1,0:T(8,128)(2,1)}, u32[]{:S(2)}) copy-start(bf16[256,2176]{1,0:T(8,128)(2,1)} %get-tuple-element.73) | copy-start | bytes 3342340
  86.0 6.8 %collective-permute-start.6 = (bf16[256,2176]{1,0:T(8,128)(2,1)}, bf16[256,2176]{1,0:T(8,128)(2,1)S(1)}, u32[]{:S(2)}, u32[]{:S(2)}) collective-permute-start(bf16[256,2176]{1,0:T(8,128)(2,1)} %get-tuple-element.74), channel_id=1, source_target_pairs={{0,2},{1,3},{2,0},{3,1},{4,6},{5,7},{6,4},{7,5},{8,10},{9,11},{10,... | collective-permute-start | bytes 3342344 | tf_op jit(solution)/shard_map/ppermute | solution.py:547
  92.8 2.1 %copy-start = (bf16[512,1536]{1,0:T(8,128)(2,1)S(1)}, bf16[512,1536]{1,0:T(8,128)(2,1)}, u32[]{:S(2)}) copy-start(bf16[512,1536]{1,0:T(8,128)(2,1)} %w_ref.1) | copy-start | bytes 4718596
  93.1 9.6 %collective-permute-start.8 = (bf16[128,2176]{1,0:T(8,128)(2,1)S(1)}, bf16[128,2176]{1,0:T(8,128)(2,1)S(1)}, u32[]{:S(2)}, u32[]{:S(2)}) collective-permute-start(bf16[128,2176]{1,0:T(8,128)(2,1)S(1)} %slice.61), channel_id=1, source_target_pairs={{0,1},{1,0},{2,6},{3,7},{4,5},{5,4},{6,2},{7,3},{8,9},{9,8},{10,14... | collective-permute-start | bytes 1671176 | tf_op jit(solution)/shard_map/ppermute | solution.py:547
  102.9 6.6 %collective-permute-start.9 = (bf16[64,2176]{1,0:T(8,128)(2,1)S(1)}, bf16[64,2176]{1,0:T(8,128)(2,1)S(1)}, u32[]{:S(2)}, u32[]{:S(2)}) collective-permute-start(bf16[64,2176]{1,0:T(8,128)(2,1)S(1)} %slice.63), channel_id=1, source_target_pairs={{0,4},{1,5},{2,3},{3,2},{4,0},{5,1},{6,7},{7,6},{8,12},{9,13},{10,... | collective-permute-start | bytes 835592 | tf_op jit(solution)/shard_map/ppermute | solution.py:547
  104.8 11.0 %collective-permute-start.17 = (bf16[256,1024]{1,0:T(8,128)(2,1)S(1)}, bf16[256,1024]{1,0:T(8,128)(2,1)S(1)}, u32[]{:S(2)}, u32[]{:S(2)}) collective-permute-start(bf16[256,1024]{1,0:T(8,128)(2,1)S(1)} %slice.73), channel_id=1, source_target_pairs={{0,4},{1,5},{2,10},{3,11},{4,0},{5,1},{6,14},{7,15},{8,12},{9,13},... | collective-permute-start | bytes 1572872 | tf_op jit(solution)/shard_map/ppermute | solution.py:547
  109.6 8.5 %collective-permute-start.10 = (bf16[32,2176]{1,0:T(8,128)(2,1)S(1)}, bf16[32,2176]{1,0:T(8,128)(2,1)S(1)}, u32[]{:S(2)}, u32[]{:S(2)}) collective-permute-start(bf16[32,2176]{1,0:T(8,128)(2,1)S(1)} %slice.81), channel_id=1, source_target_pairs={{0,8},{1,9},{2,10},{3,11},{4,12},{5,13},{6,14},{7,15},{8,0},{9,1},... | collective-permute-start | bytes 417800 | tf_op jit(solution)/shard_map/ppermute | solution.py:547
  116.0 8.3 %collective-permute-start.18 = (bf16[128,1024]{1,0:T(8,128)(2,1)S(1)}, bf16[128,1024]{1,0:T(8,128)(2,1)S(1)}, u32[]{:S(2)}, u32[]{:S(2)}) collective-permute-start(bf16[128,1024]{1,0:T(8,128)(2,1)S(1)} %slice.85), channel_id=1, source_target_pairs={{0,8},{1,9},{2,6},{3,7},{4,12},{5,13},{6,2},{7,3},{8,0},{9,1},{10,... | collective-permute-start | bytes 786440 | tf_op jit(solution)/shard_map/ppermute | solution.py:547
  118.2 9.5 %collective-permute-start.11 = (bf16[16,2176]{1,0:T(8,128)(2,1)S(1)}, bf16[16,2176]{1,0:T(8,128)(2,1)S(1)}, u32[]{:S(2)}, u32[]{:S(2)}) collective-permute-start(bf16[16,2176]{1,0:T(8,128)(2,1)S(1)} %slice.83), channel_id=1, source_target_pairs={{0,16},{1,17},{2,18},{3,19},{4,20},{5,21},{6,22},{7,23},{8,24},{9,... | collective-permute-start | bytes 208904 | tf_op jit(solution)/shard_map/ppermute | solution.py:547
  124.3 10.2 %collective-permute-start.19 = (bf16[64,1024]{1,0:T(8,128)(2,1)S(1)}, bf16[64,1024]{1,0:T(8,128)(2,1)S(1)}, u32[]{:S(2)}, u32[]{:S(2)}) collective-permute-start(bf16[64,1024]{1,0:T(8,128)(2,1)S(1)} %slice.87), channel_id=1, source_target_pairs={{0,16},{1,17},{2,18},{3,19},{4,20},{5,21},{6,22},{7,23},{8,24},{9,... | collective-permute-start | bytes 393224 | tf_op jit(solution)/shard_map/ppermute | solution.py:547
  128.3 6.9 %collective-permute-start.12 = (bf16[16,2176]{1,0:T(8,128)(2,1)S(1)}, bf16[16,2176]{1,0:T(8,128)(2,1)S(1)}, u32[]{:S(2)}, u32[]{:S(2)}) collective-permute-start(bf16[16,2176]{1,0:T(8,128)(2,1)S(1)} %get-tuple-element.89), channel_id=1, source_target_pairs={{0,16},{1,17},{2,18},{3,19},{4,20},{5,21},{6,22},{7,23},{8,24},{9,... | collective-permute-start | bytes 208904 | tf_op jit(solution)/shard_map/ppermute | solution.py:547
  134.6 7.4 %collective-permute-start.20 = (bf16[64,1024]{1,0:T(8,128)(2,1)S(1)}, bf16[64,1024]{1,0:T(8,128)(2,1)S(1)}, u32[]{:S(2)}, u32[]{:S(2)}) collective-permute-start(bf16[64,1024]{1,0:T(8,128)(2,1)S(1)} %add_convert_fusion.9), channel_id=1, source_target_pairs={{0,16},{1,17},{2,18},{3,19},{4,20},{5,21},{6,22},{7,23},{8,24},{9,... | collective-permute-start | bytes 393224 | tf_op jit(solution)/shard_map/ppermute | solution.py:547
  135.3 7.2 %collective-permute-start.13 = (bf16[32,2176]{1,0:T(8,128)(2,1)S(1)}, bf16[32,2176]{1,0:T(8,128)(2,1)S(1)}, u32[]{:S(2)}, u32[]{:S(2)}) collective-permute-start(bf16[32,2176]{1,0:T(8,128)(2,1)S(1)} %pad_maximum_fusion.6), channel_id=1, source_target_pairs={{0,8},{1,9},{2,10},{3,11},{4,12},{5,13},{6,14},{7,15},{8,0},{9,1},... | collective-permute-start | bytes 417800 | tf_op jit(solution)/shard_map/ppermute | solution.py:547
  142.0 10.3 %collective-permute-start.21 = (bf16[128,1024]{1,0:T(8,128)(2,1)S(1)}, bf16[128,1024]{1,0:T(8,128)(2,1)S(1)}, u32[]{:S(2)}, u32[]{:S(2)}) collective-permute-start(bf16[128,1024]{1,0:T(8,128)(2,1)S(1)} %pad_maximum_fusion.5), channel_id=1, source_target_pairs={{0,8},{1,9},{2,6},{3,7},{4,12},{5,13},{6,2},{7,3},{8,0},{9,1},{10,... | collective-permute-start | bytes 786440 | tf_op jit(solution)/shard_map/ppermute | solution.py:547
  142.6 8.7 %collective-permute-start.14 = (bf16[64,2176]{1,0:T(8,128)(2,1)S(1)}, bf16[64,2176]{1,0:T(8,128)(2,1)S(1)}, u32[]{:S(2)}, u32[]{:S(2)}) collective-permute-start(bf16[64,2176]{1,0:T(8,128)(2,1)S(1)} %pad_maximum_fusion.4), channel_id=1, source_target_pairs={{0,4},{1,5},{2,3},{3,2},{4,0},{5,1},{6,7},{7,6},{8,12},{9,13},{10,... | collective-permute-start | bytes 835592 | tf_op jit(solution)/shard_map/ppermute | solution.py:547
  151.3 9.6 %collective-permute-start.15 = (bf16[128,2176]{1,0:T(8,128)(2,1)S(1)}, bf16[128,2176]{1,0:T(8,128)(2,1)S(1)}, u32[]{:S(2)}, u32[]{:S(2)}) collective-permute-start(bf16[128,2176]{1,0:T(8,128)(2,1)S(1)} %pad_maximum_fusion.1), channel_id=1, source_target_pairs={{0,1},{1,0},{2,6},{3,7},{4,5},{5,4},{6,2},{7,3},{8,9},{9,8},{10,14... | collective-permute-start | bytes 1671176 | tf_op jit(solution)/shard_map/ppermute | solution.py:547
  152.4 9.4 %collective-permute-start.22 = (bf16[256,1024]{1,0:T(8,128)(2,1)S(1)}, bf16[256,1024]{1,0:T(8,128)(2,1)S(1)}, u32[]{:S(2)}, u32[]{:S(2)}) collective-permute-start(bf16[256,1024]{1,0:T(8,128)(2,1)S(1)} %pad_maximum_fusion.3), channel_id=1, source_target_pairs={{0,4},{1,5},{2,10},{3,11},{4,0},{5,1},{6,14},{7,15},{8,12},{9,13},... | collective-permute-start | bytes 1572872 | tf_op jit(solution)/shard_map/ppermute | solution.py:547
  161.8 8.7 %collective-permute-start.16 = (bf16[256,2176]{1,0:T(8,128)(2,1)}, bf16[256,2176]{1,0:T(8,128)(2,1)}, u32[]{:S(2)}, u32[]{:S(2)}) collective-permute-start(bf16[256,2176]{1,0:T(8,128)(2,1)} %constant_dynamic-update-slice_fusion.keep_ref), channel_id=1, source_target_pairs={{0,2},{1,3},{2,0},{3,1},{4,6},{5,7},{6,4},{7,5},{8,10},{9,11},{10,... | collective-permute-start | bytes 3342344 | tf_op jit(solution)/shard_map/ppermute | solution.py:547
  161.9 4.3 %collective-permute-start.23 = (bf16[512,1024]{1,0:T(8,128)(2,1)S(1)}, bf16[512,1024]{1,0:T(8,128)(2,1)}, u32[]{:S(2)}, u32[]{:S(2)}) collective-permute-start(bf16[512,1024]{1,0:T(8,128)(2,1)S(1)} %pad_maximum_fusion.keep_ref), channel_id=1, source_target_pairs={{0,2},{1,3},{2,0},{3,1},{4,6},{5,7},{6,4},{7,5},{8,10},{9,11},{10,... | collective-permute-start | bytes 3145736 | tf_op jit(solution)/shard_map/ppermute | solution.py:547

commit v3 on v2

--- a/solution.py
+++ b/solution.py
@@ -17,8 +17,8 @@
 LANES = 128
 SUMS = 8
 TILE = 16
-TOKS = 256
-VMEM_LIMIT = 50 * 1024 * 1024
+TOKS = 512
+VMEM_LIMIT = 24 * 1024 * 1024
 
 
 def mm(a, b):
@@ -31,6 +31,14 @@
 
 def mm_tn(a, b):
     return lax.dot_general(a, b, (((0,), (0,)), ((), ())), preferred_element_type=F32)
+
+
+def near(*values):
+    return tuple(pltpu.with_memory_space_constraint(v, pltpu.VMEM) for v in values)
+
+
+def far(*values):
+    return tuple(pltpu.with_memory_space_constraint(v, pltpu.HBM) for v in values)
 
 
 def whole(*shape):
@@ -125,28 +133,32 @@
     q_id = lax.broadcasted_iota(jnp.int32, (slots, slots), 0)
     k_id = lax.broadcasted_iota(jnp.int32, (slots, slots), 1)
     eye = q_id == k_id
+    pairs = width // PAIR
+    units = [(r, p) for r in range(rows) for p in range(pairs)]
+
+    def part(r, p, which):
+        return qkv_ref[r * slots : (r + 1) * slots, which * width + p * PAIR : which * width + (p + 1) * PAIR]
+
+    masks = []
     for r in range(rows):
         here = pl.ds(at * rows + r, 1)
         seg = jnp.broadcast_to(seg_ref[here, :].astype(F32), (slots, slots))
         step = jnp.broadcast_to(step_ref[here, :].astype(F32), (slots, slots))
         live = jnp.broadcast_to(pad_ref[here, :], (slots, slots)) == 0
-        visible = ((seg == seg.T) & (step <= step.T) & live) | eye
-        span = slice(r * slots, (r + 1) * slots)
-        for p in range(width // PAIR):
-            cols = slice(p * PAIR, (p + 1) * PAIR)
-            q = qkv_ref[span, p * PAIR : (p + 1) * PAIR]
-            k = qkv_ref[span, width + p * PAIR : width + (p + 1) * PAIR]
-            v = qkv_ref[span, 2 * width + p * PAIR : 2 * width + (p + 1) * PAIR]
-            scores = mm_nt(q, by_head(k * HEAD ** (-0.5)))
-            halves = []
-            for half in (scores[:, :slots], scores[:, slots:]):
-                half = jnp.where(visible, half, -1e30)
-                weight = jnp.exp(half - jnp.max(half, axis=-1, keepdims=True))
-                total = jnp.sum(weight, axis=-1, keepdims=True)
-                halves.append((weight * (1.0 / total)).astype(BF))
-            prob = jnp.concatenate(halves, axis=1)
-            prob_ref[r, p] = prob
-            mixed_ref[span, cols] = mm(prob, by_head(v)).astype(BF)
+        masks.append(((seg == seg.T) & (step <= step.T) & live) | eye)
+    scores = [mm_nt(part(r, p, 0), by_head(part(r, p, 1) * HEAD ** (-0.5))) for r, p in units]
+    probs = []
+    for (r, p), score in zip(units, scores):
+        halves = []
+        for half in (score[:, :slots], score[:, slots:]):
+            half = jnp.where(masks[r], half, -1e30)
+            weight = jnp.exp(half - jnp.max(half, axis=-1, keepdims=True))
+            total = jnp.sum(weight, axis=-1, keepdims=True)
+            halves.append((weight * (1.0 / total)).astype(BF))
+        probs.append(jnp.concatenate(halves, axis=1))
+    for (r, p), prob in zip(units, probs):
+        prob_ref[r, p] = prob
+        mixed_ref[r * slots : (r + 1) * slots, p * PAIR : (p + 1) * PAIR] = mm(prob, by_head(part(r, p, 2))).astype(BF)
     residual = tokens + mm(mixed_ref[...], wout_ref[...])
     res_ref[...] = residual
     unit, _ = unit_parts(residual)
@@ -172,15 +184,15 @@
             rows_of(width),
         ],
         [
-            jax.ShapeDtypeStruct((n, 3 * width), BF),
-            jax.ShapeDtypeStruct((rows, pairs, slots, 2 * slots), BF),
-            jax.ShapeDtypeStruct((n, width), BF),
-            jax.ShapeDtypeStruct((n, width), F32),
-            jax.ShapeDtypeStruct((n, width), BF),
+            pltpu.HBM((n, 3 * width), BF),
+            pltpu.HBM((rows, pairs, slots, 2 * slots), BF),
+            pltpu.HBM((n, width), BF),
+            pltpu.HBM((n, width), F32),
+            pltpu.VMEM((n, width), BF),
         ],
         [],
         info,
-        (tokens, g1, c1, wqkv, wout, g2, c2, seg, step, pad),
+        far(tokens, g1, c1) + (wqkv, wout) + far(g2, c2, seg, step, pad),
     )
 
 
@@ -240,12 +252,12 @@
         + [pl.BlockSpec((1, units), chunk(i)) for i in range(2)]
         + [pl.BlockSpec((units, width), lambda t, info, i=i: (info[0] ^ i, 0)) for i in range(2)],
         [rows_of(width)] * 2 + [whole(width, 2 * units)] * 2 + [whole(1, units)] * 2,
-        [jax.ShapeDtypeStruct((n, width), F32)] * 2
+        [pltpu.VMEM((n, width), F32)] * 2
         + [jax.ShapeDtypeStruct((width, 2 * units), BF)] * 2
         + [jax.ShapeDtypeStruct((1, units), F32)] * 2,
         [pltpu.VMEM((width, 2 * units), F32)] * 2 + [pltpu.VMEM((1, units), F32)] * 2,
         info,
-        (second, dy, up, up, bias, bias, down, down),
+        near(second) + far(dy) + (up, up) + far(bias, bias) + (down, down),
     )
 
 
@@ -313,10 +325,10 @@
         + [whole(1, units)] * count,
         [
             jax.ShapeDtypeStruct((n, width), BF),
-            jax.ShapeDtypeStruct((n, width), F32),
-            jax.ShapeDtypeStruct((n, width), BF),
+            pltpu.HBM((n, width), F32),
+            pltpu.HBM((n, width), BF),
             jax.ShapeDtypeStruct((8, width), F32),
-            jax.ShapeDtypeStruct((width, width), F32),
+            pltpu.HBM((width, width), F32),
         ]
         + [jax.ShapeDtypeStruct((width, 2 * units), BF)] * count
         + [jax.ShapeDtypeStruct((1, units), F32)] * count,
@@ -324,7 +336,7 @@
         + [pltpu.VMEM((1, units), F32)] * count
         + [pltpu.VMEM((width, width), F32)],
         info,
-        (second, dy, out_part, dsec_part, residual, mixed, bdown, g2, wout)
+        near(second) + far(dy) + near(out_part, dsec_part) + far(residual, mixed) + far(bdown, g2) + (wout,)
         + tuple(c[0] for c in chunks)
         + tuple(c[1] for c in chunks),
     )
@@ -346,29 +358,33 @@
         row_ref[SUMS : SUMS + vec_ref.shape[0], :] = vec_ref[...]
 
     scale = HEAD ** (-0.5)
-    for r in range(rows):
-        span = slice(r * slots, (r + 1) * slots)
-        for p in range(pairs):
-            cols = slice(p * PAIR, (p + 1) * PAIR)
-            kcols = slice(width + p * PAIR, width + (p + 1) * PAIR)
-            vcols = slice(2 * width + p * PAIR, 2 * width + (p + 1) * PAIR)
-            q = qkv_ref[span, cols]
-            k = qkv_ref[span, kcols]
-            v = qkv_ref[span, vcols]
-            g = gmix_ref[span, cols]
-            prob = prob_ref[r, p]
-            dprob = mm_nt(g, by_head(v))
-            p32 = prob.astype(F32)
-            prod = p32 * dprob
-            first = jnp.sum(prod[:, :slots], axis=-1, keepdims=True)
-            second = jnp.sum(prod[:, slots:], axis=-1, keepdims=True)
-            ds_a = (p32[:, :slots] * (dprob[:, :slots] - first)).astype(BF)
-            ds_b = (p32[:, slots:] * (dprob[:, slots:] - second)).astype(BF)
-            dqkv_ref[span, cols] = mm(jnp.concatenate([ds_a, ds_b], axis=1), by_head(k * scale)).astype(BF)
-            dqkv_ref[span, kcols] = mm_tn(jnp.concatenate([ds_a, ds_b], axis=0), by_head(q * scale)).astype(BF)
-            dqkv_ref[span, vcols] = mm_tn(
-                jnp.concatenate([prob[:, :slots], prob[:, slots:]], axis=0), by_head(g)
-            ).astype(BF)
+    units = [(r, p) for r in range(rows) for p in range(pairs)]
+
+    def place(r, p, which):
+        return (slice(r * slots, (r + 1) * slots), slice(which * width + p * PAIR, which * width + (p + 1) * PAIR))
+
+    grads = [gmix_ref[place(r, p, 0)] for r, p in units]
+    dprobs = [mm_nt(g, by_head(qkv_ref[place(r, p, 2)])) for (r, p), g in zip(units, grads)]
+    for (r, p), g in zip(units, grads):
+        prob = prob_ref[r, p]
+        stacked = jnp.concatenate([prob[:, :slots], prob[:, slots:]], axis=0)
+        dqkv_ref[place(r, p, 2)] = mm_tn(stacked, by_head(g)).astype(BF)
+    dscores = []
+    for (r, p), dprob in zip(units, dprobs):
+        p32 = prob_ref[r, p].astype(F32)
+        prod = p32 * dprob
+        first = jnp.sum(prod[:, :slots], axis=-1, keepdims=True)
+        second = jnp.sum(prod[:, slots:], axis=-1, keepdims=True)
+        dscores.append((
+            (p32[:, :slots] * (dprob[:, :slots] - first)).astype(BF),
+            (p32[:, slots:] * (dprob[:, slots:] - second)).astype(BF),
+        ))
+    for (r, p), ds in zip(units, dscores):
+        k = qkv_ref[place(r, p, 1)]
+        dqkv_ref[place(r, p, 0)] = mm(jnp.concatenate(ds, axis=1), by_head(k * scale)).astype(BF)
+    for (r, p), ds in zip(units, dscores):
+        q = qkv_ref[place(r, p, 0)]
+        dqkv_ref[place(r, p, 1)] = mm_tn(jnp.concatenate(ds, axis=0), by_head(q * scale)).astype(BF)
     unit, _ = unit_parts(tok_ref[...].astype(F32))
     acc_ref[:, : 3 * width] += mm_tn(unit.astype(BF), dqkv_ref[...])
     grad_ref[...] = dqkv_ref[...]
@@ -407,14 +423,14 @@
             whole(width, width),
         ],
         [rows_of(3 * width)] + [whole(width // 2, 4 * width + LANES)] * 2,
-        [jax.ShapeDtypeStruct((n, 3 * width), BF)] + [jax.ShapeDtypeStruct((width // 2, 4 * width + LANES), BF)] * 2,
+        [pltpu.VMEM((n, 3 * width), BF)] + [jax.ShapeDtypeStruct((width // 2, 4 * width + LANES), BF)] * 2,
         [
             pltpu.VMEM((TOKS, 3 * width), BF),
             pltpu.VMEM((width, 4 * width + LANES), F32),
             pltpu.VMEM((LANES, width), F32),
         ],
         info,
-        (qkv, prob, gmix, tokens, vec, dwout),
+        far(qkv, prob, gmix, tokens, vec, dwout),
     )
 
 
@@ -435,7 +451,7 @@
         jax.ShapeDtypeStruct((n, width), F32),
         [],
         info,
-        (dqkv, wqkv, tokens, gres, g1),
+        near(dqkv) + (wqkv,) + far(tokens, gres, g1),
     )
 
 
@@ -606,7 +622,7 @@
     qkv, prob, mixed, residual, second = attend(
         info, tokens_in, g1, c1, w_qkv, w_out, g2, row(ln2_bias), segment_ids, step_ids, pad_mask
     )
-    second, fetched = after(second, fetched)
+    fetched = after(second, fetched)[1]
     chunks = []
     for up, down in fetched[1:]:
         chunks += [(up, down), (swap(up, core_mask), swap(down, core_mask))]

time: 177 us -> 164 us (0.927)
  Pallas kernels: 72.8 us -> 60.8 us
  local copies, waits for them, and re-layouts: 10.3 us -> 7.9 us
    pallas_call x7, Pallas kernels: 72.8 us -> 60.8 us  [call(): pl.pallas_call(kernel, grid_spec=pltpu.PrefetchScalarGridSpec(num_scalar_...]
    unnamed x45 -> x21, local copies, waits for them, and re-layouts: 5.08 us -> 2.08 us
  transfers between devices with their start and end apart: 24 -> 24, of which waited for: 14 -> 14; matrix products, arithmetic and copies ran while one was open for 4% -> 6% of each run, Pallas kernels for 38% -> 34%
where the time goes in v3:
time: 164 us
  Pallas kernels  60.8 us (37%)
  waiting for transfers between devices  58.1 us (35%)
  starting transfers between devices  27.7 us (17%)
  other arithmetic  8.22 us (5%)
  local copies, waits for them, and re-layouts  7.9 us (5%)
    pallas_call x7, Pallas kernels, call(): pl.pallas_call(kernel, grid_spec=pltpu.PrefetchScalarGridSpec(num_scalar_...  60.8 us
    ppermute x24, waiting for transfers between devices, swap(): return lax.ppermute(value, AXES, pairs)  58.1 us
    ppermute x24, starting transfers between devices, swap(): return lax.ppermute(value, AXES, pairs)  27.7 us
    convert_element_type x10, other arithmetic, add(): return (a.astype(F32) + b.astype(F32)).astype(a.dtype)  5.81 us
  transfers between devices with their start and end apart: 24, of which 14 were waited for; matrix products, arithmetic and copies ran while one was open for 6% of the time, Pallas kernels for 34%

profile of v3, /device:TPU:0, one launch (start us, length us, event | category | flops | bytes accessed | tf_op | source)
XLA Modules:
  0.0 163.7 jit_solution(3691789132609909016)
XLA Ops:
  0.7 1.2 constant_dynamic-slice_fusion.2
  1.8 0.8 dynamic_slice.13
  2.6 0.8 pad_maximum_fusion.2
  3.4 2.9 %collective-permute-start = (bf16[528,512]{1,0:T(8,128)(2,1)}, bf16[528,512]{1,0:T(8,128)(2,1)}, u32[]{:S(2)}, u32[]{:S(2)}) collective-permute-start(bf16[528,512]{1,0:T(8,128)(2,1)} %pad_maximum_fusion.2), channel_id=1, source_target_pairs={{0,1},{1,0},{2,3},{3,2},{4,5},{5,4},{6,7},{7,6},{8,9},{9,8},{10,11... | collective-permute-start | bytes 1622024 | tf_op jit(solution)/shard_map/ppermute | solution.py:563
  6.4 0.8 constant_dynamic-slice_fusion.1
  7.3 9.1 %attend.1 = (bf16[1024,1536]{1,0:T(8,128)(2,1)}, bf16[8,4,128,256]{3,2,1,0:T(8,128)(2,1)}, bf16[1024,512]{1,0:T(8,128)(2,1)}, f32[1024,512]{1,0:T(8,128)}, bf16[1024,512]{1,0:T(8,128)(2,1)S(1)}) custom-call(s32[3]{0:T(128)S(1)} %pad_add_fusion.info_ref, bf16[1024,512]{1,0:T(8,128)(2,1)} %tok_ref.5, f32[1,512]{1,0:T(1,128)} %bitcast.18, f32[1,512]{1,0:T(1,128)} %bitcast.21, ...), custom_call_target="tpu_custom_call" | custom-call | flops 1000 | bytes 1000 | tf_op jit(solution)/shard_map/attend/pallas_call | solution.py:53
  16.4 0.6 broadcast_in_dim.28.refs_2_.refs_3_
  17.0 10.9 %ffn_own.1 = (f32[1024,512]{1,0:T(8,128)S(1)}, f32[1024,512]{1,0:T(8,128)S(1)}, bf16[512,1024]{1,0:T(8,128)(2,1)S(1)}, bf16[512,1024]{1,0:T(8,128)(2,1)}, f32[1,512]{1,0:T(1,128)S(1)}, /*index=5*/f32[1,512]{1,0:T(1,128)S(1)}) custom-call(s32[3]{0:T(128)S(1)} %pad_add_fusion.info_ref, bf16[1024,512]{1,0:T(8,128)(2,1)S(1)} %get-tuple-element.49.sec_ref, ...), custom_call_target="tpu_custom_call" | custom-call | flops 1000 | bytes 1000 | tf_op jit(solution)/shard_map/ffn_own/pallas_call | solution.py:53
  27.9 2.3 %collective-permute-done.1.refs_2_ = bf16[512,512]{1,0:T(8,128)(2,1)} collective-permute-done((bf16[512,512]{1,0:T(8,128)(2,1)}, bf16[512,512]{1,0:T(8,128)(2,1)}, u32[]{:S(2)}, u32[]{:S(2)}) %collective-permute-start.1) | collective-permute-done | bytes 524320 | tf_op jit(solution)/shard_map/ppermute | solution.py:563
  30.7 2.4 %collective-permute-done.3.refs_3_ = bf16[512,512]{1,0:T(8,128)(2,1)S(1)} collective-permute-done((bf16[512,512]{1,0:T(8,128)(2,1)}, bf16[512,512]{1,0:T(8,128)(2,1)S(1)}, u32[]{:S(2)}, u32[]{:S(2)}) %collective-permute-start.3) | collective-permute-done | bytes 524320 | tf_op jit(solution)/shard_map/ppermute | solution.py:563
  33.1 15.7 %ffn_rest.1 = (bf16[1024,512]{1,0:T(8,128)(2,1)}, f32[1024,512]{1,0:T(8,128)}, bf16[1024,512]{1,0:T(8,128)(2,1)}, f32[8,512]{1,0:T(8,128)S(1)}, f32[512,512]{1,0...) custom-call(s32[3]{0:T(128)S(1)} %pad_add_fusion.info_ref, ...), custom_call_target="tpu_custom_call" | custom-call | flops 1000 | bytes 1000 | tf_op jit(solution)/shard_map/ffn_rest/pallas_call | solution.py:53
  49.1 2.9 %add_convert_fusion.3 = bf16[512,1024]{1,0:T(8,128)(2,1)} fusion(bf16[512,1024]{1,0:T(8,128)(2,1)} %collective-permute-done.4, bf16[512,1024]{1,0:T(8,128)(2,1)} %copy-done.4), kind=kLoop, calls=%fused_computation.3 | loop fusion | flops 2097152 | bytes 3145728 | tf_op jit(solution)/shard_map/convert_element_type | solution.py:566
  52.2 1.6 add_convert_fusion.2
  53.9 1.8 %collective-permute-start.7 = (bf16[512,1024]{1,0:T(8,128)(2,1)S(1)}, bf16[512,1024]{1,0:T(8,128)(2,1)S(1)}, u32[]{:S(2)}, u32[]{:S(2)}) collective-permute-start(bf16[512,1024]{1,0:T(8,128)(2,1)S(1)} %add_convert_fusion.2), channel_id=1, source_target_pairs={{0,1},{1,0},{2,3},{3,2},{4,5},{5,4},{6,7},{7,6},{8,9},{9,8},{10,11... | collective-permute-start | bytes 3145736 | tf_op jit(solution)/shard_map/ppermute | solution.py:563
  55.7 0.6 pad_maximum_fusion.7.vec_ref
  56.3 10.4 %attend_back.1 = (bf16[1024,1536]{1,0:T(8,128)(2,1)S(1)}, bf16[256,2176]{1,0:T(8,128)(2,1)S(1)}, bf16[256,2176]{1,0:T(8,128)(2,1)S(1)}) custom-call(s32[3]{0:T(128)S(1)} %pad_add_fusion.info_ref, bf16[1024,1536]{1,0:T(8,128)(2,1)} %get-tuple-element.57.qkv_ref, bf16[8,4,128,256]{3,2,1,0:T(8,128)(2,1)} %get-tuple-element.58.prob_ref, ...), custom_call_target="tpu_custom_call" | custom-call | flops 1000 | bytes 1000 | tf_op jit(solution)/shard_map/attend_back/pallas_call | solution.py:53
  66.8 12.5 %collective-permute-done.7 = bf16[512,1024]{1,0:T(8,128)(2,1)S(1)} collective-permute-done((bf16[512,1024]{1,0:T(8,128)(2,1)S(1)}, bf16[512,1024]{1,0:T(8,128)(2,1)S(1)}, u32[]{:S(2)}, u32[]{:S(2)}) %collective-permute-start.7) | collective-permute-done | bytes 1048608 | tf_op jit(solution)/shard_map/ppermute | solution.py:563
  80.2 1.8 %collective-permute-start.8 = (bf16[128,2176]{1,0:T(8,128)(2,1)S(1)}, bf16[128,2176]{1,0:T(8,128)(2,1)S(1)}, u32[]{:S(2)}, u32[]{:S(2)}) collective-permute-start(bf16[128,2176]{1,0:T(8,128)(2,1)S(1)} %slice.61), channel_id=1, source_target_pairs={{0,1},{1,0},{2,6},{3,7},{4,5},{5,4},{6,2},{7,3},{8,9},{9,8},{10,14... | collective-permute-start | bytes 1671176 | tf_op jit(solution)/shard_map/ppermute | solution.py:563
  82.0 5.5 %first_back.1 = f32[1024,512]{1,0:T(8,128)} custom-call(s32[3]{0:T(128)S(1)} %pad_add_fusion.info_ref, bf16[1024,1536]{1,0:T(8,128)(2,1)S(1)} %get-tuple-element.76.dqkv_ref, bf16[512,1536]{1,0:T(8,128)(2,1)S(1)} %copy-done, bf16[1024,512]{1,0:T(8,128)(2,1)} %tok_ref.5, f32[1024,512]{1,0:T(8,128)} %get-tuple-element.77.gres_ref, f32[1,512]{1,0:T(1,128)} %bitcast.19), custom_call_target="tpu_custom_call" | custom-call | flops 1000 | bytes 1000 | tf_op jit(solution)/shard_map/first_back/pallas_call | solution.py:53
  87.5 2.3 %collective-permute-done.8 = bf16[128,2176]{1,0:T(8,128)(2,1)S(1)} collective-permute-done((bf16[128,2176]{1,0:T(8,128)(2,1)S(1)}, bf16[128,2176]{1,0:T(8,128)(2,1)S(1)}, u32[]{:S(2)}, u32[]{:S(2)}) %collective-permute-start.8) | collective-permute-done | bytes 557088 | tf_op jit(solution)/shard_map/ppermute | solution.py:563
  90.0 1.8 %collective-permute-start.9 = (bf16[64,2176]{1,0:T(8,128)(2,1)S(1)}, bf16[64,2176]{1,0:T(8,128)(2,1)S(1)}, u32[]{:S(2)}, u32[]{:S(2)}) collective-permute-start(bf16[64,2176]{1,0:T(8,128)(2,1)S(1)} %slice.63), channel_id=1, source_target_pairs={{0,4},{1,5},{2,3},{3,2},{4,0},{5,1},{6,7},{7,6},{8,12},{9,13},{10,... | collective-permute-start | bytes 835592 | tf_op jit(solution)/shard_map/ppermute | solution.py:563
  92.2 4.4 %collective-permute-done.9 = bf16[64,2176]{1,0:T(8,128)(2,1)S(1)} collective-permute-done((bf16[64,2176]{1,0:T(8,128)(2,1)S(1)}, bf16[64,2176]{1,0:T(8,128)(2,1)S(1)}, u32[]{:S(2)}, u32[]{:S(2)}) %collective-permute-start.9) | collective-permute-done | bytes 278560 | tf_op jit(solution)/shard_map/ppermute | solution.py:563
  96.7 1.9 %collective-permute-start.10 = (bf16[32,2176]{1,0:T(8,128)(2,1)S(1)}, bf16[32,2176]{1,0:T(8,128)(2,1)S(1)}, u32[]{:S(2)}, u32[]{:S(2)}) collective-permute-start(bf16[32,2176]{1,0:T(8,128)(2,1)S(1)} %slice.81), channel_id=1, source_target_pairs={{0,8},{1,9},{2,10},{3,11},{4,12},{5,13},{6,14},{7,15},{8,0},{9,1},... | collective-permute-start | bytes 417800 | tf_op jit(solution)/shard_map/ppermute | solution.py:563
  98.6 4.2 %collective-permute-done.17 = bf16[256,1024]{1,0:T(8,128)(2,1)S(1)} collective-permute-done((bf16[256,1024]{1,0:T(8,128)(2,1)S(1)}, bf16[256,1024]{1,0:T(8,128)(2,1)S(1)}, u32[]{:S(2)}, u32[]{:S(2)}) %collective-permute-start.17) | collective-permute-done | bytes 524320 | tf_op jit(solution)/shard_map/ppermute | solution.py:563
  103.0 2.2 %collective-permute-start.18 = (bf16[128,1024]{1,0:T(8,128)(2,1)S(1)}, bf16[128,1024]{1,0:T(8,128)(2,1)S(1)}, u32[]{:S(2)}, u32[]{:S(2)}) collective-permute-start(bf16[128,1024]{1,0:T(8,128)(2,1)S(1)} %slice.85), channel_id=1, source_target_pairs={{0,8},{1,9},{2,6},{3,7},{4,12},{5,13},{6,2},{7,3},{8,0},{9,1},{10,... | collective-permute-start | bytes 786440 | tf_op jit(solution)/shard_map/ppermute | solution.py:563
  105.3 2.6 %collective-permute-start.11 = (bf16[16,2176]{1,0:T(8,128)(2,1)S(1)}, bf16[16,2176]{1,0:T(8,128)(2,1)S(1)}, u32[]{:S(2)}, u32[]{:S(2)}) collective-permute-start(bf16[16,2176]{1,0:T(8,128)(2,1)S(1)} %slice.83), channel_id=1, source_target_pairs={{0,16},{1,17},{2,18},{3,19},{4,20},{5,21},{6,22},{7,23},{8,24},{9,... | collective-permute-start | bytes 208904 | tf_op jit(solution)/shard_map/ppermute | solution.py:563
  107.9 3.4 %collective-permute-done.18 = bf16[128,1024]{1,0:T(8,128)(2,1)S(1)} collective-permute-done((bf16[128,1024]{1,0:T(8,128)(2,1)S(1)}, bf16[128,1024]{1,0:T(8,128)(2,1)S(1)}, u32[]{:S(2)}, u32[]{:S(2)}) %collective-permute-start.18) | collective-permute-done | bytes 262176 | tf_op jit(solution)/shard_map/ppermute | solution.py:563
  111.4 3.5 %collective-permute-start.19 = (bf16[64,1024]{1,0:T(8,128)(2,1)S(1)}, bf16[64,1024]{1,0:T(8,128)(2,1)S(1)}, u32[]{:S(2)}, u32[]{:S(2)}) collective-permute-start(bf16[64,1024]{1,0:T(8,128)(2,1)S(1)} %slice.87), channel_id=1, source_target_pairs={{0,16},{1,17},{2,18},{3,19},{4,20},{5,21},{6,22},{7,23},{8,24},{9,... | collective-permute-start | bytes 393224 | tf_op jit(solution)/shard_map/ppermute | solution.py:563
  114.9 0.6 constant_dynamic-update-slice_fusion.4
  115.8 5.8 %collective-permute-done.19 = bf16[64,1024]{1,0:T(8,128)(2,1)S(1)} collective-permute-done((bf16[64,1024]{1,0:T(8,128)(2,1)S(1)}, bf16[64,1024]{1,0:T(8,128)(2,1)S(1)}, u32[]{:S(2)}, u32[]{:S(2)}) %collective-permute-start.19) | collective-permute-done | bytes 131104 | tf_op jit(solution)/shard_map/ppermute | solution.py:563
  121.8 0.6 collective-permute-done.12
  122.4 3.4 %collective-permute-start.13 = (bf16[32,2176]{1,0:T(8,128)(2,1)S(1)}, bf16[32,2176]{1,0:T(8,128)(2,1)S(1)}, u32[]{:S(2)}, u32[]{:S(2)}) collective-permute-start(bf16[32,2176]{1,0:T(8,128)(2,1)S(1)} %pad_maximum_fusion.6), channel_id=1, source_target_pairs={{0,8},{1,9},{2,10},{3,11},{4,12},{5,13},{6,14},{7,15},{8,0},{9,1},... | collective-permute-start | bytes 417800 | tf_op jit(solution)/shard_map/ppermute | solution.py:563
  125.8 3.3 %collective-permute-done.20 = bf16[64,1024]{1,0:T(8,128)(2,1)S(1)} collective-permute-done((bf16[64,1024]{1,0:T(8,128)(2,1)S(1)}, bf16[64,1024]{1,0:T(8,128)(2,1)S(1)}, u32[]{:S(2)}, u32[]{:S(2)}) %collective-permute-start.20) | collective-permute-done | bytes 131104 | tf_op jit(solution)/shard_map/ppermute | solution.py:563
  129.7 1.6 collective-permute-start.14
  131.2 0.6 constant_dynamic-update-slice_fusion.3
  131.9 6.5 %collective-permute-done.14 = bf16[64,2176]{1,0:T(8,128)(2,1)S(1)} collective-permute-done((bf16[64,2176]{1,0:T(8,128)(2,1)S(1)}, bf16[64,2176]{1,0:T(8,128)(2,1)S(1)}, u32[]{:S(2)}, u32[]{:S(2)}) %collective-permute-start.14) | collective-permute-done | bytes 278560 | tf_op jit(solution)/shard_map/ppermute | solution.py:563
  138.4 0.5 collective-permute-start.15
  138.9 0.7 constant_dynamic-update-slice_fusion.2
  139.6 1.5 collective-permute-start.22
  141.1 0.7 constant_dynamic-update-slice_fusion.1
  141.9 6.1 %collective-permute-done.15 = bf16[128,2176]{1,0:T(8,128)(2,1)S(1)} collective-permute-done((bf16[128,2176]{1,0:T(8,128)(2,1)S(1)}, bf16[128,2176]{1,0:T(8,128)(2,1)S(1)}, u32[]{:S(2)}, u32[]{:S(2)}) %collective-permute-start.15) | collective-permute-done | bytes 557088 | tf_op jit(solution)/shard_map/ppermute | solution.py:563
  148.0 0.9 constant_dynamic-update-slice_fusion.keep_ref
  149.0 0.6 collective-permute-start.23
  149.5 3.7 %collective-permute-done.23.other_ref = bf16[512,1024]{1,0:T(8,128)(2,1)} collective-permute-done((bf16[512,1024]{1,0:T(8,128)(2,1)S(1)}, bf16[512,1024]{1,0:T(8,128)(2,1)}, u32[]{:S(2)}, u32[]{:S(2)}) %collective-permute-start.23) | collective-permute-done | bytes 1048608 | tf_op jit(solution)/shard_map/ppermute | solution.py:563
  153.3 4.3 %ffn_end.1 = (f32[512,1024]{1,0:T(8,128)}, f32[1024,512]{1,0:T(8,128)}) custom-call(s32[3]{0:T(128)S(1)} %pad_add_fusion.info_ref, bf16[512,1024]{1,0:T(8,128)(2,1)S(1)} %pad_maximum_fusion.keep_ref, bf16[512,1024]{1,0:T(8,128)(2,1)} %collective-permute-done.23.other_ref), custom_call_target="tpu_custom_call" | custom-call | flops 1000 | bytes 1000 | tf_op jit(solution)/shard_map/ffn_end/pallas_call | solution.py:53
  157.6 4.9 %attend_end.1 = (f32[512,1536]{1,0:T(8,128)}, f32[512,512]{1,0:T(8,128)}, f32[20,512]{1,0:T(8,128)S(1)}) custom-call(s32[3]{0:T(128)S(1)} %pad_add_fusion.info_ref, bf16[256,2176]{1,0:T(8,128)(2,1)} %constant_dynamic-update-slice_fusion.keep_ref, bf16[256,2176]{1,0:T(8,128)(2,1)} %collective-permute-done.16.other_ref, bf16[512,1536]{1,0:T(8,128)(2,1)S(1)} %copy-done, ...), custom_call_target="tpu_custom_call" | custom-call | flops 1000 | bytes 1000 | tf_op jit(solution)/shard_map/attend_end/pallas_call | solution.py:53
  162.5 0.6 fusion
  163.1 0.6 constant_dynamic-slice_fusion
  (74 shorter events, 4.1 us)
Async XLA Ops:
  0.6 5.7 %copy-start.2 = (bf16[1024,512]{1,0:T(8,128)(2,1)S(1)}, bf16[1024,512]{1,0:T(8,128)(2,1)}, u32[]{:S(2)}) copy-start(bf16[1024,512]{1,0:T(8,128)(2,1)} %refs_5_.1) | copy-start | bytes 3145732
  2.6 4.7 %copy-start = (bf16[512,1536]{1,0:T(8,128)(2,1)S(1)}, bf16[512,1536]{1,0:T(8,128)(2,1)}, u32[]{:S(2)}) copy-start(bf16[512,1536]{1,0:T(8,128)(2,1)} %w_ref.1) | copy-start | bytes 4718596
  2.6 4.7 %copy-start.3 = (bf16[512,512]{1,0:T(8,128)(2,1)S(1)}, bf16[512,512]{1,0:T(8,128)(2,1)}, u32[]{:S(2)}) copy-start(bf16[512,512]{1,0:T(8,128)(2,1)} %wout_ref.3) | copy-start | bytes 1572868
  3.4 26.8 %collective-permute-start = (bf16[528,512]{1,0:T(8,128)(2,1)}, bf16[528,512]{1,0:T(8,128)(2,1)}, u32[]{:S(2)}, u32[]{:S(2)}) collective-permute-start(bf16[528,512]{1,0:T(8,128)(2,1)} %pad_maximum_fusion.2), channel_id=1, source_target_pairs={{0,1},{1,0},{2,3},{3,2},{4,5},{5,4},{6,7},{7,6},{8,9},{9,8},{10,11... | collective-permute-start | bytes 1622024 | tf_op jit(solution)/shard_map/ppermute | solution.py:563
  7.2 23.0 %collective-permute-start.1 = (bf16[512,512]{1,0:T(8,128)(2,1)}, bf16[512,512]{1,0:T(8,128)(2,1)}, u32[]{:S(2)}, u32[]{:S(2)}) collective-permute-start(bf16[512,512]{1,0:T(8,128)(2,1)} %constant_dynamic-slice_fusion.1), channel_id=1, source_target_pairs={{0,1},{1,0},{2,3},{3,2},{4,5},{5,4},{6,7},{7,6},{8,9},{9,8},{10,11... | collective-permute-start | bytes 1572872 | tf_op jit(solution)/shard_map/ppermute | solution.py:563
  7.3 9.1 %copy-start.8 = (bf16[1024]{0:T(1024)(128)(2,1)S(1)}, bf16[1024]{0:T(1024)(128)(2,1)}, u32[]{:S(2)}) copy-start(bf16[1024]{0:T(1024)(128)(2,1)} %param.23) | copy-start | bytes 6148
  7.3 9.7 %copy-start.1 = (bf16[512,1024]{1,0:T(8,128)(2,1)S(1)}, bf16[512,1024]{1,0:T(8,128)(2,1)}, u32[]{:S(2)}) copy-start(bf16[512,1024]{1,0:T(8,128)(2,1)} %refs_1_.1) | copy-start | bytes 3145732
  27.9 20.9 %copy-start.4 = (bf16[512,1024]{1,0:T(8,128)(2,1)}, bf16[512,1024]{1,0:T(8,128)(2,1)S(1)}, u32[]{:S(2)}) copy-start(bf16[512,1024]{1,0:T(8,128)(2,1)S(1)} %get-tuple-element.60) | copy-start | bytes 3145732
  27.9 21.1 %collective-permute-start.4 = (bf16[512,1024]{1,0:T(8,128)(2,1)}, bf16[512,1024]{1,0:T(8,128)(2,1)}, u32[]{:S(2)}, u32[]{:S(2)}) collective-permute-start(bf16[512,1024]{1,0:T(8,128)(2,1)} %get-tuple-element.61), channel_id=1, source_target_pairs={{0,2},{1,3},{2,0},{3,1},{4,6},{5,7},{6,4},{7,5},{8,10},{9,11},{10,... | collective-permute-start | bytes 3145736 | tf_op jit(solution)/shard_map/ppermute | solution.py:563
  30.2 2.9 %collective-permute-start.2 = (bf16[528,512]{1,0:T(8,128)(2,1)}, bf16[528,512]{1,0:T(8,128)(2,1)S(1)}, u32[]{:S(2)}, u32[]{:S(2)}) collective-permute-start(bf16[528,512]{1,0:T(8,128)(2,1)} %collective-permute-done.refs_0_), channel_id=1, source_target_pairs={{0,2},{1,3},{2,0},{3,1},{4,6},{5,7},{6,4},{7,5},{8,10},{9,11},{10,... | collective-permute-start | bytes 1622024 | tf_op jit(solution)/shard_map/ppermute | solution.py:563
  30.2 2.9 %collective-permute-start.3 = (bf16[512,512]{1,0:T(8,128)(2,1)}, bf16[512,512]{1,0:T(8,128)(2,1)S(1)}, u32[]{:S(2)}, u32[]{:S(2)}) collective-permute-start(bf16[512,512]{1,0:T(8,128)(2,1)} %collective-permute-done.1.refs_2_), channel_id=1, source_target_pairs={{0,2},{1,3},{2,0},{3,1},{4,6},{5,7},{6,4},{7,5},{8,10},{9,11},{10,... | collective-permute-start | bytes 1572872 | tf_op jit(solution)/shard_map/ppermute | solution.py:563
  48.8 3.4 %collective-permute-start.5 = (bf16[512,1024]{1,0:T(8,128)(2,1)}, bf16[512,1024]{1,0:T(8,128)(2,1)}, u32[]{:S(2)}, u32[]{:S(2)}) collective-permute-start(bf16[512,1024]{1,0:T(8,128)(2,1)} %get-tuple-element.63), channel_id=1, source_target_pairs={{0,2},{1,3},{2,0},{3,1},{4,6},{5,7},{6,4},{7,5},{8,10},{9,11},{10,... | collective-permute-start | bytes 3145736 | tf_op jit(solution)/shard_map/ppermute | solution.py:563
  53.9 25.5 %collective-permute-start.7 = (bf16[512,1024]{1,0:T(8,128)(2,1)S(1)}, bf16[512,1024]{1,0:T(8,128)(2,1)S(1)}, u32[]{:S(2)}, u32[]{:S(2)}) collective-permute-start(bf16[512,1024]{1,0:T(8,128)(2,1)S(1)} %add_convert_fusion.2), channel_id=1, source_target_pairs={{0,1},{1,0},{2,3},{3,2},{4,5},{5,4},{6,7},{7,6},{8,9},{9,8},{10,11... | collective-permute-start | bytes 3145736 | tf_op jit(solution)/shard_map/ppermute | solution.py:563
  56.3 23.0 %copy-start.7 = (bf16[512,1024]{1,0:T(8,128)(2,1)S(1)}, bf16[512,1024]{1,0:T(8,128)(2,1)}, u32[]{:S(2)}) copy-start(bf16[512,1024]{1,0:T(8,128)(2,1)} %add_convert_fusion.3) | copy-start | bytes 3145732
  66.7 13.1 %collective-permute-start.6 = (bf16[256,2176]{1,0:T(8,128)(2,1)S(1)}, bf16[256,2176]{1,0:T(8,128)(2,1)S(1)}, u32[]{:S(2)}, u32[]{:S(2)}) collective-permute-start(bf16[256,2176]{1,0:T(8,128)(2,1)S(1)} %get-tuple-element.72), channel_id=1, source_target_pairs={{0,2},{1,3},{2,0},{3,1},{4,6},{5,7},{6,4},{7,5},{8,10},{9,11},{10,... | collective-permute-start | bytes 3342344 | tf_op jit(solution)/shard_map/ppermute | solution.py:563
  80.2 9.6 %collective-permute-start.8 = (bf16[128,2176]{1,0:T(8,128)(2,1)S(1)}, bf16[128,2176]{1,0:T(8,128)(2,1)S(1)}, u32[]{:S(2)}, u32[]{:S(2)}) collective-permute-start(bf16[128,2176]{1,0:T(8,128)(2,1)S(1)} %slice.61), channel_id=1, source_target_pairs={{0,1},{1,0},{2,6},{3,7},{4,5},{5,4},{6,2},{7,3},{8,9},{9,8},{10,14... | collective-permute-start | bytes 1671176 | tf_op jit(solution)/shard_map/ppermute | solution.py:563
  90.0 6.6 %collective-permute-start.9 = (bf16[64,2176]{1,0:T(8,128)(2,1)S(1)}, bf16[64,2176]{1,0:T(8,128)(2,1)S(1)}, u32[]{:S(2)}, u32[]{:S(2)}) collective-permute-start(bf16[64,2176]{1,0:T(8,128)(2,1)S(1)} %slice.63), channel_id=1, source_target_pairs={{0,4},{1,5},{2,3},{3,2},{4,0},{5,1},{6,7},{7,6},{8,12},{9,13},{10,... | collective-permute-start | bytes 835592 | tf_op jit(solution)/shard_map/ppermute | solution.py:563
  91.8 11.0 %collective-permute-start.17 = (bf16[256,1024]{1,0:T(8,128)(2,1)S(1)}, bf16[256,1024]{1,0:T(8,128)(2,1)S(1)}, u32[]{:S(2)}, u32[]{:S(2)}) collective-permute-start(bf16[256,1024]{1,0:T(8,128)(2,1)S(1)} %slice.73), channel_id=1, source_target_pairs={{0,4},{1,5},{2,10},{3,11},{4,0},{5,1},{6,14},{7,15},{8,12},{9,13},... | collective-permute-start | bytes 1572872 | tf_op jit(solution)/shard_map/ppermute | solution.py:563
  96.7 8.6 %collective-permute-start.10 = (bf16[32,2176]{1,0:T(8,128)(2,1)S(1)}, bf16[32,2176]{1,0:T(8,128)(2,1)S(1)}, u32[]{:S(2)}, u32[]{:S(2)}) collective-permute-start(bf16[32,2176]{1,0:T(8,128)(2,1)S(1)} %slice.81), channel_id=1, source_target_pairs={{0,8},{1,9},{2,10},{3,11},{4,12},{5,13},{6,14},{7,15},{8,0},{9,1},... | collective-permute-start | bytes 417800 | tf_op jit(solution)/shard_map/ppermute | solution.py:563
  103.0 8.3 %collective-permute-start.18 = (bf16[128,1024]{1,0:T(8,128)(2,1)S(1)}, bf16[128,1024]{1,0:T(8,128)(2,1)S(1)}, u32[]{:S(2)}, u32[]{:S(2)}) collective-permute-start(bf16[128,1024]{1,0:T(8,128)(2,1)S(1)} %slice.85), channel_id=1, source_target_pairs={{0,8},{1,9},{2,6},{3,7},{4,12},{5,13},{6,2},{7,3},{8,0},{9,1},{10,... | collective-permute-start | bytes 786440 | tf_op jit(solution)/shard_map/ppermute | solution.py:563
  105.3 9.6 %collective-permute-start.11 = (bf16[16,2176]{1,0:T(8,128)(2,1)S(1)}, bf16[16,2176]{1,0:T(8,128)(2,1)S(1)}, u32[]{:S(2)}, u32[]{:S(2)}) collective-permute-start(bf16[16,2176]{1,0:T(8,128)(2,1)S(1)} %slice.83), channel_id=1, source_target_pairs={{0,16},{1,17},{2,18},{3,19},{4,20},{5,21},{6,22},{7,23},{8,24},{9,... | collective-permute-start | bytes 208904 | tf_op jit(solution)/shard_map/ppermute | solution.py:563
  111.4 10.2 %collective-permute-start.19 = (bf16[64,1024]{1,0:T(8,128)(2,1)S(1)}, bf16[64,1024]{1,0:T(8,128)(2,1)S(1)}, u32[]{:S(2)}, u32[]{:S(2)}) collective-permute-start(bf16[64,1024]{1,0:T(8,128)(2,1)S(1)} %slice.87), channel_id=1, source_target_pairs={{0,16},{1,17},{2,18},{3,19},{4,20},{5,21},{6,22},{7,23},{8,24},{9,... | collective-permute-start | bytes 393224 | tf_op jit(solution)/shard_map/ppermute | solution.py:563
  115.5 6.8 %collective-permute-start.12 = (bf16[16,2176]{1,0:T(8,128)(2,1)S(1)}, bf16[16,2176]{1,0:T(8,128)(2,1)S(1)}, u32[]{:S(2)}, u32[]{:S(2)}) collective-permute-start(bf16[16,2176]{1,0:T(8,128)(2,1)S(1)} %get-tuple-element.87), channel_id=1, source_target_pairs={{0,16},{1,17},{2,18},{3,19},{4,20},{5,21},{6,22},{7,23},{8,24},{9,... | collective-permute-start | bytes 208904 | tf_op jit(solution)/shard_map/ppermute | solution.py:563
  121.7 7.4 %collective-permute-start.20 = (bf16[64,1024]{1,0:T(8,128)(2,1)S(1)}, bf16[64,1024]{1,0:T(8,128)(2,1)S(1)}, u32[]{:S(2)}, u32[]{:S(2)}) collective-permute-start(bf16[64,1024]{1,0:T(8,128)(2,1)S(1)} %add_convert_fusion.9), channel_id=1, source_target_pairs={{0,16},{1,17},{2,18},{3,19},{4,20},{5,21},{6,22},{7,23},{8,24},{9,... | collective-permute-start | bytes 393224 | tf_op jit(solution)/shard_map/ppermute | solution.py:563
  122.4 7.3 %collective-permute-start.13 = (bf16[32,2176]{1,0:T(8,128)(2,1)S(1)}, bf16[32,2176]{1,0:T(8,128)(2,1)S(1)}, u32[]{:S(2)}, u32[]{:S(2)}) collective-permute-start(bf16[32,2176]{1,0:T(8,128)(2,1)S(1)} %pad_maximum_fusion.6), channel_id=1, source_target_pairs={{0,8},{1,9},{2,10},{3,11},{4,12},{5,13},{6,14},{7,15},{8,0},{9,1},... | collective-permute-start | bytes 417800 | tf_op jit(solution)/shard_map/ppermute | solution.py:563
  129.1 10.4 %collective-permute-start.21 = (bf16[128,1024]{1,0:T(8,128)(2,1)S(1)}, bf16[128,1024]{1,0:T(8,128)(2,1)S(1)}, u32[]{:S(2)}, u32[]{:S(2)}) collective-permute-start(bf16[128,1024]{1,0:T(8,128)(2,1)S(1)} %pad_maximum_fusion.5), channel_id=1, source_target_pairs={{0,8},{1,9},{2,6},{3,7},{4,12},{5,13},{6,2},{7,3},{8,0},{9,1},{10,... | collective-permute-start | bytes 786440 | tf_op jit(solution)/shard_map/ppermute | solution.py:563
  129.7 8.7 %collective-permute-start.14 = (bf16[64,2176]{1,0:T(8,128)(2,1)S(1)}, bf16[64,2176]{1,0:T(8,128)(2,1)S(1)}, u32[]{:S(2)}, u32[]{:S(2)}) collective-permute-start(bf16[64,2176]{1,0:T(8,128)(2,1)S(1)} %pad_maximum_fusion.4), channel_id=1, source_target_pairs={{0,4},{1,5},{2,3},{3,2},{4,0},{5,1},{6,7},{7,6},{8,12},{9,13},{10,... | collective-permute-start | bytes 835592 | tf_op jit(solution)/shard_map/ppermute | solution.py:563
  138.4 9.6 %collective-permute-start.15 = (bf16[128,2176]{1,0:T(8,128)(2,1)S(1)}, bf16[128,2176]{1,0:T(8,128)(2,1)S(1)}, u32[]{:S(2)}, u32[]{:S(2)}) collective-permute-start(bf16[128,2176]{1,0:T(8,128)(2,1)S(1)} %pad_maximum_fusion.1), channel_id=1, source_target_pairs={{0,1},{1,0},{2,6},{3,7},{4,5},{5,4},{6,2},{7,3},{8,9},{9,8},{10,14... | collective-permute-start | bytes 1671176 | tf_op jit(solution)/shard_map/ppermute | solution.py:563
  139.6 9.3 %collective-permute-start.22 = (bf16[256,1024]{1,0:T(8,128)(2,1)S(1)}, bf16[256,1024]{1,0:T(8,128)(2,1)S(1)}, u32[]{:S(2)}, u32[]{:S(2)}) collective-permute-start(bf16[256,1024]{1,0:T(8,128)(2,1)S(1)} %pad_maximum_fusion.3), channel_id=1, source_target_pairs={{0,4},{1,5},{2,10},{3,11},{4,0},{5,1},{6,14},{7,15},{8,12},{9,13},... | collective-permute-start | bytes 1572872 | tf_op jit(solution)/shard_map/ppermute | solution.py:563
  148.9 8.7 %collective-permute-start.16 = (bf16[256,2176]{1,0:T(8,128)(2,1)}, bf16[256,2176]{1,0:T(8,128)(2,1)}, u32[]{:S(2)}, u32[]{:S(2)}) collective-permute-start(bf16[256,2176]{1,0:T(8,128)(2,1)} %constant_dynamic-update-slice_fusion.keep_ref), channel_id=1, source_target_pairs={{0,2},{1,3},{2,0},{3,1},{4,6},{5,7},{6,4},{7,5},{8,10},{9,11},{10,... | collective-permute-start | bytes 3342344 | tf_op jit(solution)/shard_map/ppermute | solution.py:563
  149.0 8.6 %copy-start.5 = (f32[512]{0:T(512)S(1)}, f32[512]{0:T(512)}, u32[]{:S(2)}) copy-start(f32[512]{0:T(512)} %param.16) | copy-start | bytes 6148
  149.0 8.6 %copy-start.6 = (f32[512]{0:T(512)S(1)}, f32[512]{0:T(512)}, u32[]{:S(2)}) copy-start(f32[512]{0:T(512)} %param.17) | copy-start | bytes 6148
  149.0 4.3 %collective-permute-start.23 = (bf16[512,1024]{1,0:T(8,128)(2,1)S(1)}, bf16[512,1024]{1,0:T(8,128)(2,1)}, u32[]{:S(2)}, u32[]{:S(2)}) collective-permute-start(bf16[512,1024]{1,0:T(8,128)(2,1)S(1)} %pad_maximum_fusion.keep_ref), channel_id=1, source_target_pairs={{0,2},{1,3},{2,0},{3,1},{4,6},{5,7},{6,4},{7,5},{8,10},{9,11},{10,... | collective-permute-start | bytes 3145736 | tf_op jit(solution)/shard_map/ppermute | solution.py:563

commit v4 on v3

--- a/solution.py
+++ b/solution.py
@@ -1,4 +1,5 @@
 import functools
+import itertools
 
 import jax
 import jax.numpy as jnp
@@ -573,41 +574,51 @@
     def after(*values):
         return lax.optimization_barrier(values)
 
-    def scatter(value, order, beside=None):
-        for step, (first, second) in enumerate(zip(*order)):
+    def scatters(order):
+        def step(first, second, value):
             half = value.shape[0] // 2
-            value = add(value[:half], swap(value[half:], first, second))
-            if beside is not None and step == 0:
-                value, beside = after(value, beside)
-        return value if beside is None else (value, beside)
-
-    def gather(value, order):
-        for first, second in reversed(list(zip(*order))):
-            value = jnp.concatenate([value, swap(value, first, second)], axis=0)
-        return value
+            return add(value[:half], swap(value[half:], first, second))
+
+        return [functools.partial(step, *pair) for pair in zip(*order)]
+
+    def exchanges(masks):
+        return [lambda value, mask=mask: add(value, swap(value, mask)) for mask in masks]
+
+    def gathers(order):
+        def step(first, second, value):
+            return jnp.concatenate([value, swap(value, first, second)], axis=0)
+
+        return [functools.partial(step, *pair) for pair in reversed(list(zip(*order)))]
 
     wide_at, narrow_at = lax.axis_index("wide"), lax.axis_index("narrow")
     core = wide_at & 1
     flat = wide_at * narrow + narrow_at
 
-    ff_order = orders(wide_masks)
-    ff_tables = tuple([owner // (2 * narrow) for owner in places(o, wide // 2)] for o in ff_order)
-    masks = narrow_masks + wide_masks
-    split = min(len(masks), (width // TILE).bit_length() - 2)
-    at_order = orders(masks[:split])
-    at_rest = masks[split:]
-    blocks = 1 << split
-    near = [places(o, blocks) for o in at_order]
-    used = [core_mask] + masks[:split]
-
-    def named(owner):
+    def named(owner, used):
         return sum((1 << b) for b, m in enumerate(used) if owner & m)
 
+    def block_of(used):
+        return sum((flat // m & 1) << b for b, m in enumerate(used))
+
+    def halved(masks, tiles):
+        count = min(len(masks) - 1, tiles.bit_length() - 1)
+        return masks[:count], masks[count:]
+
+    ff_used, ff_rest = halved(wide_masks, width // TILE)
+    ff_out = orders(ff_used)
+    ff_in = (ff_used, ff_used) if narrow == 2 else ff_out
+    ff_in_tables, ff_out_tables = (
+        tuple([named(owner, ff_used) for owner in places(o, 1 << len(ff_used))] for o in pair) for pair in (ff_in, ff_out)
+    )
+    at_masks, at_rest = halved(narrow_masks + wide_masks, width // TILE // 2)
+    at_order = orders(at_masks)
+    at_used = [core_mask] + at_masks
+    near_places = [places(o, 1 << len(at_masks)) for o in at_order]
     at_tables = tuple(
-        [named(o) for o in near[c]] + [named(o ^ core_mask) for o in near[1 - c]] for c in range(2)
-    )
-    own_block = sum((flat // m & 1) << b for b, m in enumerate(used))
-    info = jnp.stack([core, wide_at // 2, own_block]).astype(jnp.int32)
+        [named(o, at_used) for o in near_places[c]] + [named(o ^ core_mask, at_used) for o in near_places[1 - c]]
+        for c in range(2)
+    )
+    info = jnp.stack([core, block_of(ff_used), block_of(at_used)]).astype(jnp.int32)
 
     up_chunk = lax.dynamic_slice(w_up, (0, core * units), (width, units))
     bias_chunk = lax.dynamic_slice(b_up, (core * units,), (units,))
@@ -627,10 +638,10 @@
     for up, down in fetched[1:]:
         chunks += [(up, down), (swap(up, core_mask), swap(down, core_mask))]
     out_part, dsec_part, own_keep, own_send, bown_keep, bown_send = ffn_own(
-        info, ff_tables, second, cotangent, w_up, b_up[None], w_down
+        info, ff_in_tables, second, cotangent, w_up, b_up[None], w_down
     )
     rest = ffn_rest(
-        info, ff_tables, second, cotangent, out_part, dsec_part, residual, mixed, row(b_down), g2, w_out, chunks
+        info, ff_in_tables, second, cotangent, out_part, dsec_part, residual, mixed, row(b_down), g2, w_out, chunks
     )
     block_out, gres, gmix, vec, dwout = rest[:5]
     count = len(chunks)
@@ -644,22 +655,39 @@
 
     held = [add(own_keep, swap(own_send, core_mask))]
     held += [add(grads[2 * j], swap(grads[2 * j + 1], core_mask)) for j in range(narrow - 1)]
-    gmix, held = after(gmix, held)
-    for mask in reversed(narrow_masks):
-        held = [add(held[j], swap(held[j + mask], mask)) for j in range(mask)]
+    if narrow == 2:
+        top, mine, other = width // 2, *held
+        ff_keep = jnp.where(core == 0, mine, jnp.concatenate([mine[:top], other[:top]], axis=0))
+        ff_send = jnp.where(core == 0, other, jnp.concatenate([mine[top:], other[top:]], axis=0))
+        gmix, ff_keep, ff_send = after(gmix, ff_keep, ff_send)
+        ff_keep = add(ff_keep, swap(ff_send, narrow_masks[0], ff_used[0]))
+        ff_left = ([ff_used[0]] + ff_used[1:], narrow_masks + ff_used[1:])
+    else:
+        gmix, held = after(gmix, held)
+        for mask in reversed(narrow_masks):
+            held = [add(held[j], swap(held[j + mask], mask)) for j in range(mask)]
+        ff_keep, ff_left = held[0], ff_in
 
     dqkv, keep, send = attend_back(info, at_tables, qkv, prob, gmix, tokens_in, vec, dwout)
-    keep = add(keep, swap(send, core_mask))
-    keep, held = after(keep, held)
+    keep, ff_keep = after(add(keep, swap(send, core_mask)), ff_keep)
     grad_tokens = first_back(info, dqkv, w_qkv, tokens_in, gres, g1)
-    ff_keep = gather(scatter(held[0], ff_order), ff_order)
+    at_steps = scatters(at_order) + exchanges(at_rest) + gathers(at_order)
+    ff_steps = scatters(ff_left) + exchanges(ff_rest) + gathers(ff_out)
+    keep, ff_keep, grad_tokens = after(at_steps[0](keep), ff_steps[0](ff_keep), grad_tokens)
+    at_steps, ff_steps = at_steps[1:], ff_steps[1:]
+    shared = min(len(at_steps), len(ff_steps))
+    for at_step, ff_step in zip(at_steps, ff_steps):
+        keep, ff_keep = after(at_step(keep), ff_step(ff_keep))
+    for ff_step in ff_steps[shared:]:
+        ff_keep = ff_step(ff_keep)
     ff_other = swap(ff_keep, core_mask)
-    grad_w_up, grad_w_down = ffn_end(info, ff_tables, ff_keep, ff_other)
-
-    keep, grad_tokens = scatter(keep, at_order, grad_tokens)
-    for mask in at_rest:
-        keep = add(keep, swap(keep, mask))
-    keep = gather(keep, at_order)
+    for at_step in at_steps[shared : shared + 1]:
+        keep, ff_other = after(at_step(keep), ff_other)
+    ff_done = ffn_end(info, ff_out_tables, ff_keep, ff_other)
+    for at_step in at_steps[shared + 1 :]:
+        keep, ff_done = after(at_step(keep), ff_done)
+    grad_w_up, grad_w_down = ff_done
+
     grad_w_qkv, grad_w_out, vec = attend_end(
         info, at_tables, keep, swap(keep, core_mask), w_qkv, g1, c1, SUMS + vec.shape[0]
     )

time: 164 us -> 158 us (0.963)
  starting transfers between devices: 27.7 us -> 21.9 us
  local copies, waits for them, and re-layouts: 7.9 us -> 10.2 us
  Pallas kernels: 60.8 us -> 59 us
    ppermute x24 -> x22, starting transfers between devices: 27.7 us -> 21.9 us  [swap(): return lax.ppermute(value, AXES, pairs)]
    pallas_call x7, Pallas kernels: 60.8 us -> 59 us  [call(): pl.pallas_call(kernel, grid_spec=pltpu.PrefetchScalarGridSpec(num_scalar_...]
    convert_element_type x10 -> x11, other arithmetic: 5.81 us -> 4.62 us  [add(): return (a.astype(F32) + b.astype(F32)).astype(a.dtype)]
    ppermute x24 -> x22, waiting for transfers between devices: 58.1 us -> 58.6 us  [swap(): return lax.ppermute(value, AXES, pairs)]
  transfers between devices with their start and end apart: 24 -> 22, of which waited for: 14 -> 15; matrix products, arithmetic and copies ran while one was open for 6% -> 4% of each run, Pallas kernels for 34% -> 34%
where the time goes in v4:
time: 158 us
  Pallas kernels  59 us (37%)
  waiting for transfers between devices  58.6 us (37%)
  starting transfers between devices  21.9 us (14%)
  local copies, waits for them, and re-layouts  10.2 us (6%)
  other arithmetic  7.43 us (5%)
    pallas_call x7, Pallas kernels, call(): pl.pallas_call(kernel, grid_spec=pltpu.PrefetchScalarGridSpec(num_scalar_...  59 us
    ppermute x22, waiting for transfers between devices, swap(): return lax.ppermute(value, AXES, pairs)  58.6 us
    ppermute x22, starting transfers between devices, swap(): return lax.ppermute(value, AXES, pairs)  21.9 us
    convert_element_type x11, other arithmetic, add(): return (a.astype(F32) + b.astype(F32)).astype(a.dtype)  4.62 us
    unnamed x28, local copies, waits for them, and re-layouts  3.23 us
  transfers between devices with their start and end apart: 22, of which 15 were waited for; matrix products, arithmetic and copies ran while one was open for 4% of the time, Pallas kernels for 34%

profile of v4, /device:TPU:0, one launch (start us, length us, event | category | flops | bytes accessed | tf_op | source)
XLA Modules:
  0.0 158.0 jit_solution(6565131479206767646)
XLA Ops:
  0.7 1.2 constant_dynamic-slice_fusion.2
  1.9 0.8 dynamic_slice.13
  2.7 0.8 pad_maximum_fusion.3
  3.5 2.9 %collective-permute-start = (bf16[528,512]{1,0:T(8,128)(2,1)}, bf16[528,512]{1,0:T(8,128)(2,1)}, u32[]{:S(2)}, u32[]{:S(2)}) collective-permute-start(bf16[528,512]{1,0:T(8,128)(2,1)} %pad_maximum_fusion.3), channel_id=1, source_target_pairs={{0,1},{1,0},{2,3},{3,2},{4,5},{5,4},{6,7},{7,6},{8,9},{9,8},{10,11... | collective-permute-start | bytes 1622024 | tf_op jit(solution)/shard_map/ppermute | solution.py:564
  6.4 1.9 %constant_dynamic-slice_fusion.1 = bf16[512,512]{1,0:T(8,128)(2,1)} fusion(bf16[1024,512]{1,0:T(8,128)(2,1)} %refs_5_.1, s32[]{:T(128)S(6)} %select_n.62), kind=kLoop, calls=%fused_computation.24 | loop fusion | bytes 1048580 | tf_op jit(solution)/shard_map/dynamic_slice | solution.py:626
  8.5 9.1 %attend.1 = (bf16[1024,1536]{1,0:T(8,128)(2,1)}, bf16[8,4,128,256]{3,2,1,0:T(8,128)(2,1)}, bf16[1024,512]{1,0:T(8,128)(2,1)}, f32[1024,512]{1,0:T(8,128)}, bf16[1024,512]{1,0:T(8,128)(2,1)S(1)}) custom-call(s32[3]{0:T(128)S(1)} %pad_add_fusion.info_ref, bf16[1024,512]{1,0:T(8,128)(2,1)} %tok_ref.5, f32[1,512]{1,0:T(1,128)} %bitcast.18, f32[1,512]{1,0:T(1,128)} %bitcast.21, ...), custom_call_target="tpu_custom_call" | custom-call | flops 1000 | bytes 1000 | tf_op jit(solution)/shard_map/attend/pallas_call | solution.py:54
  17.6 0.6 broadcast_in_dim.28.refs_2_.refs_3_
  18.2 10.9 %ffn_own.1 = (f32[1024,512]{1,0:T(8,128)S(1)}, f32[1024,512]{1,0:T(8,128)S(1)}, bf16[512,1024]{1,0:T(8,128)(2,1)S(1)}, bf16[512,1024]{1,0:T(8,128)(2,1)}, f32[1,512]{1,0:T(1,128)S(1)}, /*index=5*/f32[1,512]{1,0:T(1,128)S(1)}) custom-call(s32[3]{0:T(128)S(1)} %pad_add_fusion.info_ref, bf16[1024,512]{1,0:T(8,128)(2,1)S(1)} %get-tuple-element.63.sec_ref, ...), custom_call_target="tpu_custom_call" | custom-call | flops 1000 | bytes 1000 | tf_op jit(solution)/shard_map/ffn_own/pallas_call | solution.py:54
  29.1 1.0 copy-done.4
  30.8 3.7 %collective-permute-done.3.refs_3_ = bf16[512,512]{1,0:T(8,128)(2,1)S(1)} collective-permute-done((bf16[512,512]{1,0:T(8,128)(2,1)}, bf16[512,512]{1,0:T(8,128)(2,1)S(1)}, u32[]{:S(2)}, u32[]{:S(2)}) %collective-permute-start.3) | collective-permute-done | bytes 524320 | tf_op jit(solution)/shard_map/ppermute | solution.py:564
  34.5 15.5 %ffn_rest.1 = (bf16[1024,512]{1,0:T(8,128)(2,1)}, f32[1024,512]{1,0:T(8,128)}, bf16[1024,512]{1,0:T(8,128)(2,1)}, f32[8,512]{1,0:T(8,128)S(1)}, f32[512,512]{1,0...) custom-call(s32[3]{0:T(128)S(1)} %pad_add_fusion.info_ref, ...), custom_call_target="tpu_custom_call" | custom-call | flops 1000 | bytes 1000 | tf_op jit(solution)/shard_map/ffn_rest/pallas_call | solution.py:54
  49.9 1.0 copy-done.6
  51.1 1.6 %add_convert_fusion.3 = bf16[512,1024]{1,0:T(8,128)(2,1)S(1)} fusion(bf16[512,1024]{1,0:T(8,128)(2,1)} %collective-permute-done.4, bf16[512,1024]{1,0:T(8,128)(2,1)S(1)} %copy-done.5), kind=kLoop, calls=%fused_computation.3 | loop fusion | flops 2097152 | bytes 3145728 | tf_op jit(solution)/shard_map/convert_element_type | solution.py:567
  52.7 1.0 copy-done.10
  53.7 0.9 fusion
  55.1 1.7 %add_convert_fusion.2 = bf16[512,1024]{1,0:T(8,128)(2,1)S(1)} fusion(bf16[512,1024]{1,0:T(8,128)(2,1)} %collective-permute-done.5, bf16[512,1024]{1,0:T(8,128)(2,1)S(1)} %copy-done.7), kind=kLoop, calls=%fused_computation.2 | loop fusion | flops 2097152 | bytes 3145728 | tf_op jit(solution)/shard_map/convert_element_type | solution.py:567
  56.9 1.0 maximum_select_fusion
  57.9 2.0 %collective-permute-start.7 = (bf16[512,1024]{1,0:T(8,128)(2,1)S(1)}, bf16[512,1024]{1,0:T(8,128)(2,1)S(1)}, u32[]{:S(2)}, u32[]{:S(2)}) collective-permute-start(bf16[512,1024]{1,0:T(8,128)(2,1)S(1)} %get-tuple-element.88), channel_id=1, source_target_pairs={{0,1},{1,0},{2,6},{3,7},{4,5},{5,4},{6,2},{7,3},{8,9},{9,8},{10,14... | collective-permute-start | bytes 3145736 | tf_op jit(solution)/shard_map/ppermute | solution.py:564
  59.9 0.6 pad_maximum_fusion.6.vec_ref
  60.5 10.4 %attend_back.1 = (bf16[1024,1536]{1,0:T(8,128)(2,1)S(1)}, bf16[256,2176]{1,0:T(8,128)(2,1)S(1)}, bf16[256,2176]{1,0:T(8,128)(2,1)S(1)}) custom-call(s32[3]{0:T(128)S(1)} %pad_add_fusion.info_ref, bf16[1024,1536]{1,0:T(8,128)(2,1)} %get-tuple-element.71.qkv_ref, bf16[8,4,128,256]{3,2,1,0:T(8,128)(2,1)} %get-tuple-element.72.prob_ref, ...), custom_call_target="tpu_custom_call" | custom-call | flops 1000 | bytes 1000 | tf_op jit(solution)/shard_map/attend_back/pallas_call | solution.py:54
  71.1 1.7 %collective-permute-done.7 = bf16[512,1024]{1,0:T(8,128)(2,1)S(1)} collective-permute-done((bf16[512,1024]{1,0:T(8,128)(2,1)S(1)}, bf16[512,1024]{1,0:T(8,128)(2,1)S(1)}, u32[]{:S(2)}, u32[]{:S(2)}) %collective-permute-start.7) | collective-permute-done | bytes 1048608 | tf_op jit(solution)/shard_map/ppermute | solution.py:564
  73.2 0.6 collective-permute-done.6
  74.1 1.6 %collective-permute-start.9 = (bf16[256,1024]{1,0:T(8,128)(2,1)S(1)}, bf16[256,1024]{1,0:T(8,128)(2,1)S(1)}, u32[]{:S(2)}, u32[]{:S(2)}) collective-permute-start(bf16[256,1024]{1,0:T(8,128)(2,1)S(1)} %slice.67), channel_id=1, source_target_pairs={{0,4},{1,5},{2,3},{3,2},{4,0},{5,1},{6,7},{7,6},{8,12},{9,13},{10,... | collective-permute-start | bytes 1572872 | tf_op jit(solution)/shard_map/ppermute | solution.py:564
  75.7 1.4 collective-permute-start.8
  77.1 5.5 %first_back.1 = f32[1024,512]{1,0:T(8,128)} custom-call(s32[3]{0:T(128)S(1)} %pad_add_fusion.info_ref, bf16[1024,1536]{1,0:T(8,128)(2,1)S(1)} %get-tuple-element.91.dqkv_ref, bf16[512,1536]{1,0:T(8,128)(2,1)S(1)} %copy-done, bf16[1024,512]{1,0:T(8,128)(2,1)} %tok_ref.5, f32[1024,512]{1,0:T(8,128)} %get-tuple-element.92.gres_ref, f32[1,512]{1,0:T(1,128)} %bitcast.19), custom_call_target="tpu_custom_call" | custom-call | flops 1000 | bytes 1000 | tf_op jit(solution)/shard_map/first_back/pallas_call | solution.py:54
  82.6 5.9 %collective-permute-done.9 = bf16[256,1024]{1,0:T(8,128)(2,1)S(1)} collective-permute-done((bf16[256,1024]{1,0:T(8,128)(2,1)S(1)}, bf16[256,1024]{1,0:T(8,128)(2,1)S(1)}, u32[]{:S(2)}, u32[]{:S(2)}) %collective-permute-start.9) | collective-permute-done | bytes 524320 | tf_op jit(solution)/shard_map/ppermute | solution.py:564
  88.9 1.6 %collective-permute-start.11 = (bf16[128,1024]{1,0:T(8,128)(2,1)S(1)}, bf16[128,1024]{1,0:T(8,128)(2,1)S(1)}, u32[]{:S(2)}, u32[]{:S(2)}) collective-permute-start(bf16[128,1024]{1,0:T(8,128)(2,1)S(1)} %slice.71), channel_id=1, source_target_pairs={{0,8},{1,9},{2,10},{3,11},{4,12},{5,13},{6,14},{7,15},{8,0},{9,1},... | collective-permute-start | bytes 786440 | tf_op jit(solution)/shard_map/ppermute | solution.py:564
  90.6 2.0 %collective-permute-start.10 = (bf16[64,2176]{1,0:T(8,128)(2,1)S(1)}, bf16[64,2176]{1,0:T(8,128)(2,1)S(1)}, u32[]{:S(2)}, u32[]{:S(2)}) collective-permute-start(bf16[64,2176]{1,0:T(8,128)(2,1)S(1)} %slice.69), channel_id=1, source_target_pairs={{0,4},{1,5},{2,3},{3,2},{4,0},{5,1},{6,7},{7,6},{8,12},{9,13},{10,... | collective-permute-start | bytes 835592 | tf_op jit(solution)/shard_map/ppermute | solution.py:564
  92.6 5.0 %collective-permute-done.11 = bf16[128,1024]{1,0:T(8,128)(2,1)S(1)} collective-permute-done((bf16[128,1024]{1,0:T(8,128)(2,1)S(1)}, bf16[128,1024]{1,0:T(8,128)(2,1)S(1)}, u32[]{:S(2)}, u32[]{:S(2)}) %collective-permute-start.11) | collective-permute-done | bytes 262176 | tf_op jit(solution)/shard_map/ppermute | solution.py:564
  97.7 1.6 %collective-permute-start.12 = (bf16[32,2176]{1,0:T(8,128)(2,1)S(1)}, bf16[32,2176]{1,0:T(8,128)(2,1)S(1)}, u32[]{:S(2)}, u32[]{:S(2)}) collective-permute-start(bf16[32,2176]{1,0:T(8,128)(2,1)S(1)} %slice.73), channel_id=1, source_target_pairs={{0,8},{1,9},{2,10},{3,11},{4,12},{5,13},{6,14},{7,15},{8,0},{9,1},... | collective-permute-start | bytes 417800 | tf_op jit(solution)/shard_map/ppermute | solution.py:564
  99.4 2.6 %collective-permute-start.13 = (bf16[128,1024]{1,0:T(8,128)(2,1)S(1)}, bf16[128,1024]{1,0:T(8,128)(2,1)S(1)}, u32[]{:S(2)}, u32[]{:S(2)}) collective-permute-start(bf16[128,1024]{1,0:T(8,128)(2,1)S(1)} %add_convert_fusion.8), channel_id=1, source_target_pairs={{0,16},{1,17},{2,18},{3,19},{4,20},{5,21},{6,22},{7,23},{8,24},{9,... | collective-permute-start | bytes 786440 | tf_op jit(solution)/shard_map/ppermute | solution.py:564
  102.0 3.0 %collective-permute-done.12 = bf16[32,2176]{1,0:T(8,128)(2,1)S(1)} collective-permute-done((bf16[32,2176]{1,0:T(8,128)(2,1)S(1)}, bf16[32,2176]{1,0:T(8,128)(2,1)S(1)}, u32[]{:S(2)}, u32[]{:S(2)}) %collective-permute-start.12) | collective-permute-done | bytes 139296 | tf_op jit(solution)/shard_map/ppermute | solution.py:564
  105.0 8.4 %collective-permute-done.13 = bf16[128,1024]{1,0:T(8,128)(2,1)S(1)} collective-permute-done((bf16[128,1024]{1,0:T(8,128)(2,1)S(1)}, bf16[128,1024]{1,0:T(8,128)(2,1)S(1)}, u32[]{:S(2)}, u32[]{:S(2)}) %collective-permute-start.13) | collective-permute-done | bytes 262176 | tf_op jit(solution)/shard_map/ppermute | solution.py:564
  113.6 3.0 %collective-permute-start.15 = (bf16[128,1024]{1,0:T(8,128)(2,1)S(1)}, bf16[128,1024]{1,0:T(8,128)(2,1)S(1)}, u32[]{:S(2)}, u32[]{:S(2)}) collective-permute-start(bf16[128,1024]{1,0:T(8,128)(2,1)S(1)} %add_convert_fusion.7), channel_id=1, source_target_pairs={{0,8},{1,9},{2,6},{3,7},{4,12},{5,13},{6,2},{7,3},{8,0},{9,1},{10,... | collective-permute-start | bytes 786440 | tf_op jit(solution)/shard_map/ppermute | solution.py:564
  116.6 5.1 %collective-permute-done.14 = bf16[32,2176]{1,0:T(8,128)(2,1)S(1)} collective-permute-done((bf16[32,2176]{1,0:T(8,128)(2,1)S(1)}, bf16[32,2176]{1,0:T(8,128)(2,1)S(1)}, u32[]{:S(2)}, u32[]{:S(2)}) %collective-permute-start.14) | collective-permute-done | bytes 139296 | tf_op jit(solution)/shard_map/ppermute | solution.py:564
  121.7 1.7 %collective-permute-done.15 = bf16[128,1024]{1,0:T(8,128)(2,1)S(1)} collective-permute-done((bf16[128,1024]{1,0:T(8,128)(2,1)S(1)}, bf16[128,1024]{1,0:T(8,128)(2,1)S(1)}, u32[]{:S(2)}, u32[]{:S(2)}) %collective-permute-start.15) | collective-permute-done | bytes 262176 | tf_op jit(solution)/shard_map/ppermute | solution.py:564
  123.5 0.7 collective-permute-start.17
  124.2 6.6 %collective-permute-done.16 = bf16[32,2176]{1,0:T(8,128)(2,1)S(1)} collective-permute-done((bf16[32,2176]{1,0:T(8,128)(2,1)S(1)}, bf16[32,2176]{1,0:T(8,128)(2,1)S(1)}, u32[]{:S(2)}, u32[]{:S(2)}) %collective-permute-start.16) | collective-permute-done | bytes 139296 | tf_op jit(solution)/shard_map/ppermute | solution.py:564
  130.8 1.9 %collective-permute-done.17 = bf16[256,1024]{1,0:T(8,128)(2,1)S(1)} collective-permute-done((bf16[256,1024]{1,0:T(8,128)(2,1)S(1)}, bf16[256,1024]{1,0:T(8,128)(2,1)S(1)}, u32[]{:S(2)}, u32[]{:S(2)}) %collective-permute-start.17) | collective-permute-done | bytes 524320 | tf_op jit(solution)/shard_map/ppermute | solution.py:564
  132.9 0.7 collective-permute-start.18
  133.6 5.9 %collective-permute-done.18 = bf16[64,2176]{1,0:T(8,128)(2,1)S(1)} collective-permute-done((bf16[64,2176]{1,0:T(8,128)(2,1)S(1)}, bf16[64,2176]{1,0:T(8,128)(2,1)S(1)}, u32[]{:S(2)}, u32[]{:S(2)}) %collective-permute-start.18) | collective-permute-done | bytes 278560 | tf_op jit(solution)/shard_map/ppermute | solution.py:564
  139.6 0.6 collective-permute-start.20
  140.1 3.1 %ffn_end.1 = (f32[512,1024]{1,0:T(8,128)}, f32[1024,512]{1,0:T(8,128)}) custom-call(s32[3]{0:T(128)S(1)} %pad_add_fusion.info_ref, bf16[512,1024]{1,0:T(8,128)(2,1)S(1)} %pad_maximum_fusion.1.keep_ref, bf16[512,1024]{1,0:T(8,128)(2,1)S(1)} %collective-permute-done.19.other_ref), custom_call_target="tpu_custom_call" | custom-call | flops 1000 | bytes 1000 | tf_op jit(solution)/shard_map/ffn_end/pallas_call | solution.py:54
  143.2 6.0 %collective-permute-done.20 = bf16[128,2176]{1,0:T(8,128)(2,1)S(1)} collective-permute-done((bf16[128,2176]{1,0:T(8,128)(2,1)S(1)}, bf16[128,2176]{1,0:T(8,128)(2,1)S(1)}, u32[]{:S(2)}, u32[]{:S(2)}) %collective-permute-start.20) | collective-permute-done | bytes 557088 | tf_op jit(solution)/shard_map/ppermute | solution.py:564
  149.4 2.9 %collective-permute-done.21.other_ref = bf16[256,2176]{1,0:T(8,128)(2,1)} collective-permute-done((bf16[256,2176]{1,0:T(8,128)(2,1)S(1)}, bf16[256,2176]{1,0:T(8,128)(2,1)}, u32[]{:S(2)}, u32[]{:S(2)}) %collective-permute-start.21) | collective-permute-done | bytes 1114144 | tf_op jit(solution)/shard_map/ppermute | solution.py:564
  152.2 4.6 %attend_end.1 = (f32[512,1536]{1,0:T(8,128)}, f32[512,512]{1,0:T(8,128)}, f32[20,512]{1,0:T(8,128)S(1)}) custom-call(s32[3]{0:T(128)S(1)} %pad_add_fusion.info_ref, bf16[256,2176]{1,0:T(8,128)(2,1)S(1)} %pad_maximum_fusion.keep_ref, bf16[256,2176]{1,0:T(8,128)(2,1)} %collective-permute-done.21.other_ref, bf16[512,1536]{1,0:T(8,128)(2,1)S(1)} %copy-done, ...), custom_call_target="tpu_custom_call" | custom-call | flops 1000 | bytes 1000 | tf_op jit(solution)/shard_map/attend_end/pallas_call | solution.py:54
  156.8 0.6 fusion.2
  157.4 0.6 constant_dynamic-slice_fusion
  (76 shorter events, 3.8 us)
Async XLA Ops:
  0.6 7.8 %copy-start = (bf16[512,1536]{1,0:T(8,128)(2,1)S(1)}, bf16[512,1536]{1,0:T(8,128)(2,1)}, u32[]{:S(2)}) copy-start(bf16[512,1536]{1,0:T(8,128)(2,1)} %w_ref.1) | copy-start | bytes 4718596
  0.7 7.8 %copy-start.3 = (bf16[512,512]{1,0:T(8,128)(2,1)S(1)}, bf16[512,512]{1,0:T(8,128)(2,1)}, u32[]{:S(2)}) copy-start(bf16[512,512]{1,0:T(8,128)(2,1)} %wout_ref.3) | copy-start | bytes 1572868
  3.5 14.1 %copy-start.13 = (bf16[1024]{0:T(1024)(128)(2,1)S(1)}, bf16[1024]{0:T(1024)(128)(2,1)}, u32[]{:S(2)}) copy-start(bf16[1024]{0:T(1024)(128)(2,1)} %param.23) | copy-start | bytes 6148
  3.5 14.7 %copy-start.1 = (bf16[512,1024]{1,0:T(8,128)(2,1)S(1)}, bf16[512,1024]{1,0:T(8,128)(2,1)}, u32[]{:S(2)}) copy-start(bf16[512,1024]{1,0:T(8,128)(2,1)} %refs_1_.1) | copy-start | bytes 3145732
  3.5 26.8 %collective-permute-start = (bf16[528,512]{1,0:T(8,128)(2,1)}, bf16[528,512]{1,0:T(8,128)(2,1)}, u32[]{:S(2)}, u32[]{:S(2)}) collective-permute-start(bf16[528,512]{1,0:T(8,128)(2,1)} %pad_maximum_fusion.3), channel_id=1, source_target_pairs={{0,1},{1,0},{2,3},{3,2},{4,5},{5,4},{6,7},{7,6},{8,9},{9,8},{10,11... | collective-permute-start | bytes 1622024 | tf_op jit(solution)/shard_map/ppermute | solution.py:564
  8.3 22.0 %collective-permute-start.1 = (bf16[512,512]{1,0:T(8,128)(2,1)}, bf16[512,512]{1,0:T(8,128)(2,1)}, u32[]{:S(2)}, u32[]{:S(2)}) collective-permute-start(bf16[512,512]{1,0:T(8,128)(2,1)} %constant_dynamic-slice_fusion.1), channel_id=1, source_target_pairs={{0,1},{1,0},{2,3},{3,2},{4,5},{5,4},{6,7},{7,6},{8,9},{9,8},{10,11... | collective-permute-start | bytes 1572872 | tf_op jit(solution)/shard_map/ppermute | solution.py:564
  8.4 9.8 %copy-start.2 = (bf16[1024,512]{1,0:T(8,128)(2,1)S(1)}, bf16[1024,512]{1,0:T(8,128)(2,1)}, u32[]{:S(2)}) copy-start(bf16[1024,512]{1,0:T(8,128)(2,1)} %refs_5_.1) | copy-start | bytes 3145732
  29.1 1.0 copy-start.4
  30.1 21.0 %collective-permute-start.4 = (bf16[512,1024]{1,0:T(8,128)(2,1)}, bf16[512,1024]{1,0:T(8,128)(2,1)}, u32[]{:S(2)}, u32[]{:S(2)}) collective-permute-start(bf16[512,1024]{1,0:T(8,128)(2,1)} %get-tuple-element.75), channel_id=1, source_target_pairs={{0,2},{1,3},{2,0},{3,1},{4,6},{5,7},{6,4},{7,5},{8,10},{9,11},{10,... | collective-permute-start | bytes 3145736 | tf_op jit(solution)/shard_map/ppermute | solution.py:564
  30.3 4.2 %collective-permute-start.2 = (bf16[528,512]{1,0:T(8,128)(2,1)}, bf16[528,512]{1,0:T(8,128)(2,1)S(1)}, u32[]{:S(2)}, u32[]{:S(2)}) collective-permute-start(bf16[528,512]{1,0:T(8,128)(2,1)} %collective-permute-done.refs_0_), channel_id=1, source_target_pairs={{0,2},{1,3},{2,0},{3,1},{4,6},{5,7},{6,4},{7,5},{8,10},{9,11},{10,... | collective-permute-start | bytes 1622024 | tf_op jit(solution)/shard_map/ppermute | solution.py:564
  30.6 3.9 %collective-permute-start.3 = (bf16[512,512]{1,0:T(8,128)(2,1)}, bf16[512,512]{1,0:T(8,128)(2,1)S(1)}, u32[]{:S(2)}, u32[]{:S(2)}) collective-permute-start(bf16[512,512]{1,0:T(8,128)(2,1)} %collective-permute-done.1.refs_2_), channel_id=1, source_target_pairs={{0,2},{1,3},{2,0},{3,1},{4,6},{5,7},{6,4},{7,5},{8,10},{9,11},{10,... | collective-permute-start | bytes 1572872 | tf_op jit(solution)/shard_map/ppermute | solution.py:564
  34.5 16.6 %copy-start.5 = (bf16[512,1024]{1,0:T(8,128)(2,1)S(1)}, bf16[512,1024]{1,0:T(8,128)(2,1)}, u32[]{:S(2)}) copy-start(bf16[512,1024]{1,0:T(8,128)(2,1)} %copy-done.4) | copy-start | bytes 3145732
  49.9 1.0 copy-start.6
  50.9 3.9 %collective-permute-start.5 = (bf16[512,1024]{1,0:T(8,128)(2,1)}, bf16[512,1024]{1,0:T(8,128)(2,1)}, u32[]{:S(2)}, u32[]{:S(2)}) collective-permute-start(bf16[512,1024]{1,0:T(8,128)(2,1)} %get-tuple-element.77), channel_id=1, source_target_pairs={{0,2},{1,3},{2,0},{3,1},{4,6},{5,7},{6,4},{7,5},{8,10},{9,11},{10,... | collective-permute-start | bytes 3145736 | tf_op jit(solution)/shard_map/ppermute | solution.py:564
  52.7 1.0 copy-start.10
  53.6 1.4 copy-start.7
  55.1 1.8 %copy-start.11 = (bf16[512,1024]{1,0:T(8,128)(2,1)S(1)}, bf16[512,1024]{1,0:T(8,128)(2,1)}, u32[]{:S(2)}) copy-start(bf16[512,1024]{1,0:T(8,128)(2,1)} %copy-done.10) | copy-start | bytes 3145732
  55.1 1.8 %copy-start.12 = (bf16[256,1024]{1,0:T(8,128)(2,1)S(1)}, bf16[256,1024]{1,0:T(8,128)(2,1)}, u32[]{:S(2)}) copy-start(bf16[256,1024]{1,0:T(8,128)(2,1)} %get-tuple-element.115) | copy-start | bytes 1572868
  57.9 14.9 %collective-permute-start.7 = (bf16[512,1024]{1,0:T(8,128)(2,1)S(1)}, bf16[512,1024]{1,0:T(8,128)(2,1)S(1)}, u32[]{:S(2)}, u32[]{:S(2)}) collective-permute-start(bf16[512,1024]{1,0:T(8,128)(2,1)S(1)} %get-tuple-element.88), channel_id=1, source_target_pairs={{0,1},{1,0},{2,6},{3,7},{4,5},{5,4},{6,2},{7,3},{8,9},{9,8},{10,14... | collective-permute-start | bytes 3145736 | tf_op jit(solution)/shard_map/ppermute | solution.py:564
  70.9 2.8 %collective-permute-start.6 = (bf16[256,2176]{1,0:T(8,128)(2,1)S(1)}, bf16[256,2176]{1,0:T(8,128)(2,1)S(1)}, u32[]{:S(2)}, u32[]{:S(2)}) collective-permute-start(bf16[256,2176]{1,0:T(8,128)(2,1)S(1)} %get-tuple-element.86), channel_id=1, source_target_pairs={{0,2},{1,3},{2,0},{3,1},{4,6},{5,7},{6,4},{7,5},{8,10},{9,11},{10,... | collective-permute-start | bytes 3342344 | tf_op jit(solution)/shard_map/ppermute | solution.py:564
  74.1 14.5 %collective-permute-start.9 = (bf16[256,1024]{1,0:T(8,128)(2,1)S(1)}, bf16[256,1024]{1,0:T(8,128)(2,1)S(1)}, u32[]{:S(2)}, u32[]{:S(2)}) collective-permute-start(bf16[256,1024]{1,0:T(8,128)(2,1)S(1)} %slice.67), channel_id=1, source_target_pairs={{0,4},{1,5},{2,3},{3,2},{4,0},{5,1},{6,7},{7,6},{8,12},{9,13},{10,... | collective-permute-start | bytes 1572872 | tf_op jit(solution)/shard_map/ppermute | solution.py:564
  75.7 13.0 %collective-permute-start.8 = (bf16[128,2176]{1,0:T(8,128)(2,1)S(1)}, bf16[128,2176]{1,0:T(8,128)(2,1)S(1)}, u32[]{:S(2)}, u32[]{:S(2)}) collective-permute-start(bf16[128,2176]{1,0:T(8,128)(2,1)S(1)} %slice.65), channel_id=1, source_target_pairs={{0,1},{1,0},{2,6},{3,7},{4,5},{5,4},{6,2},{7,3},{8,9},{9,8},{10,14... | collective-permute-start | bytes 1671176 | tf_op jit(solution)/shard_map/ppermute | solution.py:564
  88.9 8.6 %collective-permute-start.11 = (bf16[128,1024]{1,0:T(8,128)(2,1)S(1)}, bf16[128,1024]{1,0:T(8,128)(2,1)S(1)}, u32[]{:S(2)}, u32[]{:S(2)}) collective-permute-start(bf16[128,1024]{1,0:T(8,128)(2,1)S(1)} %slice.71), channel_id=1, source_target_pairs={{0,8},{1,9},{2,10},{3,11},{4,12},{5,13},{6,14},{7,15},{8,0},{9,1},... | collective-permute-start | bytes 786440 | tf_op jit(solution)/shard_map/ppermute | solution.py:564
  90.6 7.0 %collective-permute-start.10 = (bf16[64,2176]{1,0:T(8,128)(2,1)S(1)}, bf16[64,2176]{1,0:T(8,128)(2,1)S(1)}, u32[]{:S(2)}, u32[]{:S(2)}) collective-permute-start(bf16[64,2176]{1,0:T(8,128)(2,1)S(1)} %slice.69), channel_id=1, source_target_pairs={{0,4},{1,5},{2,3},{3,2},{4,0},{5,1},{6,7},{7,6},{8,12},{9,13},{10,... | collective-permute-start | bytes 835592 | tf_op jit(solution)/shard_map/ppermute | solution.py:564
  97.7 7.2 %collective-permute-start.12 = (bf16[32,2176]{1,0:T(8,128)(2,1)S(1)}, bf16[32,2176]{1,0:T(8,128)(2,1)S(1)}, u32[]{:S(2)}, u32[]{:S(2)}) collective-permute-start(bf16[32,2176]{1,0:T(8,128)(2,1)S(1)} %slice.73), channel_id=1, source_target_pairs={{0,8},{1,9},{2,10},{3,11},{4,12},{5,13},{6,14},{7,15},{8,0},{9,1},... | collective-permute-start | bytes 417800 | tf_op jit(solution)/shard_map/ppermute | solution.py:564
  99.4 14.0 %collective-permute-start.13 = (bf16[128,1024]{1,0:T(8,128)(2,1)S(1)}, bf16[128,1024]{1,0:T(8,128)(2,1)S(1)}, u32[]{:S(2)}, u32[]{:S(2)}) collective-permute-start(bf16[128,1024]{1,0:T(8,128)(2,1)S(1)} %add_convert_fusion.8), channel_id=1, source_target_pairs={{0,16},{1,17},{2,18},{3,19},{4,20},{5,21},{6,22},{7,23},{8,24},{9,... | collective-permute-start | bytes 786440 | tf_op jit(solution)/shard_map/ppermute | solution.py:564
  113.5 8.2 %collective-permute-start.14 = (bf16[32,2176]{1,0:T(8,128)(2,1)S(1)}, bf16[32,2176]{1,0:T(8,128)(2,1)S(1)}, u32[]{:S(2)}, u32[]{:S(2)}) collective-permute-start(bf16[32,2176]{1,0:T(8,128)(2,1)S(1)} %add_convert_fusion.10), channel_id=1, source_target_pairs={{0,16},{1,17},{2,18},{3,19},{4,20},{5,21},{6,22},{7,23},{8,24},{9,... | collective-permute-start | bytes 417800 | tf_op jit(solution)/shard_map/ppermute | solution.py:564
  113.6 9.9 %collective-permute-start.15 = (bf16[128,1024]{1,0:T(8,128)(2,1)S(1)}, bf16[128,1024]{1,0:T(8,128)(2,1)S(1)}, u32[]{:S(2)}, u32[]{:S(2)}) collective-permute-start(bf16[128,1024]{1,0:T(8,128)(2,1)S(1)} %add_convert_fusion.7), channel_id=1, source_target_pairs={{0,8},{1,9},{2,6},{3,7},{4,12},{5,13},{6,2},{7,3},{8,0},{9,1},{10,... | collective-permute-start | bytes 786440 | tf_op jit(solution)/shard_map/ppermute | solution.py:564
  123.5 9.2 %collective-permute-start.17 = (bf16[256,1024]{1,0:T(8,128)(2,1)S(1)}, bf16[256,1024]{1,0:T(8,128)(2,1)S(1)}, u32[]{:S(2)}, u32[]{:S(2)}) collective-permute-start(bf16[256,1024]{1,0:T(8,128)(2,1)S(1)} %pad_maximum_fusion.4), channel_id=1, source_target_pairs={{0,4},{1,5},{2,10},{3,11},{4,0},{5,1},{6,14},{7,15},{8,12},{9,13},... | collective-permute-start | bytes 1572872 | tf_op jit(solution)/shard_map/ppermute | solution.py:564
  124.2 6.6 %collective-permute-start.16 = (bf16[32,2176]{1,0:T(8,128)(2,1)S(1)}, bf16[32,2176]{1,0:T(8,128)(2,1)S(1)}, u32[]{:S(2)}, u32[]{:S(2)}) collective-permute-start(bf16[32,2176]{1,0:T(8,128)(2,1)S(1)} %add_convert_fusion.9), channel_id=1, source_target_pairs={{0,8},{1,9},{2,10},{3,11},{4,12},{5,13},{6,14},{7,15},{8,0},{9,1},... | collective-permute-start | bytes 417800 | tf_op jit(solution)/shard_map/ppermute | solution.py:564
  132.8 6.8 %collective-permute-start.19 = (bf16[512,1024]{1,0:T(8,128)(2,1)S(1)}, bf16[512,1024]{1,0:T(8,128)(2,1)S(1)}, u32[]{:S(2)}, u32[]{:S(2)}) collective-permute-start(bf16[512,1024]{1,0:T(8,128)(2,1)S(1)} %pad_maximum_fusion.1.keep_ref), channel_id=1, source_target_pairs={{0,2},{1,3},{2,0},{3,1},{4,6},{5,7},{6,4},{7,5},{8,10},{9,11},{10,... | collective-permute-start | bytes 3145736 | tf_op jit(solution)/shard_map/ppermute | solution.py:564
  132.9 6.6 %collective-permute-start.18 = (bf16[64,2176]{1,0:T(8,128)(2,1)S(1)}, bf16[64,2176]{1,0:T(8,128)(2,1)S(1)}, u32[]{:S(2)}, u32[]{:S(2)}) collective-permute-start(bf16[64,2176]{1,0:T(8,128)(2,1)S(1)} %pad_maximum_fusion.5), channel_id=1, source_target_pairs={{0,4},{1,5},{2,3},{3,2},{4,0},{5,1},{6,7},{7,6},{8,12},{9,13},{10,... | collective-permute-start | bytes 835592 | tf_op jit(solution)/shard_map/ppermute | solution.py:564
  139.6 12.7 %copy-start.8 = (f32[512]{0:T(512)S(1)}, f32[512]{0:T(512)}, u32[]{:S(2)}) copy-start(f32[512]{0:T(512)} %param.16) | copy-start | bytes 6148
  139.6 12.7 %copy-start.9 = (f32[512]{0:T(512)S(1)}, f32[512]{0:T(512)}, u32[]{:S(2)}) copy-start(f32[512]{0:T(512)} %param.17) | copy-start | bytes 6148
  139.6 9.6 %collective-permute-start.20 = (bf16[128,2176]{1,0:T(8,128)(2,1)S(1)}, bf16[128,2176]{1,0:T(8,128)(2,1)S(1)}, u32[]{:S(2)}, u32[]{:S(2)}) collective-permute-start(bf16[128,2176]{1,0:T(8,128)(2,1)S(1)} %pad_maximum_fusion.2), channel_id=1, source_target_pairs={{0,1},{1,0},{2,6},{3,7},{4,5},{5,4},{6,2},{7,3},{8,9},{9,8},{10,14... | collective-permute-start | bytes 1671176 | tf_op jit(solution)/shard_map/ppermute | solution.py:564
  149.3 3.0 %collective-permute-start.21 = (bf16[256,2176]{1,0:T(8,128)(2,1)S(1)}, bf16[256,2176]{1,0:T(8,128)(2,1)}, u32[]{:S(2)}, u32[]{:S(2)}) collective-permute-start(bf16[256,2176]{1,0:T(8,128)(2,1)S(1)} %pad_maximum_fusion.keep_ref), channel_id=1, source_target_pairs={{0,2},{1,3},{2,0},{3,1},{4,6},{5,7},{6,4},{7,5},{8,10},{9,11},{10,... | collective-permute-start | bytes 3342344 | tf_op jit(solution)/shard_map/ppermute | solution.py:564

commit v5 on v4

--- a/solution.py
+++ b/solution.py
@@ -19,7 +19,7 @@
 SUMS = 8
 TILE = 16
 TOKS = 512
-VMEM_LIMIT = 24 * 1024 * 1024
+VMEM_LIMIT = 32 * 1024 * 1024
 
 
 def mm(a, b):
@@ -110,13 +110,13 @@
     return own ^ jnp.where(core == 0, first, second)
 
 
-def permuted(dst_ref, acc_ref, tables, core, own):
+def permuted(dst_ref, acc_ref, chunk, tables, core, own):
     blocks = len(tables[0])
-    size = acc_ref.shape[0] // blocks
+    size = dst_ref.shape[0] // blocks
     for place in range(blocks):
         block = block_at(place, tables, core, own)
         rows = pl.ds(pl.multiple_of(block * size, size), size)
-        dst_ref[place * size : (place + 1) * size, :] = acc_ref[rows, :].astype(dst_ref.dtype)
+        dst_ref[place * size : (place + 1) * size, :] = acc_ref[chunk, rows, :].astype(dst_ref.dtype)
 
 
 def attend_kernel(
@@ -197,68 +197,89 @@
     )
 
 
-def ffn_block(sec, sec_t, dy, dy_t, up, bias, down, acc_ref, bacc_ref, out, dsec):
-    units = up.shape[1]
+def pack_kernel(info_ref, up_ref, bias_ref, down_ref, up_out, down_out):
+    width = up_ref.shape[0]
+    up_out[:width, :] = up_ref[...]
+    up_out[width:, :] = jnp.broadcast_to(bias_ref[...], (TILE, bias_ref.shape[1]))
+    down_out[...] = down_ref[...]
+
+
+def pack(info, up, bias, down):
+    width, units = up.shape[0], up.shape[1] // 2
+    return call(
+        pack_kernel,
+        "pack",
+        (1,),
+        [
+            pl.BlockSpec((width, units), lambda t, info: (0, info[0])),
+            pl.BlockSpec((1, units), lambda t, info: (0, info[0])),
+            pl.BlockSpec((units, width), lambda t, info: (info[0], 0)),
+        ],
+        [whole(width + TILE, units), whole(units, width)],
+        [jax.ShapeDtypeStruct((width + TILE, units), BF), jax.ShapeDtypeStruct((units, width), BF)],
+        [],
+        info,
+        far(up, bias, down),
+    )
+
+
+def ffn_block(sec, dy, up, bias, down, acc_ref, bacc_ref):
     pre = mm(sec, up) + bias
+    dhid = mm_nt(dy, down)
     hid, slope = gelu_pair(pre)
     hid = hid.astype(BF)
-    dpre = (mm_nt(dy, down) * slope).astype(BF)
-    acc_ref[:, :units] += mm(sec_t, dpre)
-    acc_ref[:, units:] += mm(dy_t, hid)
-    bacc_ref[...] += jnp.sum(dpre.astype(F32), axis=0, keepdims=True)
-    o = mm(hid, down)
-    d = mm_nt(dpre, up)
-    return (o if out is None else out + o), (d if dsec is None else dsec + d)
-
-
-def ffn_own_kernel(tables, info_ref, sec_ref, dy_ref, *refs):
-    ups, biases, downs = refs[:2], refs[2:4], refs[4:6]
-    out_ref, dsec_ref = refs[6:8]
-    grads, bgrads, accs, baccs = refs[8:10], refs[10:12], refs[12:14], refs[14:16]
+    dpre = (dhid * slope).astype(BF)
+    grad_up = mm(sec.T, dpre)
+    grad_down = mm(dy.T, hid)
+    sums = jnp.sum(dpre.astype(F32), axis=0, keepdims=True)
+    chunks, _, double = acc_ref.shape
+    units = double // 2
+    for i in range(chunks):
+        cols = slice(i * units, (i + 1) * units)
+        acc_ref[i, :, :units] += grad_up[:, cols]
+        acc_ref[i, :, units:] += grad_down[:, cols]
+        bacc_ref[i : i + 1, :] += sums[:, cols]
+    return mm(hid, down), mm_nt(dpre, up)
+
+
+def ffn_own_kernel(
+    tables, info_ref, sec_ref, dy_ref, up_ref, bias_ref, down_ref, out_ref, dsec_ref, keep_ref, send_ref, bias_out, acc_ref
+):
     at, last = pl.program_id(0), pl.num_programs(0) - 1
 
     @pl.when(at == 0)
     def _():
-        for ref in accs + baccs:
-            ref[...] = jnp.zeros_like(ref)
-
-    sec, dy = sec_ref[...], dy_ref[...]
-    sec_t, dy_t = sec.T, dy.T
-    out = dsec = None
-    for i in range(2):
-        out, dsec = ffn_block(
-            sec, sec_t, dy, dy_t, ups[i][...], biases[i][...].astype(F32), downs[i][...], accs[i], baccs[i], out, dsec
-        )
+        acc_ref[...] = jnp.zeros_like(acc_ref)
+        bias_out[...] = jnp.zeros_like(bias_out)
+
+    out, dsec = ffn_block(
+        sec_ref[...], dy_ref[...], up_ref[...], bias_ref[...].astype(F32), down_ref[...], acc_ref, bias_out
+    )
     out_ref[...] = out
     dsec_ref[...] = dsec
 
     @pl.when(at == last)
     def _():
-        core, own = info_ref[0], info_ref[1]
-        for i in range(2):
-            permuted(grads[i], accs[i], tables, core ^ i, own)
-            bgrads[i][...] = baccs[i][...]
+        core, own, other = info_ref[0], info_ref[1], info_ref[2]
+        permuted(keep_ref, acc_ref, core, tables, core, own)
+        permuted(send_ref, acc_ref, core ^ 1, tables, core ^ 1, other)
 
 
 def ffn_own(info, tables, second, dy, up, bias, down):
     n, width = second.shape
     units = up.shape[1] // 2
-    chunk = lambda i: (lambda t, info: (0, info[0] ^ i))
     return call(
         functools.partial(ffn_own_kernel, tables),
         "ffn_own",
         (n // TOKS,),
-        [rows_of(width), rows_of(width)]
-        + [pl.BlockSpec((width, units), chunk(i)) for i in range(2)]
-        + [pl.BlockSpec((1, units), chunk(i)) for i in range(2)]
-        + [pl.BlockSpec((units, width), lambda t, info, i=i: (info[0] ^ i, 0)) for i in range(2)],
-        [rows_of(width)] * 2 + [whole(width, 2 * units)] * 2 + [whole(1, units)] * 2,
+        [rows_of(width), rows_of(width), whole(*up.shape), whole(*bias.shape), whole(*down.shape)],
+        [rows_of(width)] * 2 + [whole(width, 2 * units)] * 2 + [whole(2, units)],
         [pltpu.VMEM((n, width), F32)] * 2
         + [jax.ShapeDtypeStruct((width, 2 * units), BF)] * 2
-        + [jax.ShapeDtypeStruct((1, units), F32)] * 2,
-        [pltpu.VMEM((width, 2 * units), F32)] * 2 + [pltpu.VMEM((1, units), F32)] * 2,
+        + [jax.ShapeDtypeStruct((2, units), F32)],
+        [pltpu.VMEM((2, width, 2 * units), F32)],
         info,
-        near(second) + far(dy) + (up, up) + far(bias, bias) + (down, down),
+        near(second) + far(dy) + (up,) + far(bias) + (down,),
     )
 
 
@@ -266,25 +287,26 @@
     tables, count, info_ref, sec_ref, dy_ref, out_part_ref, dsec_part_ref, res_ref, mixed_ref, bdown_ref, g2_ref, wout_ref, *refs
 ):
     ups, downs = refs[:count], refs[count : 2 * count]
-    block_ref, gres_ref, gmix_ref, vec_ref, dwout_ref = refs[2 * count : 2 * count + 5]
-    rest = refs[2 * count + 5 :]
-    grads, bgrads = rest[:count], rest[count : 2 * count]
-    accs, baccs = rest[2 * count : 3 * count], rest[3 * count : 4 * count]
-    wacc_ref = rest[4 * count]
+    block_ref, gres_ref, gmix_ref, vec_ref, dwout_ref, bias_out = refs[2 * count : 2 * count + 6]
+    grads = refs[2 * count + 6 : 3 * count + 6]
+    acc_ref, up_ref, bias_ref, down_ref = refs[3 * count + 6 :]
     at, last = pl.program_id(0), pl.num_programs(0) - 1
-    width = sec_ref.shape[1]
+    width, units = wout_ref.shape[0], ups[0].shape[1]
 
     @pl.when(at == 0)
     def _():
-        for ref in accs + baccs + (wacc_ref, vec_ref):
+        for ref in (acc_ref, bias_out, vec_ref, dwout_ref):
             ref[...] = jnp.zeros_like(ref)
-
-    sec, dy = sec_ref[...], dy_ref[...]
-    sec_t, dy_t = sec.T, dy.T
-    out, dsec = out_part_ref[...], dsec_part_ref[...]
-    for i in range(count):
-        bias = ups[i][width : width + TILE, :].astype(F32)[:1]
-        out, dsec = ffn_block(sec, sec_t, dy, dy_t, ups[i][:width, :], bias, downs[i][...], accs[i], baccs[i], out, dsec)
+        for i in range(count):
+            cols = slice(i * units, (i + 1) * units)
+            up_ref[:, cols] = ups[i][:width, :]
+            bias_ref[:, cols] = ups[i][width : width + TILE, :].astype(F32)[:8]
+            down_ref[cols, :] = downs[i][...]
+
+    dy = dy_ref[...]
+    out, dsec = ffn_block(sec_ref[...], dy, up_ref[...], bias_ref[0:1, :], down_ref[...], acc_ref, bias_out)
+    out += out_part_ref[...]
+    dsec += dsec_part_ref[...]
     residual = res_ref[...]
     block_ref[...] = (residual + (out + bdown_ref[...])).astype(BF)
     dy32 = dy.astype(F32)
@@ -296,15 +318,13 @@
     gres_ref[...] = gres
     branch = gres.astype(BF)
     gmix_ref[...] = mm_nt(branch, wout_ref[...]).astype(BF)
-    wacc_ref[...] += mm_tn(mixed_ref[...], branch)
+    dwout_ref[...] += mm_tn(mixed_ref[...], branch)
 
     @pl.when(at == last)
     def _():
-        core, own = info_ref[0], info_ref[1]
+        core, own, other = info_ref[0], info_ref[1], info_ref[2]
         for i in range(count):
-            permuted(grads[i], accs[i], tables, core ^ (i % 2), own)
-            bgrads[i][...] = baccs[i][...]
-        dwout_ref[...] = wacc_ref[...]
+            permuted(grads[i], acc_ref, i, tables, core ^ (i % 2), other if i % 2 else own)
 
 
 def ffn_rest(info, tables, second, dy, out_part, dsec_part, residual, mixed, bdown, g2, wout, chunks):
@@ -321,25 +341,62 @@
         + [whole(width + TILE, units)] * count
         + [whole(units, width)] * count,
         [rows_of(width)] * 3
-        + [whole(8, width), whole(width, width)]
-        + [whole(width, 2 * units)] * count
-        + [whole(1, units)] * count,
+        + [whole(8, width), whole(width, width), whole(count, units)]
+        + [whole(width, 2 * units)] * count,
         [
             jax.ShapeDtypeStruct((n, width), BF),
             pltpu.HBM((n, width), F32),
             pltpu.HBM((n, width), BF),
             jax.ShapeDtypeStruct((8, width), F32),
             pltpu.HBM((width, width), F32),
+            jax.ShapeDtypeStruct((count, units), F32),
         ]
-        + [jax.ShapeDtypeStruct((width, 2 * units), BF)] * count
-        + [jax.ShapeDtypeStruct((1, units), F32)] * count,
-        [pltpu.VMEM((width, 2 * units), F32)] * count
-        + [pltpu.VMEM((1, units), F32)] * count
-        + [pltpu.VMEM((width, width), F32)],
+        + [jax.ShapeDtypeStruct((width, 2 * units), BF)] * count,
+        [
+            pltpu.VMEM((count, width, 2 * units), F32),
+            pltpu.VMEM((width, count * units), BF),
+            pltpu.VMEM((8, count * units), F32),
+            pltpu.VMEM((count * units, width), BF),
+        ],
         info,
-        near(second) + far(dy) + near(out_part, dsec_part) + far(residual, mixed) + far(bdown, g2) + (wout,)
+        near(second)
+        + far(dy)
+        + near(out_part, dsec_part)
+        + far(residual, mixed, bdown, g2)
+        + (wout,)
         + tuple(c[0] for c in chunks)
         + tuple(c[1] for c in chunks),
+    )
+
+
+def mix_kernel(info_ref, mine_ref, other_ref, got_ref, keep_ref, send_ref):
+    top = mine_ref.shape[0] // 2
+    both = (other_ref[...].astype(F32) + got_ref[...].astype(F32)).astype(BF)
+    keep_ref[:top, :] = mine_ref[:top, :]
+
+    @pl.when(info_ref[0] == 0)
+    def _():
+        keep_ref[top:, :] = mine_ref[top:, :]
+        send_ref[...] = both
+
+    @pl.when(info_ref[0] == 1)
+    def _():
+        keep_ref[top:, :] = both[:top, :]
+        send_ref[:top, :] = mine_ref[top:, :]
+        send_ref[top:, :] = both[top:, :]
+
+
+def mix(info, mine, other, got):
+    return call(
+        mix_kernel,
+        "mix",
+        (1,),
+        [whole(*mine.shape)] * 3,
+        [whole(*mine.shape)] * 2,
+        [jax.ShapeDtypeStruct(mine.shape, BF)] * 2,
+        [],
+        info,
+        (mine, other, got),
     )
 
 
@@ -395,13 +452,13 @@
 
     @pl.when(at == last)
     def _():
-        core, own = info_ref[0], info_ref[2]
+        core, own, other = info_ref[0], info_ref[3], info_ref[4]
         acc_ref[:, 4 * width :] = row_ref[...].T
         half = width // 2
         size = width // len(tables[0])
         for place in range(len(tables[0])):
             dst = dw_keep_ref if place * size < half else dw_send_ref
-            block = block_at(place, tables, core, own)
+            block = block_at(place, tables, core, own if place * size < half else other)
             rows_at = pl.ds(pl.multiple_of(block * size, size), size)
             to = place * size % half
             dst[to : to + size, :] = acc_ref[rows_at, :].astype(BF)
@@ -457,14 +514,14 @@
 
 
 def ffn_end_kernel(tables, info_ref, keep_ref, other_ref, up_ref, down_ref, full_ref):
-    core, own = info_ref[0], info_ref[1]
+    core = info_ref[0]
     units = up_ref.shape[1]
     blocks = len(tables[0])
     size = keep_ref.shape[0] // blocks
 
-    def lay(src_ref, whose):
+    def lay(src_ref, whose, base):
         for place in range(blocks):
-            block = block_at(place, tables, whose, own)
+            block = block_at(place, tables, whose, base)
             rows = pl.ds(pl.multiple_of(block * size, size), size)
             part = src_ref[place * size : (place + 1) * size, :].astype(F32)
             up_ref[rows, :] = part[:, :units]
@@ -473,11 +530,11 @@
 
     @pl.when(pl.program_id(0) == 0)
     def _():
-        lay(keep_ref, core)
+        lay(keep_ref, core, info_ref[1])
 
     @pl.when(pl.program_id(0) == 1)
     def _():
-        lay(other_ref, core ^ 1)
+        lay(other_ref, core ^ 1, info_ref[2])
 
 
 def ffn_end(info, tables, keep, other):
@@ -499,52 +556,93 @@
     )
 
 
-def attend_end_kernel(tables, info_ref, keep_ref, other_ref, w_ref, g1_ref, c1_ref, qkv_ref, out_ref, vec_ref, sum_ref, col_ref):
-    core, own = info_ref[0], info_ref[2]
+def attend_end_kernel(
+    tables, shares, info_ref, keep_ref, other_ref, w_ref, g1_ref, c1_ref, qkv_hbm, out_hbm, *refs
+):
+    vec_refs, (qkv_ref, out_ref, col_ref, row_ref, sems) = refs[:6], refs[6:]
+    core, own, away = info_ref[0], info_ref[3], info_ref[4]
     width = out_ref.shape[1]
     blocks = len(tables[0])
     size = out_ref.shape[0] // blocks
     half = out_ref.shape[0] // 2
+    spots = []
     for place in range(blocks):
-        src = keep_ref if place * size < half else other_ref
+        mine = place * size < half
+        block = block_at(place, tables, core, own if mine else away)
         at = place * size % half
-        block = block_at(place, tables, core, own)
-        rows = pl.ds(pl.multiple_of(block * size, size), size)
-        part = src[at : at + size, :].astype(F32)
-        sum_ref[rows, :] = part[:, : 3 * width]
-        out_ref[rows, :] = part[:, 3 * width : 4 * width]
-        col_ref[rows, :] = part[:, 4 * width :]
+        spots.append((keep_ref if mine else other_ref, slice(at, at + size), pl.multiple_of(block * size, size)))
+    copies = []
+    for i, (src, rows, to) in enumerate(spots):
+        to = pl.ds(to, size)
+        col_ref[to, :] = src[rows, 4 * width :].astype(F32)
+        out_ref[rows if src is keep_ref else slice(rows.start + half, rows.stop + half), :] = src[
+            rows, 3 * width : 4 * width
+        ].astype(F32)
+    for i, (src, rows, to) in enumerate(spots):
+        rows = rows if src is keep_ref else slice(rows.start + half, rows.stop + half)
+        copies.append(pltpu.make_async_copy(out_ref.at[rows, :], out_hbm.at[pl.ds(to, size), :], sems.at[i]))
+        copies[-1].start()
     vec = col_ref[...].T
+    row_ref[...] = vec
     wide_row = jnp.concatenate([vec[i : i + 1, :] for i in range(3)], axis=1)
     pair = jnp.concatenate([g1_ref[...], c1_ref[...], jnp.zeros((LANES - 2, width), F32)], axis=0).T
-    gain, bias = pair[:, 0:1], pair[:, 1:2]
-    w = w_ref[...].astype(F32)
-    sums = sum_ref[...]
-    qkv_ref[...] = gain * sums + bias * wide_row
-    lane = lax.broadcasted_iota(jnp.int32, (width, LANES), 1)
-    d_gain = jnp.sum(w * sums, axis=1, keepdims=True)
-    d_bias = jnp.sum(w * wide_row, axis=1, keepdims=True)
-    both = jnp.where(lane == 0, d_gain, jnp.where(lane == 1, d_bias, 0.0)).T
-    vec_ref[...] = vec[: vec_ref.shape[0], :]
-    vec_ref[0:2, :] = both[0:2, :]
-
-
-def attend_end(info, tables, keep, other, w_qkv, g1, c1, count):
+    col_ref[...] = pair
+    lane = lax.broadcasted_iota(jnp.int32, (size, LANES), 1)
+    for i, (src, rows, to) in enumerate(spots):
+        here = pl.ds(to, size)
+        gain_bias = col_ref[here, :]
+        gain, bias = gain_bias[:, 0:1], gain_bias[:, 1:2]
+        sums = src[rows, : 3 * width].astype(F32)
+        w = w_ref[here, :].astype(F32)
+        rows = rows if src is keep_ref else slice(rows.start + half, rows.stop + half)
+        qkv_ref[rows, :] = gain * sums + bias * wide_row
+        copies.append(pltpu.make_async_copy(qkv_ref.at[rows, :], qkv_hbm.at[here, :], sems.at[blocks + i]))
+        copies[-1].start()
+        d_gain = jnp.sum(w * sums, axis=1, keepdims=True)
+        d_bias = jnp.sum(w * wide_row, axis=1, keepdims=True)
+        col_ref[here, :] = jnp.where(lane == 0, d_gain, jnp.where(lane == 1, d_bias, 0.0))
+    both = col_ref[...].T
+    flat = lambda row: row.reshape(row.shape[1])
+    vec_refs[0][...] = flat(both[0:1, :])
+    vec_refs[1][...] = flat(both[1:2, :])
+    for i in range(3):
+        vec_refs[2 + i][...] = flat(vec[SUMS + i : SUMS + i + 1, :])
+    units = vec_refs[5].shape[0]
+    if units >= width:
+        first = SUMS + 8 + info_ref[5] * (units // width)
+        for i in range(units // width):
+            vec_refs[5][i * width : (i + 1) * width] = flat(row_ref[pl.ds(first + i, 1), :])
+    else:
+        row = row_ref[pl.ds(SUMS + 8 + info_ref[5] // shares, 1), :]
+        share = row[:, :units]
+        for i in range(1, shares):
+            share = jnp.where(info_ref[5] % shares == i, row[:, i * units : (i + 1) * units], share)
+        vec_refs[5][...] = flat(share)
+    for copy in copies:
+        copy.wait()
+
+
+def attend_end(info, tables, keep, other, w_qkv, g1, c1, units):
     rows, width = 2 * keep.shape[0], w_qkv.shape[0]
+    blocks = len(tables[0])
     return call(
-        functools.partial(attend_end_kernel, tables),
+        functools.partial(attend_end_kernel, tables, max(1, width // units)),
         "attend_end",
         (1,),
         [whole(*keep.shape)] * 2 + [whole(*w_qkv.shape)] + [whole(1, width)] * 2,
-        [whole(rows, 3 * width), whole(rows, width), whole(count, width)],
+        [pl.BlockSpec(memory_space=pl.ANY)] * 2 + [whole(width)] * 5 + [whole(units)],
+        [jax.ShapeDtypeStruct((rows, 3 * width), F32), jax.ShapeDtypeStruct((rows, width), F32)]
+        + [jax.ShapeDtypeStruct((width,), F32)] * 5
+        + [jax.ShapeDtypeStruct((units,), F32)],
         [
-            jax.ShapeDtypeStruct((rows, 3 * width), F32),
-            jax.ShapeDtypeStruct((rows, width), F32),
-            jax.ShapeDtypeStruct((count, width), F32),
+            pltpu.VMEM((rows, 3 * width), F32),
+            pltpu.VMEM((rows, width), F32),
+            pltpu.VMEM((rows, LANES), F32),
+            pltpu.VMEM((LANES, width), F32),
+            pltpu.SemaphoreType.DMA((2 * blocks,)),
         ],
-        [pltpu.VMEM((rows, 3 * width), F32), pltpu.VMEM((rows, LANES), F32)],
         info,
-        (keep, other, w_qkv, g1, c1),
+        (keep, other, w_qkv) + far(g1, c1),
     )
 
 
@@ -566,11 +664,6 @@
     def add(a, b):
         return (a.astype(F32) + b.astype(F32)).astype(a.dtype)
 
-    def orders(masks):
-        if len(masks) < 2:
-            return (masks, masks)
-        return (masks, [masks[1], masks[0]] + masks[2:])
-
     def after(*values):
         return lax.optimization_barrier(values)
 
@@ -581,8 +674,11 @@
 
         return [functools.partial(step, *pair) for pair in zip(*order)]
 
-    def exchanges(masks):
-        return [lambda value, mask=mask: add(value, swap(value, mask)) for mask in masks]
+    def exchanges(order):
+        def step(first, second, value):
+            return add(value, swap(value, first, second))
+
+        return [functools.partial(step, *pair) for pair in zip(*order)]
 
     def gathers(order):
         def step(first, second, value):
@@ -598,33 +694,43 @@
         return sum((1 << b) for b, m in enumerate(used) if owner & m)
 
     def block_of(used):
-        return sum((flat // m & 1) << b for b, m in enumerate(used))
-
-    def halved(masks, tiles):
-        count = min(len(masks) - 1, tiles.bit_length() - 1)
-        return masks[:count], masks[count:]
-
-    ff_used, ff_rest = halved(wide_masks, width // TILE)
-    ff_out = orders(ff_used)
-    ff_in = (ff_used, ff_used) if narrow == 2 else ff_out
+        return sum(((flat & m) != 0).astype(jnp.int32) << b for b, m in enumerate(used))
+
+    def split_at(pair, count):
+        return tuple(o[:count] for o in pair), tuple(o[count:] for o in pair)
+
+    def by_core(values):
+        return jnp.where(core == 0, values[0], values[1]), jnp.where(core == 0, values[1], values[0])
+
+    if narrow == 2 and len(wide_masks) == 3:
+        y, low, high = wide_masks
+        ff_in, ff_rest = ([y, high], [y, low]), ([low], [high])
+        ff_out = ([y, high], [low, y])
+        at_order = ([1, y, low], [y, 1, high])
+        at_rest = ([high], [low])
+    else:
+        ff_in, ff_rest = split_at((wide_masks, wide_masks), min(len(wide_masks) - 1, (width // TILE).bit_length() - 1))
+        ff_out = ff_in
+        masks = narrow_masks + wide_masks
+        at_order, at_rest = split_at((masks, masks), min(len(masks) - 1, (width // TILE // 2).bit_length() - 1))
+    ff_used = tuple(sorted(o) for o in ff_in)
     ff_in_tables, ff_out_tables = (
-        tuple([named(owner, ff_used) for owner in places(o, 1 << len(ff_used))] for o in pair) for pair in (ff_in, ff_out)
-    )
-    at_masks, at_rest = halved(narrow_masks + wide_masks, width // TILE // 2)
-    at_order = orders(at_masks)
-    at_used = [core_mask] + at_masks
-    near_places = [places(o, 1 << len(at_masks)) for o in at_order]
+        tuple([named(owner, ff_used[c]) for owner in places(pair[c], 1 << len(ff_used[c]))] for c in range(2))
+        for pair in (ff_in, ff_out)
+    )
+    at_used = tuple([core_mask] + sorted(o) for o in at_order)
+    at_places = [places(o, 1 << len(o)) for o in at_order]
     at_tables = tuple(
-        [named(o, at_used) for o in near_places[c]] + [named(o ^ core_mask, at_used) for o in near_places[1 - c]]
+        [named(o, at_used[c]) for o in at_places[c]]
+        + [named(o ^ core_mask, at_used[1 - c]) for o in at_places[1 - c]]
         for c in range(2)
     )
-    info = jnp.stack([core, block_of(ff_used), block_of(at_used)]).astype(jnp.int32)
-
-    up_chunk = lax.dynamic_slice(w_up, (0, core * units), (width, units))
-    bias_chunk = lax.dynamic_slice(b_up, (core * units,), (units,))
-    up_chunk = jnp.concatenate([up_chunk, jnp.broadcast_to(bias_chunk[None], (TILE, units))], axis=0)
-    down_chunk = lax.dynamic_slice(w_down, (core * units, 0), (units, width))
-    fetched = [(up_chunk, down_chunk)]
+    ff_block = by_core([block_of(used) for used in ff_used])
+    at_block = by_core([block_of(used) for used in at_used])
+    info = jnp.stack([core, *ff_block, *at_block, narrow_at]).astype(jnp.int32)
+
+    packed, tokens_in = after(pack(info, w_up, b_up[None], w_down), tokens_in)
+    fetched = [packed]
     for mask in narrow_masks:
         fetched = fetched + [(swap(u, mask), swap(d, mask)) for u, d in fetched]
 
@@ -633,36 +739,36 @@
     qkv, prob, mixed, residual, second = attend(
         info, tokens_in, g1, c1, w_qkv, w_out, g2, row(ln2_bias), segment_ids, step_ids, pad_mask
     )
-    fetched = after(second, fetched)[1]
+    out_part, dsec_part, own_keep, own_send, bias_own = ffn_own(
+        info, ff_in_tables, second, cotangent, w_up, b_up[None], w_down
+    )
+    own_send, fetched = after(own_send, fetched)
     chunks = []
     for up, down in fetched[1:]:
         chunks += [(up, down), (swap(up, core_mask), swap(down, core_mask))]
-    out_part, dsec_part, own_keep, own_send, bown_keep, bown_send = ffn_own(
-        info, ff_in_tables, second, cotangent, w_up, b_up[None], w_down
-    )
+    own_keep, second = after(add(own_keep, swap(own_send, core_mask)), second)
     rest = ffn_rest(
         info, ff_in_tables, second, cotangent, out_part, dsec_part, residual, mixed, row(b_down), g2, w_out, chunks
     )
-    block_out, gres, gmix, vec, dwout = rest[:5]
-    count = len(chunks)
-    grads, bgrads = rest[5 : 5 + count], rest[5 + count :]
-
-    b_all = jnp.concatenate([bown_keep, bown_send, *bgrads], axis=0)
-    for bit in range(narrow.bit_length()):
-        flipped = jnp.flip(b_all.reshape(-1, 2, 1 << bit, units), axis=1).reshape(b_all.shape)
-        b_all = jnp.where((narrow_at * 2 + core) >> bit & 1, flipped, b_all)
+    block_out, gres, gmix, vec, dwout, bias_rest = rest[:6]
+    grads = rest[6:]
+
+    b_rest = bias_rest.reshape(-1, 2, units)
+    b_rest = jnp.where(core == 0, b_rest, jnp.flip(b_rest, axis=1))
+    b_all = jnp.concatenate([bias_own[None], b_rest], axis=0)
+    for bit in range(narrow.bit_length() - 1):
+        flipped = jnp.flip(b_all.reshape(-1, 2, (1 << bit) * 2, units), axis=1).reshape(b_all.shape)
+        b_all = jnp.where(narrow_at >> bit & 1, flipped, b_all)
     vec = jnp.concatenate([vec, b_all.reshape(-1, width)], axis=0)
 
-    held = [add(own_keep, swap(own_send, core_mask))]
-    held += [add(grads[2 * j], swap(grads[2 * j + 1], core_mask)) for j in range(narrow - 1)]
-    if narrow == 2:
-        top, mine, other = width // 2, *held
-        ff_keep = jnp.where(core == 0, mine, jnp.concatenate([mine[:top], other[:top]], axis=0))
-        ff_send = jnp.where(core == 0, other, jnp.concatenate([mine[top:], other[top:]], axis=0))
+    got = [swap(grads[2 * j + 1], core_mask) for j in range(narrow - 1)]
+    if narrow == 2 and len(wide_masks) == 3:
+        ff_keep, ff_send = mix(info, own_keep, grads[0], got[0])
         gmix, ff_keep, ff_send = after(gmix, ff_keep, ff_send)
-        ff_keep = add(ff_keep, swap(ff_send, narrow_masks[0], ff_used[0]))
-        ff_left = ([ff_used[0]] + ff_used[1:], narrow_masks + ff_used[1:])
+        ff_keep = add(ff_keep, swap(ff_send, 1, y))
+        ff_left = ([y, high], [1, low])
     else:
+        held = [own_keep] + [add(grads[2 * j], got[j]) for j in range(narrow - 1)]
         gmix, held = after(gmix, held)
         for mask in reversed(narrow_masks):
             held = [add(held[j], swap(held[j + mask], mask)) for j in range(mask)]
@@ -688,24 +794,12 @@
         keep, ff_done = after(at_step(keep), ff_done)
     grad_w_up, grad_w_down = ff_done
 
-    grad_w_qkv, grad_w_out, vec = attend_end(
-        info, at_tables, keep, swap(keep, core_mask), w_qkv, g1, c1, SUMS + vec.shape[0]
-    )
-    b_sum = vec[SUMS + 8 :].reshape(narrow, 2 * units)
-    grad_b_up = lax.dynamic_slice(b_sum, (narrow_at, 0), (1, 2 * units))[0]
+    grad_w_qkv, grad_w_out, d_gain1, d_bias1, d_gain2, d_bias2, d_bdown, grad_b_up = attend_end(
+        info, at_tables, keep, swap(keep, core_mask), w_qkv, g1, c1, 2 * units
+    )
     return (
-        block_out,
-        grad_tokens,
-        vec[0],
-        vec[1],
-        grad_w_qkv,
-        grad_w_out,
-        vec[SUMS],
-        vec[SUMS + 1],
-        grad_w_up,
-        grad_b_up,
-        grad_w_down,
-        vec[SUMS + 2],
+        block_out, grad_tokens, d_gain1, d_bias1, grad_w_qkv, grad_w_out, d_gain2, d_bias2, grad_w_up, grad_b_up, grad_w_down,
+        d_bdown,
     )
 
 

time: 158 us -> 161 us (1.019)
  waiting for transfers between devices: 58.6 us -> 65.5 us
  local copies, waits for them, and re-layouts: 10.2 us -> 4.92 us
  other arithmetic: 7.43 us -> 2.61 us
  Pallas kernels: 59 us -> 63 us
    ppermute x22, waiting for transfers between devices: 58.6 us -> 65.5 us  [swap(): return lax.ppermute(value, AXES, pairs)]
    dynamic_slice x4 -> x0, local copies, waits for them, and re-layouts: 4.45 us -> none  [the longest x1 1.86 us: local(): down_chunk = lax.dynamic_slice(w_down, (core * units, 0), (units, width))]
    pallas_call x7 -> x9, Pallas kernels: 59 us -> 63 us  [call(): pl.pallas_call(kernel, grid_spec=pltpu.PrefetchScalarGridSpec(num_scalar_...]
    convert_element_type x11 -> x10, other arithmetic: 4.62 us -> 1.73 us  [add(): return (a.astype(F32) + b.astype(F32)).astype(a.dtype)]
    unnamed x28 -> x16, local copies, waits for them, and re-layouts: 3.23 us -> 3.18 us
  transfers between devices with their start and end apart: 22 -> 22, of which waited for: 15 -> 17; matrix products, arithmetic and copies ran while one was open for 4% -> 1% of each run, Pallas kernels for 34% -> 24%
where the time goes in v5:
time: 161 us; the launch traced here: 160 us
  waiting for transfers between devices  65.5 us (41%)
  Pallas kernels  63 us (39%)
  starting transfers between devices  23.2 us (14%)
  local copies, waits for them, and re-layouts  4.92 us (3%)
  other arithmetic  2.61 us (2%)
    ppermute x22, waiting for transfers between devices, swap(): return lax.ppermute(value, AXES, pairs)  65.5 us
    pallas_call x9, Pallas kernels, call(): pl.pallas_call(kernel, grid_spec=pltpu.PrefetchScalarGridSpec(num_scalar_...  63 us
    ppermute x22, starting transfers between devices, swap(): return lax.ppermute(value, AXES, pairs)  23.2 us
  transfers between devices with their start and end apart: 22, of which 17 were waited for; matrix products, arithmetic and copies ran while one was open for 1% of the time, Pallas kernels for 24%

profile of v5, /device:TPU:0, one launch (start us, length us, event | category | flops | bytes accessed | tf_op | source)
XLA Modules:
  0.0 160.4 jit_solution(12013799999670202902)
XLA Ops:
  0.7 1.4 broadcast_in_dim.22.bias_ref
  2.2 1.8 %pack.1 = (bf16[528,512]{1,0:T(8,128)(2,1)S(1)}, bf16[512,512]{1,0:T(8,128)(2,1)S(1)}) custom-call(s32[6]{0:T(128)S(1)} %stack.27.info_ref, bf16[512,1024]{1,0:T(8,128)(2,1)} %up_ref.3, bf16[1,1024]{1,0:T(2,128)(2,1)} %broadcast_in_dim.22.bias_ref, bf16[1024,512]{1,0:T(8,128)(2,1)} %down_ref.3), custom_call_target="tpu_custom_call" | custom-call | flops 1000 | bytes 1000 | tf_op jit(solution)/shard_map/pack/pallas_call | solution.py:54
  4.1 3.0 %collective-permute-start = (bf16[528,512]{1,0:T(8,128)(2,1)S(1)}, bf16[528,512]{1,0:T(8,128)(2,1)S(1)}, u32[]{:S(2)}, u32[]{:S(2)}) collective-permute-start(bf16[528,512]{1,0:T(8,128)(2,1)S(1)} %get-tuple-element.82), channel_id=1, source_target_pairs={{0,1},{1,0},{2,3},{3,2},{4,5},{5,4},{6,7},{7,6},{8,9},{9,8},{10,11... | collective-permute-start | bytes 1622024 | tf_op jit(solution)/shard_map/ppermute | solution.py:662
  7.2 9.1 %attend.1 = (bf16[1024,1536]{1,0:T(8,128)(2,1)}, bf16[8,4,128,256]{3,2,1,0:T(8,128)(2,1)}, bf16[1024,512]{1,0:T(8,128)(2,1)}, f32[1024,512]{1,0:T(8,128)}, bf16[1024,512]{1,0:T(8,128)(2,1)S(1)}) custom-call(s32[6]{0:T(128)S(1)} %stack.27.info_ref, bf16[1024,512]{1,0:T(8,128)(2,1)} %tok_ref.2, f32[1,512]{1,0:T(1,128)} %bitcast.15, f32[1,512]{1,0:T(1,128)} %bitcast.18, ...), custom_call_target="tpu_custom_call" | custom-call | flops 1000 | bytes 1000 | tf_op jit(solution)/shard_map/attend/pallas_call | solution.py:54
  16.3 9.7 %ffn_own.1 = (f32[1024,512]{1,0:T(8,128)S(1)}, f32[1024,512]{1,0:T(8,128)S(1)}, bf16[512,1024]{1,0:T(8,128)(2,1)S(1)}, bf16[512,1024]{1,0:T(8,128)(2,1)S(1)}, f32[2,512]{1,0:T(2,128)S(1)}) custom-call(s32[6]{0:T(128)S(1)} %stack.27.info_ref, bf16[1024,512]{1,0:T(8,128)(2,1)S(1)} %get-tuple-element.85.sec_ref, bf16[1024,512]{1,0:T(8,128)(2,1)} %dy_ref.3, ...), custom_call_target="tpu_custom_call" | custom-call | flops 1000 | bytes 1000 | tf_op jit(solution)/shard_map/ffn_own/pallas_call | solution.py:54
  25.9 4.6 %collective-permute-done.1.refs_2_ = bf16[512,512]{1,0:T(8,128)(2,1)S(1)} collective-permute-done((bf16[512,512]{1,0:T(8,128)(2,1)S(1)}, bf16[512,512]{1,0:T(8,128)(2,1)S(1)}, u32[]{:S(2)}, u32[]{:S(2)}) %collective-permute-start.1) | collective-permute-done | bytes 524320 | tf_op jit(solution)/shard_map/ppermute | solution.py:662
  30.6 0.5 collective-permute-start.3
  31.1 2.1 %collective-permute-done.2 = bf16[512,1024]{1,0:T(8,128)(2,1)S(1)} collective-permute-done((bf16[512,1024]{1,0:T(8,128)(2,1)S(1)}, bf16[512,1024]{1,0:T(8,128)(2,1)S(1)}, u32[]{:S(2)}, u32[]{:S(2)}) %collective-permute-start.2) | collective-permute-done | bytes 1048608 | tf_op jit(solution)/shard_map/ppermute | solution.py:662
  33.2 0.4 add_convert_fusion.2.mine_ref
  33.7 1.1 collective-permute-done.4.refs_3_
  34.8 14.9 %ffn_rest.1 = (bf16[1024,512]{1,0:T(8,128)(2,1)}, f32[1024,512]{1,0:T(8,128)}, bf16[1024,512]{1,0:T(8,128)(2,1)}, f32[8,512]{1,0:T(8,128)S(1)}, f32[512,512]{1,0...) custom-call(s32[6]{0:T(128)S(1)} %stack.27.info_ref, ...), custom_call_target="tpu_custom_call" | custom-call | flops 1000 | bytes 1000 | tf_op jit(solution)/shard_map/ffn_rest/pallas_call | solution.py:54
  49.6 1.0 copy-done.6
  50.8 2.8 %collective-permute-done.5.got_ref = bf16[512,1024]{1,0:T(8,128)(2,1)} collective-permute-done((bf16[512,1024]{1,0:T(8,128)(2,1)}, bf16[512,1024]{1,0:T(8,128)(2,1)}, u32[]{:S(2)}, u32[]{:S(2)}) %collective-permute-start.5) | collective-permute-done | bytes 1048608 | tf_op jit(solution)/shard_map/ppermute | solution.py:662
  53.6 1.2 copy-done.7
  54.8 3.3 %mix.1 = (bf16[512,1024]{1,0:T(8,128)(2,1)S(1)}, bf16[512,1024]{1,0:T(8,128)(2,1)}) custom-call(s32[6]{0:T(128)S(1)} %stack.27.info_ref, bf16[512,1024]{1,0:T(8,128)(2,1)S(1)} %add_convert_fusion.2.mine_ref, bf16[512,1024]{1,0:T(8,128)(2,1)S(1)} %copy-done.7, bf16[512,1024]{1,0:T(8,128)(2,1)} %collective-permute-done.5.got_ref), custom_call_target="tpu_custom_call" | custom-call | flops 1000 | bytes 1000 | tf_op jit(solution)/shard_map/mix/pallas_call | solution.py:54
  58.1 1.0 copy-done.4
  59.1 1.7 %collective-permute-start.7 = (bf16[512,1024]{1,0:T(8,128)(2,1)}, bf16[512,1024]{1,0:T(8,128)(2,1)S(1)}, u32[]{:S(2)}, u32[]{:S(2)}) collective-permute-start(bf16[512,1024]{1,0:T(8,128)(2,1)} %get-tuple-element.109), channel_id=1, source_target_pairs={{0,1},{1,0},{2,6},{3,7},{4,5},{5,4},{6,2},{7,3},{8,9},{9,8},{10,14... | collective-permute-start | bytes 3145736 | tf_op jit(solution)/shard_map/ppermute | solution.py:662
  60.8 0.6 pad_maximum_fusion.5.vec_ref
  61.4 10.6 %attend_back.1 = (bf16[1024,1536]{1,0:T(8,128)(2,1)S(1)}, bf16[256,2176]{1,0:T(8,128)(2,1)S(1)}, bf16[256,2176]{1,0:T(8,128)(2,1)S(1)}) custom-call(s32[6]{0:T(128)S(1)} %stack.27.info_ref, bf16[1024,1536]{1,0:T(8,128)(2,1)} %get-tuple-element.93.qkv_ref, bf16[8,4,128,256]{3,2,1,0:T(8,128)(2,1)} %get-tuple-element.94.prob_ref, ...), custom_call_target="tpu_custom_call" | custom-call | flops 1000 | bytes 1000 | tf_op jit(solution)/shard_map/attend_back/pallas_call | solution.py:54
  72.1 2.0 %collective-permute-done.7 = bf16[512,1024]{1,0:T(8,128)(2,1)S(1)} collective-permute-done((bf16[512,1024]{1,0:T(8,128)(2,1)}, bf16[512,1024]{1,0:T(8,128)(2,1)S(1)}, u32[]{:S(2)}, u32[]{:S(2)}) %collective-permute-start.7) | collective-permute-done | bytes 1048608 | tf_op jit(solution)/shard_map/ppermute | solution.py:662
  74.1 0.4 add_convert_fusion.1
  74.5 0.3 collective-permute-done.6
  74.8 0.3 add_convert_fusion
  75.2 1.6 %collective-permute-start.9 = (bf16[256,1024]{1,0:T(8,128)(2,1)S(1)}, bf16[256,1024]{1,0:T(8,128)(2,1)S(1)}, u32[]{:S(2)}, u32[]{:S(2)}) collective-permute-start(bf16[256,1024]{1,0:T(8,128)(2,1)S(1)} %slice.33), channel_id=1, source_target_pairs={{0,4},{1,5},{2,3},{3,2},{4,0},{5,1},{6,7},{7,6},{8,12},{9,13},{10,... | collective-permute-start | bytes 1572872 | tf_op jit(solution)/shard_map/ppermute | solution.py:662
  76.8 1.5 collective-permute-start.8
  78.3 5.5 %first_back.1 = f32[1024,512]{1,0:T(8,128)} custom-call(s32[6]{0:T(128)S(1)} %stack.27.info_ref, bf16[1024,1536]{1,0:T(8,128)(2,1)S(1)} %get-tuple-element.112.dqkv_ref, bf16[512,1536]{1,0:T(8,128)(2,1)S(1)} %copy-done, bf16[1024,512]{1,0:T(8,128)(2,1)} %tok_ref.2, f32[1024,512]{1,0:T(8,128)} %get-tuple-element.113.gres_ref, f32[1,512]{1,0:T(1,128)} %bitcast.16), custom_call_target="tpu_custom_call" | custom-call | flops 1000 | bytes 1000 | tf_op jit(solution)/shard_map/first_back/pallas_call | solution.py:54
  83.8 6.0 %collective-permute-done.9 = bf16[256,1024]{1,0:T(8,128)(2,1)S(1)} collective-permute-done((bf16[256,1024]{1,0:T(8,128)(2,1)S(1)}, bf16[256,1024]{1,0:T(8,128)(2,1)S(1)}, u32[]{:S(2)}, u32[]{:S(2)}) %collective-permute-start.9) | collective-permute-done | bytes 524320 | tf_op jit(solution)/shard_map/ppermute | solution.py:662
  89.8 0.2 add_convert_fusion.4
  90.2 2.7 %collective-permute-start.11 = (bf16[128,1024]{1,0:T(8,128)(2,1)S(1)}, bf16[128,1024]{1,0:T(8,128)(2,1)S(1)}, u32[]{:S(2)}, u32[]{:S(2)}) collective-permute-start(bf16[128,1024]{1,0:T(8,128)(2,1)S(1)} %slice.37), channel_id=1, source_target_pairs={{0,16},{1,17},{2,10},{3,11},{4,20},{5,21},{6,14},{7,15},{8,24},{9,... | collective-permute-start | bytes 786440 | tf_op jit(solution)/shard_map/ppermute | solution.py:662
  92.9 1.7 %collective-permute-start.10 = (bf16[64,2176]{1,0:T(8,128)(2,1)S(1)}, bf16[64,2176]{1,0:T(8,128)(2,1)S(1)}, u32[]{:S(2)}, u32[]{:S(2)}) collective-permute-start(bf16[64,2176]{1,0:T(8,128)(2,1)S(1)} %slice.35), channel_id=1, source_target_pairs={{0,4},{1,5},{2,3},{3,2},{4,0},{5,1},{6,7},{7,6},{8,12},{9,13},{10,... | collective-permute-start | bytes 835592 | tf_op jit(solution)/shard_map/ppermute | solution.py:662
  94.6 4.8 %collective-permute-done.11 = bf16[128,1024]{1,0:T(8,128)(2,1)S(1)} collective-permute-done((bf16[128,1024]{1,0:T(8,128)(2,1)S(1)}, bf16[128,1024]{1,0:T(8,128)(2,1)S(1)}, u32[]{:S(2)}, u32[]{:S(2)}) %collective-permute-start.11) | collective-permute-done | bytes 262176 | tf_op jit(solution)/shard_map/ppermute | solution.py:662
  99.6 1.9 %collective-permute-start.12 = (bf16[32,2176]{1,0:T(8,128)(2,1)S(1)}, bf16[32,2176]{1,0:T(8,128)(2,1)S(1)}, u32[]{:S(2)}, u32[]{:S(2)}) collective-permute-start(bf16[32,2176]{1,0:T(8,128)(2,1)S(1)} %slice.39), channel_id=1, source_target_pairs={{0,8},{1,9},{2,18},{3,19},{4,12},{5,13},{6,22},{7,23},{8,0},{9,1},... | collective-permute-start | bytes 417800 | tf_op jit(solution)/shard_map/ppermute | solution.py:662
  101.7 4.0 %collective-permute-done.12 = bf16[32,2176]{1,0:T(8,128)(2,1)S(1)} collective-permute-done((bf16[32,2176]{1,0:T(8,128)(2,1)S(1)}, bf16[32,2176]{1,0:T(8,128)(2,1)S(1)}, u32[]{:S(2)}, u32[]{:S(2)}) %collective-permute-start.12) | collective-permute-done | bytes 139296 | tf_op jit(solution)/shard_map/ppermute | solution.py:662
  105.7 6.0 %collective-permute-done.13 = bf16[128,1024]{1,0:T(8,128)(2,1)S(1)} collective-permute-done((bf16[128,1024]{1,0:T(8,128)(2,1)S(1)}, bf16[128,1024]{1,0:T(8,128)(2,1)S(1)}, u32[]{:S(2)}, u32[]{:S(2)}) %collective-permute-start.13) | collective-permute-done | bytes 262176 | tf_op jit(solution)/shard_map/ppermute | solution.py:662
  111.8 1.3 collective-permute-start.14
  113.1 1.6 %collective-permute-start.15 = (bf16[128,1024]{1,0:T(8,128)(2,1)S(1)}, bf16[128,1024]{1,0:T(8,128)(2,1)S(1)}, u32[]{:S(2)}, u32[]{:S(2)}) collective-permute-start(bf16[128,1024]{1,0:T(8,128)(2,1)S(1)} %add_convert_fusion.6), channel_id=1, source_target_pairs={{0,16},{1,17},{2,6},{3,7},{4,20},{5,21},{6,2},{7,3},{8,24},{9,25},... | collective-permute-start | bytes 786440 | tf_op jit(solution)/shard_map/ppermute | solution.py:662
  114.8 4.6 %collective-permute-done.14 = bf16[32,2176]{1,0:T(8,128)(2,1)S(1)} collective-permute-done((bf16[32,2176]{1,0:T(8,128)(2,1)S(1)}, bf16[32,2176]{1,0:T(8,128)(2,1)S(1)}, u32[]{:S(2)}, u32[]{:S(2)}) %collective-permute-start.14) | collective-permute-done | bytes 139296 | tf_op jit(solution)/shard_map/ppermute | solution.py:662
  119.4 7.1 %collective-permute-done.15 = bf16[128,1024]{1,0:T(8,128)(2,1)S(1)} collective-permute-done((bf16[128,1024]{1,0:T(8,128)(2,1)S(1)}, bf16[128,1024]{1,0:T(8,128)(2,1)S(1)}, u32[]{:S(2)}, u32[]{:S(2)}) %collective-permute-start.15) | collective-permute-done | bytes 262176 | tf_op jit(solution)/shard_map/ppermute | solution.py:662
  126.6 1.9 %collective-permute-start.17 = (bf16[256,1024]{1,0:T(8,128)(2,1)S(1)}, bf16[256,1024]{1,0:T(8,128)(2,1)S(1)}, u32[]{:S(2)}, u32[]{:S(2)}) collective-permute-start(bf16[256,1024]{1,0:T(8,128)(2,1)S(1)} %pad_maximum_fusion.3), channel_id=1, source_target_pairs={{0,4},{1,5},{2,10},{3,11},{4,0},{5,1},{6,14},{7,15},{8,12},{9,13},... | collective-permute-start | bytes 1572872 | tf_op jit(solution)/shard_map/ppermute | solution.py:662
  128.5 5.1 %collective-permute-done.16 = bf16[32,2176]{1,0:T(8,128)(2,1)S(1)} collective-permute-done((bf16[32,2176]{1,0:T(8,128)(2,1)S(1)}, bf16[32,2176]{1,0:T(8,128)(2,1)S(1)}, u32[]{:S(2)}, u32[]{:S(2)}) %collective-permute-start.16) | collective-permute-done | bytes 139296 | tf_op jit(solution)/shard_map/ppermute | solution.py:662
  133.6 2.3 %collective-permute-done.17 = bf16[256,1024]{1,0:T(8,128)(2,1)S(1)} collective-permute-done((bf16[256,1024]{1,0:T(8,128)(2,1)S(1)}, bf16[256,1024]{1,0:T(8,128)(2,1)S(1)}, u32[]{:S(2)}, u32[]{:S(2)}) %collective-permute-start.17) | collective-permute-done | bytes 524320 | tf_op jit(solution)/shard_map/ppermute | solution.py:662
  136.0 1.9 %collective-permute-start.18 = (bf16[64,2176]{1,0:T(8,128)(2,1)S(1)}, bf16[64,2176]{1,0:T(8,128)(2,1)S(1)}, u32[]{:S(2)}, u32[]{:S(2)}) collective-permute-start(bf16[64,2176]{1,0:T(8,128)(2,1)S(1)} %pad_maximum_fusion.4), channel_id=1, source_target_pairs={{0,4},{1,5},{2,3},{3,2},{4,0},{5,1},{6,7},{7,6},{8,12},{9,13},{10,... | collective-permute-start | bytes 835592 | tf_op jit(solution)/shard_map/ppermute | solution.py:662
  137.9 4.7 %collective-permute-done.18 = bf16[64,2176]{1,0:T(8,128)(2,1)S(1)} collective-permute-done((bf16[64,2176]{1,0:T(8,128)(2,1)S(1)}, bf16[64,2176]{1,0:T(8,128)(2,1)S(1)}, u32[]{:S(2)}, u32[]{:S(2)}) %collective-permute-start.18) | collective-permute-done | bytes 278560 | tf_op jit(solution)/shard_map/ppermute | solution.py:662
  142.6 1.2 collective-permute-start.20
  143.8 3.1 %ffn_end.1 = (f32[512,1024]{1,0:T(8,128)}, f32[1024,512]{1,0:T(8,128)}) custom-call(s32[6]{0:T(128)S(1)} %stack.27.info_ref, bf16[512,1024]{1,0:T(8,128)(2,1)S(1)} %pad_maximum_fusion.1.keep_ref, bf16[512,1024]{1,0:T(8,128)(2,1)S(1)} %collective-permute-done.19.other_ref), custom_call_target="tpu_custom_call" | custom-call | flops 1000 | bytes 1000 | tf_op jit(solution)/shard_map/ffn_end/pallas_call | solution.py:54
  146.9 5.3 %collective-permute-done.20 = bf16[128,2176]{1,0:T(8,128)(2,1)S(1)} collective-permute-done((bf16[128,2176]{1,0:T(8,128)(2,1)S(1)}, bf16[128,2176]{1,0:T(8,128)(2,1)S(1)}, u32[]{:S(2)}, u32[]{:S(2)}) %collective-permute-start.20) | collective-permute-done | bytes 557088 | tf_op jit(solution)/shard_map/ppermute | solution.py:662
  152.4 2.7 %collective-permute-done.21.other_ref = bf16[256,2176]{1,0:T(8,128)(2,1)S(1)} collective-permute-done((bf16[256,2176]{1,0:T(8,128)(2,1)S(1)}, bf16[256,2176]{1,0:T(8,128)(2,1)S(1)}, u32[]{:S(2)}, u32[]{:S(2)}) %collective-permute-start.21) | collective-permute-done | bytes 1114144 | tf_op jit(solution)/shard_map/ppermute | solution.py:662
  155.1 5.1 %attend_end.1 = (f32[512,1536]{1,0:T(8,128)}, f32[512,512]{1,0:T(8,128)}, f32[512]{0:T(512)}, f32[512]{0:T(512)}, f32[512]{0:T(512)}, /*index=5*/f32[512]{0:T(512)}, f32[512]{0:T(512)}, f32[1024]{0:T(1024)}) custom-call(s32[6]{0:T(128)S(1)} %stack.27.info_ref, bf16[256,2176]{1,0:T(8,128)(2,1)S(1)} %pad_maximum_fusion.keep_ref, ...), custom_call_target="tpu_custom_call" | custom-call | flops 1000 | bytes 1000 | tf_op jit(solution)/shard_map/attend_end/pallas_call | solution.py:54
  (49 shorter events, 1.7 us)
Async XLA Ops:
  0.6 6.5 %copy-start = (bf16[512,1536]{1,0:T(8,128)(2,1)S(1)}, bf16[512,1536]{1,0:T(8,128)(2,1)}, u32[]{:S(2)}) copy-start(bf16[512,1536]{1,0:T(8,128)(2,1)} %w_ref.1) | copy-start | bytes 4718596
  0.7 6.5 %copy-start.3 = (bf16[512,512]{1,0:T(8,128)(2,1)S(1)}, bf16[512,512]{1,0:T(8,128)(2,1)}, u32[]{:S(2)}) copy-start(bf16[512,512]{1,0:T(8,128)(2,1)} %wout_ref.3) | copy-start | bytes 1572868
  4.0 12.2 %copy-start.1 = (bf16[512,1024]{1,0:T(8,128)(2,1)S(1)}, bf16[512,1024]{1,0:T(8,128)(2,1)}, u32[]{:S(2)}) copy-start(bf16[512,1024]{1,0:T(8,128)(2,1)} %up_ref.3) | copy-start | bytes 3145732
  4.1 12.2 %copy-start.2 = (bf16[1024,512]{1,0:T(8,128)(2,1)S(1)}, bf16[1024,512]{1,0:T(8,128)(2,1)}, u32[]{:S(2)}) copy-start(bf16[1024,512]{1,0:T(8,128)(2,1)} %down_ref.3) | copy-start | bytes 3145732
  4.1 26.5 %collective-permute-start = (bf16[528,512]{1,0:T(8,128)(2,1)S(1)}, bf16[528,512]{1,0:T(8,128)(2,1)S(1)}, u32[]{:S(2)}, u32[]{:S(2)}) collective-permute-start(bf16[528,512]{1,0:T(8,128)(2,1)S(1)} %get-tuple-element.82), channel_id=1, source_target_pairs={{0,1},{1,0},{2,3},{3,2},{4,5},{5,4},{6,7},{7,6},{8,9},{9,8},{10,11... | collective-permute-start | bytes 1622024 | tf_op jit(solution)/shard_map/ppermute | solution.py:662
  7.1 23.5 %collective-permute-start.1 = (bf16[512,512]{1,0:T(8,128)(2,1)S(1)}, bf16[512,512]{1,0:T(8,128)(2,1)S(1)}, u32[]{:S(2)}, u32[]{:S(2)}) collective-permute-start(bf16[512,512]{1,0:T(8,128)(2,1)S(1)} %get-tuple-element.83), channel_id=1, source_target_pairs={{0,1},{1,0},{2,3},{3,2},{4,5},{5,4},{6,7},{7,6},{8,9},{9,8},{10,11... | collective-permute-start | bytes 1572872 | tf_op jit(solution)/shard_map/ppermute | solution.py:662
  30.6 2.7 %collective-permute-start.2 = (bf16[512,1024]{1,0:T(8,128)(2,1)S(1)}, bf16[512,1024]{1,0:T(8,128)(2,1)S(1)}, u32[]{:S(2)}, u32[]{:S(2)}) collective-permute-start(bf16[512,1024]{1,0:T(8,128)(2,1)S(1)} %get-tuple-element.84), channel_id=1, source_target_pairs={{0,2},{1,3},{2,0},{3,1},{4,6},{5,7},{6,4},{7,5},{8,10},{9,11},{10,... | collective-permute-start | bytes 3145736 | tf_op jit(solution)/shard_map/ppermute | solution.py:662
  30.6 4.2 %collective-permute-start.3 = (bf16[528,512]{1,0:T(8,128)(2,1)S(1)}, bf16[528,512]{1,0:T(8,128)(2,1)S(1)}, u32[]{:S(2)}, u32[]{:S(2)}) collective-permute-start(bf16[528,512]{1,0:T(8,128)(2,1)S(1)} %collective-permute-done.refs_0_), channel_id=1, source_target_pairs={{0,2},{1,3},{2,0},{3,1},{4,6},{5,7},{6,4},{7,5},{8,10},{9,11},{10,... | collective-permute-start | bytes 1622024 | tf_op jit(solution)/shard_map/ppermute | solution.py:662
  31.1 3.7 %collective-permute-start.4 = (bf16[512,512]{1,0:T(8,128)(2,1)S(1)}, bf16[512,512]{1,0:T(8,128)(2,1)S(1)}, u32[]{:S(2)}, u32[]{:S(2)}) collective-permute-start(bf16[512,512]{1,0:T(8,128)(2,1)S(1)} %collective-permute-done.1.refs_2_), channel_id=1, source_target_pairs={{0,2},{1,3},{2,0},{3,1},{4,6},{5,7},{6,4},{7,5},{8,10},{9,11},{10,... | collective-permute-start | bytes 1572872 | tf_op jit(solution)/shard_map/ppermute | solution.py:662
  49.6 1.0 copy-start.6
  50.6 3.0 %collective-permute-start.5 = (bf16[512,1024]{1,0:T(8,128)(2,1)}, bf16[512,1024]{1,0:T(8,128)(2,1)}, u32[]{:S(2)}, u32[]{:S(2)}) collective-permute-start(bf16[512,1024]{1,0:T(8,128)(2,1)} %get-tuple-element.98), channel_id=1, source_target_pairs={{0,2},{1,3},{2,0},{3,1},{4,6},{5,7},{6,4},{7,5},{8,10},{9,11},{10,... | collective-permute-start | bytes 3145736 | tf_op jit(solution)/shard_map/ppermute | solution.py:662
  53.6 1.2 copy-start.7
  58.1 1.0 copy-start.4
  59.1 15.0 %collective-permute-start.7 = (bf16[512,1024]{1,0:T(8,128)(2,1)}, bf16[512,1024]{1,0:T(8,128)(2,1)S(1)}, u32[]{:S(2)}, u32[]{:S(2)}) collective-permute-start(bf16[512,1024]{1,0:T(8,128)(2,1)} %get-tuple-element.109), channel_id=1, source_target_pairs={{0,1},{1,0},{2,6},{3,7},{4,5},{5,4},{6,2},{7,3},{8,9},{9,8},{10,14... | collective-permute-start | bytes 3145736 | tf_op jit(solution)/shard_map/ppermute | solution.py:662
  61.4 12.7 %copy-start.5 = (bf16[512,1024]{1,0:T(8,128)(2,1)S(1)}, bf16[512,1024]{1,0:T(8,128)(2,1)}, u32[]{:S(2)}) copy-start(bf16[512,1024]{1,0:T(8,128)(2,1)} %copy-done.4) | copy-start | bytes 3145732
  72.0 2.8 %collective-permute-start.6 = (bf16[256,2176]{1,0:T(8,128)(2,1)S(1)}, bf16[256,2176]{1,0:T(8,128)(2,1)S(1)}, u32[]{:S(2)}, u32[]{:S(2)}) collective-permute-start(bf16[256,2176]{1,0:T(8,128)(2,1)S(1)} %get-tuple-element.107), channel_id=1, source_target_pairs={{0,2},{1,3},{2,0},{3,1},{4,6},{5,7},{6,4},{7,5},{8,10},{9,11},{10,... | collective-permute-start | bytes 3342344 | tf_op jit(solution)/shard_map/ppermute | solution.py:662
  75.2 14.6 %collective-permute-start.9 = (bf16[256,1024]{1,0:T(8,128)(2,1)S(1)}, bf16[256,1024]{1,0:T(8,128)(2,1)S(1)}, u32[]{:S(2)}, u32[]{:S(2)}) collective-permute-start(bf16[256,1024]{1,0:T(8,128)(2,1)S(1)} %slice.33), channel_id=1, source_target_pairs={{0,4},{1,5},{2,3},{3,2},{4,0},{5,1},{6,7},{7,6},{8,12},{9,13},{10,... | collective-permute-start | bytes 1572872 | tf_op jit(solution)/shard_map/ppermute | solution.py:662
  76.8 13.2 %collective-permute-start.8 = (bf16[128,2176]{1,0:T(8,128)(2,1)S(1)}, bf16[128,2176]{1,0:T(8,128)(2,1)S(1)}, u32[]{:S(2)}, u32[]{:S(2)}) collective-permute-start(bf16[128,2176]{1,0:T(8,128)(2,1)S(1)} %slice.31), channel_id=1, source_target_pairs={{0,1},{1,0},{2,6},{3,7},{4,5},{5,4},{6,2},{7,3},{8,9},{9,8},{10,14... | collective-permute-start | bytes 1671176 | tf_op jit(solution)/shard_map/ppermute | solution.py:662
  90.2 9.2 %collective-permute-start.11 = (bf16[128,1024]{1,0:T(8,128)(2,1)S(1)}, bf16[128,1024]{1,0:T(8,128)(2,1)S(1)}, u32[]{:S(2)}, u32[]{:S(2)}) collective-permute-start(bf16[128,1024]{1,0:T(8,128)(2,1)S(1)} %slice.37), channel_id=1, source_target_pairs={{0,16},{1,17},{2,10},{3,11},{4,20},{5,21},{6,14},{7,15},{8,24},{9,... | collective-permute-start | bytes 786440 | tf_op jit(solution)/shard_map/ppermute | solution.py:662
  92.9 6.6 %collective-permute-start.10 = (bf16[64,2176]{1,0:T(8,128)(2,1)S(1)}, bf16[64,2176]{1,0:T(8,128)(2,1)S(1)}, u32[]{:S(2)}, u32[]{:S(2)}) collective-permute-start(bf16[64,2176]{1,0:T(8,128)(2,1)S(1)} %slice.35), channel_id=1, source_target_pairs={{0,4},{1,5},{2,3},{3,2},{4,0},{5,1},{6,7},{7,6},{8,12},{9,13},{10,... | collective-permute-start | bytes 835592 | tf_op jit(solution)/shard_map/ppermute | solution.py:662
  99.6 6.1 %collective-permute-start.12 = (bf16[32,2176]{1,0:T(8,128)(2,1)S(1)}, bf16[32,2176]{1,0:T(8,128)(2,1)S(1)}, u32[]{:S(2)}, u32[]{:S(2)}) collective-permute-start(bf16[32,2176]{1,0:T(8,128)(2,1)S(1)} %slice.39), channel_id=1, source_target_pairs={{0,8},{1,9},{2,18},{3,19},{4,12},{5,13},{6,22},{7,23},{8,0},{9,1},... | collective-permute-start | bytes 417800 | tf_op jit(solution)/shard_map/ppermute | solution.py:662
  101.5 10.2 %collective-permute-start.13 = (bf16[128,1024]{1,0:T(8,128)(2,1)S(1)}, bf16[128,1024]{1,0:T(8,128)(2,1)S(1)}, u32[]{:S(2)}, u32[]{:S(2)}) collective-permute-start(bf16[128,1024]{1,0:T(8,128)(2,1)S(1)} %add_convert_fusion.7), channel_id=1, source_target_pairs={{0,8},{1,9},{2,18},{3,19},{4,12},{5,13},{6,22},{7,23},{8,0},{9,1},... | collective-permute-start | bytes 786440 | tf_op jit(solution)/shard_map/ppermute | solution.py:662
  111.8 7.6 %collective-permute-start.14 = (bf16[32,2176]{1,0:T(8,128)(2,1)S(1)}, bf16[32,2176]{1,0:T(8,128)(2,1)S(1)}, u32[]{:S(2)}, u32[]{:S(2)}) collective-permute-start(bf16[32,2176]{1,0:T(8,128)(2,1)S(1)} %add_convert_fusion.9), channel_id=1, source_target_pairs={{0,16},{1,17},{2,10},{3,11},{4,20},{5,21},{6,14},{7,15},{8,24},{9,... | collective-permute-start | bytes 417800 | tf_op jit(solution)/shard_map/ppermute | solution.py:662
  113.1 13.4 %collective-permute-start.15 = (bf16[128,1024]{1,0:T(8,128)(2,1)S(1)}, bf16[128,1024]{1,0:T(8,128)(2,1)S(1)}, u32[]{:S(2)}, u32[]{:S(2)}) collective-permute-start(bf16[128,1024]{1,0:T(8,128)(2,1)S(1)} %add_convert_fusion.6), channel_id=1, source_target_pairs={{0,16},{1,17},{2,6},{3,7},{4,20},{5,21},{6,2},{7,3},{8,24},{9,25},... | collective-permute-start | bytes 786440 | tf_op jit(solution)/shard_map/ppermute | solution.py:662
  126.6 9.2 %collective-permute-start.17 = (bf16[256,1024]{1,0:T(8,128)(2,1)S(1)}, bf16[256,1024]{1,0:T(8,128)(2,1)S(1)}, u32[]{:S(2)}, u32[]{:S(2)}) collective-permute-start(bf16[256,1024]{1,0:T(8,128)(2,1)S(1)} %pad_maximum_fusion.3), channel_id=1, source_target_pairs={{0,4},{1,5},{2,10},{3,11},{4,0},{5,1},{6,14},{7,15},{8,12},{9,13},... | collective-permute-start | bytes 1572872 | tf_op jit(solution)/shard_map/ppermute | solution.py:662
  128.5 5.1 %collective-permute-start.16 = (bf16[32,2176]{1,0:T(8,128)(2,1)S(1)}, bf16[32,2176]{1,0:T(8,128)(2,1)S(1)}, u32[]{:S(2)}, u32[]{:S(2)}) collective-permute-start(bf16[32,2176]{1,0:T(8,128)(2,1)S(1)} %add_convert_fusion.8), channel_id=1, source_target_pairs={{0,8},{1,9},{2,18},{3,19},{4,12},{5,13},{6,22},{7,23},{8,0},{9,1},... | collective-permute-start | bytes 417800 | tf_op jit(solution)/shard_map/ppermute | solution.py:662
  135.9 6.7 %collective-permute-start.19 = (bf16[512,1024]{1,0:T(8,128)(2,1)S(1)}, bf16[512,1024]{1,0:T(8,128)(2,1)S(1)}, u32[]{:S(2)}, u32[]{:S(2)}) collective-permute-start(bf16[512,1024]{1,0:T(8,128)(2,1)S(1)} %pad_maximum_fusion.1.keep_ref), channel_id=1, source_target_pairs={{0,2},{1,3},{2,0},{3,1},{4,6},{5,7},{6,4},{7,5},{8,10},{9,11},{10,... | collective-permute-start | bytes 3145736 | tf_op jit(solution)/shard_map/ppermute | solution.py:662
  136.0 6.6 %collective-permute-start.18 = (bf16[64,2176]{1,0:T(8,128)(2,1)S(1)}, bf16[64,2176]{1,0:T(8,128)(2,1)S(1)}, u32[]{:S(2)}, u32[]{:S(2)}) collective-permute-start(bf16[64,2176]{1,0:T(8,128)(2,1)S(1)} %pad_maximum_fusion.4), channel_id=1, source_target_pairs={{0,4},{1,5},{2,3},{3,2},{4,0},{5,1},{6,7},{7,6},{8,12},{9,13},{10,... | collective-permute-start | bytes 835592 | tf_op jit(solution)/shard_map/ppermute | solution.py:662
  142.6 9.6 %collective-permute-start.20 = (bf16[128,2176]{1,0:T(8,128)(2,1)S(1)}, bf16[128,2176]{1,0:T(8,128)(2,1)S(1)}, u32[]{:S(2)}, u32[]{:S(2)}) collective-permute-start(bf16[128,2176]{1,0:T(8,128)(2,1)S(1)} %pad_maximum_fusion.2), channel_id=1, source_target_pairs={{0,1},{1,0},{2,6},{3,7},{4,5},{5,4},{6,2},{7,3},{8,9},{9,8},{10,14... | collective-permute-start | bytes 1671176 | tf_op jit(solution)/shard_map/ppermute | solution.py:662
  152.3 2.8 %collective-permute-start.21 = (bf16[256,2176]{1,0:T(8,128)(2,1)S(1)}, bf16[256,2176]{1,0:T(8,128)(2,1)S(1)}, u32[]{:S(2)}, u32[]{:S(2)}) collective-permute-start(bf16[256,2176]{1,0:T(8,128)(2,1)S(1)} %pad_maximum_fusion.keep_ref), channel_id=1, source_target_pairs={{0,2},{1,3},{2,0},{3,1},{4,6},{5,7},{6,4},{7,5},{8,10},{9,11},{10,... | collective-permute-start | bytes 3342344 | tf_op jit(solution)/shard_map/ppermute | solution.py:662

commit v6 on v5

--- a/solution.py
+++ b/solution.py
@@ -110,13 +110,14 @@
     return own ^ jnp.where(core == 0, first, second)
 
 
-def permuted(dst_ref, acc_ref, chunk, tables, core, own):
+def permuted(dst_ref, acc_ref, chunk, tables, core, own, turned=0):
     blocks = len(tables[0])
     size = dst_ref.shape[0] // blocks
     for place in range(blocks):
         block = block_at(place, tables, core, own)
         rows = pl.ds(pl.multiple_of(block * size, size), size)
-        dst_ref[place * size : (place + 1) * size, :] = acc_ref[chunk, rows, :].astype(dst_ref.dtype)
+        to = pl.ds(pl.multiple_of(((place + turned * (blocks // 2)) & (blocks - 1)) * size, size), size)
+        dst_ref[to, :] = acc_ref[chunk, rows, :].astype(dst_ref.dtype)
 
 
 def attend_kernel(
@@ -200,7 +201,10 @@
 def pack_kernel(info_ref, up_ref, bias_ref, down_ref, up_out, down_out):
     width = up_ref.shape[0]
     up_out[:width, :] = up_ref[...]
-    up_out[width:, :] = jnp.broadcast_to(bias_ref[...], (TILE, bias_ref.shape[1]))
+    units = up_ref.shape[1]
+    bias = bias_ref[...].reshape(1, 2 * units)
+    bias = jnp.where(info_ref[0] == 0, bias[:, :units], bias[:, units:])
+    up_out[width:, :] = jnp.broadcast_to(bias, (TILE, units))
     down_out[...] = down_ref[...]
 
 
@@ -212,7 +216,7 @@
         (1,),
         [
             pl.BlockSpec((width, units), lambda t, info: (0, info[0])),
-            pl.BlockSpec((1, units), lambda t, info: (0, info[0])),
+            whole(2 * units),
             pl.BlockSpec((units, width), lambda t, info: (info[0], 0)),
         ],
         [whole(width + TILE, units), whole(units, width)],
@@ -243,7 +247,8 @@
 
 
 def ffn_own_kernel(
-    tables, info_ref, sec_ref, dy_ref, up_ref, bias_ref, down_ref, out_ref, dsec_ref, keep_ref, send_ref, bias_out, acc_ref
+    tables, mixing, info_ref, sec_ref, dy_ref, up_ref, bias_ref, down_ref, out_ref, dsec_ref, keep_ref, send_ref, bias_out,
+    acc_ref,
 ):
     at, last = pl.program_id(0), pl.num_programs(0) - 1
 
@@ -252,24 +257,23 @@
         acc_ref[...] = jnp.zeros_like(acc_ref)
         bias_out[...] = jnp.zeros_like(bias_out)
 
-    out, dsec = ffn_block(
-        sec_ref[...], dy_ref[...], up_ref[...], bias_ref[...].astype(F32), down_ref[...], acc_ref, bias_out
-    )
-    out_ref[...] = out
-    dsec_ref[...] = dsec
+    bias = bias_ref[...].astype(F32).reshape(1, up_ref.shape[1])
+    out_ref[...], dsec_ref[...] = ffn_block(
+        sec_ref[...], dy_ref[...], up_ref[...], bias, down_ref[...], acc_ref, bias_out
+    )
 
     @pl.when(at == last)
     def _():
         core, own, other = info_ref[0], info_ref[1], info_ref[2]
         permuted(keep_ref, acc_ref, core, tables, core, own)
-        permuted(send_ref, acc_ref, core ^ 1, tables, core ^ 1, other)
-
-
-def ffn_own(info, tables, second, dy, up, bias, down):
+        permuted(send_ref, acc_ref, core ^ 1, tables, core ^ 1, other, core ^ 1 if mixing else 0)
+
+
+def ffn_own(info, tables, mixing, second, dy, up, bias, down):
     n, width = second.shape
     units = up.shape[1] // 2
     return call(
-        functools.partial(ffn_own_kernel, tables),
+        functools.partial(ffn_own_kernel, tables, mixing),
         "ffn_own",
         (n // TOKS,),
         [rows_of(width), rows_of(width), whole(*up.shape), whole(*bias.shape), whole(*down.shape)],
@@ -284,12 +288,12 @@
 
 
 def ffn_rest_kernel(
-    tables, count, info_ref, sec_ref, dy_ref, out_part_ref, dsec_part_ref, res_ref, mixed_ref, bdown_ref, g2_ref, wout_ref, *refs
+    tables, count, mixing, info_ref, sec_ref, dy_ref, out_part_ref, dsec_part_ref, res_ref, mixed_ref, bdown_ref, g2_ref,
+    wout_ref, mine_ref, *refs
 ):
     ups, downs = refs[:count], refs[count : 2 * count]
     block_ref, gres_ref, gmix_ref, vec_ref, dwout_ref, bias_out = refs[2 * count : 2 * count + 6]
-    grads = refs[2 * count + 6 : 3 * count + 6]
-    acc_ref, up_ref, bias_ref, down_ref = refs[3 * count + 6 :]
+    *grads, acc_ref, up_ref, bias_ref, down_ref = refs[2 * count + 6 :]
     at, last = pl.program_id(0), pl.num_programs(0) - 1
     width, units = wout_ref.shape[0], ups[0].shape[1]
 
@@ -322,27 +326,60 @@
 
     @pl.when(at == last)
     def _():
-        core, own, other = info_ref[0], info_ref[1], info_ref[2]
-        for i in range(count):
-            permuted(grads[i], acc_ref, i, tables, core ^ (i % 2), other if i % 2 else own)
-
-
-def ffn_rest(info, tables, second, dy, out_part, dsec_part, residual, mixed, bdown, g2, wout, chunks):
+        core = info_ref[0]
+        blocks = len(tables[0])
+        size = width // blocks
+
+        def rows_at(i, place):
+            block = block_at(place, tables, core ^ (i % 2), info_ref[1 + i % 2])
+            rows = pl.ds(pl.multiple_of(block * size, size), size)
+            return acc_ref[i, rows, :].astype(BF)
+
+        def put(ref, row, part):
+            ref[row : row + size, :] = part
+
+        for i in range(1 if mixing else 0, count):
+            for place in range(blocks):
+                put(grads[i + 1 if mixing else i], place * size, rows_at(i, place))
+        if not mixing:
+            return
+        keep_ref, send_ref = grads[:2]
+        half = width // 2
+        for place in range(blocks // 2, blocks):
+            put(send_ref, place * size, rows_at(0, place))
+
+        @pl.when(core == 0)
+        def _():
+            for place in range(blocks // 2):
+                put(send_ref, place * size, rows_at(0, place))
+            keep_ref[...] = mine_ref[...]
+
+        @pl.when(core == 1)
+        def _():
+            for place in range(blocks // 2):
+                put(keep_ref, place * size, rows_at(0, place))
+            keep_ref[half:, :] = mine_ref[:half, :]
+            send_ref[:half, :] = mine_ref[half:, :]
+
+
+def ffn_rest(
+    info, tables, mixing, second, dy, out_part, dsec_part, residual, mixed, bdown, g2, wout, mine, chunks
+):
     n, width = second.shape
     count = len(chunks)
     units = chunks[0][0].shape[1]
     return call(
-        functools.partial(ffn_rest_kernel, tables, count),
+        functools.partial(ffn_rest_kernel, tables, count, mixing),
         "ffn_rest",
         (n // TOKS,),
         [rows_of(width)] * 6
         + [whole(1, width)] * 2
-        + [whole(width, width)]
+        + [whole(width, width), whole(*mine.shape)]
         + [whole(width + TILE, units)] * count
         + [whole(units, width)] * count,
         [rows_of(width)] * 3
         + [whole(8, width), whole(width, width), whole(count, units)]
-        + [whole(width, 2 * units)] * count,
+        + [whole(width, 2 * units)] * (count + mixing),
         [
             jax.ShapeDtypeStruct((n, width), BF),
             pltpu.HBM((n, width), F32),
@@ -351,7 +388,7 @@
             pltpu.HBM((width, width), F32),
             jax.ShapeDtypeStruct((count, units), F32),
         ]
-        + [jax.ShapeDtypeStruct((width, 2 * units), BF)] * count,
+        + [jax.ShapeDtypeStruct((width, 2 * units), BF)] * (count + mixing),
         [
             pltpu.VMEM((count, width, 2 * units), F32),
             pltpu.VMEM((width, count * units), BF),
@@ -363,40 +400,9 @@
         + far(dy)
         + near(out_part, dsec_part)
         + far(residual, mixed, bdown, g2)
-        + (wout,)
+        + (wout, mine)
         + tuple(c[0] for c in chunks)
         + tuple(c[1] for c in chunks),
-    )
-
-
-def mix_kernel(info_ref, mine_ref, other_ref, got_ref, keep_ref, send_ref):
-    top = mine_ref.shape[0] // 2
-    both = (other_ref[...].astype(F32) + got_ref[...].astype(F32)).astype(BF)
-    keep_ref[:top, :] = mine_ref[:top, :]
-
-    @pl.when(info_ref[0] == 0)
-    def _():
-        keep_ref[top:, :] = mine_ref[top:, :]
-        send_ref[...] = both
-
-    @pl.when(info_ref[0] == 1)
-    def _():
-        keep_ref[top:, :] = both[:top, :]
-        send_ref[:top, :] = mine_ref[top:, :]
-        send_ref[top:, :] = both[top:, :]
-
-
-def mix(info, mine, other, got):
-    return call(
-        mix_kernel,
-        "mix",
-        (1,),
-        [whole(*mine.shape)] * 3,
-        [whole(*mine.shape)] * 2,
-        [jax.ShapeDtypeStruct(mine.shape, BF)] * 2,
-        [],
-        info,
-        (mine, other, got),
     )
 
 
@@ -702,12 +708,13 @@
     def by_core(values):
         return jnp.where(core == 0, values[0], values[1]), jnp.where(core == 0, values[1], values[0])
 
-    if narrow == 2 and len(wide_masks) == 3:
+    mixing = narrow == 2 and len(wide_masks) == 3
+    if mixing:
         y, low, high = wide_masks
-        ff_in, ff_rest = ([y, high], [y, low]), ([low], [high])
-        ff_out = ([y, high], [low, y])
-        at_order = ([1, y, low], [y, 1, high])
-        at_rest = ([high], [low])
+        ff_in, ff_rest = ([y, low], [y, low]), ([high], [high])
+        ff_out = ([y, low], [low, y])
+        at_order = ([1, y, low], [y, 1, low])
+        at_rest = ([high], [high])
     else:
         ff_in, ff_rest = split_at((wide_masks, wide_masks), min(len(wide_masks) - 1, (width // TILE).bit_length() - 1))
         ff_out = ff_in
@@ -729,7 +736,7 @@
     at_block = by_core([block_of(used) for used in at_used])
     info = jnp.stack([core, *ff_block, *at_block, narrow_at]).astype(jnp.int32)
 
-    packed, tokens_in = after(pack(info, w_up, b_up[None], w_down), tokens_in)
+    packed, tokens_in = after(pack(info, w_up, b_up, w_down), tokens_in)
     fetched = [packed]
     for mask in narrow_masks:
         fetched = fetched + [(swap(u, mask), swap(d, mask)) for u, d in fetched]
@@ -740,15 +747,15 @@
         info, tokens_in, g1, c1, w_qkv, w_out, g2, row(ln2_bias), segment_ids, step_ids, pad_mask
     )
     out_part, dsec_part, own_keep, own_send, bias_own = ffn_own(
-        info, ff_in_tables, second, cotangent, w_up, b_up[None], w_down
+        info, ff_in_tables, mixing, second, cotangent, w_up, b_up, w_down
     )
     own_send, fetched = after(own_send, fetched)
     chunks = []
     for up, down in fetched[1:]:
         chunks += [(up, down), (swap(up, core_mask), swap(down, core_mask))]
-    own_keep, second = after(add(own_keep, swap(own_send, core_mask)), second)
     rest = ffn_rest(
-        info, ff_in_tables, second, cotangent, out_part, dsec_part, residual, mixed, row(b_down), g2, w_out, chunks
+        info, ff_in_tables, mixing, second, cotangent, out_part, dsec_part, residual, mixed, row(b_down), g2, w_out, own_keep,
+        chunks,
     )
     block_out, gres, gmix, vec, dwout, bias_rest = rest[:6]
     grads = rest[6:]
@@ -761,26 +768,37 @@
         b_all = jnp.where(narrow_at >> bit & 1, flipped, b_all)
     vec = jnp.concatenate([vec, b_all.reshape(-1, width)], axis=0)
 
-    got = [swap(grads[2 * j + 1], core_mask) for j in range(narrow - 1)]
-    if narrow == 2 and len(wide_masks) == 3:
-        ff_keep, ff_send = mix(info, own_keep, grads[0], got[0])
-        gmix, ff_keep, ff_send = after(gmix, ff_keep, ff_send)
-        ff_keep = add(ff_keep, swap(ff_send, 1, y))
-        ff_left = ([y, high], [1, low])
+    if mixing:
+        ff_keep, ff_send, away = grads
+        got_own, got = swap(own_send, core_mask), swap(away, core_mask)
+        chunk = (core == 0) | (lax.broadcasted_iota(jnp.int32, got.shape, 0) >= width // 2)
+        ff_send = add(ff_send, jnp.where(chunk, got, got_own))
+        gmix, ff_send = after(gmix, ff_send)
+        ff_got = swap(ff_send, 1, y)
+        top = width // 2
+        ff_keep = add(ff_keep, jnp.where(chunk, got_own, got))
+        ff_send = add(jnp.where(core == 0, ff_keep[top:], ff_keep[:top]), ff_got[top:])
+        ff_keep = add(jnp.where(core == 0, ff_keep[:top], ff_keep[top:]), ff_got[:top])
     else:
-        held = [own_keep] + [add(grads[2 * j], got[j]) for j in range(narrow - 1)]
+        held = [add(own_keep, swap(own_send, core_mask))] + [add(grads[2 * j], swap(grads[2 * j + 1], core_mask)) for j in range(narrow - 1)]
         gmix, held = after(gmix, held)
         for mask in reversed(narrow_masks):
             held = [add(held[j], swap(held[j + mask], mask)) for j in range(mask)]
-        ff_keep, ff_left = held[0], ff_in
+        ff_keep = ff_send = held[0]
 
     dqkv, keep, send = attend_back(info, at_tables, qkv, prob, gmix, tokens_in, vec, dwout)
-    keep, ff_keep = after(add(keep, swap(send, core_mask)), ff_keep)
+    keep, ff_keep, ff_send = after(add(keep, swap(send, core_mask)), ff_keep, ff_send)
     grad_tokens = first_back(info, dqkv, w_qkv, tokens_in, gres, g1)
     at_steps = scatters(at_order) + exchanges(at_rest) + gathers(at_order)
-    ff_steps = scatters(ff_left) + exchanges(ff_rest) + gathers(ff_out)
-    keep, ff_keep, grad_tokens = after(at_steps[0](keep), ff_steps[0](ff_keep), grad_tokens)
-    at_steps, ff_steps = at_steps[1:], ff_steps[1:]
+    ff_steps = exchanges(ff_rest) + gathers(ff_out)
+    if mixing:
+        ff_keep = add(ff_keep, swap(ff_send, y, 1))
+        ff_steps = scatters(([low], [low])) + ff_steps
+    else:
+        first, *ff_steps = scatters(ff_in) + ff_steps
+        ff_keep = first(ff_keep)
+    keep, ff_keep, grad_tokens = after(at_steps[0](keep), ff_keep, grad_tokens)
+    at_steps = at_steps[1:]
     shared = min(len(at_steps), len(ff_steps))
     for at_step, ff_step in zip(at_steps, ff_steps):
         keep, ff_keep = after(at_step(keep), ff_step(ff_keep))

time: 161 us -> 154 us (0.957)
  local copies, waits for them, and re-layouts: 4.92 us -> 1.28 us
  other arithmetic: 2.61 us -> 6.07 us
  waiting for transfers between devices: 65.5 us -> 62.6 us
  Pallas kernels: 63 us -> 60.2 us
    convert_element_type x10, other arithmetic: 1.73 us -> 5.18 us  [add(): return (a.astype(F32) + b.astype(F32)).astype(a.dtype)]
    ppermute x22, waiting for transfers between devices: 65.5 us -> 62.6 us  [swap(): return lax.ppermute(value, AXES, pairs)]
    pallas_call x9 -> x8, Pallas kernels: 63 us -> 60.2 us  [call(): pl.pallas_call(kernel, grid_spec=pltpu.PrefetchScalarGridSpec(num_scalar_...]
    unnamed x16 -> x12, local copies, waits for them, and re-layouts: 3.18 us -> 0.99 us
  transfers between devices with their start and end apart: 22 -> 22, of which waited for: 17 -> 16; matrix products, arithmetic and copies ran while one was open for 1% -> 1% of each run, Pallas kernels for 24% -> 35%
where the time goes in v6:
time: 154 us
  waiting for transfers between devices  62.6 us (41%)
  Pallas kernels  60.2 us (39%)
  starting transfers between devices  22.5 us (15%)
  other arithmetic  6.07 us (4%)
    ppermute x22, waiting for transfers between devices, swap(): return lax.ppermute(value, AXES, pairs)  62.6 us
    pallas_call x8, Pallas kernels, call(): pl.pallas_call(kernel, grid_spec=pltpu.PrefetchScalarGridSpec(num_scalar_...  60.2 us
    ppermute x22, starting transfers between devices, swap(): return lax.ppermute(value, AXES, pairs)  22.5 us
    convert_element_type x10, other arithmetic, add(): return (a.astype(F32) + b.astype(F32)).astype(a.dtype)  5.18 us
  transfers between devices with their start and end apart: 22, of which 16 were waited for; matrix products, arithmetic and copies ran while one was open for 1% of the time, Pallas kernels for 35%

profile of v6, /device:TPU:0, one launch (start us, length us, event | category | flops | bytes accessed | tf_op | source)
XLA Modules:
  0.0 153.8 jit_solution(12310572609611307473)
XLA Ops:
  0.7 0.1 stack.21.info_ref
  0.8 1.8 %pack.1 = (bf16[528,512]{1,0:T(8,128)(2,1)S(1)}, bf16[512,512]{1,0:T(8,128)(2,1)S(1)}) custom-call(s32[6]{0:T(128)S(1)} %stack.21.info_ref, bf16[512,1024]{1,0:T(8,128)(2,1)} %up_ref.3, bf16[1024]{0:T(1024)(128)(2,1)} %bias_ref.3, bf16[1024,512]{1,0:T(8,128)(2,1)} %down_ref.3), custom_call_target="tpu_custom_call" | custom-call | flops 1000 | bytes 1000 | tf_op jit(solution)/shard_map/pack/pallas_call | solution.py:54
  2.6 3.0 %collective-permute-start = (bf16[528,512]{1,0:T(8,128)(2,1)S(1)}, bf16[528,512]{1,0:T(8,128)(2,1)S(1)}, u32[]{:S(2)}, u32[]{:S(2)}) collective-permute-start(bf16[528,512]{1,0:T(8,128)(2,1)S(1)} %get-tuple-element.83), channel_id=1, source_target_pairs={{0,1},{1,0},{2,3},{3,2},{4,5},{5,4},{6,7},{7,6},{8,9},{9,8},{10,11... | collective-permute-start | bytes 1622024 | tf_op jit(solution)/shard_map/ppermute | solution.py:668
  5.7 9.1 %attend.1 = (bf16[1024,1536]{1,0:T(8,128)(2,1)}, bf16[8,4,128,256]{3,2,1,0:T(8,128)(2,1)}, bf16[1024,512]{1,0:T(8,128)(2,1)}, f32[1024,512]{1,0:T(8,128)}, bf16[1024,512]{1,0:T(8,128)(2,1)S(1)}) custom-call(s32[6]{0:T(128)S(1)} %stack.21.info_ref, bf16[1024,512]{1,0:T(8,128)(2,1)} %tok_ref.2, f32[1,512]{1,0:T(1,128)} %bitcast.13, f32[1,512]{1,0:T(1,128)} %bitcast.18, ...), custom_call_target="tpu_custom_call" | custom-call | flops 1000 | bytes 1000 | tf_op jit(solution)/shard_map/attend/pallas_call | solution.py:54
  14.8 10.7 %ffn_own.1 = (f32[1024,512]{1,0:T(8,128)S(1)}, f32[1024,512]{1,0:T(8,128)S(1)}, bf16[512,1024]{1,0:T(8,128)(2,1)S(1)}, bf16[512,1024]{1,0:T(8,128)(2,1)}, f32[2,512]{1,0:T(2,128)S(1)}) custom-call(s32[6]{0:T(128)S(1)} %stack.21.info_ref, bf16[1024,512]{1,0:T(8,128)(2,1)S(1)} %get-tuple-element.76.sec_ref, bf16[1024,512]{1,0:T(8,128)(2,1)} %dy_ref.3, ...), custom_call_target="tpu_custom_call" | custom-call | flops 1000 | bytes 1000 | tf_op jit(solution)/shard_map/ffn_own/pallas_call | solution.py:54
  25.5 3.6 %collective-permute-done.1.refs_2_ = bf16[512,512]{1,0:T(8,128)(2,1)S(1)} collective-permute-done((bf16[512,512]{1,0:T(8,128)(2,1)S(1)}, bf16[512,512]{1,0:T(8,128)(2,1)S(1)}, u32[]{:S(2)}, u32[]{:S(2)}) %collective-permute-start.1) | collective-permute-done | bytes 524320 | tf_op jit(solution)/shard_map/ppermute | solution.py:668
  29.1 0.5 collective-permute-start.3
  29.7 2.9 %collective-permute-done.3.refs_3_ = bf16[512,512]{1,0:T(8,128)(2,1)S(1)} collective-permute-done((bf16[512,512]{1,0:T(8,128)(2,1)S(1)}, bf16[512,512]{1,0:T(8,128)(2,1)S(1)}, u32[]{:S(2)}, u32[]{:S(2)}) %collective-permute-start.3) | collective-permute-done | bytes 524320 | tf_op jit(solution)/shard_map/ppermute | solution.py:668
  32.6 14.6 %ffn_rest.1 = (bf16[1024,512]{1,0:T(8,128)(2,1)}, f32[1024,512]{1,0:T(8,128)}, bf16[1024,512]{1,0:T(8,128)(2,1)}, f32[8,512]{1,0:T(8,128)S(1)}, f32[512,512]{1,0...) custom-call(s32[6]{0:T(128)S(1)} %stack.21.info_ref, ...), custom_call_target="tpu_custom_call" | custom-call | flops 1000 | bytes 1000 | tf_op jit(solution)/shard_map/ffn_rest/pallas_call | solution.py:54
  47.2 1.0 copy-done.4
  48.2 0.1 collective-permute-start.4
  48.3 0.1 reverse.6
  48.4 2.7 %collective-permute-done.4 = bf16[512,1024]{1,0:T(8,128)(2,1)} collective-permute-done((bf16[512,1024]{1,0:T(8,128)(2,1)}, bf16[512,1024]{1,0:T(8,128)(2,1)}, u32[]{:S(2)}, u32[]{:S(2)}) %collective-permute-start.4) | collective-permute-done | bytes 1048608 | tf_op jit(solution)/shard_map/ppermute | solution.py:668
  51.2 3.9 %add_convert_fusion.1 = (bf16[512,1024]{1,0:T(8,128)(2,1)}, bf16[512,1024]{1,0:T(8,128)(2,1)}) fusion(bf16[512,1024]{1,0:T(8,128)(2,1)S(1)} %get-tuple-element.101, bf16[512,1024]{1,0:T(8,128)(2,1)} %collective-permute-done.5, bf16[512,1024]{1,0:T(8,128)(2,1)} %collective-permute-done.4, pred[512]{0:T(512)(128)(4,1)S(1)} %fusion, bf16[512,1024]{1,0:T(8,128)(2,1)} %copy-done.4), kind=kLoop, calls=%fused_computation.1 | loop fusion | flops 5242880 | bytes 6291968 | tf_op jit(solution)/shard_map/convert_element_type | solution.py:671
  55.1 1.8 %collective-permute-start.7 = (bf16[512,1024]{1,0:T(8,128)(2,1)}, bf16[512,1024]{1,0:T(8,128)(2,1)S(1)}, u32[]{:S(2)}, u32[]{:S(2)}) collective-permute-start(bf16[512,1024]{1,0:T(8,128)(2,1)} %get-tuple-element.102), channel_id=1, source_target_pairs={{0,1},{1,0},{2,6},{3,7},{4,5},{5,4},{6,2},{7,3},{8,9},{9,8},{10,14... | collective-permute-start | bytes 3145736 | tf_op jit(solution)/shard_map/ppermute | solution.py:668
  56.8 0.6 pad_maximum_fusion.5.vec_ref
  57.5 10.4 %attend_back.1 = (bf16[1024,1536]{1,0:T(8,128)(2,1)S(1)}, bf16[256,2176]{1,0:T(8,128)(2,1)S(1)}, bf16[256,2176]{1,0:T(8,128)(2,1)S(1)}) custom-call(s32[6]{0:T(128)S(1)} %stack.21.info_ref, bf16[1024,1536]{1,0:T(8,128)(2,1)} %get-tuple-element.88.qkv_ref, bf16[8,4,128,256]{3,2,1,0:T(8,128)(2,1)} %get-tuple-element.89.prob_ref, ...), custom_call_target="tpu_custom_call" | custom-call | flops 1000 | bytes 1000 | tf_op jit(solution)/shard_map/attend_back/pallas_call | solution.py:54
  67.9 2.1 %collective-permute-done.7 = bf16[512,1024]{1,0:T(8,128)(2,1)S(1)} collective-permute-done((bf16[512,1024]{1,0:T(8,128)(2,1)}, bf16[512,1024]{1,0:T(8,128)(2,1)S(1)}, u32[]{:S(2)}, u32[]{:S(2)}) %collective-permute-start.7) | collective-permute-done | bytes 1048608 | tf_op jit(solution)/shard_map/ppermute | solution.py:668
  70.1 0.4 add_convert_fusion.5
  70.5 0.2 collective-permute-done.6
  70.7 0.3 add_convert_fusion
  71.0 1.7 %collective-permute-start.9 = (bf16[256,1024]{1,0:T(8,128)(2,1)S(1)}, bf16[256,1024]{1,0:T(8,128)(2,1)S(1)}, u32[]{:S(2)}, u32[]{:S(2)}) collective-permute-start(bf16[256,1024]{1,0:T(8,128)(2,1)S(1)} %get-tuple-element.105), channel_id=1, source_target_pairs={{0,4},{1,5},{2,3},{3,2},{4,0},{5,1},{6,7},{7,6},{8,12},{9,13},{10,... | collective-permute-start | bytes 1572872 | tf_op jit(solution)/shard_map/ppermute | solution.py:668
  72.7 1.6 %collective-permute-start.8 = (bf16[128,2176]{1,0:T(8,128)(2,1)S(1)}, bf16[128,2176]{1,0:T(8,128)(2,1)S(1)}, u32[]{:S(2)}, u32[]{:S(2)}) collective-permute-start(bf16[128,2176]{1,0:T(8,128)(2,1)S(1)} %slice.43), channel_id=1, source_target_pairs={{0,1},{1,0},{2,6},{3,7},{4,5},{5,4},{6,2},{7,3},{8,9},{9,8},{10,14... | collective-permute-start | bytes 1671176 | tf_op jit(solution)/shard_map/ppermute | solution.py:668
  74.2 5.5 %first_back.1 = f32[1024,512]{1,0:T(8,128)} custom-call(s32[6]{0:T(128)S(1)} %stack.21.info_ref, bf16[1024,1536]{1,0:T(8,128)(2,1)S(1)} %get-tuple-element.106.dqkv_ref, bf16[512,1536]{1,0:T(8,128)(2,1)S(1)} %copy-done, bf16[1024,512]{1,0:T(8,128)(2,1)} %tok_ref.2, f32[1024,512]{1,0:T(8,128)} %get-tuple-element.107.gres_ref, f32[1,512]{1,0:T(1,128)} %bitcast.14), custom_call_target="tpu_custom_call" | custom-call | flops 1000 | bytes 1000 | tf_op jit(solution)/shard_map/first_back/pallas_call | solution.py:54
  79.7 5.9 %collective-permute-done.9 = bf16[256,1024]{1,0:T(8,128)(2,1)S(1)} collective-permute-done((bf16[256,1024]{1,0:T(8,128)(2,1)S(1)}, bf16[256,1024]{1,0:T(8,128)(2,1)S(1)}, u32[]{:S(2)}, u32[]{:S(2)}) %collective-permute-start.9) | collective-permute-done | bytes 524320 | tf_op jit(solution)/shard_map/ppermute | solution.py:668
  85.6 0.2 add_convert_fusion.4
  85.8 0.1 add_convert_fusion.3
  86.0 1.8 %collective-permute-start.11 = (bf16[128,1024]{1,0:T(8,128)(2,1)S(1)}, bf16[128,1024]{1,0:T(8,128)(2,1)S(1)}, u32[]{:S(2)}, u32[]{:S(2)}) collective-permute-start(bf16[128,1024]{1,0:T(8,128)(2,1)S(1)} %slice.47), channel_id=1, source_target_pairs={{0,8},{1,9},{2,10},{3,11},{4,12},{5,13},{6,14},{7,15},{8,0},{9,1},... | collective-permute-start | bytes 786440 | tf_op jit(solution)/shard_map/ppermute | solution.py:668
  87.8 1.6 %collective-permute-start.10 = (bf16[64,2176]{1,0:T(8,128)(2,1)S(1)}, bf16[64,2176]{1,0:T(8,128)(2,1)S(1)}, u32[]{:S(2)}, u32[]{:S(2)}) collective-permute-start(bf16[64,2176]{1,0:T(8,128)(2,1)S(1)} %slice.45), channel_id=1, source_target_pairs={{0,4},{1,5},{2,3},{3,2},{4,0},{5,1},{6,7},{7,6},{8,12},{9,13},{10,... | collective-permute-start | bytes 835592 | tf_op jit(solution)/shard_map/ppermute | solution.py:668
  89.4 5.0 %collective-permute-done.11 = bf16[128,1024]{1,0:T(8,128)(2,1)S(1)} collective-permute-done((bf16[128,1024]{1,0:T(8,128)(2,1)S(1)}, bf16[128,1024]{1,0:T(8,128)(2,1)S(1)}, u32[]{:S(2)}, u32[]{:S(2)}) %collective-permute-start.11) | collective-permute-done | bytes 262176 | tf_op jit(solution)/shard_map/ppermute | solution.py:668
  94.6 1.7 %collective-permute-start.12 = (bf16[32,2176]{1,0:T(8,128)(2,1)S(1)}, bf16[32,2176]{1,0:T(8,128)(2,1)S(1)}, u32[]{:S(2)}, u32[]{:S(2)}) collective-permute-start(bf16[32,2176]{1,0:T(8,128)(2,1)S(1)} %slice.49), channel_id=1, source_target_pairs={{0,8},{1,9},{2,10},{3,11},{4,12},{5,13},{6,14},{7,15},{8,0},{9,1},... | collective-permute-start | bytes 417800 | tf_op jit(solution)/shard_map/ppermute | solution.py:668
  96.3 2.6 %collective-permute-start.13 = (bf16[128,1024]{1,0:T(8,128)(2,1)S(1)}, bf16[128,1024]{1,0:T(8,128)(2,1)S(1)}, u32[]{:S(2)}, u32[]{:S(2)}) collective-permute-start(bf16[128,1024]{1,0:T(8,128)(2,1)S(1)} %add_convert_fusion.9), channel_id=1, source_target_pairs={{0,16},{1,17},{2,18},{3,19},{4,20},{5,21},{6,22},{7,23},{8,24},{9,... | collective-permute-start | bytes 786440 | tf_op jit(solution)/shard_map/ppermute | solution.py:668
  98.9 2.6 %collective-permute-done.12 = bf16[32,2176]{1,0:T(8,128)(2,1)S(1)} collective-permute-done((bf16[32,2176]{1,0:T(8,128)(2,1)S(1)}, bf16[32,2176]{1,0:T(8,128)(2,1)S(1)}, u32[]{:S(2)}, u32[]{:S(2)}) %collective-permute-start.12) | collective-permute-done | bytes 139296 | tf_op jit(solution)/shard_map/ppermute | solution.py:668
  101.6 8.5 %collective-permute-done.13 = bf16[128,1024]{1,0:T(8,128)(2,1)S(1)} collective-permute-done((bf16[128,1024]{1,0:T(8,128)(2,1)S(1)}, bf16[128,1024]{1,0:T(8,128)(2,1)S(1)}, u32[]{:S(2)}, u32[]{:S(2)}) %collective-permute-start.13) | collective-permute-done | bytes 262176 | tf_op jit(solution)/shard_map/ppermute | solution.py:668
  110.3 3.0 %collective-permute-start.15 = (bf16[128,1024]{1,0:T(8,128)(2,1)S(1)}, bf16[128,1024]{1,0:T(8,128)(2,1)S(1)}, u32[]{:S(2)}, u32[]{:S(2)}) collective-permute-start(bf16[128,1024]{1,0:T(8,128)(2,1)S(1)} %add_convert_fusion.8), channel_id=1, source_target_pairs={{0,8},{1,9},{2,6},{3,7},{4,12},{5,13},{6,2},{7,3},{8,0},{9,1},{10,... | collective-permute-start | bytes 786440 | tf_op jit(solution)/shard_map/ppermute | solution.py:668
  113.3 5.0 %collective-permute-done.14 = bf16[32,2176]{1,0:T(8,128)(2,1)S(1)} collective-permute-done((bf16[32,2176]{1,0:T(8,128)(2,1)S(1)}, bf16[32,2176]{1,0:T(8,128)(2,1)S(1)}, u32[]{:S(2)}, u32[]{:S(2)}) %collective-permute-start.14) | collective-permute-done | bytes 139296 | tf_op jit(solution)/shard_map/ppermute | solution.py:668
  118.3 1.6 %collective-permute-done.15 = bf16[128,1024]{1,0:T(8,128)(2,1)S(1)} collective-permute-done((bf16[128,1024]{1,0:T(8,128)(2,1)S(1)}, bf16[128,1024]{1,0:T(8,128)(2,1)S(1)}, u32[]{:S(2)}, u32[]{:S(2)}) %collective-permute-start.15) | collective-permute-done | bytes 262176 | tf_op jit(solution)/shard_map/ppermute | solution.py:668
  120.0 1.1 collective-permute-start.17
  121.1 6.6 %collective-permute-done.16 = bf16[32,2176]{1,0:T(8,128)(2,1)S(1)} collective-permute-done((bf16[32,2176]{1,0:T(8,128)(2,1)S(1)}, bf16[32,2176]{1,0:T(8,128)(2,1)S(1)}, u32[]{:S(2)}, u32[]{:S(2)}) %collective-permute-start.16) | collective-permute-done | bytes 139296 | tf_op jit(solution)/shard_map/ppermute | solution.py:668
  127.7 1.5 collective-permute-done.17
  129.4 1.1 collective-permute-start.18
  130.5 5.5 %collective-permute-done.18 = bf16[64,2176]{1,0:T(8,128)(2,1)S(1)} collective-permute-done((bf16[64,2176]{1,0:T(8,128)(2,1)S(1)}, bf16[64,2176]{1,0:T(8,128)(2,1)S(1)}, u32[]{:S(2)}, u32[]{:S(2)}) %collective-permute-start.18) | collective-permute-done | bytes 278560 | tf_op jit(solution)/shard_map/ppermute | solution.py:668
  136.0 0.5 collective-permute-start.20
  136.5 3.1 %ffn_end.1 = (f32[512,1024]{1,0:T(8,128)}, f32[1024,512]{1,0:T(8,128)}) custom-call(s32[6]{0:T(128)S(1)} %stack.21.info_ref, bf16[512,1024]{1,0:T(8,128)(2,1)S(1)} %pad_maximum_fusion.1.keep_ref, bf16[512,1024]{1,0:T(8,128)(2,1)S(1)} %collective-permute-done.19.other_ref), custom_call_target="tpu_custom_call" | custom-call | flops 1000 | bytes 1000 | tf_op jit(solution)/shard_map/ffn_end/pallas_call | solution.py:54
  139.6 6.0 %collective-permute-done.20 = bf16[128,2176]{1,0:T(8,128)(2,1)S(1)} collective-permute-done((bf16[128,2176]{1,0:T(8,128)(2,1)S(1)}, bf16[128,2176]{1,0:T(8,128)(2,1)S(1)}, u32[]{:S(2)}, u32[]{:S(2)}) %collective-permute-start.20) | collective-permute-done | bytes 557088 | tf_op jit(solution)/shard_map/ppermute | solution.py:668
  145.6 0.1 pad_maximum_fusion.keep_ref
  145.8 2.7 %collective-permute-done.21.other_ref = bf16[256,2176]{1,0:T(8,128)(2,1)S(1)} collective-permute-done((bf16[256,2176]{1,0:T(8,128)(2,1)S(1)}, bf16[256,2176]{1,0:T(8,128)(2,1)S(1)}, u32[]{:S(2)}, u32[]{:S(2)}) %collective-permute-start.21) | collective-permute-done | bytes 1114144 | tf_op jit(solution)/shard_map/ppermute | solution.py:668
  148.5 5.1 %attend_end.1 = (f32[512,1536]{1,0:T(8,128)}, f32[512,512]{1,0:T(8,128)}, f32[512]{0:T(512)}, f32[512]{0:T(512)}, f32[512]{0:T(512)}, /*index=5*/f32[512]{0:T(512)}, f32[512]{0:T(512)}, f32[1024]{0:T(1024)}) custom-call(s32[6]{0:T(128)S(1)} %stack.21.info_ref, bf16[256,2176]{1,0:T(8,128)(2,1)S(1)} %pad_maximum_fusion.keep_ref, ...), custom_call_target="tpu_custom_call" | custom-call | flops 1000 | bytes 1000 | tf_op jit(solution)/shard_map/attend_end/pallas_call | solution.py:54
  (43 shorter events, 1.0 us)
Async XLA Ops:
  0.6 5.1 %copy-start = (bf16[512,1536]{1,0:T(8,128)(2,1)S(1)}, bf16[512,1536]{1,0:T(8,128)(2,1)}, u32[]{:S(2)}) copy-start(bf16[512,1536]{1,0:T(8,128)(2,1)} %w_ref.1) | copy-start | bytes 4718596
  0.7 5.1 %copy-start.3 = (bf16[512,512]{1,0:T(8,128)(2,1)S(1)}, bf16[512,512]{1,0:T(8,128)(2,1)}, u32[]{:S(2)}) copy-start(bf16[512,512]{1,0:T(8,128)(2,1)} %wout_ref.3) | copy-start | bytes 1572868
  2.6 12.2 %copy-start.1 = (bf16[512,1024]{1,0:T(8,128)(2,1)S(1)}, bf16[512,1024]{1,0:T(8,128)(2,1)}, u32[]{:S(2)}) copy-start(bf16[512,1024]{1,0:T(8,128)(2,1)} %up_ref.3) | copy-start | bytes 3145732
  2.6 12.2 %copy-start.2 = (bf16[1024,512]{1,0:T(8,128)(2,1)S(1)}, bf16[1024,512]{1,0:T(8,128)(2,1)}, u32[]{:S(2)}) copy-start(bf16[1024,512]{1,0:T(8,128)(2,1)} %down_ref.3) | copy-start | bytes 3145732
  2.6 26.5 %collective-permute-start = (bf16[528,512]{1,0:T(8,128)(2,1)S(1)}, bf16[528,512]{1,0:T(8,128)(2,1)S(1)}, u32[]{:S(2)}, u32[]{:S(2)}) collective-permute-start(bf16[528,512]{1,0:T(8,128)(2,1)S(1)} %get-tuple-element.83), channel_id=1, source_target_pairs={{0,1},{1,0},{2,3},{3,2},{4,5},{5,4},{6,7},{7,6},{8,9},{9,8},{10,11... | collective-permute-start | bytes 1622024 | tf_op jit(solution)/shard_map/ppermute | solution.py:668
  5.6 23.5 %collective-permute-start.1 = (bf16[512,512]{1,0:T(8,128)(2,1)S(1)}, bf16[512,512]{1,0:T(8,128)(2,1)S(1)}, u32[]{:S(2)}, u32[]{:S(2)}) collective-permute-start(bf16[512,512]{1,0:T(8,128)(2,1)S(1)} %get-tuple-element.84), channel_id=1, source_target_pairs={{0,1},{1,0},{2,3},{3,2},{4,5},{5,4},{6,7},{7,6},{8,9},{9,8},{10,11... | collective-permute-start | bytes 1572872 | tf_op jit(solution)/shard_map/ppermute | solution.py:668
  29.1 3.4 %collective-permute-start.2 = (bf16[528,512]{1,0:T(8,128)(2,1)S(1)}, bf16[528,512]{1,0:T(8,128)(2,1)S(1)}, u32[]{:S(2)}, u32[]{:S(2)}) collective-permute-start(bf16[528,512]{1,0:T(8,128)(2,1)S(1)} %collective-permute-done.refs_0_), channel_id=1, source_target_pairs={{0,2},{1,3},{2,0},{3,1},{4,6},{5,7},{6,4},{7,5},{8,10},{9,11},{10,... | collective-permute-start | bytes 1622024 | tf_op jit(solution)/shard_map/ppermute | solution.py:668
  29.1 3.4 %collective-permute-start.3 = (bf16[512,512]{1,0:T(8,128)(2,1)S(1)}, bf16[512,512]{1,0:T(8,128)(2,1)S(1)}, u32[]{:S(2)}, u32[]{:S(2)}) collective-permute-start(bf16[512,512]{1,0:T(8,128)(2,1)S(1)} %collective-permute-done.1.refs_2_), channel_id=1, source_target_pairs={{0,2},{1,3},{2,0},{3,1},{4,6},{5,7},{6,4},{7,5},{8,10},{9,11},{10,... | collective-permute-start | bytes 1572872 | tf_op jit(solution)/shard_map/ppermute | solution.py:668
  29.7 18.8 %collective-permute-start.5 = (bf16[512,1024]{1,0:T(8,128)(2,1)}, bf16[512,1024]{1,0:T(8,128)(2,1)}, u32[]{:S(2)}, u32[]{:S(2)}) collective-permute-start(bf16[512,1024]{1,0:T(8,128)(2,1)} %get-tuple-element.93), channel_id=1, source_target_pairs={{0,2},{1,3},{2,0},{3,1},{4,6},{5,7},{6,4},{7,5},{8,10},{9,11},{10,... | collective-permute-start | bytes 3145736 | tf_op jit(solution)/shard_map/ppermute | solution.py:668
  47.2 1.0 copy-start.4
  48.2 3.0 %collective-permute-start.4 = (bf16[512,1024]{1,0:T(8,128)(2,1)}, bf16[512,1024]{1,0:T(8,128)(2,1)}, u32[]{:S(2)}, u32[]{:S(2)}) collective-permute-start(bf16[512,1024]{1,0:T(8,128)(2,1)} %get-tuple-element.92), channel_id=1, source_target_pairs={{0,2},{1,3},{2,0},{3,1},{4,6},{5,7},{6,4},{7,5},{8,10},{9,11},{10,... | collective-permute-start | bytes 3145736 | tf_op jit(solution)/shard_map/ppermute | solution.py:668
  55.1 15.0 %collective-permute-start.7 = (bf16[512,1024]{1,0:T(8,128)(2,1)}, bf16[512,1024]{1,0:T(8,128)(2,1)S(1)}, u32[]{:S(2)}, u32[]{:S(2)}) collective-permute-start(bf16[512,1024]{1,0:T(8,128)(2,1)} %get-tuple-element.102), channel_id=1, source_target_pairs={{0,1},{1,0},{2,6},{3,7},{4,5},{5,4},{6,2},{7,3},{8,9},{9,8},{10,14... | collective-permute-start | bytes 3145736 | tf_op jit(solution)/shard_map/ppermute | solution.py:668
  57.5 12.6 %copy-start.5 = (bf16[512,1024]{1,0:T(8,128)(2,1)S(1)}, bf16[512,1024]{1,0:T(8,128)(2,1)}, u32[]{:S(2)}) copy-start(bf16[512,1024]{1,0:T(8,128)(2,1)} %get-tuple-element.134) | copy-start | bytes 3145732
  67.9 2.8 %collective-permute-start.6 = (bf16[256,2176]{1,0:T(8,128)(2,1)S(1)}, bf16[256,2176]{1,0:T(8,128)(2,1)S(1)}, u32[]{:S(2)}, u32[]{:S(2)}) collective-permute-start(bf16[256,2176]{1,0:T(8,128)(2,1)S(1)} %get-tuple-element.100), channel_id=1, source_target_pairs={{0,2},{1,3},{2,0},{3,1},{4,6},{5,7},{6,4},{7,5},{8,10},{9,11},{10,... | collective-permute-start | bytes 3342344 | tf_op jit(solution)/shard_map/ppermute | solution.py:668
  71.0 14.6 %collective-permute-start.9 = (bf16[256,1024]{1,0:T(8,128)(2,1)S(1)}, bf16[256,1024]{1,0:T(8,128)(2,1)S(1)}, u32[]{:S(2)}, u32[]{:S(2)}) collective-permute-start(bf16[256,1024]{1,0:T(8,128)(2,1)S(1)} %get-tuple-element.105), channel_id=1, source_target_pairs={{0,4},{1,5},{2,3},{3,2},{4,0},{5,1},{6,7},{7,6},{8,12},{9,13},{10,... | collective-permute-start | bytes 1572872 | tf_op jit(solution)/shard_map/ppermute | solution.py:668
  72.7 13.1 %collective-permute-start.8 = (bf16[128,2176]{1,0:T(8,128)(2,1)S(1)}, bf16[128,2176]{1,0:T(8,128)(2,1)S(1)}, u32[]{:S(2)}, u32[]{:S(2)}) collective-permute-start(bf16[128,2176]{1,0:T(8,128)(2,1)S(1)} %slice.43), channel_id=1, source_target_pairs={{0,1},{1,0},{2,6},{3,7},{4,5},{5,4},{6,2},{7,3},{8,9},{9,8},{10,14... | collective-permute-start | bytes 1671176 | tf_op jit(solution)/shard_map/ppermute | solution.py:668
  86.0 8.5 %collective-permute-start.11 = (bf16[128,1024]{1,0:T(8,128)(2,1)S(1)}, bf16[128,1024]{1,0:T(8,128)(2,1)S(1)}, u32[]{:S(2)}, u32[]{:S(2)}) collective-permute-start(bf16[128,1024]{1,0:T(8,128)(2,1)S(1)} %slice.47), channel_id=1, source_target_pairs={{0,8},{1,9},{2,10},{3,11},{4,12},{5,13},{6,14},{7,15},{8,0},{9,1},... | collective-permute-start | bytes 786440 | tf_op jit(solution)/shard_map/ppermute | solution.py:668
  87.8 6.7 %collective-permute-start.10 = (bf16[64,2176]{1,0:T(8,128)(2,1)S(1)}, bf16[64,2176]{1,0:T(8,128)(2,1)S(1)}, u32[]{:S(2)}, u32[]{:S(2)}) collective-permute-start(bf16[64,2176]{1,0:T(8,128)(2,1)S(1)} %slice.45), channel_id=1, source_target_pairs={{0,4},{1,5},{2,3},{3,2},{4,0},{5,1},{6,7},{7,6},{8,12},{9,13},{10,... | collective-permute-start | bytes 835592 | tf_op jit(solution)/shard_map/ppermute | solution.py:668
  94.6 7.0 %collective-permute-start.12 = (bf16[32,2176]{1,0:T(8,128)(2,1)S(1)}, bf16[32,2176]{1,0:T(8,128)(2,1)S(1)}, u32[]{:S(2)}, u32[]{:S(2)}) collective-permute-start(bf16[32,2176]{1,0:T(8,128)(2,1)S(1)} %slice.49), channel_id=1, source_target_pairs={{0,8},{1,9},{2,10},{3,11},{4,12},{5,13},{6,14},{7,15},{8,0},{9,1},... | collective-permute-start | bytes 417800 | tf_op jit(solution)/shard_map/ppermute | solution.py:668
  96.3 13.8 %collective-permute-start.13 = (bf16[128,1024]{1,0:T(8,128)(2,1)S(1)}, bf16[128,1024]{1,0:T(8,128)(2,1)S(1)}, u32[]{:S(2)}, u32[]{:S(2)}) collective-permute-start(bf16[128,1024]{1,0:T(8,128)(2,1)S(1)} %add_convert_fusion.9), channel_id=1, source_target_pairs={{0,16},{1,17},{2,18},{3,19},{4,20},{5,21},{6,22},{7,23},{8,24},{9,... | collective-permute-start | bytes 786440 | tf_op jit(solution)/shard_map/ppermute | solution.py:668
  110.2 8.1 %collective-permute-start.14 = (bf16[32,2176]{1,0:T(8,128)(2,1)S(1)}, bf16[32,2176]{1,0:T(8,128)(2,1)S(1)}, u32[]{:S(2)}, u32[]{:S(2)}) collective-permute-start(bf16[32,2176]{1,0:T(8,128)(2,1)S(1)} %add_convert_fusion.11), channel_id=1, source_target_pairs={{0,16},{1,17},{2,18},{3,19},{4,20},{5,21},{6,22},{7,23},{8,24},{9,... | collective-permute-start | bytes 417800 | tf_op jit(solution)/shard_map/ppermute | solution.py:668
  110.3 9.7 %collective-permute-start.15 = (bf16[128,1024]{1,0:T(8,128)(2,1)S(1)}, bf16[128,1024]{1,0:T(8,128)(2,1)S(1)}, u32[]{:S(2)}, u32[]{:S(2)}) collective-permute-start(bf16[128,1024]{1,0:T(8,128)(2,1)S(1)} %add_convert_fusion.8), channel_id=1, source_target_pairs={{0,8},{1,9},{2,6},{3,7},{4,12},{5,13},{6,2},{7,3},{8,0},{9,1},{10,... | collective-permute-start | bytes 786440 | tf_op jit(solution)/shard_map/ppermute | solution.py:668
  120.0 9.2 %collective-permute-start.17 = (bf16[256,1024]{1,0:T(8,128)(2,1)S(1)}, bf16[256,1024]{1,0:T(8,128)(2,1)S(1)}, u32[]{:S(2)}, u32[]{:S(2)}) collective-permute-start(bf16[256,1024]{1,0:T(8,128)(2,1)S(1)} %pad_maximum_fusion.3), channel_id=1, source_target_pairs={{0,4},{1,5},{2,10},{3,11},{4,0},{5,1},{6,14},{7,15},{8,12},{9,13},... | collective-permute-start | bytes 1572872 | tf_op jit(solution)/shard_map/ppermute | solution.py:668
  121.1 6.6 %collective-permute-start.16 = (bf16[32,2176]{1,0:T(8,128)(2,1)S(1)}, bf16[32,2176]{1,0:T(8,128)(2,1)S(1)}, u32[]{:S(2)}, u32[]{:S(2)}) collective-permute-start(bf16[32,2176]{1,0:T(8,128)(2,1)S(1)} %add_convert_fusion.10), channel_id=1, source_target_pairs={{0,8},{1,9},{2,10},{3,11},{4,12},{5,13},{6,14},{7,15},{8,0},{9,1},... | collective-permute-start | bytes 417800 | tf_op jit(solution)/shard_map/ppermute | solution.py:668
  129.3 6.7 %collective-permute-start.19 = (bf16[512,1024]{1,0:T(8,128)(2,1)S(1)}, bf16[512,1024]{1,0:T(8,128)(2,1)S(1)}, u32[]{:S(2)}, u32[]{:S(2)}) collective-permute-start(bf16[512,1024]{1,0:T(8,128)(2,1)S(1)} %pad_maximum_fusion.1.keep_ref), channel_id=1, source_target_pairs={{0,2},{1,3},{2,0},{3,1},{4,6},{5,7},{6,4},{7,5},{8,10},{9,11},{10,... | collective-permute-start | bytes 3145736 | tf_op jit(solution)/shard_map/ppermute | solution.py:668
  129.4 6.6 %collective-permute-start.18 = (bf16[64,2176]{1,0:T(8,128)(2,1)S(1)}, bf16[64,2176]{1,0:T(8,128)(2,1)S(1)}, u32[]{:S(2)}, u32[]{:S(2)}) collective-permute-start(bf16[64,2176]{1,0:T(8,128)(2,1)S(1)} %pad_maximum_fusion.4), channel_id=1, source_target_pairs={{0,4},{1,5},{2,3},{3,2},{4,0},{5,1},{6,7},{7,6},{8,12},{9,13},{10,... | collective-permute-start | bytes 835592 | tf_op jit(solution)/shard_map/ppermute | solution.py:668
  136.0 9.6 %collective-permute-start.20 = (bf16[128,2176]{1,0:T(8,128)(2,1)S(1)}, bf16[128,2176]{1,0:T(8,128)(2,1)S(1)}, u32[]{:S(2)}, u32[]{:S(2)}) collective-permute-start(bf16[128,2176]{1,0:T(8,128)(2,1)S(1)} %pad_maximum_fusion.2), channel_id=1, source_target_pairs={{0,1},{1,0},{2,6},{3,7},{4,5},{5,4},{6,2},{7,3},{8,9},{9,8},{10,14... | collective-permute-start | bytes 1671176 | tf_op jit(solution)/shard_map/ppermute | solution.py:668
  145.7 2.8 %collective-permute-start.21 = (bf16[256,2176]{1,0:T(8,128)(2,1)S(1)}, bf16[256,2176]{1,0:T(8,128)(2,1)S(1)}, u32[]{:S(2)}, u32[]{:S(2)}) collective-permute-start(bf16[256,2176]{1,0:T(8,128)(2,1)S(1)} %pad_maximum_fusion.keep_ref), channel_id=1, source_target_pairs={{0,2},{1,3},{2,0},{3,1},{4,6},{5,7},{6,4},{7,5},{8,10},{9,11},{10,... | collective-permute-start | bytes 3342344 | tf_op jit(solution)/shard_map/ppermute | solution.py:668

commit v7 on v6

--- a/solution.py
+++ b/solution.py
@@ -19,7 +19,7 @@
 SUMS = 8
 TILE = 16
 TOKS = 512
-VMEM_LIMIT = 32 * 1024 * 1024
+VMEM_LIMIT = 30 * 1024 * 1024
 
 
 def mm(a, b):
@@ -673,24 +673,25 @@
     def after(*values):
         return lax.optimization_barrier(values)
 
-    def scatters(order):
-        def step(first, second, value):
+    def steps_of(halved, exchanged, gathered):
+        pairs = lambda order: list(zip(*order))
+        return (
+            [("halve", *pair) for pair in pairs(halved)]
+            + [("exchange", *pair) for pair in pairs(exchanged)]
+            + [("gather", *pair) for pair in reversed(pairs(gathered))]
+        )
+
+    def start(value, step):
+        kind, *masks = step
+        if kind == "halve":
             half = value.shape[0] // 2
-            return add(value[:half], swap(value[half:], first, second))
-
-        return [functools.partial(step, *pair) for pair in zip(*order)]
-
-    def exchanges(order):
-        def step(first, second, value):
-            return add(value, swap(value, first, second))
-
-        return [functools.partial(step, *pair) for pair in zip(*order)]
-
-    def gathers(order):
-        def step(first, second, value):
-            return jnp.concatenate([value, swap(value, first, second)], axis=0)
-
-        return [functools.partial(step, *pair) for pair in reversed(list(zip(*order)))]
+            return value[:half], swap(value[half:], *masks)
+        return value, swap(value, *masks)
+
+    def finish(kept, got, step):
+        if step[0] == "gather":
+            return jnp.concatenate([kept, got], axis=0)
+        return (kept, got) if step[0] == "core" else add(kept, got)
 
     wide_at, narrow_at = lax.axis_index("wide"), lax.axis_index("narrow")
     core = wide_at & 1
@@ -711,27 +712,28 @@
     mixing = narrow == 2 and len(wide_masks) == 3
     if mixing:
         y, low, high = wide_masks
-        ff_in, ff_rest = ([y, low], [y, low]), ([high], [high])
-        ff_out = ([y, low], [low, y])
-        at_order = ([1, y, low], [y, 1, low])
-        at_rest = ([high], [high])
+        ff_in, ff_rest, ff_out = ([y, high], [y, low]), ([low], [high]), ([high, y], [low, y])
+        at_in, at_rest, at_out = ([low, y, 1], [high, 1, y]), ([high], [low]), ([y, 1, low], [1, y, high])
+        turns = "FAFAAFAFAAFAFA"
     else:
         ff_in, ff_rest = split_at((wide_masks, wide_masks), min(len(wide_masks) - 1, (width // TILE).bit_length() - 1))
-        ff_out = ff_in
         masks = narrow_masks + wide_masks
-        at_order, at_rest = split_at((masks, masks), min(len(masks) - 1, (width // TILE // 2).bit_length() - 1))
+        at_in, at_rest = split_at((masks, masks), min(len(masks) - 1, (width // TILE // 2).bit_length() - 1))
+        ff_out, at_out, turns = ff_in, at_in, ""
     ff_used = tuple(sorted(o) for o in ff_in)
     ff_in_tables, ff_out_tables = (
         tuple([named(owner, ff_used[c]) for owner in places(pair[c], 1 << len(ff_used[c]))] for c in range(2))
         for pair in (ff_in, ff_out)
     )
-    at_used = tuple([core_mask] + sorted(o) for o in at_order)
-    at_places = [places(o, 1 << len(o)) for o in at_order]
-    at_tables = tuple(
-        [named(o, at_used[c]) for o in at_places[c]]
-        + [named(o ^ core_mask, at_used[1 - c]) for o in at_places[1 - c]]
-        for c in range(2)
-    )
+    at_used = tuple([core_mask] + sorted(o) for o in at_in)
+
+    def at_tables(order):
+        owners = [places(o, 1 << len(o)) for o in order]
+        return tuple(
+            [named(o, at_used[c]) for o in owners[c]] + [named(o ^ core_mask, at_used[1 - c]) for o in owners[1 - c]]
+            for c in range(2)
+        )
+
     ff_block = by_core([block_of(used) for used in ff_used])
     at_block = by_core([block_of(used) for used in at_used])
     info = jnp.stack([core, *ff_block, *at_block, narrow_at]).astype(jnp.int32)
@@ -774,7 +776,7 @@
         chunk = (core == 0) | (lax.broadcasted_iota(jnp.int32, got.shape, 0) >= width // 2)
         ff_send = add(ff_send, jnp.where(chunk, got, got_own))
         gmix, ff_send = after(gmix, ff_send)
-        ff_got = swap(ff_send, 1, y)
+        ff_got, ff_keep, got_own, got = after(swap(ff_send, 1, y), ff_keep, got_own, got)
         top = width // 2
         ff_keep = add(ff_keep, jnp.where(chunk, got_own, got))
         ff_send = add(jnp.where(core == 0, ff_keep[top:], ff_keep[:top]), ff_got[top:])
@@ -786,34 +788,44 @@
             held = [add(held[j], swap(held[j + mask], mask)) for j in range(mask)]
         ff_keep = ff_send = held[0]
 
-    dqkv, keep, send = attend_back(info, at_tables, qkv, prob, gmix, tokens_in, vec, dwout)
+    dqkv, keep, send = attend_back(info, at_tables(at_in), qkv, prob, gmix, tokens_in, vec, dwout)
     keep, ff_keep, ff_send = after(add(keep, swap(send, core_mask)), ff_keep, ff_send)
     grad_tokens = first_back(info, dqkv, w_qkv, tokens_in, gres, g1)
-    at_steps = scatters(at_order) + exchanges(at_rest) + gathers(at_order)
-    ff_steps = exchanges(ff_rest) + gathers(ff_out)
+    steps = {
+        "A": steps_of(at_in, at_rest, at_out) + [("core", core_mask)],
+        "F": steps_of(ff_in, ff_rest, ff_out) + [("core", core_mask)],
+    }
     if mixing:
-        ff_keep = add(ff_keep, swap(ff_send, y, 1))
-        ff_steps = scatters(([low], [low])) + ff_steps
+        steps["F"] = [("halve", y, 1)] + steps["F"][1:]
+        first = (ff_keep, swap(ff_send, y, 1))
     else:
-        first, *ff_steps = scatters(ff_in) + ff_steps
-        ff_keep = first(ff_keep)
-    keep, ff_keep, grad_tokens = after(at_steps[0](keep), ff_keep, grad_tokens)
-    at_steps = at_steps[1:]
-    shared = min(len(at_steps), len(ff_steps))
-    for at_step, ff_step in zip(at_steps, ff_steps):
-        keep, ff_keep = after(at_step(keep), ff_step(ff_keep))
-    for ff_step in ff_steps[shared:]:
-        ff_keep = ff_step(ff_keep)
-    ff_other = swap(ff_keep, core_mask)
-    for at_step in at_steps[shared : shared + 1]:
-        keep, ff_other = after(at_step(keep), ff_other)
-    ff_done = ffn_end(info, ff_out_tables, ff_keep, ff_other)
-    for at_step in at_steps[shared + 1 :]:
-        keep, ff_done = after(at_step(keep), ff_done)
-    grad_w_up, grad_w_down = ff_done
-
+        first = start(ff_keep, steps["F"][0])
+    turns = turns or "".join(a + f for a, f in itertools.zip_longest("A" * len(steps["A"]), "F" * len(steps["F"]), fillvalue=""))
+    under_way = {"A": start(keep, steps["A"][0]), "F": first}
+    done, beside = (), (grad_tokens,)
+    for turn in turns:
+        other = "A" if turn == "F" else "F"
+        kept, got = under_way.pop(turn)
+        if other in under_way:
+            other_kept, other_got = under_way[other]
+            kept, other_kept, *beside = after(kept, other_kept, *beside)
+            under_way[other] = other_kept, other_got
+        else:
+            kept, *beside = after(kept, *beside)
+        if len(beside) == 1:
+            (grad_tokens,), beside = beside, ()
+        elif beside:
+            (grad_w_up, grad_w_down), beside = beside, ()
+        step, *steps[turn] = steps[turn]
+        value = finish(kept, got, step)
+        if steps[turn]:
+            under_way[turn] = start(value, steps[turn][0])
+        elif turn == "F":
+            beside = ffn_end(info, ff_out_tables, *value)
+        else:
+            done = value
     grad_w_qkv, grad_w_out, d_gain1, d_bias1, d_gain2, d_bias2, d_bdown, grad_b_up = attend_end(
-        info, at_tables, keep, swap(keep, core_mask), w_qkv, g1, c1, 2 * units
+        info, at_tables(at_out), *done, w_qkv, g1, c1, 2 * units
     )
     return (
         block_out, grad_tokens, d_gain1, d_bias1, grad_w_qkv, grad_w_out, d_gain2, d_bias2, grad_w_up, grad_b_up, grad_w_down,

time: 154 us -> 157 us (1.019)
  starting transfers between devices: 22.5 us -> 30.8 us
  waiting for transfers between devices: 62.6 us -> 54.8 us
  other arithmetic: 6.07 us -> 8.43 us
    ppermute x22, starting transfers between devices: 22.5 us -> 30.8 us  [swap(): return lax.ppermute(value, AXES, pairs)]
    ppermute x22, waiting for transfers between devices: 62.6 us -> 54.8 us  [swap(): return lax.ppermute(value, AXES, pairs)]
    convert_element_type x10 -> x11, other arithmetic: 5.18 us -> 7.78 us  [add(): return (a.astype(F32) + b.astype(F32)).astype(a.dtype)]
  transfers between devices with their start and end apart: 22 -> 22, of which waited for: 16 -> 14; matrix products, arithmetic and copies ran while one was open for 1% -> 3% of each run, Pallas kernels for 35% -> 34%
where the time goes in v7:
time: 157 us
  Pallas kernels  60.1 us (38%)
  waiting for transfers between devices  54.8 us (35%)
  starting transfers between devices  30.8 us (20%)
  other arithmetic  8.43 us (5%)
  local copies, waits for them, and re-layouts  1.64 us (1%)
    pallas_call x8, Pallas kernels, call(): pl.pallas_call(kernel, grid_spec=pltpu.PrefetchScalarGridSpec(num_scalar_...  60.1 us
    ppermute x22, waiting for transfers between devices, swap(): return lax.ppermute(value, AXES, pairs)  54.8 us
    ppermute x22, starting transfers between devices, swap(): return lax.ppermute(value, AXES, pairs)  30.8 us
    convert_element_type x11, other arithmetic, add(): return (a.astype(F32) + b.astype(F32)).astype(a.dtype)  7.78 us
  transfers between devices with their start and end apart: 22, of which 14 were waited for; matrix products, arithmetic and copies ran while one was open for 3% of the time, Pallas kernels for 34%

profile of v7, /device:TPU:0, one launch (start us, length us, event | category | flops | bytes accessed | tf_op | source)
XLA Modules:
  0.0 156.9 jit_solution(14309590392490721543)
XLA Ops:
  0.7 0.1 stack.27.info_ref
  0.8 1.8 %pack.1 = (bf16[528,512]{1,0:T(8,128)(2,1)S(1)}, bf16[512,512]{1,0:T(8,128)(2,1)S(1)}) custom-call(s32[6]{0:T(128)S(1)} %stack.27.info_ref, bf16[512,1024]{1,0:T(8,128)(2,1)} %up_ref.3, bf16[1024]{0:T(1024)(128)(2,1)} %bias_ref.3, bf16[1024,512]{1,0:T(8,128)(2,1)} %down_ref.3), custom_call_target="tpu_custom_call" | custom-call | flops 1000 | bytes 1000 | tf_op jit(solution)/shard_map/pack/pallas_call | solution.py:54
  2.6 3.0 %collective-permute-start = (bf16[528,512]{1,0:T(8,128)(2,1)S(1)}, bf16[528,512]{1,0:T(8,128)(2,1)S(1)}, u32[]{:S(2)}, u32[]{:S(2)}) collective-permute-start(bf16[528,512]{1,0:T(8,128)(2,1)S(1)} %get-tuple-element.101), channel_id=1, source_target_pairs={{0,1},{1,0},{2,3},{3,2},{4,5},{5,4},{6,7},{7,6},{8,9},{9,8},{10,11... | collective-permute-start | bytes 1622024 | tf_op jit(solution)/shard_map/ppermute | solution.py:668
  5.7 9.1 %attend.1 = (bf16[1024,1536]{1,0:T(8,128)(2,1)}, bf16[8,4,128,256]{3,2,1,0:T(8,128)(2,1)}, bf16[1024,512]{1,0:T(8,128)(2,1)}, f32[1024,512]{1,0:T(8,128)}, bf16[1024,512]{1,0:T(8,128)(2,1)S(1)}) custom-call(s32[6]{0:T(128)S(1)} %stack.27.info_ref, bf16[1024,512]{1,0:T(8,128)(2,1)} %tok_ref.2, f32[1,512]{1,0:T(1,128)} %bitcast.15, f32[1,512]{1,0:T(1,128)} %bitcast.20, ...), custom_call_target="tpu_custom_call" | custom-call | flops 1000 | bytes 1000 | tf_op jit(solution)/shard_map/attend/pallas_call | solution.py:54
  14.8 10.6 %ffn_own.1 = (f32[1024,512]{1,0:T(8,128)S(1)}, f32[1024,512]{1,0:T(8,128)S(1)}, bf16[512,1024]{1,0:T(8,128)(2,1)S(1)}, bf16[512,1024]{1,0:T(8,128)(2,1)}, f32[2,512]{1,0:T(2,128)S(1)}) custom-call(s32[6]{0:T(128)S(1)} %stack.27.info_ref, bf16[1024,512]{1,0:T(8,128)(2,1)S(1)} %get-tuple-element.94.sec_ref, bf16[1024,512]{1,0:T(8,128)(2,1)} %dy_ref.3, ...), custom_call_target="tpu_custom_call" | custom-call | flops 1000 | bytes 1000 | tf_op jit(solution)/shard_map/ffn_own/pallas_call | solution.py:54
  25.5 3.7 %collective-permute-done.1.refs_2_ = bf16[512,512]{1,0:T(8,128)(2,1)S(1)} collective-permute-done((bf16[512,512]{1,0:T(8,128)(2,1)S(1)}, bf16[512,512]{1,0:T(8,128)(2,1)S(1)}, u32[]{:S(2)}, u32[]{:S(2)}) %collective-permute-start.1) | collective-permute-done | bytes 524320 | tf_op jit(solution)/shard_map/ppermute | solution.py:668
  29.2 0.5 collective-permute-start.3
  29.7 2.9 %collective-permute-done.3.refs_3_ = bf16[512,512]{1,0:T(8,128)(2,1)S(1)} collective-permute-done((bf16[512,512]{1,0:T(8,128)(2,1)S(1)}, bf16[512,512]{1,0:T(8,128)(2,1)S(1)}, u32[]{:S(2)}, u32[]{:S(2)}) %collective-permute-start.3) | collective-permute-done | bytes 524320 | tf_op jit(solution)/shard_map/ppermute | solution.py:668
  32.6 14.6 %ffn_rest.1 = (bf16[1024,512]{1,0:T(8,128)(2,1)}, f32[1024,512]{1,0:T(8,128)}, bf16[1024,512]{1,0:T(8,128)(2,1)}, f32[8,512]{1,0:T(8,128)S(1)}, f32[512,512]{1,0...) custom-call(s32[6]{0:T(128)S(1)} %stack.27.info_ref, ...), custom_call_target="tpu_custom_call" | custom-call | flops 1000 | bytes 1000 | tf_op jit(solution)/shard_map/ffn_rest/pallas_call | solution.py:54
  47.2 1.0 copy-done.4
  48.2 0.1 collective-permute-start.4
  48.3 0.1 reverse.6
  48.4 2.8 %collective-permute-done.4 = bf16[512,1024]{1,0:T(8,128)(2,1)} collective-permute-done((bf16[512,1024]{1,0:T(8,128)(2,1)}, bf16[512,1024]{1,0:T(8,128)(2,1)}, u32[]{:S(2)}, u32[]{:S(2)}) %collective-permute-start.4) | collective-permute-done | bytes 1048608 | tf_op jit(solution)/shard_map/ppermute | solution.py:668
  51.2 3.3 %add_convert_fusion.2 = bf16[512,1024]{1,0:T(8,128)(2,1)} fusion(bf16[512,1024]{1,0:T(8,128)(2,1)} %copy-done.4, bf16[512,1024]{1,0:T(8,128)(2,1)} %collective-permute-done.4, bf16[512,1024]{1,0:T(8,128)(2,1)} %collective-permute-done.5, pred[512]{0:T(512)(128)(4,1)S(1)} %fusion), kind=kLoop, calls=%fused_computation.2 | loop fusion | flops 2621440 | bytes 4194816 | tf_op jit(solution)/shard_map/convert_element_type | solution.py:671
  54.4 1.7 %collective-permute-start.7 = (bf16[512,1024]{1,0:T(8,128)(2,1)}, bf16[512,1024]{1,0:T(8,128)(2,1)}, u32[]{:S(2)}, u32[]{:S(2)}) collective-permute-start(bf16[512,1024]{1,0:T(8,128)(2,1)} %add_convert_fusion.2), channel_id=1, source_target_pairs={{0,1},{1,0},{2,6},{3,7},{4,5},{5,4},{6,2},{7,3},{8,9},{9,8},{10,14... | collective-permute-start | bytes 3145736 | tf_op jit(solution)/shard_map/ppermute | solution.py:668
  56.2 0.6 pad_maximum_fusion.vec_ref
  56.8 10.4 %attend_back.1 = (bf16[1024,1536]{1,0:T(8,128)(2,1)S(1)}, bf16[256,2176]{1,0:T(8,128)(2,1)S(1)}, bf16[256,2176]{1,0:T(8,128)(2,1)S(1)}) custom-call(s32[6]{0:T(128)S(1)} %stack.27.info_ref, bf16[1024,1536]{1,0:T(8,128)(2,1)} %get-tuple-element.106.qkv_ref, bf16[8,4,128,256]{3,2,1,0:T(8,128)(2,1)} %get-tuple-element.107.prob_ref, ...), custom_call_target="tpu_custom_call" | custom-call | flops 1000 | bytes 1000 | tf_op jit(solution)/shard_map/attend_back/pallas_call | solution.py:54
  67.3 2.2 %collective-permute-done.7 = bf16[512,1024]{1,0:T(8,128)(2,1)} collective-permute-done((bf16[512,1024]{1,0:T(8,128)(2,1)}, bf16[512,1024]{1,0:T(8,128)(2,1)}, u32[]{:S(2)}, u32[]{:S(2)}) %collective-permute-start.7) | collective-permute-done | bytes 1048608 | tf_op jit(solution)/shard_map/ppermute | solution.py:668
  69.5 2.0 %add_convert_fusion.1 = bf16[512,1024]{1,0:T(8,128)(2,1)S(1)} fusion(bf16[512,1024]{1,0:T(8,128)(2,1)S(1)} %get-tuple-element.121, bf16[512,1024]{1,0:T(8,128)(2,1)} %collective-permute-done.5, bf16[512,1024]{1,0:T(8,128)(2,1)} %collective-permute-done.4, pred[512]{0:T(512)(128)(4,1)S(1)} %fusion), kind=kLoop, calls=%fused_computation.1 | loop fusion | flops 2621440 | bytes 4194816 | tf_op jit(solution)/shard_map/convert_element_type | solution.py:671
  71.5 1.6 %add_convert_fusion.5 = (bf16[256,1024]{1,0:T(8,128)(2,1)S(1)}, bf16[256,1024]{1,0:T(8,128)(2,1)S(1)}) fusion(bf16[512,1024]{1,0:T(8,128)(2,1)} %collective-permute-done.7, pred[]{:T(512)S(6)} %eq.2, bf16[512,1024]{1,0:T(8,128)(2,1)S(1)} %add_convert_fusion.1), kind=kLoop, calls=%fused_computation.5 | loop fusion | flops 2621440 | bytes 3145729 | tf_op jit(solution)/shard_map/convert_element_type | solution.py:671
  73.2 0.3 add_convert_fusion
  73.5 1.8 %collective-permute-start.8 = (bf16[256,1024]{1,0:T(8,128)(2,1)S(1)}, bf16[256,1024]{1,0:T(8,128)(2,1)S(1)}, u32[]{:S(2)}, u32[]{:S(2)}) collective-permute-start(bf16[256,1024]{1,0:T(8,128)(2,1)S(1)} %get-tuple-element.132), channel_id=1, source_target_pairs={{0,4},{1,5},{2,3},{3,2},{4,0},{5,1},{6,7},{7,6},{8,12},{9,13},{10,... | collective-permute-start | bytes 1572872 | tf_op jit(solution)/shard_map/ppermute | solution.py:668
  75.4 1.6 %collective-permute-start.9 = (bf16[128,2176]{1,0:T(8,128)(2,1)S(1)}, bf16[128,2176]{1,0:T(8,128)(2,1)S(1)}, u32[]{:S(2)}, u32[]{:S(2)}) collective-permute-start(bf16[128,2176]{1,0:T(8,128)(2,1)S(1)} %get-tuple-element.172), channel_id=1, source_target_pairs={{0,8},{1,9},{2,18},{3,19},{4,12},{5,13},{6,22},{7,23},{8,0},{9,1},... | collective-permute-start | bytes 1671176 | tf_op jit(solution)/shard_map/ppermute | solution.py:668
  77.0 5.5 %first_back.1 = f32[1024,512]{1,0:T(8,128)} custom-call(s32[6]{0:T(128)S(1)} %stack.27.info_ref, bf16[1024,1536]{1,0:T(8,128)(2,1)S(1)} %get-tuple-element.127.dqkv_ref, bf16[512,1536]{1,0:T(8,128)(2,1)S(1)} %copy-done, bf16[1024,512]{1,0:T(8,128)(2,1)} %tok_ref.2, f32[1024,512]{1,0:T(8,128)} %get-tuple-element.128.gres_ref, f32[1,512]{1,0:T(1,128)} %bitcast.16), custom_call_target="tpu_custom_call" | custom-call | flops 1000 | bytes 1000 | tf_op jit(solution)/shard_map/first_back/pallas_call | solution.py:54
  82.5 0.2 collective-permute-done.8
  82.7 0.2 add_convert_fusion.4
  83.0 2.9 %collective-permute-start.10 = (bf16[128,1024]{1,0:T(8,128)(2,1)S(1)}, bf16[128,1024]{1,0:T(8,128)(2,1)S(1)}, u32[]{:S(2)}, u32[]{:S(2)}) collective-permute-start(bf16[128,1024]{1,0:T(8,128)(2,1)S(1)} %get-tuple-element.176), channel_id=1, source_target_pairs={{0,16},{1,17},{2,10},{3,11},{4,20},{5,21},{6,14},{7,15},{8,24},{9,... | collective-permute-start | bytes 786440 | tf_op jit(solution)/shard_map/ppermute | solution.py:668
  85.9 8.6 %collective-permute-done.9 = bf16[128,2176]{1,0:T(8,128)(2,1)S(1)} collective-permute-done((bf16[128,2176]{1,0:T(8,128)(2,1)S(1)}, bf16[128,2176]{1,0:T(8,128)(2,1)S(1)}, u32[]{:S(2)}, u32[]{:S(2)}) %collective-permute-start.9) | collective-permute-done | bytes 557088 | tf_op jit(solution)/shard_map/ppermute | solution.py:668
  94.5 0.1 add_convert_fusion.3
  94.7 1.7 %collective-permute-start.11 = (bf16[64,2176]{1,0:T(8,128)(2,1)S(1)}, bf16[64,2176]{1,0:T(8,128)(2,1)S(1)}, u32[]{:S(2)}, u32[]{:S(2)}) collective-permute-start(bf16[64,2176]{1,0:T(8,128)(2,1)S(1)} %get-tuple-element.175), channel_id=1, source_target_pairs={{0,4},{1,5},{2,3},{3,2},{4,0},{5,1},{6,7},{7,6},{8,12},{9,13},{10,... | collective-permute-start | bytes 835592 | tf_op jit(solution)/shard_map/ppermute | solution.py:668
  96.4 6.0 %collective-permute-done.11 = bf16[64,2176]{1,0:T(8,128)(2,1)S(1)} collective-permute-done((bf16[64,2176]{1,0:T(8,128)(2,1)S(1)}, bf16[64,2176]{1,0:T(8,128)(2,1)S(1)}, u32[]{:S(2)}, u32[]{:S(2)}) %collective-permute-start.11) | collective-permute-done | bytes 278560 | tf_op jit(solution)/shard_map/ppermute | solution.py:668
  102.5 2.2 %collective-permute-start.12 = (bf16[32,2176]{1,0:T(8,128)(2,1)S(1)}, bf16[32,2176]{1,0:T(8,128)(2,1)S(1)}, u32[]{:S(2)}, u32[]{:S(2)}) collective-permute-start(bf16[32,2176]{1,0:T(8,128)(2,1)S(1)} %get-tuple-element.178), channel_id=1, source_target_pairs={{0,1},{1,0},{2,6},{3,7},{4,5},{5,4},{6,2},{7,3},{8,9},{9,8},{10,14... | collective-permute-start | bytes 417800 | tf_op jit(solution)/shard_map/ppermute | solution.py:668
  104.7 3.0 %collective-permute-done.12 = bf16[32,2176]{1,0:T(8,128)(2,1)S(1)} collective-permute-done((bf16[32,2176]{1,0:T(8,128)(2,1)S(1)}, bf16[32,2176]{1,0:T(8,128)(2,1)S(1)}, u32[]{:S(2)}, u32[]{:S(2)}) %collective-permute-start.12) | collective-permute-done | bytes 139296 | tf_op jit(solution)/shard_map/ppermute | solution.py:668
  107.8 2.8 %collective-permute-start.14 = (bf16[32,2176]{1,0:T(8,128)(2,1)S(1)}, bf16[32,2176]{1,0:T(8,128)(2,1)S(1)}, u32[]{:S(2)}, u32[]{:S(2)}) collective-permute-start(bf16[32,2176]{1,0:T(8,128)(2,1)S(1)} %add_convert_fusion.11), channel_id=1, source_target_pairs={{0,16},{1,17},{2,10},{3,11},{4,20},{5,21},{6,14},{7,15},{8,24},{9,... | collective-permute-start | bytes 417800 | tf_op jit(solution)/shard_map/ppermute | solution.py:668
  110.6 0.5 collective-permute-done.13
  111.2 1.6 %collective-permute-start.15 = (bf16[128,1024]{1,0:T(8,128)(2,1)S(1)}, bf16[128,1024]{1,0:T(8,128)(2,1)S(1)}, u32[]{:S(2)}, u32[]{:S(2)}) collective-permute-start(bf16[128,1024]{1,0:T(8,128)(2,1)S(1)} %add_convert_fusion.8), channel_id=1, source_target_pairs={{0,4},{1,5},{2,6},{3,7},{4,0},{5,1},{6,2},{7,3},{8,12},{9,13},{10,... | collective-permute-start | bytes 786440 | tf_op jit(solution)/shard_map/ppermute | solution.py:668
  112.8 5.0 %collective-permute-done.14 = bf16[32,2176]{1,0:T(8,128)(2,1)S(1)} collective-permute-done((bf16[32,2176]{1,0:T(8,128)(2,1)S(1)}, bf16[32,2176]{1,0:T(8,128)(2,1)S(1)}, u32[]{:S(2)}, u32[]{:S(2)}) %collective-permute-start.14) | collective-permute-done | bytes 139296 | tf_op jit(solution)/shard_map/ppermute | solution.py:668
  117.8 0.2 collective-permute-start.16
  118.0 5.1 %collective-permute-start.18 = (bf16[256,1024]{1,0:T(8,128)(2,1)S(1)}, bf16[256,1024]{1,0:T(8,128)(2,1)S(1)}, u32[]{:S(2)}, u32[]{:S(2)}) collective-permute-start(bf16[256,1024]{1,0:T(8,128)(2,1)S(1)} %constant_dynamic-update-slice_fusion), channel_id=1, source_target_pairs={{0,16},{1,17},{2,10},{3,11},{4,20},{5,21},{6,14},{7,15},{8,24},{9,... | collective-permute-start | bytes 1572872 | tf_op jit(solution)/shard_map/ppermute | solution.py:668
  123.2 0.5 collective-permute-done.16
  123.7 1.2 collective-permute-start.17
  125.0 8.3 %collective-permute-done.17 = bf16[64,2176]{1,0:T(8,128)(2,1)S(1)} collective-permute-done((bf16[64,2176]{1,0:T(8,128)(2,1)S(1)}, bf16[64,2176]{1,0:T(8,128)(2,1)S(1)}, u32[]{:S(2)}, u32[]{:S(2)}) %collective-permute-start.17) | collective-permute-done | bytes 278560 | tf_op jit(solution)/shard_map/ppermute | solution.py:668
  133.3 3.4 %collective-permute-start.19 = (bf16[128,2176]{1,0:T(8,128)(2,1)S(1)}, bf16[128,2176]{1,0:T(8,128)(2,1)S(1)}, u32[]{:S(2)}, u32[]{:S(2)}) collective-permute-start(bf16[128,2176]{1,0:T(8,128)(2,1)S(1)} %constant_dynamic-update-slice_fusion.4), channel_id=1, source_target_pairs={{0,4},{1,5},{2,3},{3,2},{4,0},{5,1},{6,7},{7,6},{8,12},{9,13},{10,... | collective-permute-start | bytes 1671176 | tf_op jit(solution)/shard_map/ppermute | solution.py:668
  136.9 7.4 %collective-permute-done.19 = bf16[128,2176]{1,0:T(8,128)(2,1)S(1)} collective-permute-done((bf16[128,2176]{1,0:T(8,128)(2,1)S(1)}, bf16[128,2176]{1,0:T(8,128)(2,1)S(1)}, u32[]{:S(2)}, u32[]{:S(2)}) %collective-permute-start.19) | collective-permute-done | bytes 557088 | tf_op jit(solution)/shard_map/ppermute | solution.py:668
  144.4 0.5 collective-permute-start.20
  144.9 3.7 %collective-permute-done.20.other_ref = bf16[512,1024]{1,0:T(8,128)(2,1)S(1)} collective-permute-done((bf16[512,1024]{1,0:T(8,128)(2,1)S(1)}, bf16[512,1024]{1,0:T(8,128)(2,1)S(1)}, u32[]{:S(2)}, u32[]{:S(2)}) %collective-permute-start.20) | collective-permute-done | bytes 1048608 | tf_op jit(solution)/shard_map/ppermute | solution.py:668
  148.6 3.1 %ffn_end.1 = (f32[512,1024]{1,0:T(8,128)}, f32[1024,512]{1,0:T(8,128)}) custom-call(s32[6]{0:T(128)S(1)} %stack.27.info_ref, bf16[512,1024]{1,0:T(8,128)(2,1)S(1)} %constant_dynamic-update-slice_fusion.6.keep_ref, bf16[512,1024]{1,0:T(8,128)(2,1)S(1)} %collective-permute-done.20.other_ref), custom_call_target="tpu_custom_call" | custom-call | flops 1000 | bytes 1000 | tf_op jit(solution)/shard_map/ffn_end/pallas_call | solution.py:54
  151.7 5.1 %attend_end.1 = (f32[512,1536]{1,0:T(8,128)}, f32[512,512]{1,0:T(8,128)}, f32[512]{0:T(512)}, f32[512]{0:T(512)}, f32[512]{0:T(512)}, /*index=5*/f32[512]{0:T(512)}, f32[512]{0:T(512)}, f32[1024]{0:T(1024)}) custom-call(s32[6]{0:T(128)S(1)} %stack.27.info_ref, bf16[256,2176]{1,0:T(8,128)(2,1)S(1)} %constant_dynamic-update-slice_fusion.8.keep_ref, ...), custom_call_target="tpu_custom_call" | custom-call | flops 1000 | bytes 1000 | tf_op jit(solution)/shard_map/attend_end/pallas_call | solution.py:54
  (47 shorter events, 1.0 us)
Async XLA Ops:
  0.6 5.1 %copy-start = (bf16[512,1536]{1,0:T(8,128)(2,1)S(1)}, bf16[512,1536]{1,0:T(8,128)(2,1)}, u32[]{:S(2)}) copy-start(bf16[512,1536]{1,0:T(8,128)(2,1)} %w_ref.1) | copy-start | bytes 4718596
  0.7 5.1 %copy-start.3 = (bf16[512,512]{1,0:T(8,128)(2,1)S(1)}, bf16[512,512]{1,0:T(8,128)(2,1)}, u32[]{:S(2)}) copy-start(bf16[512,512]{1,0:T(8,128)(2,1)} %wout_ref.3) | copy-start | bytes 1572868
  2.6 12.2 %copy-start.1 = (bf16[512,1024]{1,0:T(8,128)(2,1)S(1)}, bf16[512,1024]{1,0:T(8,128)(2,1)}, u32[]{:S(2)}) copy-start(bf16[512,1024]{1,0:T(8,128)(2,1)} %up_ref.3) | copy-start | bytes 3145732
  2.6 12.2 %copy-start.2 = (bf16[1024,512]{1,0:T(8,128)(2,1)S(1)}, bf16[1024,512]{1,0:T(8,128)(2,1)}, u32[]{:S(2)}) copy-start(bf16[1024,512]{1,0:T(8,128)(2,1)} %down_ref.3) | copy-start | bytes 3145732
  2.6 26.5 %collective-permute-start = (bf16[528,512]{1,0:T(8,128)(2,1)S(1)}, bf16[528,512]{1,0:T(8,128)(2,1)S(1)}, u32[]{:S(2)}, u32[]{:S(2)}) collective-permute-start(bf16[528,512]{1,0:T(8,128)(2,1)S(1)} %get-tuple-element.101), channel_id=1, source_target_pairs={{0,1},{1,0},{2,3},{3,2},{4,5},{5,4},{6,7},{7,6},{8,9},{9,8},{10,11... | collective-permute-start | bytes 1622024 | tf_op jit(solution)/shard_map/ppermute | solution.py:668
  5.6 23.5 %collective-permute-start.1 = (bf16[512,512]{1,0:T(8,128)(2,1)S(1)}, bf16[512,512]{1,0:T(8,128)(2,1)S(1)}, u32[]{:S(2)}, u32[]{:S(2)}) collective-permute-start(bf16[512,512]{1,0:T(8,128)(2,1)S(1)} %get-tuple-element.102), channel_id=1, source_target_pairs={{0,1},{1,0},{2,3},{3,2},{4,5},{5,4},{6,7},{7,6},{8,9},{9,8},{10,11... | collective-permute-start | bytes 1572872 | tf_op jit(solution)/shard_map/ppermute | solution.py:668
  29.2 3.4 %collective-permute-start.2 = (bf16[528,512]{1,0:T(8,128)(2,1)S(1)}, bf16[528,512]{1,0:T(8,128)(2,1)S(1)}, u32[]{:S(2)}, u32[]{:S(2)}) collective-permute-start(bf16[528,512]{1,0:T(8,128)(2,1)S(1)} %collective-permute-done.refs_0_), channel_id=1, source_target_pairs={{0,2},{1,3},{2,0},{3,1},{4,6},{5,7},{6,4},{7,5},{8,10},{9,11},{10,... | collective-permute-start | bytes 1622024 | tf_op jit(solution)/shard_map/ppermute | solution.py:668
  29.2 3.4 %collective-permute-start.3 = (bf16[512,512]{1,0:T(8,128)(2,1)S(1)}, bf16[512,512]{1,0:T(8,128)(2,1)S(1)}, u32[]{:S(2)}, u32[]{:S(2)}) collective-permute-start(bf16[512,512]{1,0:T(8,128)(2,1)S(1)} %collective-permute-done.1.refs_2_), channel_id=1, source_target_pairs={{0,2},{1,3},{2,0},{3,1},{4,6},{5,7},{6,4},{7,5},{8,10},{9,11},{10,... | collective-permute-start | bytes 1572872 | tf_op jit(solution)/shard_map/ppermute | solution.py:668
  29.7 18.7 %collective-permute-start.5 = (bf16[512,1024]{1,0:T(8,128)(2,1)}, bf16[512,1024]{1,0:T(8,128)(2,1)}, u32[]{:S(2)}, u32[]{:S(2)}) collective-permute-start(bf16[512,1024]{1,0:T(8,128)(2,1)} %get-tuple-element.111), channel_id=1, source_target_pairs={{0,2},{1,3},{2,0},{3,1},{4,6},{5,7},{6,4},{7,5},{8,10},{9,11},{10,... | collective-permute-start | bytes 3145736 | tf_op jit(solution)/shard_map/ppermute | solution.py:668
  47.2 1.0 copy-start.4
  48.2 3.0 %collective-permute-start.4 = (bf16[512,1024]{1,0:T(8,128)(2,1)}, bf16[512,1024]{1,0:T(8,128)(2,1)}, u32[]{:S(2)}, u32[]{:S(2)}) collective-permute-start(bf16[512,1024]{1,0:T(8,128)(2,1)} %get-tuple-element.110), channel_id=1, source_target_pairs={{0,2},{1,3},{2,0},{3,1},{4,6},{5,7},{6,4},{7,5},{8,10},{9,11},{10,... | collective-permute-start | bytes 3145736 | tf_op jit(solution)/shard_map/ppermute | solution.py:668
  54.4 15.1 %collective-permute-start.7 = (bf16[512,1024]{1,0:T(8,128)(2,1)}, bf16[512,1024]{1,0:T(8,128)(2,1)}, u32[]{:S(2)}, u32[]{:S(2)}) collective-permute-start(bf16[512,1024]{1,0:T(8,128)(2,1)} %add_convert_fusion.2), channel_id=1, source_target_pairs={{0,1},{1,0},{2,6},{3,7},{4,5},{5,4},{6,2},{7,3},{8,9},{9,8},{10,14... | collective-permute-start | bytes 3145736 | tf_op jit(solution)/shard_map/ppermute | solution.py:668
  67.2 5.9 %collective-permute-start.6 = (bf16[256,2176]{1,0:T(8,128)(2,1)S(1)}, bf16[256,2176]{1,0:T(8,128)(2,1)S(1)}, u32[]{:S(2)}, u32[]{:S(2)}) collective-permute-start(bf16[256,2176]{1,0:T(8,128)(2,1)S(1)} %get-tuple-element.118), channel_id=1, source_target_pairs={{0,2},{1,3},{2,0},{3,1},{4,6},{5,7},{6,4},{7,5},{8,10},{9,11},{10,... | collective-permute-start | bytes 3342344 | tf_op jit(solution)/shard_map/ppermute | solution.py:668
  73.5 9.2 %collective-permute-start.8 = (bf16[256,1024]{1,0:T(8,128)(2,1)S(1)}, bf16[256,1024]{1,0:T(8,128)(2,1)S(1)}, u32[]{:S(2)}, u32[]{:S(2)}) collective-permute-start(bf16[256,1024]{1,0:T(8,128)(2,1)S(1)} %get-tuple-element.132), channel_id=1, source_target_pairs={{0,4},{1,5},{2,3},{3,2},{4,0},{5,1},{6,7},{7,6},{8,12},{9,13},{10,... | collective-permute-start | bytes 1572872 | tf_op jit(solution)/shard_map/ppermute | solution.py:668
  75.4 19.1 %collective-permute-start.9 = (bf16[128,2176]{1,0:T(8,128)(2,1)S(1)}, bf16[128,2176]{1,0:T(8,128)(2,1)S(1)}, u32[]{:S(2)}, u32[]{:S(2)}) collective-permute-start(bf16[128,2176]{1,0:T(8,128)(2,1)S(1)} %get-tuple-element.172), channel_id=1, source_target_pairs={{0,8},{1,9},{2,18},{3,19},{4,12},{5,13},{6,22},{7,23},{8,0},{9,1},... | collective-permute-start | bytes 1671176 | tf_op jit(solution)/shard_map/ppermute | solution.py:668
  83.0 13.4 %collective-permute-start.10 = (bf16[128,1024]{1,0:T(8,128)(2,1)S(1)}, bf16[128,1024]{1,0:T(8,128)(2,1)S(1)}, u32[]{:S(2)}, u32[]{:S(2)}) collective-permute-start(bf16[128,1024]{1,0:T(8,128)(2,1)S(1)} %get-tuple-element.176), channel_id=1, source_target_pairs={{0,16},{1,17},{2,10},{3,11},{4,20},{5,21},{6,14},{7,15},{8,24},{9,... | collective-permute-start | bytes 786440 | tf_op jit(solution)/shard_map/ppermute | solution.py:668
  94.7 7.7 %collective-permute-start.11 = (bf16[64,2176]{1,0:T(8,128)(2,1)S(1)}, bf16[64,2176]{1,0:T(8,128)(2,1)S(1)}, u32[]{:S(2)}, u32[]{:S(2)}) collective-permute-start(bf16[64,2176]{1,0:T(8,128)(2,1)S(1)} %get-tuple-element.175), channel_id=1, source_target_pairs={{0,4},{1,5},{2,3},{3,2},{4,0},{5,1},{6,7},{7,6},{8,12},{9,13},{10,... | collective-permute-start | bytes 835592 | tf_op jit(solution)/shard_map/ppermute | solution.py:668
  102.5 5.3 %collective-permute-start.12 = (bf16[32,2176]{1,0:T(8,128)(2,1)S(1)}, bf16[32,2176]{1,0:T(8,128)(2,1)S(1)}, u32[]{:S(2)}, u32[]{:S(2)}) collective-permute-start(bf16[32,2176]{1,0:T(8,128)(2,1)S(1)} %get-tuple-element.178), channel_id=1, source_target_pairs={{0,1},{1,0},{2,6},{3,7},{4,5},{5,4},{6,2},{7,3},{8,9},{9,8},{10,14... | collective-permute-start | bytes 417800 | tf_op jit(solution)/shard_map/ppermute | solution.py:668
  104.7 6.4 %collective-permute-start.13 = (bf16[128,1024]{1,0:T(8,128)(2,1)S(1)}, bf16[128,1024]{1,0:T(8,128)(2,1)S(1)}, u32[]{:S(2)}, u32[]{:S(2)}) collective-permute-start(bf16[128,1024]{1,0:T(8,128)(2,1)S(1)} %add_convert_fusion.9), channel_id=1, source_target_pairs={{0,8},{1,9},{2,18},{3,19},{4,12},{5,13},{6,22},{7,23},{8,0},{9,1},... | collective-permute-start | bytes 786440 | tf_op jit(solution)/shard_map/ppermute | solution.py:668
  107.8 9.9 %collective-permute-start.14 = (bf16[32,2176]{1,0:T(8,128)(2,1)S(1)}, bf16[32,2176]{1,0:T(8,128)(2,1)S(1)}, u32[]{:S(2)}, u32[]{:S(2)}) collective-permute-start(bf16[32,2176]{1,0:T(8,128)(2,1)S(1)} %add_convert_fusion.11), channel_id=1, source_target_pairs={{0,16},{1,17},{2,10},{3,11},{4,20},{5,21},{6,14},{7,15},{8,24},{9,... | collective-permute-start | bytes 417800 | tf_op jit(solution)/shard_map/ppermute | solution.py:668
  111.2 6.8 %collective-permute-start.15 = (bf16[128,1024]{1,0:T(8,128)(2,1)S(1)}, bf16[128,1024]{1,0:T(8,128)(2,1)S(1)}, u32[]{:S(2)}, u32[]{:S(2)}) collective-permute-start(bf16[128,1024]{1,0:T(8,128)(2,1)S(1)} %add_convert_fusion.8), channel_id=1, source_target_pairs={{0,4},{1,5},{2,6},{3,7},{4,0},{5,1},{6,2},{7,3},{8,12},{9,13},{10,... | collective-permute-start | bytes 786440 | tf_op jit(solution)/shard_map/ppermute | solution.py:668
  117.8 5.9 %collective-permute-start.16 = (bf16[32,2176]{1,0:T(8,128)(2,1)S(1)}, bf16[32,2176]{1,0:T(8,128)(2,1)S(1)}, u32[]{:S(2)}, u32[]{:S(2)}) collective-permute-start(bf16[32,2176]{1,0:T(8,128)(2,1)S(1)} %add_convert_fusion.10), channel_id=1, source_target_pairs={{0,8},{1,9},{2,18},{3,19},{4,12},{5,13},{6,22},{7,23},{8,0},{9,1},... | collective-permute-start | bytes 417800 | tf_op jit(solution)/shard_map/ppermute | solution.py:668
  118.0 18.8 %collective-permute-start.18 = (bf16[256,1024]{1,0:T(8,128)(2,1)S(1)}, bf16[256,1024]{1,0:T(8,128)(2,1)S(1)}, u32[]{:S(2)}, u32[]{:S(2)}) collective-permute-start(bf16[256,1024]{1,0:T(8,128)(2,1)S(1)} %constant_dynamic-update-slice_fusion), channel_id=1, source_target_pairs={{0,16},{1,17},{2,10},{3,11},{4,20},{5,21},{6,14},{7,15},{8,24},{9,... | collective-permute-start | bytes 1572872 | tf_op jit(solution)/shard_map/ppermute | solution.py:668
  123.7 9.6 %collective-permute-start.17 = (bf16[64,2176]{1,0:T(8,128)(2,1)S(1)}, bf16[64,2176]{1,0:T(8,128)(2,1)S(1)}, u32[]{:S(2)}, u32[]{:S(2)}) collective-permute-start(bf16[64,2176]{1,0:T(8,128)(2,1)S(1)} %constant_dynamic-update-slice_fusion.2), channel_id=1, source_target_pairs={{0,1},{1,0},{2,6},{3,7},{4,5},{5,4},{6,2},{7,3},{8,9},{9,8},{10,14... | collective-permute-start | bytes 835592 | tf_op jit(solution)/shard_map/ppermute | solution.py:668
  133.3 11.0 %collective-permute-start.19 = (bf16[128,2176]{1,0:T(8,128)(2,1)S(1)}, bf16[128,2176]{1,0:T(8,128)(2,1)S(1)}, u32[]{:S(2)}, u32[]{:S(2)}) collective-permute-start(bf16[128,2176]{1,0:T(8,128)(2,1)S(1)} %constant_dynamic-update-slice_fusion.4), channel_id=1, source_target_pairs={{0,4},{1,5},{2,3},{3,2},{4,0},{5,1},{6,7},{7,6},{8,12},{9,13},{10,... | collective-permute-start | bytes 1671176 | tf_op jit(solution)/shard_map/ppermute | solution.py:668
  144.3 7.4 %collective-permute-start.21 = (bf16[256,2176]{1,0:T(8,128)(2,1)S(1)}, bf16[256,2176]{1,0:T(8,128)(2,1)S(1)}, u32[]{:S(2)}, u32[]{:S(2)}) collective-permute-start(bf16[256,2176]{1,0:T(8,128)(2,1)S(1)} %constant_dynamic-update-slice_fusion.8.keep_ref), channel_id=1, source_target_pairs={{0,2},{1,3},{2,0},{3,1},{4,6},{5,7},{6,4},{7,5},{8,10},{9,11},{10,... | collective-permute-start | bytes 3342344 | tf_op jit(solution)/shard_map/ppermute | solution.py:668
  144.4 4.2 %collective-permute-start.20 = (bf16[512,1024]{1,0:T(8,128)(2,1)S(1)}, bf16[512,1024]{1,0:T(8,128)(2,1)S(1)}, u32[]{:S(2)}, u32[]{:S(2)}) collective-permute-start(bf16[512,1024]{1,0:T(8,128)(2,1)S(1)} %constant_dynamic-update-slice_fusion.6.keep_ref), channel_id=1, source_target_pairs={{0,2},{1,3},{2,0},{3,1},{4,6},{5,7},{6,4},{7,5},{8,10},{9,11},{10,... | collective-permute-start | bytes 3145736 | tf_op jit(solution)/shard_map/ppermute | solution.py:668

commit v8 on v7

--- a/solution.py
+++ b/solution.py
@@ -20,6 +20,7 @@
 TILE = 16
 TOKS = 512
 VMEM_LIMIT = 30 * 1024 * 1024
+REST_LIMIT = 36 * 1024 * 1024
 
 
 def mm(a, b):
@@ -50,14 +51,14 @@
     return pl.BlockSpec((toks, width), lambda i, *_: (i, 0))
 
 
-def call(kernel, name, grid, in_specs, out_specs, out_shape, scratch, info, args):
+def call(kernel, name, grid, in_specs, out_specs, out_shape, scratch, info, args, vmem=VMEM_LIMIT):
     return pl.pallas_call(
         kernel,
         grid_spec=pltpu.PrefetchScalarGridSpec(
             num_scalar_prefetch=1, grid=grid, in_specs=in_specs, out_specs=out_specs, scratch_shapes=scratch
         ),
         out_shape=out_shape,
-        compiler_params=pltpu.CompilerParams(vmem_limit_bytes=VMEM_LIMIT),
+        compiler_params=pltpu.CompilerParams(vmem_limit_bytes=vmem),
         cost_estimate=pl.CostEstimate(flops=1000, bytes_accessed=1000, transcendentals=0),
         name=name,
     )(info, *args)
@@ -108,6 +109,16 @@
     if first == second:
         return own ^ first
     return own ^ jnp.where(core == 0, first, second)
+
+
+def place_of(block, tables, core, own):
+    wanted = own ^ block
+    places_by_core = [[table.index(owner) for owner in range(len(table))] for table in tables]
+    place = jnp.int32(0)
+    for owner in range(len(tables[0])):
+        first, second = places_by_core[0][owner], places_by_core[1][owner]
+        place = jnp.where(wanted == owner, jnp.where(core == 0, first, second), place)
+    return place
 
 
 def permuted(dst_ref, acc_ref, chunk, tables, core, own, turned=0):
@@ -243,7 +254,7 @@
         acc_ref[i, :, :units] += grad_up[:, cols]
         acc_ref[i, :, units:] += grad_down[:, cols]
         bacc_ref[i : i + 1, :] += sums[:, cols]
-    return mm(hid, down), mm_nt(dpre, up)
+    return hid, dpre
 
 
 def ffn_own_kernel(
@@ -258,9 +269,9 @@
         bias_out[...] = jnp.zeros_like(bias_out)
 
     bias = bias_ref[...].astype(F32).reshape(1, up_ref.shape[1])
-    out_ref[...], dsec_ref[...] = ffn_block(
-        sec_ref[...], dy_ref[...], up_ref[...], bias, down_ref[...], acc_ref, bias_out
-    )
+    hid, dpre = ffn_block(sec_ref[...], dy_ref[...], up_ref[...], bias, down_ref[...], acc_ref, bias_out)
+    out_ref[...] = mm(hid, down_ref[...])
+    dsec_ref[...] = mm_nt(dpre, up_ref[...])
 
     @pl.when(at == last)
     def _():
@@ -279,7 +290,7 @@
         [rows_of(width), rows_of(width), whole(*up.shape), whole(*bias.shape), whole(*down.shape)],
         [rows_of(width)] * 2 + [whole(width, 2 * units)] * 2 + [whole(2, units)],
         [pltpu.VMEM((n, width), F32)] * 2
-        + [jax.ShapeDtypeStruct((width, 2 * units), BF)] * 2
+        + [pltpu.HBM((width, 2 * units), BF)] * 2
         + [jax.ShapeDtypeStruct((2, units), F32)],
         [pltpu.VMEM((2, width, 2 * units), F32)],
         info,
@@ -288,98 +299,145 @@
 
 
 def ffn_rest_kernel(
-    tables, count, mixing, info_ref, sec_ref, dy_ref, out_part_ref, dsec_part_ref, res_ref, mixed_ref, bdown_ref, g2_ref,
-    wout_ref, mine_ref, *refs
+    tables, count, mixing, info_ref, sec_in, dy_in, out_in, dsec_in, res_in, mixed_in, mine_ref, bdown_ref, g2_ref, wout_ref, *refs
 ):
     ups, downs = refs[:count], refs[count : 2 * count]
-    block_ref, gres_ref, gmix_ref, vec_ref, dwout_ref, bias_out = refs[2 * count : 2 * count + 6]
-    *grads, acc_ref, up_ref, bias_ref, down_ref = refs[2 * count + 6 :]
-    at, last = pl.program_id(0), pl.num_programs(0) - 1
-    width, units = wout_ref.shape[0], ups[0].shape[1]
-
-    @pl.when(at == 0)
-    def _():
-        for ref in (acc_ref, bias_out, vec_ref, dwout_ref):
-            ref[...] = jnp.zeros_like(ref)
-        for i in range(count):
-            cols = slice(i * units, (i + 1) * units)
-            up_ref[:, cols] = ups[i][:width, :]
-            bias_ref[:, cols] = ups[i][width : width + TILE, :].astype(F32)[:8]
-            down_ref[cols, :] = downs[i][...]
-
-    dy = dy_ref[...]
-    out, dsec = ffn_block(sec_ref[...], dy, up_ref[...], bias_ref[0:1, :], down_ref[...], acc_ref, bias_out)
-    out += out_part_ref[...]
-    dsec += dsec_part_ref[...]
-    residual = res_ref[...]
-    block_ref[...] = (residual + (out + bdown_ref[...])).astype(BF)
-    dy32 = dy.astype(F32)
-    unit, inv = unit_parts(residual)
-    vec_ref[0:1, :] += jnp.sum(dsec * unit, axis=0, keepdims=True)
-    vec_ref[1:2, :] += jnp.sum(dsec, axis=0, keepdims=True)
-    vec_ref[2:3, :] += jnp.sum(dy32, axis=0, keepdims=True)
-    gres = dy32 + norm_back(dsec, unit, inv, g2_ref[...])
-    gres_ref[...] = gres
-    branch = gres.astype(BF)
-    gmix_ref[...] = mm_nt(branch, wout_ref[...]).astype(BF)
-    dwout_ref[...] += mm_tn(mixed_ref[...], branch)
-
-    @pl.when(at == last)
-    def _():
-        core = info_ref[0]
-        blocks = len(tables[0])
-        size = width // blocks
-
-        def rows_at(i, place):
-            block = block_at(place, tables, core ^ (i % 2), info_ref[1 + i % 2])
-            rows = pl.ds(pl.multiple_of(block * size, size), size)
-            return acc_ref[i, rows, :].astype(BF)
-
-        def put(ref, row, part):
-            ref[row : row + size, :] = part
-
-        for i in range(1 if mixing else 0, count):
-            for place in range(blocks):
-                put(grads[i + 1 if mixing else i], place * size, rows_at(i, place))
-        if not mixing:
-            return
-        keep_ref, send_ref = grads[:2]
-        half = width // 2
-        for place in range(blocks // 2, blocks):
-            put(send_ref, place * size, rows_at(0, place))
-
-        @pl.when(core == 0)
-        def _():
-            for place in range(blocks // 2):
-                put(send_ref, place * size, rows_at(0, place))
-            keep_ref[...] = mine_ref[...]
-
-        @pl.when(core == 1)
-        def _():
-            for place in range(blocks // 2):
-                put(keep_ref, place * size, rows_at(0, place))
-            keep_ref[half:, :] = mine_ref[:half, :]
-            send_ref[:half, :] = mine_ref[half:, :]
-
-
-def ffn_rest(
-    info, tables, mixing, second, dy, out_part, dsec_part, residual, mixed, bdown, g2, wout, mine, chunks
-):
+    block_out, gres_out, gmix_out, vec_ref, dwout_ref, bias_out = refs[2 * count : 2 * count + 6]
+    grads, refs = refs[2 * count + 6 : 3 * count + 6 + mixing], refs[3 * count + 6 + mixing :]
+    sec_ref, dy_ref, out_ref, dsec_ref, res_ref, mixed_ref, branch_ref, up_ref, bias_ref, down_ref, laid_ref, sems = refs
+    n, width = sec_ref.shape
+    units = down_ref.shape[0] // count
+    core = info_ref[0]
+    half = width // 2
+    top, low = pl.ds(0, half), pl.ds(half, half)
+    used = iter(range(sems.shape[0]))
+
+    def move(*pairs):
+        copies = [pltpu.make_async_copy(*pair, sems.at[next(used)]) for pair in pairs]
+        for copy in copies:
+            copy.start()
+        return copies
+
+    def arrived(copies):
+        for copy in copies:
+            copy.wait()
+
+    def by_core(first, *sets):
+        def each(act):
+            for odd, pairs in enumerate(sets):
+
+                @pl.when(core == odd)
+                def _(pairs=pairs):
+                    for i, pair in enumerate(pairs):
+                        act(pltpu.make_async_copy(*pair, sems.at[first + i]))
+
+        return lambda: each(lambda copy: copy.start()), lambda: each(lambda copy: copy.wait())
+
+    cols = [pl.ds(i * units, units) for i in range(count)]
+    first = move(
+        (sec_in, sec_ref),
+        *[(ups[i].at[pl.ds(0, width), :], up_ref.at[:, cols[i]]) for i in range(count)],
+        *[(ups[i].at[pl.ds(width, TILE), :], bias_ref.at[:, cols[i]]) for i in range(count)],
+    )
+    second = move((dy_in, dy_ref), *[(downs[i], down_ref.at[cols[i], :]) for i in range(count)])
+    third = move((out_in, out_ref), (dsec_in, dsec_ref), (res_in, res_ref), (mixed_in, mixed_ref))
+    if mixing:
+        keep_ref, send_ref, away_ref = grads
+        own_start, own_wait = by_core(
+            next(used),
+            [(mine_ref, keep_ref)],
+            [(mine_ref.at[top], keep_ref.at[low]), (mine_ref.at[low], send_ref.at[top])],
+        )
+        next(used)
+        chunk_start, chunk_wait = by_core(
+            next(used),
+            [(laid_ref.at[0], send_ref)],
+            [(laid_ref.at[0, top], keep_ref.at[top]), (laid_ref.at[0, low], send_ref.at[low])],
+        )
+        next(used)
+        own_start()
+
+    arrived(first)
+    toks = n if count <= 2 else n // 2
+    grad_up = grad_down = sums = None
+    parts = []
+    for t in range(n // toks):
+        rows = slice(t * toks, (t + 1) * toks)
+        sec = sec_ref[rows, :]
+        pre = mm(sec, up_ref[...]) + bias_ref[...].astype(F32)[:1]
+        if t == 0:
+            arrived(second)
+        dy = dy_ref[rows, :]
+        dhid = mm_nt(dy, down_ref[...])
+        hid, slope = gelu_pair(pre)
+        hid = hid.astype(BF)
+        dpre = (dhid * slope).astype(BF)
+        more = (mm(sec.T, dpre), mm(dy.T, hid), jnp.sum(dpre.astype(F32), axis=0, keepdims=True))
+        if t:
+            more = (grad_up + more[0], grad_down + more[1], sums + more[2])
+        grad_up, grad_down, sums = more
+        parts.append((hid, dpre))
+    blocks = len(tables[0])
+    size = width // blocks
+    for i in range(count):
+        at = slice(i * units, (i + 1) * units)
+        bias_out[i : i + 1, :] = sums[:, at]
+        for block in range(blocks):
+            owner = core ^ (i % 2)
+            place = place_of(block, tables, owner, info_ref[1 + i % 2])
+            to = pl.ds(pl.multiple_of(place * size, size), size)
+            rows = slice(block * size, (block + 1) * size)
+            laid_ref[i, to, :units] = grad_up[rows, at].astype(BF)
+            laid_ref[i, to, units:] = grad_down[rows, at].astype(BF)
+    if mixing:
+        chunk_start()
+        gone = move((laid_ref.at[1], away_ref))
+    else:
+        gone = move(*[(laid_ref.at[i], grads[i]) for i in range(count)])
+
+    arrived(third)
+    step = min(TOKS // 2, toks)
+    for t, (hid, dpre) in enumerate(parts):
+        out_all, dsec_all = mm(hid, down_ref[...]), mm_nt(dpre, up_ref[...])
+        for r in range(0, toks, step):
+            rows = slice(t * toks + r, t * toks + r + step)
+            span = pl.ds(rows.start, step)
+            dy32 = dy_ref[rows, :].astype(F32)
+            residual = res_ref[rows, :]
+            dsec = dsec_all[r : r + step] + dsec_ref[rows, :]
+            dy_ref[rows, :] = (residual + (out_all[r : r + step] + out_ref[rows, :] + bdown_ref[...])).astype(BF)
+            unit, inv = unit_parts(residual)
+            sums = [jnp.sum(v, axis=0, keepdims=True) for v in (dsec * unit, dsec, dy32)]
+            for i, row in enumerate(sums):
+                if rows.start:
+                    vec_ref[i : i + 1, :] += row
+                else:
+                    vec_ref[i : i + 1, :] = row
+            gres = dy32 + norm_back(dsec, unit, inv, g2_ref[...])
+            out_ref[rows, :] = gres
+            branch_ref[rows, :] = gres.astype(BF)
+            gone += move((dy_ref.at[span, :], block_out.at[span, :]), (out_ref.at[span, :], gres_out.at[span, :]))
+    vec_ref[3:, :] = jnp.zeros((vec_ref.shape[0] - 3, width), F32)
+    sec_ref[...] = mm_nt(branch_ref[...], wout_ref[...]).astype(BF)
+    gone += move((sec_ref, gmix_out))
+    dwout_ref[...] = mm_tn(mixed_ref[...], branch_ref[...])
+    arrived(gone)
+    if mixing:
+        own_wait()
+        chunk_wait()
+
+
+def ffn_rest(info, tables, mixing, second, dy, out_part, dsec_part, residual, mixed, bdown, g2, wout, mine, chunks):
     n, width = second.shape
     count = len(chunks)
     units = chunks[0][0].shape[1]
+    anywhere = pl.BlockSpec(memory_space=pl.ANY)
     return call(
         functools.partial(ffn_rest_kernel, tables, count, mixing),
         "ffn_rest",
-        (n // TOKS,),
-        [rows_of(width)] * 6
-        + [whole(1, width)] * 2
-        + [whole(width, width), whole(*mine.shape)]
-        + [whole(width + TILE, units)] * count
-        + [whole(units, width)] * count,
-        [rows_of(width)] * 3
-        + [whole(8, width), whole(width, width), whole(count, units)]
-        + [whole(width, 2 * units)] * (count + mixing),
+        (1,),
+        [anywhere] * 7 + [whole(1, width)] * 2 + [whole(width, width)] + [anywhere] * (2 * count),
+        [anywhere] * 3 + [whole(8, width), whole(width, width), whole(count, units)] + [anywhere] * (count + mixing),
         [
             jax.ShapeDtypeStruct((n, width), BF),
             pltpu.HBM((n, width), F32),
@@ -390,20 +448,84 @@
         ]
         + [jax.ShapeDtypeStruct((width, 2 * units), BF)] * (count + mixing),
         [
-            pltpu.VMEM((count, width, 2 * units), F32),
+            pltpu.VMEM((n, width), BF),
+            pltpu.VMEM((n, width), BF),
+            pltpu.VMEM((n, width), F32),
+            pltpu.VMEM((n, width), F32),
+            pltpu.VMEM((n, width), F32),
+            pltpu.VMEM((n, width), BF),
+            pltpu.VMEM((n, width), BF),
             pltpu.VMEM((width, count * units), BF),
-            pltpu.VMEM((8, count * units), F32),
+            pltpu.VMEM((TILE, count * units), BF),
             pltpu.VMEM((count * units, width), BF),
+            pltpu.VMEM((count, width, 2 * units), BF),
+            pltpu.SemaphoreType.DMA((24 + 4 * count,)),
         ],
         info,
         near(second)
         + far(dy)
         + near(out_part, dsec_part)
-        + far(residual, mixed, bdown, g2)
-        + (wout, mine)
+        + far(residual, mixed, mine, bdown, g2)
+        + (wout,)
         + tuple(c[0] for c in chunks)
         + tuple(c[1] for c in chunks),
-    )
+        REST_LIMIT if count <= 2 else 56 * 1024 * 1024,
+    )
+
+
+def join_kernel(info_ref, send_ref, got_ref, own_ref, out_ref):
+    half = send_ref.shape[0] // 2
+    out_ref[half:, :] = (send_ref[half:, :].astype(F32) + got_ref[half:, :].astype(F32)).astype(BF)
+
+    @pl.when(info_ref[0] == 0)
+    def _():
+        out_ref[:half, :] = (send_ref[:half, :].astype(F32) + got_ref[:half, :].astype(F32)).astype(BF)
+
+    @pl.when(info_ref[0] == 1)
+    def _():
+        out_ref[:half, :] = (send_ref[:half, :].astype(F32) + own_ref[:half, :].astype(F32)).astype(BF)
+
+
+def split_kernel(info_ref, keep_ref, got_ref, own_ref, arrived_ref, keep_out, send_out):
+    half = keep_ref.shape[0] // 2
+    top, low = slice(0, half), slice(half, 2 * half)
+
+    def total(*parts):
+        value = parts[0].astype(F32)
+        for part in parts[1:]:
+            value += part.astype(F32)
+        return value.astype(BF)
+
+    @pl.when(info_ref[0] == 0)
+    def _():
+        keep_out[...] = total(keep_ref[top, :], own_ref[top, :], arrived_ref[top, :])
+        send_out[...] = total(keep_ref[low, :], own_ref[low, :], arrived_ref[low, :])
+
+    @pl.when(info_ref[0] == 1)
+    def _():
+        keep_out[...] = total(keep_ref[low, :], own_ref[low, :], arrived_ref[top, :])
+        send_out[...] = total(keep_ref[top, :], got_ref[top, :], arrived_ref[low, :])
+
+
+def direct(kernel, name, info, out_shape, args):
+    return pl.pallas_call(
+        kernel,
+        in_specs=[pl.BlockSpec(memory_space=pltpu.SMEM)] + [pl.BlockSpec(memory_space=pltpu.VMEM)] * len(args),
+        out_specs=jax.tree.map(lambda _: pl.BlockSpec(memory_space=pltpu.VMEM), out_shape),
+        out_shape=out_shape,
+        compiler_params=pltpu.CompilerParams(vmem_limit_bytes=VMEM_LIMIT),
+        cost_estimate=pl.CostEstimate(flops=1000, bytes_accessed=1000, transcendentals=0),
+        name=name,
+    )(info, *args)
+
+
+def join(info, send, got, own):
+    return direct(join_kernel, "join", info, jax.ShapeDtypeStruct(send.shape, BF), (send, got, own))
+
+
+def split(info, keep, got, own, arrived):
+    shape = jax.ShapeDtypeStruct((keep.shape[0] // 2, keep.shape[1]), BF)
+    return direct(split_kernel, "split", info, [shape, shape], (keep, got, own, arrived))
 
 
 def attend_back_kernel(
@@ -712,9 +834,9 @@
     mixing = narrow == 2 and len(wide_masks) == 3
     if mixing:
         y, low, high = wide_masks
-        ff_in, ff_rest, ff_out = ([y, high], [y, low]), ([low], [high]), ([high, y], [low, y])
-        at_in, at_rest, at_out = ([low, y, 1], [high, 1, y]), ([high], [low]), ([y, 1, low], [1, y, high])
-        turns = "FAFAAFAFAAFAFA"
+        ff_in, ff_rest, ff_out = ([y, low], [y, low]), ([high], [high]), ([y, low], [y, low])
+        at_in, at_rest, at_out = ([y, 1, low], [low, y, 1]), ([high], [high]), ([y, 1, low], [low, 1, y])
+        turns = "FAFAAFAFAAFFAA"
     else:
         ff_in, ff_rest = split_at((wide_masks, wide_masks), min(len(wide_masks) - 1, (width // TILE).bit_length() - 1))
         masks = narrow_masks + wide_masks
@@ -773,23 +895,21 @@
     if mixing:
         ff_keep, ff_send, away = grads
         got_own, got = swap(own_send, core_mask), swap(away, core_mask)
-        chunk = (core == 0) | (lax.broadcasted_iota(jnp.int32, got.shape, 0) >= width // 2)
-        ff_send = add(ff_send, jnp.where(chunk, got, got_own))
+        ff_send = join(info, ff_send, got, got_own)
         gmix, ff_send = after(gmix, ff_send)
-        ff_got, ff_keep, got_own, got = after(swap(ff_send, 1, y), ff_keep, got_own, got)
-        top = width // 2
-        ff_keep = add(ff_keep, jnp.where(chunk, got_own, got))
-        ff_send = add(jnp.where(core == 0, ff_keep[top:], ff_keep[:top]), ff_got[top:])
-        ff_keep = add(jnp.where(core == 0, ff_keep[:top], ff_keep[top:]), ff_got[:top])
+        ff_got = swap(ff_send, 1, y)
     else:
         held = [add(own_keep, swap(own_send, core_mask))] + [add(grads[2 * j], swap(grads[2 * j + 1], core_mask)) for j in range(narrow - 1)]
         gmix, held = after(gmix, held)
         for mask in reversed(narrow_masks):
             held = [add(held[j], swap(held[j + mask], mask)) for j in range(mask)]
-        ff_keep = ff_send = held[0]
+        ff_keep = held[0]
 
     dqkv, keep, send = attend_back(info, at_tables(at_in), qkv, prob, gmix, tokens_in, vec, dwout)
-    keep, ff_keep, ff_send = after(add(keep, swap(send, core_mask)), ff_keep, ff_send)
+    if mixing:
+        send, ff_got = after(send, ff_got)
+        ff_keep, ff_send = split(info, ff_keep, got, got_own, ff_got)
+    keep = add(keep, swap(send, core_mask))
     grad_tokens = first_back(info, dqkv, w_qkv, tokens_in, gres, g1)
     steps = {
         "A": steps_of(at_in, at_rest, at_out) + [("core", core_mask)],

time: 157 us -> 140 us (0.89)
  waiting for transfers between devices: 54.8 us -> 38.2 us
  other arithmetic: 8.43 us -> 1.48 us
  Pallas kernels: 60.1 us -> 63.6 us
  starting transfers between devices: 30.8 us -> 33.7 us
    ppermute x22, waiting for transfers between devices: 54.8 us -> 38.2 us  [swap(): return lax.ppermute(value, AXES, pairs)]
    convert_element_type x11 -> x8, other arithmetic: 7.78 us -> 0.85 us  [add(): return (a.astype(F32) + b.astype(F32)).astype(a.dtype)]
    pallas_call x0 -> x2, Pallas kernels: none -> 3.6 us  [direct(): pl.pallas_call(kernel, in_specs=[pl.BlockSpec(memory_space=pltpu.SMEM)] +...]
    ppermute x22, starting transfers between devices: 30.8 us -> 33.7 us  [swap(): return lax.ppermute(value, AXES, pairs)]
  transfers between devices with their start and end apart: 22 -> 22, of which waited for: 14 -> 15; matrix products, arithmetic and copies ran while one was open for 3% -> 1% of each run, Pallas kernels for 34% -> 40%
where the time goes in v8:
time: 140 us; the launch traced here: 139 us
  Pallas kernels  63.6 us (45%)
  waiting for transfers between devices  38.2 us (27%)
  starting transfers between devices  33.7 us (24%)
  other arithmetic  1.48 us (1%)
    pallas_call x8, Pallas kernels, call(): pl.pallas_call(kernel, grid_spec=pltpu.PrefetchScalarGridSpec(num_scalar_...  60 us
    ppermute x22, waiting for transfers between devices, swap(): return lax.ppermute(value, AXES, pairs)  38.2 us
    ppermute x22, starting transfers between devices, swap(): return lax.ppermute(value, AXES, pairs)  33.7 us
    pallas_call x2, Pallas kernels, direct(): pl.pallas_call(kernel, in_specs=[pl.BlockSpec(memory_space=pltpu.SMEM)] +...  3.6 us
  transfers between devices with their start and end apart: 22, of which 15 were waited for; matrix products, arithmetic and copies ran while one was open for 1% of the time, Pallas kernels for 40%

profile of v8, /device:TPU:0, one launch (start us, length us, event | category | flops | bytes accessed | tf_op | source)
XLA Modules:
  0.0 138.8 jit_solution(5090631233400639148)
XLA Ops:
  0.7 0.1 stack.21.info_ref
  0.8 1.8 %pack.1 = (bf16[528,512]{1,0:T(8,128)(2,1)S(1)}, bf16[512,512]{1,0:T(8,128)(2,1)S(1)}) custom-call(s32[6]{0:T(128)S(1)} %stack.21.info_ref, bf16[512,1024]{1,0:T(8,128)(2,1)} %up_ref.3, bf16[1024]{0:T(1024)(128)(2,1)} %bias_ref.3, bf16[1024,512]{1,0:T(8,128)(2,1)} %down_ref.3), custom_call_target="tpu_custom_call" | custom-call | flops 1000 | bytes 1000 | tf_op jit(solution)/shard_map/pack/pallas_call | solution.py:55
  2.6 3.0 %collective-permute-start = (bf16[528,512]{1,0:T(8,128)(2,1)S(1)}, bf16[528,512]{1,0:T(8,128)(2,1)S(1)}, u32[]{:S(2)}, u32[]{:S(2)}) collective-permute-start(bf16[528,512]{1,0:T(8,128)(2,1)S(1)} %get-tuple-element.96), channel_id=1, source_target_pairs={{0,1},{1,0},{2,3},{3,2},{4,5},{5,4},{6,7},{7,6},{8,9},{9,8},{10,11... | collective-permute-start | bytes 1622024 | tf_op jit(solution)/shard_map/ppermute | solution.py:790
  5.7 9.2 %attend.1 = (bf16[1024,1536]{1,0:T(8,128)(2,1)}, bf16[8,4,128,256]{3,2,1,0:T(8,128)(2,1)}, bf16[1024,512]{1,0:T(8,128)(2,1)}, f32[1024,512]{1,0:T(8,128)}, bf16[1024,512]{1,0:T(8,128)(2,1)S(1)}) custom-call(s32[6]{0:T(128)S(1)} %stack.21.info_ref, bf16[1024,512]{1,0:T(8,128)(2,1)} %tok_ref.2, f32[1,512]{1,0:T(1,128)} %bitcast.13, f32[1,512]{1,0:T(1,128)} %bitcast.18, ...), custom_call_target="tpu_custom_call" | custom-call | flops 1000 | bytes 1000 | tf_op jit(solution)/shard_map/attend/pallas_call | solution.py:55
  14.9 11.2 %ffn_own.1 = (f32[1024,512]{1,0:T(8,128)S(1)}, f32[1024,512]{1,0:T(8,128)S(1)}, bf16[512,1024]{1,0:T(8,128)(2,1)}, bf16[512,1024]{1,0:T(8,128)(2,1)}, f32[2,512]{1,0:T(2,128)S(1)}) custom-call(s32[6]{0:T(128)S(1)} %stack.21.info_ref, bf16[1024,512]{1,0:T(8,128)(2,1)S(1)} %get-tuple-element.89.sec_ref.sec_in, bf16[1024,512]{1,0:T(8,128)(2,1)} %dy_in.1, ...), custom_call_target="tpu_custom_call" | custom-call | flops 1000 | bytes 1000 | tf_op jit(solution)/shard_map/ffn_own/pallas_call | solution.py:55
  26.1 3.0 %collective-permute-done.1.refs_2_ = bf16[512,512]{1,0:T(8,128)(2,1)S(1)} collective-permute-done((bf16[512,512]{1,0:T(8,128)(2,1)S(1)}, bf16[512,512]{1,0:T(8,128)(2,1)S(1)}, u32[]{:S(2)}, u32[]{:S(2)}) %collective-permute-start.1) | collective-permute-done | bytes 524320 | tf_op jit(solution)/shard_map/ppermute | solution.py:790
  29.1 0.5 collective-permute-start.3
  29.6 2.9 %collective-permute-done.3.refs_3_ = bf16[512,512]{1,0:T(8,128)(2,1)S(1)} collective-permute-done((bf16[512,512]{1,0:T(8,128)(2,1)S(1)}, bf16[512,512]{1,0:T(8,128)(2,1)S(1)}, u32[]{:S(2)}, u32[]{:S(2)}) %collective-permute-start.3) | collective-permute-done | bytes 524320 | tf_op jit(solution)/shard_map/ppermute | solution.py:790
  32.6 13.7 %ffn_rest.1 = (bf16[1024,512]{1,0:T(8,128)(2,1)}, f32[1024,512]{1,0:T(8,128)}, bf16[1024,512]{1,0:T(8,128)(2,1)}, f32[8,512]{1,0:T(8,128)S(1)}, f32[512,512]{1,0...) custom-call(s32[6]{0:T(128)S(1)} %stack.21.info_ref, ...), custom_call_target="tpu_custom_call" | custom-call | flops 1000 | bytes 1000 | tf_op jit(solution)/shard_map/ffn_rest/pallas_call | solution.py:55
  46.3 0.2 collective-permute-start.4
  46.5 2.5 %collective-permute-done.4.got_ref = bf16[512,1024]{1,0:T(8,128)(2,1)S(1)} collective-permute-done((bf16[512,1024]{1,0:T(8,128)(2,1)S(1)}, bf16[512,1024]{1,0:T(8,128)(2,1)S(1)}, u32[]{:S(2)}, u32[]{:S(2)}) %collective-permute-start.4) | collective-permute-done | bytes 1048608 | tf_op jit(solution)/shard_map/ppermute | solution.py:790
  49.0 1.8 %join.1 = bf16[512,1024]{1,0:T(8,128)(2,1)} custom-call(s32[6]{0:T(128)S(1)} %stack.21.info_ref, bf16[512,1024]{1,0:T(8,128)(2,1)S(1)} %get-tuple-element.107.send_ref, bf16[512,1024]{1,0:T(8,128)(2,1)S(1)} %collective-permute-done.4.got_ref, bf16[512,1024]{1,0:T(8,128)(2,1)S(1)} %collective-permute-done.5.own_ref), custom_call_target="tpu_custom_call" | custom-call | flops 1000 | bytes 1000 | tf_op jit(solution)/shard_map/join/pallas_call | solution.py:511
  50.8 1.7 %collective-permute-start.6 = (bf16[512,1024]{1,0:T(8,128)(2,1)}, bf16[512,1024]{1,0:T(8,128)(2,1)}, u32[]{:S(2)}, u32[]{:S(2)}) collective-permute-start(bf16[512,1024]{1,0:T(8,128)(2,1)} %join.1), channel_id=1, source_target_pairs={{0,1},{1,0},{2,6},{3,7},{4,5},{5,4},{6,2},{7,3},{8,9},{9,8},{10,14... | collective-permute-start | bytes 3145736 | tf_op jit(solution)/shard_map/ppermute | solution.py:790
  52.5 0.1 reverse.6
  52.7 0.6 pad_maximum_fusion.vec_ref
  53.3 10.4 %attend_back.1 = (bf16[1024,1536]{1,0:T(8,128)(2,1)S(1)}, bf16[256,2176]{1,0:T(8,128)(2,1)S(1)}, bf16[256,2176]{1,0:T(8,128)(2,1)S(1)}) custom-call(s32[6]{0:T(128)S(1)} %stack.21.info_ref, bf16[1024,1536]{1,0:T(8,128)(2,1)} %get-tuple-element.104.qkv_ref, bf16[8,4,128,256]{3,2,1,0:T(8,128)(2,1)} %get-tuple-element.105.prob_ref, ...), custom_call_target="tpu_custom_call" | custom-call | flops 1000 | bytes 1000 | tf_op jit(solution)/shard_map/attend_back/pallas_call | solution.py:55
  63.7 2.2 %collective-permute-done.6.arrived_ref = bf16[512,1024]{1,0:T(8,128)(2,1)} collective-permute-done((bf16[512,1024]{1,0:T(8,128)(2,1)}, bf16[512,1024]{1,0:T(8,128)(2,1)}, u32[]{:S(2)}, u32[]{:S(2)}) %collective-permute-start.6) | collective-permute-done | bytes 1048608 | tf_op jit(solution)/shard_map/ppermute | solution.py:790
  65.9 1.8 %split.1 = (bf16[256,1024]{1,0:T(8,128)(2,1)S(1)}, bf16[256,1024]{1,0:T(8,128)(2,1)S(1)}) custom-call(s32[6]{0:T(128)S(1)} %stack.21.info_ref, bf16[512,1024]{1,0:T(8,128)(2,1)S(1)} %copy-done.7, bf16[512,1024]{1,0:T(8,128)(2,1)S(1)} %copy-done.2, bf16[512,1024]{1,0:T(8,128)(2,1)S(1)} %collective-permute-done.5.own_ref, ...), custom_call_target="tpu_custom_call" | custom-call | flops 1000 | bytes 1000 | tf_op jit(solution)/shard_map/split/pallas_call | solution.py:511
  67.8 1.8 %collective-permute-start.8 = (bf16[256,1024]{1,0:T(8,128)(2,1)S(1)}, bf16[256,1024]{1,0:T(8,128)(2,1)S(1)}, u32[]{:S(2)}, u32[]{:S(2)}) collective-permute-start(bf16[256,1024]{1,0:T(8,128)(2,1)S(1)} %get-tuple-element.124), channel_id=1, source_target_pairs={{0,4},{1,5},{2,3},{3,2},{4,0},{5,1},{6,7},{7,6},{8,12},{9,13},{10,... | collective-permute-start | bytes 1572872 | tf_op jit(solution)/shard_map/ppermute | solution.py:790
  69.6 0.3 add_convert_fusion
  69.9 0.1 fusion
  70.0 0.9 collective-permute-start.9
  70.8 5.5 %first_back.1 = f32[1024,512]{1,0:T(8,128)} custom-call(s32[6]{0:T(128)S(1)} %stack.21.info_ref, bf16[1024,1536]{1,0:T(8,128)(2,1)S(1)} %get-tuple-element.119.dqkv_ref, bf16[512,1536]{1,0:T(8,128)(2,1)S(1)} %copy-done, bf16[1024,512]{1,0:T(8,128)(2,1)} %tok_ref.2, f32[1024,512]{1,0:T(8,128)} %get-tuple-element.120.gres_ref, f32[1,512]{1,0:T(1,128)} %bitcast.14), custom_call_target="tpu_custom_call" | custom-call | flops 1000 | bytes 1000 | tf_op jit(solution)/shard_map/first_back/pallas_call | solution.py:55
  76.4 0.6 collective-permute-done.8
  77.0 0.2 add_convert_fusion.2
  77.3 1.9 %collective-permute-start.10 = (bf16[128,1024]{1,0:T(8,128)(2,1)S(1)}, bf16[128,1024]{1,0:T(8,128)(2,1)S(1)}, u32[]{:S(2)}, u32[]{:S(2)}) collective-permute-start(bf16[128,1024]{1,0:T(8,128)(2,1)S(1)} %get-tuple-element.164), channel_id=1, source_target_pairs={{0,8},{1,9},{2,10},{3,11},{4,12},{5,13},{6,14},{7,15},{8,0},{9,1},... | collective-permute-start | bytes 786440 | tf_op jit(solution)/shard_map/ppermute | solution.py:790
  79.2 5.0 %collective-permute-done.9 = bf16[128,2176]{1,0:T(8,128)(2,1)S(1)} collective-permute-done((bf16[128,2176]{1,0:T(8,128)(2,1)S(1)}, bf16[128,2176]{1,0:T(8,128)(2,1)S(1)}, u32[]{:S(2)}, u32[]{:S(2)}) %collective-permute-start.9) | collective-permute-done | bytes 557088 | tf_op jit(solution)/shard_map/ppermute | solution.py:790
  84.2 0.1 add_convert_fusion.1
  84.3 2.4 %collective-permute-start.11 = (bf16[64,2176]{1,0:T(8,128)(2,1)S(1)}, bf16[64,2176]{1,0:T(8,128)(2,1)S(1)}, u32[]{:S(2)}, u32[]{:S(2)}) collective-permute-start(bf16[64,2176]{1,0:T(8,128)(2,1)S(1)} %get-tuple-element.163), channel_id=1, source_target_pairs={{0,1},{1,0},{2,6},{3,7},{4,5},{5,4},{6,2},{7,3},{8,9},{9,8},{10,14... | collective-permute-start | bytes 835592 | tf_op jit(solution)/shard_map/ppermute | solution.py:790
  86.8 5.9 %collective-permute-done.11 = bf16[64,2176]{1,0:T(8,128)(2,1)S(1)} collective-permute-done((bf16[64,2176]{1,0:T(8,128)(2,1)S(1)}, bf16[64,2176]{1,0:T(8,128)(2,1)S(1)}, u32[]{:S(2)}, u32[]{:S(2)}) %collective-permute-start.11) | collective-permute-done | bytes 278560 | tf_op jit(solution)/shard_map/ppermute | solution.py:790
  92.9 2.0 %collective-permute-start.12 = (bf16[32,2176]{1,0:T(8,128)(2,1)S(1)}, bf16[32,2176]{1,0:T(8,128)(2,1)S(1)}, u32[]{:S(2)}, u32[]{:S(2)}) collective-permute-start(bf16[32,2176]{1,0:T(8,128)(2,1)S(1)} %get-tuple-element.166), channel_id=1, source_target_pairs={{0,8},{1,9},{2,3},{3,2},{4,12},{5,13},{6,7},{7,6},{8,0},{9,1},{10,... | collective-permute-start | bytes 417800 | tf_op jit(solution)/shard_map/ppermute | solution.py:790
  94.9 2.6 %collective-permute-start.13 = (bf16[128,1024]{1,0:T(8,128)(2,1)S(1)}, bf16[128,1024]{1,0:T(8,128)(2,1)S(1)}, u32[]{:S(2)}, u32[]{:S(2)}) collective-permute-start(bf16[128,1024]{1,0:T(8,128)(2,1)S(1)} %add_convert_fusion.5), channel_id=1, source_target_pairs={{0,16},{1,17},{2,18},{3,19},{4,20},{5,21},{6,22},{7,23},{8,24},{9,... | collective-permute-start | bytes 786440 | tf_op jit(solution)/shard_map/ppermute | solution.py:790
  97.5 0.6 collective-permute-done.12
  98.2 5.6 %collective-permute-start.14 = (bf16[32,2176]{1,0:T(8,128)(2,1)S(1)}, bf16[32,2176]{1,0:T(8,128)(2,1)S(1)}, u32[]{:S(2)}, u32[]{:S(2)}) collective-permute-start(bf16[32,2176]{1,0:T(8,128)(2,1)S(1)} %add_convert_fusion.7), channel_id=1, source_target_pairs={{0,16},{1,17},{2,18},{3,19},{4,20},{5,21},{6,22},{7,23},{8,24},{9,... | collective-permute-start | bytes 417800 | tf_op jit(solution)/shard_map/ppermute | solution.py:790
  103.8 1.4 collective-permute-done.13
  105.2 1.7 %collective-permute-start.15 = (bf16[128,1024]{1,0:T(8,128)(2,1)S(1)}, bf16[128,1024]{1,0:T(8,128)(2,1)S(1)}, u32[]{:S(2)}, u32[]{:S(2)}) collective-permute-start(bf16[128,1024]{1,0:T(8,128)(2,1)S(1)} %add_convert_fusion.4), channel_id=1, source_target_pairs={{0,8},{1,9},{2,10},{3,11},{4,12},{5,13},{6,14},{7,15},{8,0},{9,1},... | collective-permute-start | bytes 786440 | tf_op jit(solution)/shard_map/ppermute | solution.py:790
  106.9 3.0 %collective-permute-start.16 = (bf16[32,2176]{1,0:T(8,128)(2,1)S(1)}, bf16[32,2176]{1,0:T(8,128)(2,1)S(1)}, u32[]{:S(2)}, u32[]{:S(2)}) collective-permute-start(bf16[32,2176]{1,0:T(8,128)(2,1)S(1)} %add_convert_fusion.6), channel_id=1, source_target_pairs={{0,8},{1,9},{2,6},{3,7},{4,12},{5,13},{6,2},{7,3},{8,0},{9,1},{10,... | collective-permute-start | bytes 417800 | tf_op jit(solution)/shard_map/ppermute | solution.py:790
  109.9 1.7 %collective-permute-done.15 = bf16[128,1024]{1,0:T(8,128)(2,1)S(1)} collective-permute-done((bf16[128,1024]{1,0:T(8,128)(2,1)S(1)}, bf16[128,1024]{1,0:T(8,128)(2,1)S(1)}, u32[]{:S(2)}, u32[]{:S(2)}) %collective-permute-start.15) | collective-permute-done | bytes 262176 | tf_op jit(solution)/shard_map/ppermute | solution.py:790
  111.7 1.6 %collective-permute-start.18 = (bf16[256,1024]{1,0:T(8,128)(2,1)S(1)}, bf16[256,1024]{1,0:T(8,128)(2,1)S(1)}, u32[]{:S(2)}, u32[]{:S(2)}) collective-permute-start(bf16[256,1024]{1,0:T(8,128)(2,1)S(1)} %constant_dynamic-update-slice_fusion), channel_id=1, source_target_pairs={{0,4},{1,5},{2,6},{3,7},{4,0},{5,1},{6,2},{7,3},{8,12},{9,13},{10,... | collective-permute-start | bytes 1572872 | tf_op jit(solution)/shard_map/ppermute | solution.py:790
  113.4 2.8 %collective-permute-start.17 = (bf16[64,2176]{1,0:T(8,128)(2,1)S(1)}, bf16[64,2176]{1,0:T(8,128)(2,1)S(1)}, u32[]{:S(2)}, u32[]{:S(2)}) collective-permute-start(bf16[64,2176]{1,0:T(8,128)(2,1)S(1)} %constant_dynamic-update-slice_fusion.2), channel_id=1, source_target_pairs={{0,1},{1,0},{2,3},{3,2},{4,5},{5,4},{6,7},{7,6},{8,9},{9,8},{10,11... | collective-permute-start | bytes 835592 | tf_op jit(solution)/shard_map/ppermute | solution.py:790
  116.2 4.5 %collective-permute-done.17 = bf16[64,2176]{1,0:T(8,128)(2,1)S(1)} collective-permute-done((bf16[64,2176]{1,0:T(8,128)(2,1)S(1)}, bf16[64,2176]{1,0:T(8,128)(2,1)S(1)}, u32[]{:S(2)}, u32[]{:S(2)}) %collective-permute-start.17) | collective-permute-done | bytes 278560 | tf_op jit(solution)/shard_map/ppermute | solution.py:790
  120.8 0.1 collective-permute-done.18
  121.0 1.6 %collective-permute-start.20 = (bf16[128,2176]{1,0:T(8,128)(2,1)S(1)}, bf16[128,2176]{1,0:T(8,128)(2,1)S(1)}, u32[]{:S(2)}, u32[]{:S(2)}) collective-permute-start(bf16[128,2176]{1,0:T(8,128)(2,1)S(1)} %constant_dynamic-update-slice_fusion.4), channel_id=1, source_target_pairs={{0,4},{1,5},{2,10},{3,11},{4,0},{5,1},{6,14},{7,15},{8,12},{9,13},... | collective-permute-start | bytes 1671176 | tf_op jit(solution)/shard_map/ppermute | solution.py:790
  122.7 1.0 collective-permute-done.19.other_ref
  123.7 3.1 %ffn_end.1 = (f32[512,1024]{1,0:T(8,128)}, f32[1024,512]{1,0:T(8,128)}) custom-call(s32[6]{0:T(128)S(1)} %stack.21.info_ref, bf16[512,1024]{1,0:T(8,128)(2,1)S(1)} %constant_dynamic-update-slice_fusion.6.keep_ref, bf16[512,1024]{1,0:T(8,128)(2,1)S(1)} %collective-permute-done.19.other_ref), custom_call_target="tpu_custom_call" | custom-call | flops 1000 | bytes 1000 | tf_op jit(solution)/shard_map/ffn_end/pallas_call | solution.py:55
  126.8 3.8 %collective-permute-done.20 = bf16[128,2176]{1,0:T(8,128)(2,1)S(1)} collective-permute-done((bf16[128,2176]{1,0:T(8,128)(2,1)S(1)}, bf16[128,2176]{1,0:T(8,128)(2,1)S(1)}, u32[]{:S(2)}, u32[]{:S(2)}) %collective-permute-start.20) | collective-permute-done | bytes 557088 | tf_op jit(solution)/shard_map/ppermute | solution.py:790
  130.8 2.7 %collective-permute-done.21.other_ref = bf16[256,2176]{1,0:T(8,128)(2,1)S(1)} collective-permute-done((bf16[256,2176]{1,0:T(8,128)(2,1)S(1)}, bf16[256,2176]{1,0:T(8,128)(2,1)S(1)}, u32[]{:S(2)}, u32[]{:S(2)}) %collective-permute-start.21) | collective-permute-done | bytes 1114144 | tf_op jit(solution)/shard_map/ppermute | solution.py:790
  133.5 5.1 %attend_end.1 = (f32[512,1536]{1,0:T(8,128)}, f32[512,512]{1,0:T(8,128)}, f32[512]{0:T(512)}, f32[512]{0:T(512)}, f32[512]{0:T(512)}, /*index=5*/f32[512]{0:T(512)}, f32[512]{0:T(512)}, f32[1024]{0:T(1024)}) custom-call(s32[6]{0:T(128)S(1)} %stack.21.info_ref, bf16[256,2176]{1,0:T(8,128)(2,1)S(1)} %constant_dynamic-update-slice_fusion.8.keep_ref, ...), custom_call_target="tpu_custom_call" | custom-call | flops 1000 | bytes 1000 | tf_op jit(solution)/shard_map/attend_end/pallas_call | solution.py:55
  (51 shorter events, 1.0 us)
Async XLA Ops:
  0.6 5.0 %copy-start = (bf16[512,1536]{1,0:T(8,128)(2,1)S(1)}, bf16[512,1536]{1,0:T(8,128)(2,1)}, u32[]{:S(2)}) copy-start(bf16[512,1536]{1,0:T(8,128)(2,1)} %w_ref.1) | copy-start | bytes 4718596
  0.7 5.0 %copy-start.5 = (bf16[512,512]{1,0:T(8,128)(2,1)S(1)}, bf16[512,512]{1,0:T(8,128)(2,1)}, u32[]{:S(2)}) copy-start(bf16[512,512]{1,0:T(8,128)(2,1)} %wout_ref.3) | copy-start | bytes 1572868
  2.6 26.5 %collective-permute-start = (bf16[528,512]{1,0:T(8,128)(2,1)S(1)}, bf16[528,512]{1,0:T(8,128)(2,1)S(1)}, u32[]{:S(2)}, u32[]{:S(2)}) collective-permute-start(bf16[528,512]{1,0:T(8,128)(2,1)S(1)} %get-tuple-element.96), channel_id=1, source_target_pairs={{0,1},{1,0},{2,3},{3,2},{4,5},{5,4},{6,7},{7,6},{8,9},{9,8},{10,11... | collective-permute-start | bytes 1622024 | tf_op jit(solution)/shard_map/ppermute | solution.py:790
  5.6 23.5 %collective-permute-start.1 = (bf16[512,512]{1,0:T(8,128)(2,1)S(1)}, bf16[512,512]{1,0:T(8,128)(2,1)S(1)}, u32[]{:S(2)}, u32[]{:S(2)}) collective-permute-start(bf16[512,512]{1,0:T(8,128)(2,1)S(1)} %get-tuple-element.97), channel_id=1, source_target_pairs={{0,1},{1,0},{2,3},{3,2},{4,5},{5,4},{6,7},{7,6},{8,9},{9,8},{10,11... | collective-permute-start | bytes 1572872 | tf_op jit(solution)/shard_map/ppermute | solution.py:790
  5.7 9.2 %copy-start.3 = (bf16[512,1024]{1,0:T(8,128)(2,1)S(1)}, bf16[512,1024]{1,0:T(8,128)(2,1)}, u32[]{:S(2)}) copy-start(bf16[512,1024]{1,0:T(8,128)(2,1)} %up_ref.3) | copy-start | bytes 3145732
  5.7 9.2 %copy-start.4 = (bf16[1024,512]{1,0:T(8,128)(2,1)S(1)}, bf16[1024,512]{1,0:T(8,128)(2,1)}, u32[]{:S(2)}) copy-start(bf16[1024,512]{1,0:T(8,128)(2,1)} %down_ref.3) | copy-start | bytes 3145732
  29.1 3.4 %collective-permute-start.2 = (bf16[528,512]{1,0:T(8,128)(2,1)S(1)}, bf16[528,512]{1,0:T(8,128)(2,1)S(1)}, u32[]{:S(2)}, u32[]{:S(2)}) collective-permute-start(bf16[528,512]{1,0:T(8,128)(2,1)S(1)} %collective-permute-done.refs_0_), channel_id=1, source_target_pairs={{0,2},{1,3},{2,0},{3,1},{4,6},{5,7},{6,4},{7,5},{8,10},{9,11},{10,... | collective-permute-start | bytes 1622024 | tf_op jit(solution)/shard_map/ppermute | solution.py:790
  29.1 3.4 %collective-permute-start.3 = (bf16[512,512]{1,0:T(8,128)(2,1)S(1)}, bf16[512,512]{1,0:T(8,128)(2,1)S(1)}, u32[]{:S(2)}, u32[]{:S(2)}) collective-permute-start(bf16[512,512]{1,0:T(8,128)(2,1)S(1)} %collective-permute-done.1.refs_2_), channel_id=1, source_target_pairs={{0,2},{1,3},{2,0},{3,1},{4,6},{5,7},{6,4},{7,5},{8,10},{9,11},{10,... | collective-permute-start | bytes 1572872 | tf_op jit(solution)/shard_map/ppermute | solution.py:790
  29.6 16.9 %collective-permute-start.5 = (bf16[512,1024]{1,0:T(8,128)(2,1)}, bf16[512,1024]{1,0:T(8,128)(2,1)S(1)}, u32[]{:S(2)}, u32[]{:S(2)}) collective-permute-start(bf16[512,1024]{1,0:T(8,128)(2,1)} %get-tuple-element.103), channel_id=1, source_target_pairs={{0,2},{1,3},{2,0},{3,1},{4,6},{5,7},{6,4},{7,5},{8,10},{9,11},{10,... | collective-permute-start | bytes 3145736 | tf_op jit(solution)/shard_map/ppermute | solution.py:790
  46.3 4.5 %copy-start.6 = (bf16[512,1024]{1,0:T(8,128)(2,1)}, bf16[512,1024]{1,0:T(8,128)(2,1)S(1)}, u32[]{:S(2)}) copy-start(bf16[512,1024]{1,0:T(8,128)(2,1)S(1)} %get-tuple-element.101.keep_ref) | copy-start | bytes 3145732
  46.3 2.7 %collective-permute-start.4 = (bf16[512,1024]{1,0:T(8,128)(2,1)S(1)}, bf16[512,1024]{1,0:T(8,128)(2,1)S(1)}, u32[]{:S(2)}, u32[]{:S(2)}) collective-permute-start(bf16[512,1024]{1,0:T(8,128)(2,1)S(1)} %get-tuple-element.102), channel_id=1, source_target_pairs={{0,2},{1,3},{2,0},{3,1},{4,6},{5,7},{6,4},{7,5},{8,10},{9,11},{10,... | collective-permute-start | bytes 3145736 | tf_op jit(solution)/shard_map/ppermute | solution.py:790
  49.0 1.8 %copy-start.1 = (bf16[512,1024]{1,0:T(8,128)(2,1)}, bf16[512,1024]{1,0:T(8,128)(2,1)S(1)}, u32[]{:S(2)}) copy-start(bf16[512,1024]{1,0:T(8,128)(2,1)S(1)} %collective-permute-done.4.got_ref) | copy-start | bytes 3145732
  50.8 15.1 %collective-permute-start.6 = (bf16[512,1024]{1,0:T(8,128)(2,1)}, bf16[512,1024]{1,0:T(8,128)(2,1)}, u32[]{:S(2)}, u32[]{:S(2)}) collective-permute-start(bf16[512,1024]{1,0:T(8,128)(2,1)} %join.1), channel_id=1, source_target_pairs={{0,1},{1,0},{2,6},{3,7},{4,5},{5,4},{6,2},{7,3},{8,9},{9,8},{10,14... | collective-permute-start | bytes 3145736 | tf_op jit(solution)/shard_map/ppermute | solution.py:790
  53.3 12.6 %copy-start.2 = (bf16[512,1024]{1,0:T(8,128)(2,1)S(1)}, bf16[512,1024]{1,0:T(8,128)(2,1)}, u32[]{:S(2)}) copy-start(bf16[512,1024]{1,0:T(8,128)(2,1)} %copy-done.1) | copy-start | bytes 3145732
  53.3 12.6 %copy-start.7 = (bf16[512,1024]{1,0:T(8,128)(2,1)S(1)}, bf16[512,1024]{1,0:T(8,128)(2,1)}, u32[]{:S(2)}) copy-start(bf16[512,1024]{1,0:T(8,128)(2,1)} %copy-done.6) | copy-start | bytes 3145732
  65.9 3.7 %collective-permute-start.7 = (bf16[256,2176]{1,0:T(8,128)(2,1)S(1)}, bf16[256,2176]{1,0:T(8,128)(2,1)S(1)}, u32[]{:S(2)}, u32[]{:S(2)}) collective-permute-start(bf16[256,2176]{1,0:T(8,128)(2,1)S(1)} %get-tuple-element.118), channel_id=1, source_target_pairs={{0,2},{1,3},{2,0},{3,1},{4,6},{5,7},{6,4},{7,5},{8,10},{9,11},{10,... | collective-permute-start | bytes 3342344 | tf_op jit(solution)/shard_map/ppermute | solution.py:790
  67.8 9.2 %collective-permute-start.8 = (bf16[256,1024]{1,0:T(8,128)(2,1)S(1)}, bf16[256,1024]{1,0:T(8,128)(2,1)S(1)}, u32[]{:S(2)}, u32[]{:S(2)}) collective-permute-start(bf16[256,1024]{1,0:T(8,128)(2,1)S(1)} %get-tuple-element.124), channel_id=1, source_target_pairs={{0,4},{1,5},{2,3},{3,2},{4,0},{5,1},{6,7},{7,6},{8,12},{9,13},{10,... | collective-permute-start | bytes 1572872 | tf_op jit(solution)/shard_map/ppermute | solution.py:790
  70.0 14.2 %collective-permute-start.9 = (bf16[128,2176]{1,0:T(8,128)(2,1)S(1)}, bf16[128,2176]{1,0:T(8,128)(2,1)S(1)}, u32[]{:S(2)}, u32[]{:S(2)}) collective-permute-start(bf16[128,2176]{1,0:T(8,128)(2,1)S(1)} %get-tuple-element.160), channel_id=1, source_target_pairs={{0,4},{1,5},{2,10},{3,11},{4,0},{5,1},{6,14},{7,15},{8,12},{9,13},... | collective-permute-start | bytes 1671176 | tf_op jit(solution)/shard_map/ppermute | solution.py:790
  77.3 9.5 %collective-permute-start.10 = (bf16[128,1024]{1,0:T(8,128)(2,1)S(1)}, bf16[128,1024]{1,0:T(8,128)(2,1)S(1)}, u32[]{:S(2)}, u32[]{:S(2)}) collective-permute-start(bf16[128,1024]{1,0:T(8,128)(2,1)S(1)} %get-tuple-element.164), channel_id=1, source_target_pairs={{0,8},{1,9},{2,10},{3,11},{4,12},{5,13},{6,14},{7,15},{8,0},{9,1},... | collective-permute-start | bytes 786440 | tf_op jit(solution)/shard_map/ppermute | solution.py:790
  84.3 8.4 %collective-permute-start.11 = (bf16[64,2176]{1,0:T(8,128)(2,1)S(1)}, bf16[64,2176]{1,0:T(8,128)(2,1)S(1)}, u32[]{:S(2)}, u32[]{:S(2)}) collective-permute-start(bf16[64,2176]{1,0:T(8,128)(2,1)S(1)} %get-tuple-element.163), channel_id=1, source_target_pairs={{0,1},{1,0},{2,6},{3,7},{4,5},{5,4},{6,2},{7,3},{8,9},{9,8},{10,14... | collective-permute-start | bytes 835592 | tf_op jit(solution)/shard_map/ppermute | solution.py:790
  92.9 5.2 %collective-permute-start.12 = (bf16[32,2176]{1,0:T(8,128)(2,1)S(1)}, bf16[32,2176]{1,0:T(8,128)(2,1)S(1)}, u32[]{:S(2)}, u32[]{:S(2)}) collective-permute-start(bf16[32,2176]{1,0:T(8,128)(2,1)S(1)} %get-tuple-element.166), channel_id=1, source_target_pairs={{0,8},{1,9},{2,3},{3,2},{4,12},{5,13},{6,7},{7,6},{8,0},{9,1},{10,... | collective-permute-start | bytes 417800 | tf_op jit(solution)/shard_map/ppermute | solution.py:790
  94.9 10.2 %collective-permute-start.13 = (bf16[128,1024]{1,0:T(8,128)(2,1)S(1)}, bf16[128,1024]{1,0:T(8,128)(2,1)S(1)}, u32[]{:S(2)}, u32[]{:S(2)}) collective-permute-start(bf16[128,1024]{1,0:T(8,128)(2,1)S(1)} %add_convert_fusion.5), channel_id=1, source_target_pairs={{0,16},{1,17},{2,18},{3,19},{4,20},{5,21},{6,22},{7,23},{8,24},{9,... | collective-permute-start | bytes 786440 | tf_op jit(solution)/shard_map/ppermute | solution.py:790
  98.2 8.7 %collective-permute-start.14 = (bf16[32,2176]{1,0:T(8,128)(2,1)S(1)}, bf16[32,2176]{1,0:T(8,128)(2,1)S(1)}, u32[]{:S(2)}, u32[]{:S(2)}) collective-permute-start(bf16[32,2176]{1,0:T(8,128)(2,1)S(1)} %add_convert_fusion.7), channel_id=1, source_target_pairs={{0,16},{1,17},{2,18},{3,19},{4,20},{5,21},{6,22},{7,23},{8,24},{9,... | collective-permute-start | bytes 417800 | tf_op jit(solution)/shard_map/ppermute | solution.py:790
  105.2 6.4 %collective-permute-start.15 = (bf16[128,1024]{1,0:T(8,128)(2,1)S(1)}, bf16[128,1024]{1,0:T(8,128)(2,1)S(1)}, u32[]{:S(2)}, u32[]{:S(2)}) collective-permute-start(bf16[128,1024]{1,0:T(8,128)(2,1)S(1)} %add_convert_fusion.4), channel_id=1, source_target_pairs={{0,8},{1,9},{2,10},{3,11},{4,12},{5,13},{6,14},{7,15},{8,0},{9,1},... | collective-permute-start | bytes 786440 | tf_op jit(solution)/shard_map/ppermute | solution.py:790
  106.9 6.4 %collective-permute-start.16 = (bf16[32,2176]{1,0:T(8,128)(2,1)S(1)}, bf16[32,2176]{1,0:T(8,128)(2,1)S(1)}, u32[]{:S(2)}, u32[]{:S(2)}) collective-permute-start(bf16[32,2176]{1,0:T(8,128)(2,1)S(1)} %add_convert_fusion.6), channel_id=1, source_target_pairs={{0,8},{1,9},{2,6},{3,7},{4,12},{5,13},{6,2},{7,3},{8,0},{9,1},{10,... | collective-permute-start | bytes 417800 | tf_op jit(solution)/shard_map/ppermute | solution.py:790
  111.7 9.2 %collective-permute-start.18 = (bf16[256,1024]{1,0:T(8,128)(2,1)S(1)}, bf16[256,1024]{1,0:T(8,128)(2,1)S(1)}, u32[]{:S(2)}, u32[]{:S(2)}) collective-permute-start(bf16[256,1024]{1,0:T(8,128)(2,1)S(1)} %constant_dynamic-update-slice_fusion), channel_id=1, source_target_pairs={{0,4},{1,5},{2,6},{3,7},{4,0},{5,1},{6,2},{7,3},{8,12},{9,13},{10,... | collective-permute-start | bytes 1572872 | tf_op jit(solution)/shard_map/ppermute | solution.py:790
  113.4 7.4 %collective-permute-start.17 = (bf16[64,2176]{1,0:T(8,128)(2,1)S(1)}, bf16[64,2176]{1,0:T(8,128)(2,1)S(1)}, u32[]{:S(2)}, u32[]{:S(2)}) collective-permute-start(bf16[64,2176]{1,0:T(8,128)(2,1)S(1)} %constant_dynamic-update-slice_fusion.2), channel_id=1, source_target_pairs={{0,1},{1,0},{2,3},{3,2},{4,5},{5,4},{6,7},{7,6},{8,9},{9,8},{10,11... | collective-permute-start | bytes 835592 | tf_op jit(solution)/shard_map/ppermute | solution.py:790
  120.9 2.7 %collective-permute-start.19 = (bf16[512,1024]{1,0:T(8,128)(2,1)S(1)}, bf16[512,1024]{1,0:T(8,128)(2,1)S(1)}, u32[]{:S(2)}, u32[]{:S(2)}) collective-permute-start(bf16[512,1024]{1,0:T(8,128)(2,1)S(1)} %constant_dynamic-update-slice_fusion.6.keep_ref), channel_id=1, source_target_pairs={{0,2},{1,3},{2,0},{3,1},{4,6},{5,7},{6,4},{7,5},{8,10},{9,11},{10,... | collective-permute-start | bytes 3145736 | tf_op jit(solution)/shard_map/ppermute | solution.py:790
  121.0 9.6 %collective-permute-start.20 = (bf16[128,2176]{1,0:T(8,128)(2,1)S(1)}, bf16[128,2176]{1,0:T(8,128)(2,1)S(1)}, u32[]{:S(2)}, u32[]{:S(2)}) collective-permute-start(bf16[128,2176]{1,0:T(8,128)(2,1)S(1)} %constant_dynamic-update-slice_fusion.4), channel_id=1, source_target_pairs={{0,4},{1,5},{2,10},{3,11},{4,0},{5,1},{6,14},{7,15},{8,12},{9,13},... | collective-permute-start | bytes 1671176 | tf_op jit(solution)/shard_map/ppermute | solution.py:790
  130.7 2.8 %collective-permute-start.21 = (bf16[256,2176]{1,0:T(8,128)(2,1)S(1)}, bf16[256,2176]{1,0:T(8,128)(2,1)S(1)}, u32[]{:S(2)}, u32[]{:S(2)}) collective-permute-start(bf16[256,2176]{1,0:T(8,128)(2,1)S(1)} %constant_dynamic-update-slice_fusion.8.keep_ref), channel_id=1, source_target_pairs={{0,2},{1,3},{2,0},{3,1},{4,6},{5,7},{6,4},{7,5},{8,10},{9,11},{10,... | collective-permute-start | bytes 3342344 | tf_op jit(solution)/shard_map/ppermute | solution.py:790

commit v9 on v8

--- a/solution.py
+++ b/solution.py
@@ -157,21 +157,22 @@
         here = pl.ds(at * rows + r, 1)
         seg = jnp.broadcast_to(seg_ref[here, :].astype(F32), (slots, slots))
         step = jnp.broadcast_to(step_ref[here, :].astype(F32), (slots, slots))
-        live = jnp.broadcast_to(pad_ref[here, :], (slots, slots)) == 0
-        masks.append(((seg == seg.T) & (step <= step.T) & live) | eye)
-    scores = [mm_nt(part(r, p, 0), by_head(part(r, p, 1) * HEAD ** (-0.5))) for r, p in units]
+        live = jnp.broadcast_to(pad_ref[here, :].astype(F32), (slots, slots)).T == 0
+        masks.append(((seg == seg.T) & (step.T <= step) & live) | eye)
+    scores = [mm_nt(part(r, p, 1), by_head(part(r, p, 0) * HEAD ** (-0.5))) for r, p in units]
     probs = []
     for (r, p), score in zip(units, scores):
         halves = []
         for half in (score[:, :slots], score[:, slots:]):
             half = jnp.where(masks[r], half, -1e30)
-            weight = jnp.exp(half - jnp.max(half, axis=-1, keepdims=True))
-            total = jnp.sum(weight, axis=-1, keepdims=True)
+            weight = jnp.exp(half - jnp.max(half, axis=0, keepdims=True))
+            total = jnp.sum(weight, axis=0, keepdims=True)
             halves.append((weight * (1.0 / total)).astype(BF))
-        probs.append(jnp.concatenate(halves, axis=1))
-    for (r, p), prob in zip(units, probs):
-        prob_ref[r, p] = prob
-        mixed_ref[r * slots : (r + 1) * slots, p * PAIR : (p + 1) * PAIR] = mm(prob, by_head(part(r, p, 2))).astype(BF)
+        probs.append(halves)
+    for (r, p), halves in zip(units, probs):
+        prob_ref[r, p] = jnp.concatenate(halves, axis=1)
+        mixed = mm_tn(jnp.concatenate(halves, axis=0), by_head(part(r, p, 2)))
+        mixed_ref[r * slots : (r + 1) * slots, p * PAIR : (p + 1) * PAIR] = mixed.astype(BF)
     residual = tokens + mm(mixed_ref[...], wout_ref[...])
     res_ref[...] = residual
     unit, _ = unit_parts(residual)
@@ -550,27 +551,21 @@
         return (slice(r * slots, (r + 1) * slots), slice(which * width + p * PAIR, which * width + (p + 1) * PAIR))
 
     grads = [gmix_ref[place(r, p, 0)] for r, p in units]
-    dprobs = [mm_nt(g, by_head(qkv_ref[place(r, p, 2)])) for (r, p), g in zip(units, grads)]
-    for (r, p), g in zip(units, grads):
-        prob = prob_ref[r, p]
-        stacked = jnp.concatenate([prob[:, :slots], prob[:, slots:]], axis=0)
-        dqkv_ref[place(r, p, 2)] = mm_tn(stacked, by_head(g)).astype(BF)
+    by_grad = [by_head(g) for g in grads]
+    dprobs = [mm_nt(qkv_ref[place(r, p, 2)], g) for (r, p), g in zip(units, by_grad)]
+    for (r, p), g in zip(units, by_grad):
+        dqkv_ref[place(r, p, 2)] = mm(prob_ref[r, p], g).astype(BF)
     dscores = []
     for (r, p), dprob in zip(units, dprobs):
         p32 = prob_ref[r, p].astype(F32)
-        prod = p32 * dprob
-        first = jnp.sum(prod[:, :slots], axis=-1, keepdims=True)
-        second = jnp.sum(prod[:, slots:], axis=-1, keepdims=True)
-        dscores.append((
-            (p32[:, :slots] * (dprob[:, :slots] - first)).astype(BF),
-            (p32[:, slots:] * (dprob[:, slots:] - second)).astype(BF),
-        ))
+        dscores.append((p32 * (dprob - jnp.sum(p32 * dprob, axis=0, keepdims=True))).astype(BF))
+    for (r, p), ds in zip(units, dscores):
+        q = qkv_ref[place(r, p, 0)]
+        dqkv_ref[place(r, p, 1)] = mm(ds, by_head(q * scale)).astype(BF)
     for (r, p), ds in zip(units, dscores):
         k = qkv_ref[place(r, p, 1)]
-        dqkv_ref[place(r, p, 0)] = mm(jnp.concatenate(ds, axis=1), by_head(k * scale)).astype(BF)
-    for (r, p), ds in zip(units, dscores):
-        q = qkv_ref[place(r, p, 0)]
-        dqkv_ref[place(r, p, 1)] = mm_tn(jnp.concatenate(ds, axis=0), by_head(q * scale)).astype(BF)
+        stacked = jnp.concatenate([ds[:, :slots], ds[:, slots:]], axis=0)
+        dqkv_ref[place(r, p, 0)] = mm_tn(stacked, by_head(k * scale)).astype(BF)
     unit, _ = unit_parts(tok_ref[...].astype(F32))
     acc_ref[:, : 3 * width] += mm_tn(unit.astype(BF), dqkv_ref[...])
     grad_ref[...] = dqkv_ref[...]
@@ -685,30 +680,28 @@
 
 
 def attend_end_kernel(
-    tables, shares, info_ref, keep_ref, other_ref, w_ref, g1_ref, c1_ref, qkv_hbm, out_hbm, *refs
+    tables, shares, info_ref, *refs
 ):
-    vec_refs, (qkv_ref, out_ref, col_ref, row_ref, sems) = refs[:6], refs[6:]
+    quarters, (w_hbm, g1_ref, c1_ref, qkv_hbm, out_hbm), refs = refs[:4], refs[4:9], refs[9:]
+    vec_refs, (qkv_ref, out_ref, col_ref, row_ref, w_ref, sems) = refs[:6], refs[6:]
     core, own, away = info_ref[0], info_ref[3], info_ref[4]
+    weights = pltpu.make_async_copy(w_hbm, w_ref, sems.at[2 * len(tables[0])])
+    weights.start()
     width = out_ref.shape[1]
     blocks = len(tables[0])
     size = out_ref.shape[0] // blocks
-    half = out_ref.shape[0] // 2
+    quarter = out_ref.shape[0] // 4
     spots = []
     for place in range(blocks):
-        mine = place * size < half
-        block = block_at(place, tables, core, own if mine else away)
-        at = place * size % half
-        spots.append((keep_ref if mine else other_ref, slice(at, at + size), pl.multiple_of(block * size, size)))
+        row = place * size
+        block = block_at(place, tables, core, own if row < 2 * quarter else away)
+        at = row % quarter
+        spots.append((quarters[row // quarter], slice(at, at + size), slice(row, row + size), pl.multiple_of(block * size, size)))
     copies = []
-    for i, (src, rows, to) in enumerate(spots):
-        to = pl.ds(to, size)
-        col_ref[to, :] = src[rows, 4 * width :].astype(F32)
-        out_ref[rows if src is keep_ref else slice(rows.start + half, rows.stop + half), :] = src[
-            rows, 3 * width : 4 * width
-        ].astype(F32)
-    for i, (src, rows, to) in enumerate(spots):
-        rows = rows if src is keep_ref else slice(rows.start + half, rows.stop + half)
-        copies.append(pltpu.make_async_copy(out_ref.at[rows, :], out_hbm.at[pl.ds(to, size), :], sems.at[i]))
+    for i, (src, rows, here, to) in enumerate(spots):
+        col_ref[pl.ds(to, size), :] = src[rows, 4 * width :].astype(F32)
+        out_ref[here, :] = src[rows, 3 * width : 4 * width].astype(F32)
+        copies.append(pltpu.make_async_copy(out_ref.at[here, :], out_hbm.at[pl.ds(to, size), :], sems.at[i]))
         copies[-1].start()
     vec = col_ref[...].T
     row_ref[...] = vec
@@ -716,16 +709,17 @@
     pair = jnp.concatenate([g1_ref[...], c1_ref[...], jnp.zeros((LANES - 2, width), F32)], axis=0).T
     col_ref[...] = pair
     lane = lax.broadcasted_iota(jnp.int32, (size, LANES), 1)
-    for i, (src, rows, to) in enumerate(spots):
+    for i, (src, rows, here, to) in enumerate(spots):
+        gain_bias = col_ref[pl.ds(to, size), :]
+        sums = src[rows, : 3 * width].astype(F32)
+        qkv_ref[here, :] = gain_bias[:, 0:1] * sums + gain_bias[:, 1:2] * wide_row
+        copies.append(pltpu.make_async_copy(qkv_ref.at[here, :], qkv_hbm.at[pl.ds(to, size), :], sems.at[blocks + i]))
+        copies[-1].start()
+    weights.wait()
+    for src, rows, _, to in spots:
         here = pl.ds(to, size)
-        gain_bias = col_ref[here, :]
-        gain, bias = gain_bias[:, 0:1], gain_bias[:, 1:2]
         sums = src[rows, : 3 * width].astype(F32)
         w = w_ref[here, :].astype(F32)
-        rows = rows if src is keep_ref else slice(rows.start + half, rows.stop + half)
-        qkv_ref[rows, :] = gain * sums + bias * wide_row
-        copies.append(pltpu.make_async_copy(qkv_ref.at[rows, :], qkv_hbm.at[here, :], sems.at[blocks + i]))
-        copies[-1].start()
         d_gain = jnp.sum(w * sums, axis=1, keepdims=True)
         d_bias = jnp.sum(w * wide_row, axis=1, keepdims=True)
         col_ref[here, :] = jnp.where(lane == 0, d_gain, jnp.where(lane == 1, d_bias, 0.0))
@@ -750,14 +744,14 @@
         copy.wait()
 
 
-def attend_end(info, tables, keep, other, w_qkv, g1, c1, units):
-    rows, width = 2 * keep.shape[0], w_qkv.shape[0]
+def attend_end(info, tables, quarters, w_qkv, g1, c1, units):
+    rows, width = 4 * quarters[0].shape[0], w_qkv.shape[0]
     blocks = len(tables[0])
     return call(
         functools.partial(attend_end_kernel, tables, max(1, width // units)),
         "attend_end",
         (1,),
-        [whole(*keep.shape)] * 2 + [whole(*w_qkv.shape)] + [whole(1, width)] * 2,
+        [whole(*quarters[0].shape)] * 4 + [pl.BlockSpec(memory_space=pl.ANY)] + [whole(1, width)] * 2,
         [pl.BlockSpec(memory_space=pl.ANY)] * 2 + [whole(width)] * 5 + [whole(units)],
         [jax.ShapeDtypeStruct((rows, 3 * width), F32), jax.ShapeDtypeStruct((rows, width), F32)]
         + [jax.ShapeDtypeStruct((width,), F32)] * 5
@@ -767,10 +761,11 @@
             pltpu.VMEM((rows, width), F32),
             pltpu.VMEM((rows, LANES), F32),
             pltpu.VMEM((LANES, width), F32),
-            pltpu.SemaphoreType.DMA((2 * blocks,)),
+            pltpu.VMEM(w_qkv.shape, BF),
+            pltpu.SemaphoreType.DMA((2 * blocks + 1,)),
         ],
         info,
-        (keep, other, w_qkv) + far(g1, c1),
+        tuple(quarters) + far(w_qkv, g1, c1),
     )
 
 
@@ -813,7 +808,7 @@
     def finish(kept, got, step):
         if step[0] == "gather":
             return jnp.concatenate([kept, got], axis=0)
-        return (kept, got) if step[0] == "core" else add(kept, got)
+        return add(kept, got) if step[0] in ("halve", "exchange") else (kept, got)
 
     wide_at, narrow_at = lax.axis_index("wide"), lax.axis_index("narrow")
     core = wide_at & 1
@@ -912,7 +907,7 @@
     keep = add(keep, swap(send, core_mask))
     grad_tokens = first_back(info, dqkv, w_qkv, tokens_in, gres, g1)
     steps = {
-        "A": steps_of(at_in, at_rest, at_out) + [("core", core_mask)],
+        "A": steps_of(at_in, at_rest, at_out)[:-1] + [("last", *steps_of(at_in, at_rest, at_out)[-1][1:]), ("core", core_mask)],
         "F": steps_of(ff_in, ff_rest, ff_out) + [("core", core_mask)],
     }
     if mixing:
@@ -931,21 +926,27 @@
             kept, other_kept, *beside = after(kept, other_kept, *beside)
             under_way[other] = other_kept, other_got
         else:
-            kept, *beside = after(kept, *beside)
+            kept, got, *beside = after(kept, got, *beside)
         if len(beside) == 1:
             (grad_tokens,), beside = beside, ()
         elif beside:
             (grad_w_up, grad_w_down), beside = beside, ()
         step, *steps[turn] = steps[turn]
+        if step[0] == "last":
+            got, crossed = after(got, crossed)
         value = finish(kept, got, step)
-        if steps[turn]:
+        if step[0] == "last":
+            under_way[turn] = value, swap(got, core_mask)
+        elif steps[turn]:
             under_way[turn] = start(value, steps[turn][0])
+            if steps[turn][0][0] == "last":
+                crossed = swap(value, core_mask)
         elif turn == "F":
             beside = ffn_end(info, ff_out_tables, *value)
         else:
-            done = value
+            done = (*value[0], crossed, value[1])
     grad_w_qkv, grad_w_out, d_gain1, d_bias1, d_gain2, d_bias2, d_bdown, grad_b_up = attend_end(
-        info, at_tables(at_out), *done, w_qkv, g1, c1, 2 * units
+        info, at_tables(at_out), done, w_qkv, g1, c1, 2 * units
     )
     return (
         block_out, grad_tokens, d_gain1, d_bias1, grad_w_qkv, grad_w_out, d_gain2, d_bias2, grad_w_up, grad_b_up, grad_w_down,

time: 140 us -> 138 us (0.986)
    ppermute x22 -> x23, waiting for transfers between devices: 38.2 us -> 38 us  [swap(): return lax.ppermute(value, AXES, pairs)]
    ppermute x22 -> x23, starting transfers between devices: 33.7 us -> 33.9 us  [swap(): return lax.ppermute(value, AXES, pairs)]
  transfers between devices with their start and end apart: 22 -> 23, of which waited for: 15 -> 15; matrix products, arithmetic and copies ran while one was open for 1% -> 1% of each run, Pallas kernels for 40% -> 39%
where the time goes in v9:
time: 138 us; the launch traced here: 137 us
  Pallas kernels  62.4 us (45%)
  waiting for transfers between devices  38 us (28%)
  starting transfers between devices  33.9 us (25%)
  other arithmetic  1.48 us (1%)
    pallas_call x8, Pallas kernels, call(): pl.pallas_call(kernel, grid_spec=pltpu.PrefetchScalarGridSpec(num_scalar_...  58.8 us
    ppermute x23, waiting for transfers between devices, swap(): return lax.ppermute(value, AXES, pairs)  38 us
    ppermute x23, starting transfers between devices, swap(): return lax.ppermute(value, AXES, pairs)  33.9 us
    pallas_call x2, Pallas kernels, direct(): pl.pallas_call(kernel, in_specs=[pl.BlockSpec(memory_space=pltpu.SMEM)] +...  3.6 us
  transfers between devices with their start and end apart: 23, of which 15 were waited for; matrix products, arithmetic and copies ran while one was open for 1% of the time, Pallas kernels for 39%

profile of v9, /device:TPU:0, one launch (start us, length us, event | category | flops | bytes accessed | tf_op | source)
XLA Modules:
  0.0 137.4 jit_solution(11894746247751609161)
XLA Ops:
  0.7 0.1 stack.21.info_ref
  0.8 1.8 %pack.1 = (bf16[528,512]{1,0:T(8,128)(2,1)S(1)}, bf16[512,512]{1,0:T(8,128)(2,1)S(1)}) custom-call(s32[6]{0:T(128)S(1)} %stack.21.info_ref, bf16[512,1024]{1,0:T(8,128)(2,1)} %up_ref.3, bf16[1024]{0:T(1024)(128)(2,1)} %bias_ref.3, bf16[1024,512]{1,0:T(8,128)(2,1)} %down_ref.3), custom_call_target="tpu_custom_call" | custom-call | flops 1000 | bytes 1000 | tf_op jit(solution)/shard_map/pack/pallas_call | solution.py:55
  2.6 3.0 %collective-permute-start = (bf16[528,512]{1,0:T(8,128)(2,1)S(1)}, bf16[528,512]{1,0:T(8,128)(2,1)S(1)}, u32[]{:S(2)}, u32[]{:S(2)}) collective-permute-start(bf16[528,512]{1,0:T(8,128)(2,1)S(1)} %get-tuple-element.102), channel_id=1, source_target_pairs={{0,1},{1,0},{2,3},{3,2},{4,5},{5,4},{6,7},{7,6},{8,9},{9,8},{10,11... | collective-permute-start | bytes 1622024 | tf_op jit(solution)/shard_map/ppermute | solution.py:785
  5.7 9.0 %attend.1 = (bf16[1024,1536]{1,0:T(8,128)(2,1)}, bf16[8,4,128,256]{3,2,1,0:T(8,128)(2,1)}, bf16[1024,512]{1,0:T(8,128)(2,1)}, f32[1024,512]{1,0:T(8,128)}, bf16[1024,512]{1,0:T(8,128)(2,1)S(1)}) custom-call(s32[6]{0:T(128)S(1)} %stack.21.info_ref, bf16[1024,512]{1,0:T(8,128)(2,1)} %tok_ref.2, f32[1,512]{1,0:T(1,128)} %bitcast.13, f32[1,512]{1,0:T(1,128)} %bitcast.18, ...), custom_call_target="tpu_custom_call" | custom-call | flops 1000 | bytes 1000 | tf_op jit(solution)/shard_map/attend/pallas_call | solution.py:55
  14.7 11.2 %ffn_own.1 = (f32[1024,512]{1,0:T(8,128)S(1)}, f32[1024,512]{1,0:T(8,128)S(1)}, bf16[512,1024]{1,0:T(8,128)(2,1)}, bf16[512,1024]{1,0:T(8,128)(2,1)}, f32[2,512]{1,0:T(2,128)S(1)}) custom-call(s32[6]{0:T(128)S(1)} %stack.21.info_ref, bf16[1024,512]{1,0:T(8,128)(2,1)S(1)} %get-tuple-element.95.sec_ref.sec_in, bf16[1024,512]{1,0:T(8,128)(2,1)} %dy_in.1, ...), custom_call_target="tpu_custom_call" | custom-call | flops 1000 | bytes 1000 | tf_op jit(solution)/shard_map/ffn_own/pallas_call | solution.py:55
  25.9 3.2 %collective-permute-done.1.refs_2_ = bf16[512,512]{1,0:T(8,128)(2,1)S(1)} collective-permute-done((bf16[512,512]{1,0:T(8,128)(2,1)S(1)}, bf16[512,512]{1,0:T(8,128)(2,1)S(1)}, u32[]{:S(2)}, u32[]{:S(2)}) %collective-permute-start.1) | collective-permute-done | bytes 524320 | tf_op jit(solution)/shard_map/ppermute | solution.py:785
  29.1 0.5 collective-permute-start.3
  29.7 2.9 %collective-permute-done.3.refs_3_ = bf16[512,512]{1,0:T(8,128)(2,1)S(1)} collective-permute-done((bf16[512,512]{1,0:T(8,128)(2,1)S(1)}, bf16[512,512]{1,0:T(8,128)(2,1)S(1)}, u32[]{:S(2)}, u32[]{:S(2)}) %collective-permute-start.3) | collective-permute-done | bytes 524320 | tf_op jit(solution)/shard_map/ppermute | solution.py:785
  32.6 13.7 %ffn_rest.1 = (bf16[1024,512]{1,0:T(8,128)(2,1)}, f32[1024,512]{1,0:T(8,128)}, bf16[1024,512]{1,0:T(8,128)(2,1)}, f32[8,512]{1,0:T(8,128)S(1)}, f32[512,512]{1,0...) custom-call(s32[6]{0:T(128)S(1)} %stack.21.info_ref, ...), custom_call_target="tpu_custom_call" | custom-call | flops 1000 | bytes 1000 | tf_op jit(solution)/shard_map/ffn_rest/pallas_call | solution.py:55
  46.3 0.2 collective-permute-start.4
  46.5 2.5 %collective-permute-done.4.got_ref = bf16[512,1024]{1,0:T(8,128)(2,1)S(1)} collective-permute-done((bf16[512,1024]{1,0:T(8,128)(2,1)S(1)}, bf16[512,1024]{1,0:T(8,128)(2,1)S(1)}, u32[]{:S(2)}, u32[]{:S(2)}) %collective-permute-start.4) | collective-permute-done | bytes 1048608 | tf_op jit(solution)/shard_map/ppermute | solution.py:785
  49.1 1.8 %join.1 = bf16[512,1024]{1,0:T(8,128)(2,1)} custom-call(s32[6]{0:T(128)S(1)} %stack.21.info_ref, bf16[512,1024]{1,0:T(8,128)(2,1)S(1)} %get-tuple-element.113.send_ref, bf16[512,1024]{1,0:T(8,128)(2,1)S(1)} %collective-permute-done.4.got_ref, bf16[512,1024]{1,0:T(8,128)(2,1)S(1)} %collective-permute-done.5.own_ref), custom_call_target="tpu_custom_call" | custom-call | flops 1000 | bytes 1000 | tf_op jit(solution)/shard_map/join/pallas_call | solution.py:512
  50.8 1.7 %collective-permute-start.6 = (bf16[512,1024]{1,0:T(8,128)(2,1)}, bf16[512,1024]{1,0:T(8,128)(2,1)}, u32[]{:S(2)}, u32[]{:S(2)}) collective-permute-start(bf16[512,1024]{1,0:T(8,128)(2,1)} %join.1), channel_id=1, source_target_pairs={{0,1},{1,0},{2,6},{3,7},{4,5},{5,4},{6,2},{7,3},{8,9},{9,8},{10,14... | collective-permute-start | bytes 3145736 | tf_op jit(solution)/shard_map/ppermute | solution.py:785
  52.6 0.1 reverse.6
  52.7 0.6 pad_maximum_fusion.vec_ref
  53.3 9.8 %attend_back.1 = (bf16[1024,1536]{1,0:T(8,128)(2,1)S(1)}, bf16[256,2176]{1,0:T(8,128)(2,1)S(1)}, bf16[256,2176]{1,0:T(8,128)(2,1)S(1)}) custom-call(s32[6]{0:T(128)S(1)} %stack.21.info_ref, bf16[1024,1536]{1,0:T(8,128)(2,1)} %get-tuple-element.110.qkv_ref, bf16[8,4,128,256]{3,2,1,0:T(8,128)(2,1)} %get-tuple-element.111.prob_ref, ...), custom_call_target="tpu_custom_call" | custom-call | flops 1000 | bytes 1000 | tf_op jit(solution)/shard_map/attend_back/pallas_call | solution.py:55
  63.2 2.8 %collective-permute-done.6.arrived_ref = bf16[512,1024]{1,0:T(8,128)(2,1)} collective-permute-done((bf16[512,1024]{1,0:T(8,128)(2,1)}, bf16[512,1024]{1,0:T(8,128)(2,1)}, u32[]{:S(2)}, u32[]{:S(2)}) %collective-permute-start.6) | collective-permute-done | bytes 1048608 | tf_op jit(solution)/shard_map/ppermute | solution.py:785
  65.9 1.8 %split.1 = (bf16[256,1024]{1,0:T(8,128)(2,1)S(1)}, bf16[256,1024]{1,0:T(8,128)(2,1)S(1)}) custom-call(s32[6]{0:T(128)S(1)} %stack.21.info_ref, bf16[512,1024]{1,0:T(8,128)(2,1)S(1)} %copy-done.7, bf16[512,1024]{1,0:T(8,128)(2,1)S(1)} %copy-done.2, bf16[512,1024]{1,0:T(8,128)(2,1)S(1)} %collective-permute-done.5.own_ref, ...), custom_call_target="tpu_custom_call" | custom-call | flops 1000 | bytes 1000 | tf_op jit(solution)/shard_map/split/pallas_call | solution.py:512
  67.8 1.8 %collective-permute-start.8 = (bf16[256,1024]{1,0:T(8,128)(2,1)S(1)}, bf16[256,1024]{1,0:T(8,128)(2,1)S(1)}, u32[]{:S(2)}, u32[]{:S(2)}) collective-permute-start(bf16[256,1024]{1,0:T(8,128)(2,1)S(1)} %get-tuple-element.130), channel_id=1, source_target_pairs={{0,4},{1,5},{2,3},{3,2},{4,0},{5,1},{6,7},{7,6},{8,12},{9,13},{10,... | collective-permute-start | bytes 1572872 | tf_op jit(solution)/shard_map/ppermute | solution.py:785
  69.6 0.3 add_convert_fusion
  70.0 0.9 collective-permute-start.9
  70.9 5.5 %first_back.1 = f32[1024,512]{1,0:T(8,128)} custom-call(s32[6]{0:T(128)S(1)} %stack.21.info_ref, bf16[1024,1536]{1,0:T(8,128)(2,1)S(1)} %get-tuple-element.125.dqkv_ref, bf16[512,1536]{1,0:T(8,128)(2,1)S(1)} %copy-done, bf16[1024,512]{1,0:T(8,128)(2,1)} %tok_ref.2, f32[1024,512]{1,0:T(8,128)} %get-tuple-element.126.gres_ref, f32[1,512]{1,0:T(1,128)} %bitcast.14), custom_call_target="tpu_custom_call" | custom-call | flops 1000 | bytes 1000 | tf_op jit(solution)/shard_map/first_back/pallas_call | solution.py:55
  76.4 0.7 collective-permute-done.8
  77.0 0.2 add_convert_fusion.2
  77.3 1.9 %collective-permute-start.10 = (bf16[128,1024]{1,0:T(8,128)(2,1)S(1)}, bf16[128,1024]{1,0:T(8,128)(2,1)S(1)}, u32[]{:S(2)}, u32[]{:S(2)}) collective-permute-start(bf16[128,1024]{1,0:T(8,128)(2,1)S(1)} %get-tuple-element.176), channel_id=1, source_target_pairs={{0,8},{1,9},{2,10},{3,11},{4,12},{5,13},{6,14},{7,15},{8,0},{9,1},... | collective-permute-start | bytes 786440 | tf_op jit(solution)/shard_map/ppermute | solution.py:785
  79.2 5.0 %collective-permute-done.9 = bf16[128,2176]{1,0:T(8,128)(2,1)S(1)} collective-permute-done((bf16[128,2176]{1,0:T(8,128)(2,1)S(1)}, bf16[128,2176]{1,0:T(8,128)(2,1)S(1)}, u32[]{:S(2)}, u32[]{:S(2)}) %collective-permute-start.9) | collective-permute-done | bytes 557088 | tf_op jit(solution)/shard_map/ppermute | solution.py:785
  84.2 0.1 add_convert_fusion.1
  84.4 2.4 %collective-permute-start.11 = (bf16[64,2176]{1,0:T(8,128)(2,1)S(1)}, bf16[64,2176]{1,0:T(8,128)(2,1)S(1)}, u32[]{:S(2)}, u32[]{:S(2)}) collective-permute-start(bf16[64,2176]{1,0:T(8,128)(2,1)S(1)} %get-tuple-element.175), channel_id=1, source_target_pairs={{0,1},{1,0},{2,6},{3,7},{4,5},{5,4},{6,2},{7,3},{8,9},{9,8},{10,14... | collective-permute-start | bytes 835592 | tf_op jit(solution)/shard_map/ppermute | solution.py:785
  86.9 5.9 %collective-permute-done.11 = bf16[64,2176]{1,0:T(8,128)(2,1)S(1)} collective-permute-done((bf16[64,2176]{1,0:T(8,128)(2,1)S(1)}, bf16[64,2176]{1,0:T(8,128)(2,1)S(1)}, u32[]{:S(2)}, u32[]{:S(2)}) %collective-permute-start.11) | collective-permute-done | bytes 278560 | tf_op jit(solution)/shard_map/ppermute | solution.py:785
  92.9 2.0 %collective-permute-start.12 = (bf16[32,2176]{1,0:T(8,128)(2,1)S(1)}, bf16[32,2176]{1,0:T(8,128)(2,1)S(1)}, u32[]{:S(2)}, u32[]{:S(2)}) collective-permute-start(bf16[32,2176]{1,0:T(8,128)(2,1)S(1)} %get-tuple-element.178), channel_id=1, source_target_pairs={{0,8},{1,9},{2,3},{3,2},{4,12},{5,13},{6,7},{7,6},{8,0},{9,1},{10,... | collective-permute-start | bytes 417800 | tf_op jit(solution)/shard_map/ppermute | solution.py:785
  94.9 2.6 %collective-permute-start.13 = (bf16[128,1024]{1,0:T(8,128)(2,1)S(1)}, bf16[128,1024]{1,0:T(8,128)(2,1)S(1)}, u32[]{:S(2)}, u32[]{:S(2)}) collective-permute-start(bf16[128,1024]{1,0:T(8,128)(2,1)S(1)} %add_convert_fusion.5), channel_id=1, source_target_pairs={{0,16},{1,17},{2,18},{3,19},{4,20},{5,21},{6,22},{7,23},{8,24},{9,... | collective-permute-start | bytes 786440 | tf_op jit(solution)/shard_map/ppermute | solution.py:785
  97.5 0.6 collective-permute-done.12
  98.2 5.5 %collective-permute-start.14 = (bf16[32,2176]{1,0:T(8,128)(2,1)S(1)}, bf16[32,2176]{1,0:T(8,128)(2,1)S(1)}, u32[]{:S(2)}, u32[]{:S(2)}) collective-permute-start(bf16[32,2176]{1,0:T(8,128)(2,1)S(1)} %add_convert_fusion.7), channel_id=1, source_target_pairs={{0,16},{1,17},{2,18},{3,19},{4,20},{5,21},{6,22},{7,23},{8,24},{9,... | collective-permute-start | bytes 417800 | tf_op jit(solution)/shard_map/ppermute | solution.py:785
  103.7 1.5 %collective-permute-done.13 = bf16[128,1024]{1,0:T(8,128)(2,1)S(1)} collective-permute-done((bf16[128,1024]{1,0:T(8,128)(2,1)S(1)}, bf16[128,1024]{1,0:T(8,128)(2,1)S(1)}, u32[]{:S(2)}, u32[]{:S(2)}) %collective-permute-start.13) | collective-permute-done | bytes 262176 | tf_op jit(solution)/shard_map/ppermute | solution.py:785
  105.2 1.6 %collective-permute-start.15 = (bf16[128,1024]{1,0:T(8,128)(2,1)S(1)}, bf16[128,1024]{1,0:T(8,128)(2,1)S(1)}, u32[]{:S(2)}, u32[]{:S(2)}) collective-permute-start(bf16[128,1024]{1,0:T(8,128)(2,1)S(1)} %add_convert_fusion.4), channel_id=1, source_target_pairs={{0,8},{1,9},{2,10},{3,11},{4,12},{5,13},{6,14},{7,15},{8,0},{9,1},... | collective-permute-start | bytes 786440 | tf_op jit(solution)/shard_map/ppermute | solution.py:785
  106.8 3.0 %collective-permute-start.16 = (bf16[32,2176]{1,0:T(8,128)(2,1)S(1)}, bf16[32,2176]{1,0:T(8,128)(2,1)S(1)}, u32[]{:S(2)}, u32[]{:S(2)}) collective-permute-start(bf16[32,2176]{1,0:T(8,128)(2,1)S(1)} %add_convert_fusion.6), channel_id=1, source_target_pairs={{0,8},{1,9},{2,6},{3,7},{4,12},{5,13},{6,2},{7,3},{8,0},{9,1},{10,... | collective-permute-start | bytes 417800 | tf_op jit(solution)/shard_map/ppermute | solution.py:785
  109.8 1.8 %collective-permute-done.15 = bf16[128,1024]{1,0:T(8,128)(2,1)S(1)} collective-permute-done((bf16[128,1024]{1,0:T(8,128)(2,1)S(1)}, bf16[128,1024]{1,0:T(8,128)(2,1)S(1)}, u32[]{:S(2)}, u32[]{:S(2)}) %collective-permute-start.15) | collective-permute-done | bytes 262176 | tf_op jit(solution)/shard_map/ppermute | solution.py:785
  111.7 1.6 %collective-permute-start.18 = (bf16[256,1024]{1,0:T(8,128)(2,1)S(1)}, bf16[256,1024]{1,0:T(8,128)(2,1)S(1)}, u32[]{:S(2)}, u32[]{:S(2)}) collective-permute-start(bf16[256,1024]{1,0:T(8,128)(2,1)S(1)} %constant_dynamic-update-slice_fusion), channel_id=1, source_target_pairs={{0,4},{1,5},{2,6},{3,7},{4,0},{5,1},{6,2},{7,3},{8,12},{9,13},{10,... | collective-permute-start | bytes 1572872 | tf_op jit(solution)/shard_map/ppermute | solution.py:785
  113.4 2.8 %collective-permute-start.17 = (bf16[64,2176]{1,0:T(8,128)(2,1)S(1)}, bf16[64,2176]{1,0:T(8,128)(2,1)S(1)}, u32[]{:S(2)}, u32[]{:S(2)}) collective-permute-start(bf16[64,2176]{1,0:T(8,128)(2,1)S(1)} %constant_dynamic-update-slice_fusion.2), channel_id=1, source_target_pairs={{0,1},{1,0},{2,3},{3,2},{4,5},{5,4},{6,7},{7,6},{8,9},{9,8},{10,11... | collective-permute-start | bytes 835592 | tf_op jit(solution)/shard_map/ppermute | solution.py:785
  116.2 4.5 %collective-permute-done.17 = bf16[64,2176]{1,0:T(8,128)(2,1)S(1)} collective-permute-done((bf16[64,2176]{1,0:T(8,128)(2,1)S(1)}, bf16[64,2176]{1,0:T(8,128)(2,1)S(1)}, u32[]{:S(2)}, u32[]{:S(2)}) %collective-permute-start.17) | collective-permute-done | bytes 278560 | tf_op jit(solution)/shard_map/ppermute | solution.py:785
  120.8 0.1 collective-permute-done.18
  121.1 1.6 %collective-permute-start.19 = (bf16[128,2176]{1,0:T(8,128)(2,1)S(1)}, bf16[128,2176]{1,0:T(8,128)(2,1)S(1)}, u32[]{:S(2)}, u32[]{:S(2)}) collective-permute-start(bf16[128,2176]{1,0:T(8,128)(2,1)S(1)} %constant_dynamic-update-slice_fusion.4.refs_0_), channel_id=1, source_target_pairs={{0,4},{1,5},{2,10},{3,11},{4,0},{5,1},{6,14},{7,15},{8,12},{9,13},... | collective-permute-start | bytes 1671176 | tf_op jit(solution)/shard_map/ppermute | solution.py:785
  122.7 0.5 collective-permute-start.21
  123.2 0.5 collective-permute-done.20.other_ref
  123.7 3.1 %ffn_end.1 = (f32[512,1024]{1,0:T(8,128)}, f32[1024,512]{1,0:T(8,128)}) custom-call(s32[6]{0:T(128)S(1)} %stack.21.info_ref, bf16[512,1024]{1,0:T(8,128)(2,1)S(1)} %constant_dynamic-update-slice_fusion.6.keep_ref, bf16[512,1024]{1,0:T(8,128)(2,1)S(1)} %collective-permute-done.20.other_ref), custom_call_target="tpu_custom_call" | custom-call | flops 1000 | bytes 1000 | tf_op jit(solution)/shard_map/ffn_end/pallas_call | solution.py:55
  126.8 3.9 %collective-permute-done.19.refs_1_ = bf16[128,2176]{1,0:T(8,128)(2,1)S(1)} collective-permute-done((bf16[128,2176]{1,0:T(8,128)(2,1)S(1)}, bf16[128,2176]{1,0:T(8,128)(2,1)S(1)}, u32[]{:S(2)}, u32[]{:S(2)}) %collective-permute-start.19) | collective-permute-done | bytes 557088 | tf_op jit(solution)/shard_map/ppermute | solution.py:785
  130.7 2.0 %collective-permute-done.22.refs_3_ = bf16[128,2176]{1,0:T(8,128)(2,1)S(1)} collective-permute-done((bf16[128,2176]{1,0:T(8,128)(2,1)S(1)}, bf16[128,2176]{1,0:T(8,128)(2,1)S(1)}, u32[]{:S(2)}, u32[]{:S(2)}) %collective-permute-start.22) | collective-permute-done | bytes 557088 | tf_op jit(solution)/shard_map/ppermute | solution.py:785
  132.6 4.6 %attend_end.1 = (f32[512,1536]{1,0:T(8,128)}, f32[512,512]{1,0:T(8,128)}, f32[512]{0:T(512)}, f32[512]{0:T(512)}, f32[512]{0:T(512)}, /*index=5*/f32[512]{0:T(512)}, f32[512]{0:T(512)}, f32[1024]{0:T(1024)}) custom-call(s32[6]{0:T(128)S(1)} %stack.21.info_ref, bf16[128,2176]{1,0:T(8,128)(2,1)S(1)} %constant_dynamic-update-slice_fusion.4.refs_0_, ...), custom_call_target="tpu_custom_call" | custom-call | flops 1000 | bytes 1000 | tf_op jit(solution)/shard_map/attend_end/pallas_call | solution.py:55
  (51 shorter events, 0.9 us)
Async XLA Ops:
  0.6 5.1 %copy-start = (bf16[512,1536]{1,0:T(8,128)(2,1)S(1)}, bf16[512,1536]{1,0:T(8,128)(2,1)}, u32[]{:S(2)}) copy-start(bf16[512,1536]{1,0:T(8,128)(2,1)} %refs_4_.1) | copy-start | bytes 4718596
  0.7 5.1 %copy-start.5 = (bf16[512,512]{1,0:T(8,128)(2,1)S(1)}, bf16[512,512]{1,0:T(8,128)(2,1)}, u32[]{:S(2)}) copy-start(bf16[512,512]{1,0:T(8,128)(2,1)} %wout_ref.3) | copy-start | bytes 1572868
  2.6 12.1 %copy-start.3 = (bf16[512,1024]{1,0:T(8,128)(2,1)S(1)}, bf16[512,1024]{1,0:T(8,128)(2,1)}, u32[]{:S(2)}) copy-start(bf16[512,1024]{1,0:T(8,128)(2,1)} %up_ref.3) | copy-start | bytes 3145732
  2.6 12.1 %copy-start.4 = (bf16[1024,512]{1,0:T(8,128)(2,1)S(1)}, bf16[1024,512]{1,0:T(8,128)(2,1)}, u32[]{:S(2)}) copy-start(bf16[1024,512]{1,0:T(8,128)(2,1)} %down_ref.3) | copy-start | bytes 3145732
  2.6 26.5 %collective-permute-start = (bf16[528,512]{1,0:T(8,128)(2,1)S(1)}, bf16[528,512]{1,0:T(8,128)(2,1)S(1)}, u32[]{:S(2)}, u32[]{:S(2)}) collective-permute-start(bf16[528,512]{1,0:T(8,128)(2,1)S(1)} %get-tuple-element.102), channel_id=1, source_target_pairs={{0,1},{1,0},{2,3},{3,2},{4,5},{5,4},{6,7},{7,6},{8,9},{9,8},{10,11... | collective-permute-start | bytes 1622024 | tf_op jit(solution)/shard_map/ppermute | solution.py:785
  5.6 23.5 %collective-permute-start.1 = (bf16[512,512]{1,0:T(8,128)(2,1)S(1)}, bf16[512,512]{1,0:T(8,128)(2,1)S(1)}, u32[]{:S(2)}, u32[]{:S(2)}) collective-permute-start(bf16[512,512]{1,0:T(8,128)(2,1)S(1)} %get-tuple-element.103), channel_id=1, source_target_pairs={{0,1},{1,0},{2,3},{3,2},{4,5},{5,4},{6,7},{7,6},{8,9},{9,8},{10,11... | collective-permute-start | bytes 1572872 | tf_op jit(solution)/shard_map/ppermute | solution.py:785
  29.1 3.4 %collective-permute-start.2 = (bf16[528,512]{1,0:T(8,128)(2,1)S(1)}, bf16[528,512]{1,0:T(8,128)(2,1)S(1)}, u32[]{:S(2)}, u32[]{:S(2)}) collective-permute-start(bf16[528,512]{1,0:T(8,128)(2,1)S(1)} %collective-permute-done.refs_0_), channel_id=1, source_target_pairs={{0,2},{1,3},{2,0},{3,1},{4,6},{5,7},{6,4},{7,5},{8,10},{9,11},{10,... | collective-permute-start | bytes 1622024 | tf_op jit(solution)/shard_map/ppermute | solution.py:785
  29.1 3.4 %collective-permute-start.3 = (bf16[512,512]{1,0:T(8,128)(2,1)S(1)}, bf16[512,512]{1,0:T(8,128)(2,1)S(1)}, u32[]{:S(2)}, u32[]{:S(2)}) collective-permute-start(bf16[512,512]{1,0:T(8,128)(2,1)S(1)} %collective-permute-done.1.refs_2_), channel_id=1, source_target_pairs={{0,2},{1,3},{2,0},{3,1},{4,6},{5,7},{6,4},{7,5},{8,10},{9,11},{10,... | collective-permute-start | bytes 1572872 | tf_op jit(solution)/shard_map/ppermute | solution.py:785
  29.7 16.9 %collective-permute-start.5 = (bf16[512,1024]{1,0:T(8,128)(2,1)}, bf16[512,1024]{1,0:T(8,128)(2,1)S(1)}, u32[]{:S(2)}, u32[]{:S(2)}) collective-permute-start(bf16[512,1024]{1,0:T(8,128)(2,1)} %get-tuple-element.109), channel_id=1, source_target_pairs={{0,2},{1,3},{2,0},{3,1},{4,6},{5,7},{6,4},{7,5},{8,10},{9,11},{10,... | collective-permute-start | bytes 3145736 | tf_op jit(solution)/shard_map/ppermute | solution.py:785
  46.3 4.5 %copy-start.6 = (bf16[512,1024]{1,0:T(8,128)(2,1)}, bf16[512,1024]{1,0:T(8,128)(2,1)S(1)}, u32[]{:S(2)}) copy-start(bf16[512,1024]{1,0:T(8,128)(2,1)S(1)} %get-tuple-element.107.keep_ref) | copy-start | bytes 3145732
  46.3 2.7 %collective-permute-start.4 = (bf16[512,1024]{1,0:T(8,128)(2,1)S(1)}, bf16[512,1024]{1,0:T(8,128)(2,1)S(1)}, u32[]{:S(2)}, u32[]{:S(2)}) collective-permute-start(bf16[512,1024]{1,0:T(8,128)(2,1)S(1)} %get-tuple-element.108), channel_id=1, source_target_pairs={{0,2},{1,3},{2,0},{3,1},{4,6},{5,7},{6,4},{7,5},{8,10},{9,11},{10,... | collective-permute-start | bytes 3145736 | tf_op jit(solution)/shard_map/ppermute | solution.py:785
  49.1 1.8 %copy-start.1 = (bf16[512,1024]{1,0:T(8,128)(2,1)}, bf16[512,1024]{1,0:T(8,128)(2,1)S(1)}, u32[]{:S(2)}) copy-start(bf16[512,1024]{1,0:T(8,128)(2,1)S(1)} %collective-permute-done.4.got_ref) | copy-start | bytes 3145732
  50.8 15.1 %collective-permute-start.6 = (bf16[512,1024]{1,0:T(8,128)(2,1)}, bf16[512,1024]{1,0:T(8,128)(2,1)}, u32[]{:S(2)}, u32[]{:S(2)}) collective-permute-start(bf16[512,1024]{1,0:T(8,128)(2,1)} %join.1), channel_id=1, source_target_pairs={{0,1},{1,0},{2,6},{3,7},{4,5},{5,4},{6,2},{7,3},{8,9},{9,8},{10,14... | collective-permute-start | bytes 3145736 | tf_op jit(solution)/shard_map/ppermute | solution.py:785
  53.3 12.6 %copy-start.2 = (bf16[512,1024]{1,0:T(8,128)(2,1)S(1)}, bf16[512,1024]{1,0:T(8,128)(2,1)}, u32[]{:S(2)}) copy-start(bf16[512,1024]{1,0:T(8,128)(2,1)} %copy-done.1) | copy-start | bytes 3145732
  53.3 12.6 %copy-start.7 = (bf16[512,1024]{1,0:T(8,128)(2,1)S(1)}, bf16[512,1024]{1,0:T(8,128)(2,1)}, u32[]{:S(2)}) copy-start(bf16[512,1024]{1,0:T(8,128)(2,1)} %copy-done.6) | copy-start | bytes 3145732
  65.9 3.7 %collective-permute-start.7 = (bf16[256,2176]{1,0:T(8,128)(2,1)S(1)}, bf16[256,2176]{1,0:T(8,128)(2,1)S(1)}, u32[]{:S(2)}, u32[]{:S(2)}) collective-permute-start(bf16[256,2176]{1,0:T(8,128)(2,1)S(1)} %get-tuple-element.124), channel_id=1, source_target_pairs={{0,2},{1,3},{2,0},{3,1},{4,6},{5,7},{6,4},{7,5},{8,10},{9,11},{10,... | collective-permute-start | bytes 3342344 | tf_op jit(solution)/shard_map/ppermute | solution.py:785
  67.8 9.2 %collective-permute-start.8 = (bf16[256,1024]{1,0:T(8,128)(2,1)S(1)}, bf16[256,1024]{1,0:T(8,128)(2,1)S(1)}, u32[]{:S(2)}, u32[]{:S(2)}) collective-permute-start(bf16[256,1024]{1,0:T(8,128)(2,1)S(1)} %get-tuple-element.130), channel_id=1, source_target_pairs={{0,4},{1,5},{2,3},{3,2},{4,0},{5,1},{6,7},{7,6},{8,12},{9,13},{10,... | collective-permute-start | bytes 1572872 | tf_op jit(solution)/shard_map/ppermute | solution.py:785
  70.0 14.2 %collective-permute-start.9 = (bf16[128,2176]{1,0:T(8,128)(2,1)S(1)}, bf16[128,2176]{1,0:T(8,128)(2,1)S(1)}, u32[]{:S(2)}, u32[]{:S(2)}) collective-permute-start(bf16[128,2176]{1,0:T(8,128)(2,1)S(1)} %get-tuple-element.172), channel_id=1, source_target_pairs={{0,4},{1,5},{2,10},{3,11},{4,0},{5,1},{6,14},{7,15},{8,12},{9,13},... | collective-permute-start | bytes 1671176 | tf_op jit(solution)/shard_map/ppermute | solution.py:785
  77.3 9.5 %collective-permute-start.10 = (bf16[128,1024]{1,0:T(8,128)(2,1)S(1)}, bf16[128,1024]{1,0:T(8,128)(2,1)S(1)}, u32[]{:S(2)}, u32[]{:S(2)}) collective-permute-start(bf16[128,1024]{1,0:T(8,128)(2,1)S(1)} %get-tuple-element.176), channel_id=1, source_target_pairs={{0,8},{1,9},{2,10},{3,11},{4,12},{5,13},{6,14},{7,15},{8,0},{9,1},... | collective-permute-start | bytes 786440 | tf_op jit(solution)/shard_map/ppermute | solution.py:785
  84.4 8.4 %collective-permute-start.11 = (bf16[64,2176]{1,0:T(8,128)(2,1)S(1)}, bf16[64,2176]{1,0:T(8,128)(2,1)S(1)}, u32[]{:S(2)}, u32[]{:S(2)}) collective-permute-start(bf16[64,2176]{1,0:T(8,128)(2,1)S(1)} %get-tuple-element.175), channel_id=1, source_target_pairs={{0,1},{1,0},{2,6},{3,7},{4,5},{5,4},{6,2},{7,3},{8,9},{9,8},{10,14... | collective-permute-start | bytes 835592 | tf_op jit(solution)/shard_map/ppermute | solution.py:785
  92.9 5.2 %collective-permute-start.12 = (bf16[32,2176]{1,0:T(8,128)(2,1)S(1)}, bf16[32,2176]{1,0:T(8,128)(2,1)S(1)}, u32[]{:S(2)}, u32[]{:S(2)}) collective-permute-start(bf16[32,2176]{1,0:T(8,128)(2,1)S(1)} %get-tuple-element.178), channel_id=1, source_target_pairs={{0,8},{1,9},{2,3},{3,2},{4,12},{5,13},{6,7},{7,6},{8,0},{9,1},{10,... | collective-permute-start | bytes 417800 | tf_op jit(solution)/shard_map/ppermute | solution.py:785
  94.9 10.2 %collective-permute-start.13 = (bf16[128,1024]{1,0:T(8,128)(2,1)S(1)}, bf16[128,1024]{1,0:T(8,128)(2,1)S(1)}, u32[]{:S(2)}, u32[]{:S(2)}) collective-permute-start(bf16[128,1024]{1,0:T(8,128)(2,1)S(1)} %add_convert_fusion.5), channel_id=1, source_target_pairs={{0,16},{1,17},{2,18},{3,19},{4,20},{5,21},{6,22},{7,23},{8,24},{9,... | collective-permute-start | bytes 786440 | tf_op jit(solution)/shard_map/ppermute | solution.py:785
  98.2 8.6 %collective-permute-start.14 = (bf16[32,2176]{1,0:T(8,128)(2,1)S(1)}, bf16[32,2176]{1,0:T(8,128)(2,1)S(1)}, u32[]{:S(2)}, u32[]{:S(2)}) collective-permute-start(bf16[32,2176]{1,0:T(8,128)(2,1)S(1)} %add_convert_fusion.7), channel_id=1, source_target_pairs={{0,16},{1,17},{2,18},{3,19},{4,20},{5,21},{6,22},{7,23},{8,24},{9,... | collective-permute-start | bytes 417800 | tf_op jit(solution)/shard_map/ppermute | solution.py:785
  105.2 6.4 %collective-permute-start.15 = (bf16[128,1024]{1,0:T(8,128)(2,1)S(1)}, bf16[128,1024]{1,0:T(8,128)(2,1)S(1)}, u32[]{:S(2)}, u32[]{:S(2)}) collective-permute-start(bf16[128,1024]{1,0:T(8,128)(2,1)S(1)} %add_convert_fusion.4), channel_id=1, source_target_pairs={{0,8},{1,9},{2,10},{3,11},{4,12},{5,13},{6,14},{7,15},{8,0},{9,1},... | collective-permute-start | bytes 786440 | tf_op jit(solution)/shard_map/ppermute | solution.py:785
  106.8 6.5 %collective-permute-start.16 = (bf16[32,2176]{1,0:T(8,128)(2,1)S(1)}, bf16[32,2176]{1,0:T(8,128)(2,1)S(1)}, u32[]{:S(2)}, u32[]{:S(2)}) collective-permute-start(bf16[32,2176]{1,0:T(8,128)(2,1)S(1)} %add_convert_fusion.6), channel_id=1, source_target_pairs={{0,8},{1,9},{2,6},{3,7},{4,12},{5,13},{6,2},{7,3},{8,0},{9,1},{10,... | collective-permute-start | bytes 417800 | tf_op jit(solution)/shard_map/ppermute | solution.py:785
  111.7 9.2 %collective-permute-start.18 = (bf16[256,1024]{1,0:T(8,128)(2,1)S(1)}, bf16[256,1024]{1,0:T(8,128)(2,1)S(1)}, u32[]{:S(2)}, u32[]{:S(2)}) collective-permute-start(bf16[256,1024]{1,0:T(8,128)(2,1)S(1)} %constant_dynamic-update-slice_fusion), channel_id=1, source_target_pairs={{0,4},{1,5},{2,6},{3,7},{4,0},{5,1},{6,2},{7,3},{8,12},{9,13},{10,... | collective-permute-start | bytes 1572872 | tf_op jit(solution)/shard_map/ppermute | solution.py:785
  113.4 7.4 %collective-permute-start.17 = (bf16[64,2176]{1,0:T(8,128)(2,1)S(1)}, bf16[64,2176]{1,0:T(8,128)(2,1)S(1)}, u32[]{:S(2)}, u32[]{:S(2)}) collective-permute-start(bf16[64,2176]{1,0:T(8,128)(2,1)S(1)} %constant_dynamic-update-slice_fusion.2), channel_id=1, source_target_pairs={{0,1},{1,0},{2,3},{3,2},{4,5},{5,4},{6,7},{7,6},{8,9},{9,8},{10,11... | collective-permute-start | bytes 835592 | tf_op jit(solution)/shard_map/ppermute | solution.py:785
  121.0 2.7 %collective-permute-start.20 = (bf16[512,1024]{1,0:T(8,128)(2,1)S(1)}, bf16[512,1024]{1,0:T(8,128)(2,1)S(1)}, u32[]{:S(2)}, u32[]{:S(2)}) collective-permute-start(bf16[512,1024]{1,0:T(8,128)(2,1)S(1)} %constant_dynamic-update-slice_fusion.6.keep_ref), channel_id=1, source_target_pairs={{0,2},{1,3},{2,0},{3,1},{4,6},{5,7},{6,4},{7,5},{8,10},{9,11},{10,... | collective-permute-start | bytes 3145736 | tf_op jit(solution)/shard_map/ppermute | solution.py:785
  121.1 9.6 %collective-permute-start.19 = (bf16[128,2176]{1,0:T(8,128)(2,1)S(1)}, bf16[128,2176]{1,0:T(8,128)(2,1)S(1)}, u32[]{:S(2)}, u32[]{:S(2)}) collective-permute-start(bf16[128,2176]{1,0:T(8,128)(2,1)S(1)} %constant_dynamic-update-slice_fusion.4.refs_0_), channel_id=1, source_target_pairs={{0,4},{1,5},{2,10},{3,11},{4,0},{5,1},{6,14},{7,15},{8,12},{9,13},... | collective-permute-start | bytes 1671176 | tf_op jit(solution)/shard_map/ppermute | solution.py:785
  122.7 8.0 %collective-permute-start.21 = (bf16[128,2176]{1,0:T(8,128)(2,1)S(1)}, bf16[128,2176]{1,0:T(8,128)(2,1)S(1)}, u32[]{:S(2)}, u32[]{:S(2)}) collective-permute-start(bf16[128,2176]{1,0:T(8,128)(2,1)S(1)} %constant_dynamic-update-slice_fusion.4.refs_0_), channel_id=1, source_target_pairs={{0,2},{1,3},{2,0},{3,1},{4,6},{5,7},{6,4},{7,5},{8,10},{9,11},{10,... | collective-permute-start | bytes 1671176 | tf_op jit(solution)/shard_map/ppermute | solution.py:785
  130.7 2.0 %collective-permute-start.22 = (bf16[128,2176]{1,0:T(8,128)(2,1)S(1)}, bf16[128,2176]{1,0:T(8,128)(2,1)S(1)}, u32[]{:S(2)}, u32[]{:S(2)}) collective-permute-start(bf16[128,2176]{1,0:T(8,128)(2,1)S(1)} %collective-permute-done.19.refs_1_), channel_id=1, source_target_pairs={{0,2},{1,3},{2,0},{3,1},{4,6},{5,7},{6,4},{7,5},{8,10},{9,11},{10,... | collective-permute-start | bytes 1671176 | tf_op jit(solution)/shard_map/ppermute | solution.py:785

commit v10 on v9

--- a/solution.py
+++ b/solution.py
@@ -292,7 +292,7 @@
         [rows_of(width)] * 2 + [whole(width, 2 * units)] * 2 + [whole(2, units)],
         [pltpu.VMEM((n, width), F32)] * 2
         + [pltpu.HBM((width, 2 * units), BF)] * 2
-        + [jax.ShapeDtypeStruct((2, units), F32)],
+        + [pltpu.HBM((2, units), F32)],
         [pltpu.VMEM((2, width, 2 * units), F32)],
         info,
         near(second) + far(dy) + (up,) + far(bias) + (down,),
@@ -443,9 +443,9 @@
             jax.ShapeDtypeStruct((n, width), BF),
             pltpu.HBM((n, width), F32),
             pltpu.HBM((n, width), BF),
-            jax.ShapeDtypeStruct((8, width), F32),
+            pltpu.HBM((8, width), F32),
             pltpu.HBM((width, width), F32),
-            jax.ShapeDtypeStruct((count, units), F32),
+            pltpu.HBM((count, units), F32),
         ]
         + [jax.ShapeDtypeStruct((width, 2 * units), BF)] * (count + mixing),
         [
@@ -530,9 +530,9 @@
 
 
 def attend_back_kernel(
-    tables, info_ref, qkv_ref, prob_ref, gmix_ref, tok_ref, vec_ref, dwout_ref, grad_ref, dw_keep_ref, dw_send_ref,
-    dqkv_ref, acc_ref, row_ref,
+    tables, info_ref, qkv_ref, prob_ref, gmix_ref, tok_ref, dwout_ref, vec_ref, *refs
 ):
+    *sums, grad_ref, dw_keep_ref, dw_send_ref, dqkv_ref, acc_ref, row_ref = refs
     at, last = pl.program_id(0), pl.num_programs(0) - 1
     toks, width = tok_ref.shape
     rows, pairs, slots, _ = prob_ref.shape
@@ -543,6 +543,12 @@
         acc_ref[:, 3 * width : 4 * width] = dwout_ref[...]
         row_ref[...] = jnp.zeros_like(row_ref)
         row_ref[SUMS : SUMS + vec_ref.shape[0], :] = vec_ref[...]
+        if sums:
+            own_ref, rest_ref = sums
+            first = SUMS + vec_ref.shape[0]
+            for i in range(2):
+                row_ref[pl.ds(first + 2 * info_ref[5] + i, 1), :] = own_ref[i : i + 1, :]
+                row_ref[pl.ds(first + 2 * (info_ref[5] ^ 1) + (info_ref[0] ^ i), 1), :] = rest_ref[i : i + 1, :]
 
     scale = HEAD ** (-0.5)
     units = [(r, p) for r in range(rows) for p in range(pairs)]
@@ -587,7 +593,7 @@
             dst[to : to + size, :] = acc_ref[rows_at, :].astype(BF)
 
 
-def attend_back(info, tables, qkv, prob, gmix, tokens, vec, dwout):
+def attend_back(info, tables, qkv, prob, gmix, tokens, dwout, *vecs):
     n, width = tokens.shape
     rows, pairs, slots, _ = prob.shape
     per = TOKS // slots
@@ -600,9 +606,9 @@
             pl.BlockSpec((per, pairs, slots, 2 * slots), lambda i, *_: (i, 0, 0, 0)),
             rows_of(width),
             rows_of(width),
-            whole(*vec.shape),
             whole(width, width),
-        ],
+        ]
+        + [whole(*vec.shape) for vec in vecs],
         [rows_of(3 * width)] + [whole(width // 2, 4 * width + LANES)] * 2,
         [pltpu.VMEM((n, 3 * width), BF)] + [jax.ShapeDtypeStruct((width // 2, 4 * width + LANES), BF)] * 2,
         [
@@ -611,7 +617,7 @@
             pltpu.VMEM((LANES, width), F32),
         ],
         info,
-        far(qkv, prob, gmix, tokens, vec, dwout),
+        far(qkv, prob, gmix, tokens, dwout, *vecs),
     )
 
 
@@ -829,7 +835,7 @@
     mixing = narrow == 2 and len(wide_masks) == 3
     if mixing:
         y, low, high = wide_masks
-        ff_in, ff_rest, ff_out = ([y, low], [y, low]), ([high], [high]), ([y, low], [y, low])
+        ff_in, ff_rest, ff_out = ([y, low], [y, low]), ([high], [high]), ([low, y], [low, y])
         at_in, at_rest, at_out = ([y, 1, low], [low, y, 1]), ([high], [high]), ([y, 1, low], [low, 1, y])
         turns = "FAFAAFAFAAFFAA"
     else:
@@ -879,13 +885,16 @@
     block_out, gres, gmix, vec, dwout, bias_rest = rest[:6]
     grads = rest[6:]
 
-    b_rest = bias_rest.reshape(-1, 2, units)
-    b_rest = jnp.where(core == 0, b_rest, jnp.flip(b_rest, axis=1))
-    b_all = jnp.concatenate([bias_own[None], b_rest], axis=0)
-    for bit in range(narrow.bit_length() - 1):
-        flipped = jnp.flip(b_all.reshape(-1, 2, (1 << bit) * 2, units), axis=1).reshape(b_all.shape)
-        b_all = jnp.where(narrow_at >> bit & 1, flipped, b_all)
-    vec = jnp.concatenate([vec, b_all.reshape(-1, width)], axis=0)
+    if narrow == 2 and units == width:
+        vecs = (vec, bias_own, bias_rest)
+    else:
+        b_rest = bias_rest.reshape(-1, 2, units)
+        b_rest = jnp.where(core == 0, b_rest, jnp.flip(b_rest, axis=1))
+        b_all = jnp.concatenate([bias_own[None], b_rest], axis=0)
+        for bit in range(narrow.bit_length() - 1):
+            flipped = jnp.flip(b_all.reshape(-1, 2, (1 << bit) * 2, units), axis=1).reshape(b_all.shape)
+            b_all = jnp.where(narrow_at >> bit & 1, flipped, b_all)
+        vecs = (jnp.concatenate([vec, b_all.reshape(-1, width)], axis=0),)
 
     if mixing:
         ff_keep, ff_send, away = grads
@@ -900,7 +909,7 @@
             held = [add(held[j], swap(held[j + mask], mask)) for j in range(mask)]
         ff_keep = held[0]
 
-    dqkv, keep, send = attend_back(info, at_tables(at_in), qkv, prob, gmix, tokens_in, vec, dwout)
+    dqkv, keep, send = attend_back(info, at_tables(at_in), qkv, prob, gmix, tokens_in, dwout, *vecs)
     if mixing:
         send, ff_got = after(send, ff_got)
         ff_keep, ff_send = split(info, ff_keep, got, got_own, ff_got)

time: 138 us -> 136 us (0.986)
  waiting for transfers between devices: 38 us -> 45.1 us
  starting transfers between devices: 33.9 us -> 28.1 us
  Pallas kernels: 62.4 us -> 60.5 us
    ppermute x23, waiting for transfers between devices: 38 us -> 45.1 us  [swap(): return lax.ppermute(value, AXES, pairs)]
    ppermute x23, starting transfers between devices: 33.9 us -> 28.1 us  [swap(): return lax.ppermute(value, AXES, pairs)]
    pallas_call x2, Pallas kernels: 3.6 us -> 1.93 us  [direct(): pl.pallas_call(kernel, in_specs=[pl.BlockSpec(memory_space=pltpu.SMEM)] +...]
where the time goes in v10:
time: 136 us
  Pallas kernels  60.5 us (44%)
  waiting for transfers between devices  45.1 us (33%)
  starting transfers between devices  28.1 us (21%)
    pallas_call x8, Pallas kernels, call(): pl.pallas_call(kernel, grid_spec=pltpu.PrefetchScalarGridSpec(num_scalar_...  58.6 us
    ppermute x23, waiting for transfers between devices, swap(): return lax.ppermute(value, AXES, pairs)  45.1 us
    ppermute x23, starting transfers between devices, swap(): return lax.ppermute(value, AXES, pairs)  28.1 us
  transfers between devices with their start and end apart: 23, of which 15 were waited for; matrix products, arithmetic and copies ran while one was open for 1% of the time, Pallas kernels for 39%

profile of v10, /device:TPU:0, one launch (start us, length us, event | category | flops | bytes accessed | tf_op | source)
XLA Modules:
  0.0 136.2 jit_solution(13512846108393017570)
XLA Ops:
  0.7 0.1 stack.21.info_ref
  0.8 1.8 %pack.1 = (bf16[528,512]{1,0:T(8,128)(2,1)S(1)}, bf16[512,512]{1,0:T(8,128)(2,1)S(1)}) custom-call(s32[6]{0:T(128)S(1)} %stack.21.info_ref, bf16[512,1024]{1,0:T(8,128)(2,1)} %up_ref.3, bf16[1024]{0:T(1024)(128)(2,1)} %bias_ref.3, bf16[1024,512]{1,0:T(8,128)(2,1)} %down_ref.3), custom_call_target="tpu_custom_call" | custom-call | flops 1000 | bytes 1000 | tf_op jit(solution)/shard_map/pack/pallas_call | solution.py:55
  2.6 3.0 %collective-permute-start = (bf16[528,512]{1,0:T(8,128)(2,1)S(1)}, bf16[528,512]{1,0:T(8,128)(2,1)S(1)}, u32[]{:S(2)}, u32[]{:S(2)}) collective-permute-start(bf16[528,512]{1,0:T(8,128)(2,1)S(1)} %get-tuple-element.102), channel_id=1, source_target_pairs={{0,1},{1,0},{2,3},{3,2},{4,5},{5,4},{6,7},{7,6},{8,9},{9,8},{10,11... | collective-permute-start | bytes 1622024 | tf_op jit(solution)/shard_map/ppermute | solution.py:791
  5.6 0.1 collective-permute-start.1
  5.7 9.0 %attend.1 = (bf16[1024,1536]{1,0:T(8,128)(2,1)}, bf16[8,4,128,256]{3,2,1,0:T(8,128)(2,1)}, bf16[1024,512]{1,0:T(8,128)(2,1)}, f32[1024,512]{1,0:T(8,128)}, bf16[1024,512]{1,0:T(8,128)(2,1)S(1)}) custom-call(s32[6]{0:T(128)S(1)} %stack.21.info_ref, bf16[1024,512]{1,0:T(8,128)(2,1)} %tok_ref.2, f32[1,512]{1,0:T(1,128)} %bitcast.9, f32[1,512]{1,0:T(1,128)} %bitcast.14, ...), custom_call_target="tpu_custom_call" | custom-call | flops 1000 | bytes 1000 | tf_op jit(solution)/shard_map/attend/pallas_call | solution.py:55
  14.7 11.1 %ffn_own.1 = (f32[1024,512]{1,0:T(8,128)S(1)}, f32[1024,512]{1,0:T(8,128)S(1)}, bf16[512,1024]{1,0:T(8,128)(2,1)}, bf16[512,1024]{1,0:T(8,128)(2,1)}, f32[2,512]{1,0:T(2,128)}) custom-call(s32[6]{0:T(128)S(1)} %stack.21.info_ref, bf16[1024,512]{1,0:T(8,128)(2,1)S(1)} %get-tuple-element.95.sec_ref.sec_in, bf16[1024,512]{1,0:T(8,128)(2,1)} %dy_in.1, ...), custom_call_target="tpu_custom_call" | custom-call | flops 1000 | bytes 1000 | tf_op jit(solution)/shard_map/ffn_own/pallas_call | solution.py:55
  25.8 3.3 %collective-permute-done.1.refs_2_ = bf16[512,512]{1,0:T(8,128)(2,1)S(1)} collective-permute-done((bf16[512,512]{1,0:T(8,128)(2,1)S(1)}, bf16[512,512]{1,0:T(8,128)(2,1)S(1)}, u32[]{:S(2)}, u32[]{:S(2)}) %collective-permute-start.1) | collective-permute-done | bytes 524320 | tf_op jit(solution)/shard_map/ppermute | solution.py:791
  29.1 0.5 collective-permute-start.3
  29.7 2.9 %collective-permute-done.3.refs_3_ = bf16[512,512]{1,0:T(8,128)(2,1)S(1)} collective-permute-done((bf16[512,512]{1,0:T(8,128)(2,1)S(1)}, bf16[512,512]{1,0:T(8,128)(2,1)S(1)}, u32[]{:S(2)}, u32[]{:S(2)}) %collective-permute-start.3) | collective-permute-done | bytes 524320 | tf_op jit(solution)/shard_map/ppermute | solution.py:791
  32.6 13.7 %ffn_rest.1 = (bf16[1024,512]{1,0:T(8,128)(2,1)}, f32[1024,512]{1,0:T(8,128)}, bf16[1024,512]{1,0:T(8,128)(2,1)}, f32[8,512]{1,0:T(8,128)}, f32[512,512]{1,0:T(8...) custom-call(s32[6]{0:T(128)S(1)} %stack.21.info_ref, ...), custom_call_target="tpu_custom_call" | custom-call | flops 1000 | bytes 1000 | tf_op jit(solution)/shard_map/ffn_rest/pallas_call | solution.py:55
  46.3 0.2 collective-permute-start.4
  46.5 2.5 %collective-permute-done.4.got_ref = bf16[512,1024]{1,0:T(8,128)(2,1)S(1)} collective-permute-done((bf16[512,1024]{1,0:T(8,128)(2,1)S(1)}, bf16[512,1024]{1,0:T(8,128)(2,1)S(1)}, u32[]{:S(2)}, u32[]{:S(2)}) %collective-permute-start.4) | collective-permute-done | bytes 1048608 | tf_op jit(solution)/shard_map/ppermute | solution.py:791
  49.0 0.8 join.1
  49.8 1.8 %collective-permute-start.6 = (bf16[512,1024]{1,0:T(8,128)(2,1)S(1)}, bf16[512,1024]{1,0:T(8,128)(2,1)S(1)}, u32[]{:S(2)}, u32[]{:S(2)}) collective-permute-start(bf16[512,1024]{1,0:T(8,128)(2,1)S(1)} %join.1), channel_id=1, source_target_pairs={{0,1},{1,0},{2,6},{3,7},{4,5},{5,4},{6,2},{7,3},{8,9},{9,8},{10,14... | collective-permute-start | bytes 3145736 | tf_op jit(solution)/shard_map/ppermute | solution.py:791
  51.6 9.8 %attend_back.1 = (bf16[1024,1536]{1,0:T(8,128)(2,1)S(1)}, bf16[256,2176]{1,0:T(8,128)(2,1)S(1)}, bf16[256,2176]{1,0:T(8,128)(2,1)S(1)}) custom-call(s32[6]{0:T(128)S(1)} %stack.21.info_ref, bf16[1024,1536]{1,0:T(8,128)(2,1)} %get-tuple-element.110.qkv_ref, bf16[8,4,128,256]{3,2,1,0:T(8,128)(2,1)} %get-tuple-element.111.prob_ref, ...), custom_call_target="tpu_custom_call" | custom-call | flops 1000 | bytes 1000 | tf_op jit(solution)/shard_map/attend_back/pallas_call | solution.py:55
  61.4 3.3 %collective-permute-done.6.arrived_ref = bf16[512,1024]{1,0:T(8,128)(2,1)S(1)} collective-permute-done((bf16[512,1024]{1,0:T(8,128)(2,1)S(1)}, bf16[512,1024]{1,0:T(8,128)(2,1)S(1)}, u32[]{:S(2)}, u32[]{:S(2)}) %collective-permute-start.6) | collective-permute-done | bytes 1048608 | tf_op jit(solution)/shard_map/ppermute | solution.py:791
  64.7 1.1 split.1
  65.9 1.8 %collective-permute-start.8 = (bf16[256,1024]{1,0:T(8,128)(2,1)S(1)}, bf16[256,1024]{1,0:T(8,128)(2,1)S(1)}, u32[]{:S(2)}, u32[]{:S(2)}) collective-permute-start(bf16[256,1024]{1,0:T(8,128)(2,1)S(1)} %get-tuple-element.130), channel_id=1, source_target_pairs={{0,4},{1,5},{2,3},{3,2},{4,0},{5,1},{6,7},{7,6},{8,12},{9,13},{10,... | collective-permute-start | bytes 1572872 | tf_op jit(solution)/shard_map/ppermute | solution.py:791
  67.7 0.3 add_convert_fusion
  67.9 0.1 fusion
  68.0 1.6 %collective-permute-start.9 = (bf16[128,2176]{1,0:T(8,128)(2,1)S(1)}, bf16[128,2176]{1,0:T(8,128)(2,1)S(1)}, u32[]{:S(2)}, u32[]{:S(2)}) collective-permute-start(bf16[128,2176]{1,0:T(8,128)(2,1)S(1)} %get-tuple-element.172), channel_id=1, source_target_pairs={{0,4},{1,5},{2,10},{3,11},{4,0},{5,1},{6,14},{7,15},{8,12},{9,13},... | collective-permute-start | bytes 1671176 | tf_op jit(solution)/shard_map/ppermute | solution.py:791
  69.6 5.5 %first_back.1 = f32[1024,512]{1,0:T(8,128)} custom-call(s32[6]{0:T(128)S(1)} %stack.21.info_ref, bf16[1024,1536]{1,0:T(8,128)(2,1)S(1)} %get-tuple-element.125.dqkv_ref, bf16[512,1536]{1,0:T(8,128)(2,1)S(1)} %copy-done, bf16[1024,512]{1,0:T(8,128)(2,1)} %tok_ref.2, f32[1024,512]{1,0:T(8,128)} %get-tuple-element.126.gres_ref, f32[1,512]{1,0:T(1,128)} %bitcast.10), custom_call_target="tpu_custom_call" | custom-call | flops 1000 | bytes 1000 | tf_op jit(solution)/shard_map/first_back/pallas_call | solution.py:55
  75.1 0.2 add_convert_fusion.2
  75.4 1.8 %collective-permute-start.10 = (bf16[128,1024]{1,0:T(8,128)(2,1)S(1)}, bf16[128,1024]{1,0:T(8,128)(2,1)S(1)}, u32[]{:S(2)}, u32[]{:S(2)}) collective-permute-start(bf16[128,1024]{1,0:T(8,128)(2,1)S(1)} %get-tuple-element.176), channel_id=1, source_target_pairs={{0,8},{1,9},{2,10},{3,11},{4,12},{5,13},{6,14},{7,15},{8,0},{9,1},... | collective-permute-start | bytes 786440 | tf_op jit(solution)/shard_map/ppermute | solution.py:791
  77.2 5.0 %collective-permute-done.9 = bf16[128,2176]{1,0:T(8,128)(2,1)S(1)} collective-permute-done((bf16[128,2176]{1,0:T(8,128)(2,1)S(1)}, bf16[128,2176]{1,0:T(8,128)(2,1)S(1)}, u32[]{:S(2)}, u32[]{:S(2)}) %collective-permute-start.9) | collective-permute-done | bytes 557088 | tf_op jit(solution)/shard_map/ppermute | solution.py:791
  82.2 0.1 add_convert_fusion.1
  82.4 2.1 %collective-permute-start.11 = (bf16[64,2176]{1,0:T(8,128)(2,1)S(1)}, bf16[64,2176]{1,0:T(8,128)(2,1)S(1)}, u32[]{:S(2)}, u32[]{:S(2)}) collective-permute-start(bf16[64,2176]{1,0:T(8,128)(2,1)S(1)} %get-tuple-element.175), channel_id=1, source_target_pairs={{0,1},{1,0},{2,6},{3,7},{4,5},{5,4},{6,2},{7,3},{8,9},{9,8},{10,14... | collective-permute-start | bytes 835592 | tf_op jit(solution)/shard_map/ppermute | solution.py:791
  84.6 5.9 %collective-permute-done.11 = bf16[64,2176]{1,0:T(8,128)(2,1)S(1)} collective-permute-done((bf16[64,2176]{1,0:T(8,128)(2,1)S(1)}, bf16[64,2176]{1,0:T(8,128)(2,1)S(1)}, u32[]{:S(2)}, u32[]{:S(2)}) %collective-permute-start.11) | collective-permute-done | bytes 278560 | tf_op jit(solution)/shard_map/ppermute | solution.py:791
  90.7 2.1 %collective-permute-start.12 = (bf16[32,2176]{1,0:T(8,128)(2,1)S(1)}, bf16[32,2176]{1,0:T(8,128)(2,1)S(1)}, u32[]{:S(2)}, u32[]{:S(2)}) collective-permute-start(bf16[32,2176]{1,0:T(8,128)(2,1)S(1)} %get-tuple-element.178), channel_id=1, source_target_pairs={{0,8},{1,9},{2,3},{3,2},{4,12},{5,13},{6,7},{7,6},{8,0},{9,1},{10,... | collective-permute-start | bytes 417800 | tf_op jit(solution)/shard_map/ppermute | solution.py:791
  92.8 2.6 %collective-permute-start.13 = (bf16[128,1024]{1,0:T(8,128)(2,1)S(1)}, bf16[128,1024]{1,0:T(8,128)(2,1)S(1)}, u32[]{:S(2)}, u32[]{:S(2)}) collective-permute-start(bf16[128,1024]{1,0:T(8,128)(2,1)S(1)} %add_convert_fusion.5), channel_id=1, source_target_pairs={{0,16},{1,17},{2,18},{3,19},{4,20},{5,21},{6,22},{7,23},{8,24},{9,... | collective-permute-start | bytes 786440 | tf_op jit(solution)/shard_map/ppermute | solution.py:791
  95.4 0.8 collective-permute-done.12
  96.2 3.9 %collective-permute-start.14 = (bf16[32,2176]{1,0:T(8,128)(2,1)S(1)}, bf16[32,2176]{1,0:T(8,128)(2,1)S(1)}, u32[]{:S(2)}, u32[]{:S(2)}) collective-permute-start(bf16[32,2176]{1,0:T(8,128)(2,1)S(1)} %add_convert_fusion.7), channel_id=1, source_target_pairs={{0,16},{1,17},{2,18},{3,19},{4,20},{5,21},{6,22},{7,23},{8,24},{9,... | collective-permute-start | bytes 417800 | tf_op jit(solution)/shard_map/ppermute | solution.py:791
  100.1 3.1 %collective-permute-done.13 = bf16[128,1024]{1,0:T(8,128)(2,1)S(1)} collective-permute-done((bf16[128,1024]{1,0:T(8,128)(2,1)S(1)}, bf16[128,1024]{1,0:T(8,128)(2,1)S(1)}, u32[]{:S(2)}, u32[]{:S(2)}) %collective-permute-start.13) | collective-permute-done | bytes 262176 | tf_op jit(solution)/shard_map/ppermute | solution.py:791
  103.3 1.6 %collective-permute-start.15 = (bf16[128,1024]{1,0:T(8,128)(2,1)S(1)}, bf16[128,1024]{1,0:T(8,128)(2,1)S(1)}, u32[]{:S(2)}, u32[]{:S(2)}) collective-permute-start(bf16[128,1024]{1,0:T(8,128)(2,1)S(1)} %add_convert_fusion.4), channel_id=1, source_target_pairs={{0,4},{1,5},{2,6},{3,7},{4,0},{5,1},{6,2},{7,3},{8,12},{9,13},{10,... | collective-permute-start | bytes 786440 | tf_op jit(solution)/shard_map/ppermute | solution.py:791
  104.9 1.4 %collective-permute-done.14 = bf16[32,2176]{1,0:T(8,128)(2,1)S(1)} collective-permute-done((bf16[32,2176]{1,0:T(8,128)(2,1)S(1)}, bf16[32,2176]{1,0:T(8,128)(2,1)S(1)}, u32[]{:S(2)}, u32[]{:S(2)}) %collective-permute-start.14) | collective-permute-done | bytes 139296 | tf_op jit(solution)/shard_map/ppermute | solution.py:791
  106.3 0.8 collective-permute-start.16
  107.2 2.5 %collective-permute-done.15 = bf16[128,1024]{1,0:T(8,128)(2,1)S(1)} collective-permute-done((bf16[128,1024]{1,0:T(8,128)(2,1)S(1)}, bf16[128,1024]{1,0:T(8,128)(2,1)S(1)}, u32[]{:S(2)}, u32[]{:S(2)}) %collective-permute-start.15) | collective-permute-done | bytes 262176 | tf_op jit(solution)/shard_map/ppermute | solution.py:791
  109.7 2.3 %collective-permute-start.18 = (bf16[256,1024]{1,0:T(8,128)(2,1)S(1)}, bf16[256,1024]{1,0:T(8,128)(2,1)S(1)}, u32[]{:S(2)}, u32[]{:S(2)}) collective-permute-start(bf16[256,1024]{1,0:T(8,128)(2,1)S(1)} %constant_dynamic-update-slice_fusion), channel_id=1, source_target_pairs={{0,8},{1,9},{2,10},{3,11},{4,12},{5,13},{6,14},{7,15},{8,0},{9,1},... | collective-permute-start | bytes 1572872 | tf_op jit(solution)/shard_map/ppermute | solution.py:791
  112.0 0.9 collective-permute-done.16
  113.0 0.1 collective-permute-start.17
  113.1 6.5 %collective-permute-done.17 = bf16[64,2176]{1,0:T(8,128)(2,1)S(1)} collective-permute-done((bf16[64,2176]{1,0:T(8,128)(2,1)S(1)}, bf16[64,2176]{1,0:T(8,128)(2,1)S(1)}, u32[]{:S(2)}, u32[]{:S(2)}) %collective-permute-start.17) | collective-permute-done | bytes 278560 | tf_op jit(solution)/shard_map/ppermute | solution.py:791
  119.8 1.1 collective-permute-start.19
  120.9 0.7 collective-permute-start.21
  121.5 0.9 collective-permute-done.20.other_ref
  122.5 3.1 %ffn_end.1 = (f32[512,1024]{1,0:T(8,128)}, f32[1024,512]{1,0:T(8,128)}) custom-call(s32[6]{0:T(128)S(1)} %stack.21.info_ref, bf16[512,1024]{1,0:T(8,128)(2,1)S(1)} %constant_dynamic-update-slice_fusion.6.keep_ref, bf16[512,1024]{1,0:T(8,128)(2,1)S(1)} %collective-permute-done.20.other_ref), custom_call_target="tpu_custom_call" | custom-call | flops 1000 | bytes 1000 | tf_op jit(solution)/shard_map/ffn_end/pallas_call | solution.py:55
  125.5 3.9 %collective-permute-done.19.refs_1_ = bf16[128,2176]{1,0:T(8,128)(2,1)S(1)} collective-permute-done((bf16[128,2176]{1,0:T(8,128)(2,1)S(1)}, bf16[128,2176]{1,0:T(8,128)(2,1)S(1)}, u32[]{:S(2)}, u32[]{:S(2)}) %collective-permute-start.19) | collective-permute-done | bytes 557088 | tf_op jit(solution)/shard_map/ppermute | solution.py:791
  129.4 2.0 %collective-permute-done.22.refs_3_ = bf16[128,2176]{1,0:T(8,128)(2,1)S(1)} collective-permute-done((bf16[128,2176]{1,0:T(8,128)(2,1)S(1)}, bf16[128,2176]{1,0:T(8,128)(2,1)S(1)}, u32[]{:S(2)}, u32[]{:S(2)}) %collective-permute-start.22) | collective-permute-done | bytes 557088 | tf_op jit(solution)/shard_map/ppermute | solution.py:791
  131.4 4.6 %attend_end.1 = (f32[512,1536]{1,0:T(8,128)}, f32[512,512]{1,0:T(8,128)}, f32[512]{0:T(512)}, f32[512]{0:T(512)}, f32[512]{0:T(512)}, /*index=5*/f32[512]{0:T(512)}, f32[512]{0:T(512)}, f32[1024]{0:T(1024)}) custom-call(s32[6]{0:T(128)S(1)} %stack.21.info_ref, bf16[128,2176]{1,0:T(8,128)(2,1)S(1)} %constant_dynamic-update-slice_fusion.4.refs_0_, ...), custom_call_target="tpu_custom_call" | custom-call | flops 1000 | bytes 1000 | tf_op jit(solution)/shard_map/attend_end/pallas_call | solution.py:55
  (37 shorter events, 0.7 us)
Async XLA Ops:
  0.6 5.1 %copy-start = (bf16[512,1536]{1,0:T(8,128)(2,1)S(1)}, bf16[512,1536]{1,0:T(8,128)(2,1)}, u32[]{:S(2)}) copy-start(bf16[512,1536]{1,0:T(8,128)(2,1)} %refs_4_.1) | copy-start | bytes 4718596
  0.7 5.1 %copy-start.3 = (bf16[512,512]{1,0:T(8,128)(2,1)S(1)}, bf16[512,512]{1,0:T(8,128)(2,1)}, u32[]{:S(2)}) copy-start(bf16[512,512]{1,0:T(8,128)(2,1)} %wout_ref.3) | copy-start | bytes 1572868
  2.6 12.1 %copy-start.1 = (bf16[512,1024]{1,0:T(8,128)(2,1)S(1)}, bf16[512,1024]{1,0:T(8,128)(2,1)}, u32[]{:S(2)}) copy-start(bf16[512,1024]{1,0:T(8,128)(2,1)} %up_ref.3) | copy-start | bytes 3145732
  2.6 12.1 %copy-start.2 = (bf16[1024,512]{1,0:T(8,128)(2,1)S(1)}, bf16[1024,512]{1,0:T(8,128)(2,1)}, u32[]{:S(2)}) copy-start(bf16[1024,512]{1,0:T(8,128)(2,1)} %down_ref.3) | copy-start | bytes 3145732
  2.6 26.5 %collective-permute-start = (bf16[528,512]{1,0:T(8,128)(2,1)S(1)}, bf16[528,512]{1,0:T(8,128)(2,1)S(1)}, u32[]{:S(2)}, u32[]{:S(2)}) collective-permute-start(bf16[528,512]{1,0:T(8,128)(2,1)S(1)} %get-tuple-element.102), channel_id=1, source_target_pairs={{0,1},{1,0},{2,3},{3,2},{4,5},{5,4},{6,7},{7,6},{8,9},{9,8},{10,11... | collective-permute-start | bytes 1622024 | tf_op jit(solution)/shard_map/ppermute | solution.py:791
  5.6 23.5 %collective-permute-start.1 = (bf16[512,512]{1,0:T(8,128)(2,1)S(1)}, bf16[512,512]{1,0:T(8,128)(2,1)S(1)}, u32[]{:S(2)}, u32[]{:S(2)}) collective-permute-start(bf16[512,512]{1,0:T(8,128)(2,1)S(1)} %get-tuple-element.103), channel_id=1, source_target_pairs={{0,1},{1,0},{2,3},{3,2},{4,5},{5,4},{6,7},{7,6},{8,9},{9,8},{10,11... | collective-permute-start | bytes 1572872 | tf_op jit(solution)/shard_map/ppermute | solution.py:791
  29.1 3.4 %collective-permute-start.2 = (bf16[528,512]{1,0:T(8,128)(2,1)S(1)}, bf16[528,512]{1,0:T(8,128)(2,1)S(1)}, u32[]{:S(2)}, u32[]{:S(2)}) collective-permute-start(bf16[528,512]{1,0:T(8,128)(2,1)S(1)} %collective-permute-done.refs_0_), channel_id=1, source_target_pairs={{0,2},{1,3},{2,0},{3,1},{4,6},{5,7},{6,4},{7,5},{8,10},{9,11},{10,... | collective-permute-start | bytes 1622024 | tf_op jit(solution)/shard_map/ppermute | solution.py:791
  29.1 3.4 %collective-permute-start.3 = (bf16[512,512]{1,0:T(8,128)(2,1)S(1)}, bf16[512,512]{1,0:T(8,128)(2,1)S(1)}, u32[]{:S(2)}, u32[]{:S(2)}) collective-permute-start(bf16[512,512]{1,0:T(8,128)(2,1)S(1)} %collective-permute-done.1.refs_2_), channel_id=1, source_target_pairs={{0,2},{1,3},{2,0},{3,1},{4,6},{5,7},{6,4},{7,5},{8,10},{9,11},{10,... | collective-permute-start | bytes 1572872 | tf_op jit(solution)/shard_map/ppermute | solution.py:791
  29.7 16.8 %collective-permute-start.5 = (bf16[512,1024]{1,0:T(8,128)(2,1)}, bf16[512,1024]{1,0:T(8,128)(2,1)S(1)}, u32[]{:S(2)}, u32[]{:S(2)}) collective-permute-start(bf16[512,1024]{1,0:T(8,128)(2,1)} %get-tuple-element.109), channel_id=1, source_target_pairs={{0,2},{1,3},{2,0},{3,1},{4,6},{5,7},{6,4},{7,5},{8,10},{9,11},{10,... | collective-permute-start | bytes 3145736 | tf_op jit(solution)/shard_map/ppermute | solution.py:791
  46.3 2.7 %collective-permute-start.4 = (bf16[512,1024]{1,0:T(8,128)(2,1)S(1)}, bf16[512,1024]{1,0:T(8,128)(2,1)S(1)}, u32[]{:S(2)}, u32[]{:S(2)}) collective-permute-start(bf16[512,1024]{1,0:T(8,128)(2,1)S(1)} %get-tuple-element.108), channel_id=1, source_target_pairs={{0,2},{1,3},{2,0},{3,1},{4,6},{5,7},{6,4},{7,5},{8,10},{9,11},{10,... | collective-permute-start | bytes 3145736 | tf_op jit(solution)/shard_map/ppermute | solution.py:791
  49.8 14.9 %collective-permute-start.6 = (bf16[512,1024]{1,0:T(8,128)(2,1)S(1)}, bf16[512,1024]{1,0:T(8,128)(2,1)S(1)}, u32[]{:S(2)}, u32[]{:S(2)}) collective-permute-start(bf16[512,1024]{1,0:T(8,128)(2,1)S(1)} %join.1), channel_id=1, source_target_pairs={{0,1},{1,0},{2,6},{3,7},{4,5},{5,4},{6,2},{7,3},{8,9},{9,8},{10,14... | collective-permute-start | bytes 3145736 | tf_op jit(solution)/shard_map/ppermute | solution.py:791
  64.7 3.0 %collective-permute-start.7 = (bf16[256,2176]{1,0:T(8,128)(2,1)S(1)}, bf16[256,2176]{1,0:T(8,128)(2,1)S(1)}, u32[]{:S(2)}, u32[]{:S(2)}) collective-permute-start(bf16[256,2176]{1,0:T(8,128)(2,1)S(1)} %get-tuple-element.124), channel_id=1, source_target_pairs={{0,2},{1,3},{2,0},{3,1},{4,6},{5,7},{6,4},{7,5},{8,10},{9,11},{10,... | collective-permute-start | bytes 3342344 | tf_op jit(solution)/shard_map/ppermute | solution.py:791
  65.9 9.3 %collective-permute-start.8 = (bf16[256,1024]{1,0:T(8,128)(2,1)S(1)}, bf16[256,1024]{1,0:T(8,128)(2,1)S(1)}, u32[]{:S(2)}, u32[]{:S(2)}) collective-permute-start(bf16[256,1024]{1,0:T(8,128)(2,1)S(1)} %get-tuple-element.130), channel_id=1, source_target_pairs={{0,4},{1,5},{2,3},{3,2},{4,0},{5,1},{6,7},{7,6},{8,12},{9,13},{10,... | collective-permute-start | bytes 1572872 | tf_op jit(solution)/shard_map/ppermute | solution.py:791
  68.0 14.2 %collective-permute-start.9 = (bf16[128,2176]{1,0:T(8,128)(2,1)S(1)}, bf16[128,2176]{1,0:T(8,128)(2,1)S(1)}, u32[]{:S(2)}, u32[]{:S(2)}) collective-permute-start(bf16[128,2176]{1,0:T(8,128)(2,1)S(1)} %get-tuple-element.172), channel_id=1, source_target_pairs={{0,4},{1,5},{2,10},{3,11},{4,0},{5,1},{6,14},{7,15},{8,12},{9,13},... | collective-permute-start | bytes 1671176 | tf_op jit(solution)/shard_map/ppermute | solution.py:791
  75.4 9.2 %collective-permute-start.10 = (bf16[128,1024]{1,0:T(8,128)(2,1)S(1)}, bf16[128,1024]{1,0:T(8,128)(2,1)S(1)}, u32[]{:S(2)}, u32[]{:S(2)}) collective-permute-start(bf16[128,1024]{1,0:T(8,128)(2,1)S(1)} %get-tuple-element.176), channel_id=1, source_target_pairs={{0,8},{1,9},{2,10},{3,11},{4,12},{5,13},{6,14},{7,15},{8,0},{9,1},... | collective-permute-start | bytes 786440 | tf_op jit(solution)/shard_map/ppermute | solution.py:791
  82.4 8.1 %collective-permute-start.11 = (bf16[64,2176]{1,0:T(8,128)(2,1)S(1)}, bf16[64,2176]{1,0:T(8,128)(2,1)S(1)}, u32[]{:S(2)}, u32[]{:S(2)}) collective-permute-start(bf16[64,2176]{1,0:T(8,128)(2,1)S(1)} %get-tuple-element.175), channel_id=1, source_target_pairs={{0,1},{1,0},{2,6},{3,7},{4,5},{5,4},{6,2},{7,3},{8,9},{9,8},{10,14... | collective-permute-start | bytes 835592 | tf_op jit(solution)/shard_map/ppermute | solution.py:791
  90.7 5.5 %collective-permute-start.12 = (bf16[32,2176]{1,0:T(8,128)(2,1)S(1)}, bf16[32,2176]{1,0:T(8,128)(2,1)S(1)}, u32[]{:S(2)}, u32[]{:S(2)}) collective-permute-start(bf16[32,2176]{1,0:T(8,128)(2,1)S(1)} %get-tuple-element.178), channel_id=1, source_target_pairs={{0,8},{1,9},{2,3},{3,2},{4,12},{5,13},{6,7},{7,6},{8,0},{9,1},{10,... | collective-permute-start | bytes 417800 | tf_op jit(solution)/shard_map/ppermute | solution.py:791
  92.8 10.4 %collective-permute-start.13 = (bf16[128,1024]{1,0:T(8,128)(2,1)S(1)}, bf16[128,1024]{1,0:T(8,128)(2,1)S(1)}, u32[]{:S(2)}, u32[]{:S(2)}) collective-permute-start(bf16[128,1024]{1,0:T(8,128)(2,1)S(1)} %add_convert_fusion.5), channel_id=1, source_target_pairs={{0,16},{1,17},{2,18},{3,19},{4,20},{5,21},{6,22},{7,23},{8,24},{9,... | collective-permute-start | bytes 786440 | tf_op jit(solution)/shard_map/ppermute | solution.py:791
  96.2 10.1 %collective-permute-start.14 = (bf16[32,2176]{1,0:T(8,128)(2,1)S(1)}, bf16[32,2176]{1,0:T(8,128)(2,1)S(1)}, u32[]{:S(2)}, u32[]{:S(2)}) collective-permute-start(bf16[32,2176]{1,0:T(8,128)(2,1)S(1)} %add_convert_fusion.7), channel_id=1, source_target_pairs={{0,16},{1,17},{2,18},{3,19},{4,20},{5,21},{6,22},{7,23},{8,24},{9,... | collective-permute-start | bytes 417800 | tf_op jit(solution)/shard_map/ppermute | solution.py:791
  103.3 6.4 %collective-permute-start.15 = (bf16[128,1024]{1,0:T(8,128)(2,1)S(1)}, bf16[128,1024]{1,0:T(8,128)(2,1)S(1)}, u32[]{:S(2)}, u32[]{:S(2)}) collective-permute-start(bf16[128,1024]{1,0:T(8,128)(2,1)S(1)} %add_convert_fusion.4), channel_id=1, source_target_pairs={{0,4},{1,5},{2,6},{3,7},{4,0},{5,1},{6,2},{7,3},{8,12},{9,13},{10,... | collective-permute-start | bytes 786440 | tf_op jit(solution)/shard_map/ppermute | solution.py:791
  106.3 6.6 %collective-permute-start.16 = (bf16[32,2176]{1,0:T(8,128)(2,1)S(1)}, bf16[32,2176]{1,0:T(8,128)(2,1)S(1)}, u32[]{:S(2)}, u32[]{:S(2)}) collective-permute-start(bf16[32,2176]{1,0:T(8,128)(2,1)S(1)} %add_convert_fusion.6), channel_id=1, source_target_pairs={{0,8},{1,9},{2,6},{3,7},{4,12},{5,13},{6,2},{7,3},{8,0},{9,1},{10,... | collective-permute-start | bytes 417800 | tf_op jit(solution)/shard_map/ppermute | solution.py:791
  109.7 9.9 %collective-permute-start.18 = (bf16[256,1024]{1,0:T(8,128)(2,1)S(1)}, bf16[256,1024]{1,0:T(8,128)(2,1)S(1)}, u32[]{:S(2)}, u32[]{:S(2)}) collective-permute-start(bf16[256,1024]{1,0:T(8,128)(2,1)S(1)} %constant_dynamic-update-slice_fusion), channel_id=1, source_target_pairs={{0,8},{1,9},{2,10},{3,11},{4,12},{5,13},{6,14},{7,15},{8,0},{9,1},... | collective-permute-start | bytes 1572872 | tf_op jit(solution)/shard_map/ppermute | solution.py:791
  113.0 6.6 %collective-permute-start.17 = (bf16[64,2176]{1,0:T(8,128)(2,1)S(1)}, bf16[64,2176]{1,0:T(8,128)(2,1)S(1)}, u32[]{:S(2)}, u32[]{:S(2)}) collective-permute-start(bf16[64,2176]{1,0:T(8,128)(2,1)S(1)} %constant_dynamic-update-slice_fusion.2), channel_id=1, source_target_pairs={{0,1},{1,0},{2,3},{3,2},{4,5},{5,4},{6,7},{7,6},{8,9},{9,8},{10,11... | collective-permute-start | bytes 835592 | tf_op jit(solution)/shard_map/ppermute | solution.py:791
  119.7 2.7 %collective-permute-start.20 = (bf16[512,1024]{1,0:T(8,128)(2,1)S(1)}, bf16[512,1024]{1,0:T(8,128)(2,1)S(1)}, u32[]{:S(2)}, u32[]{:S(2)}) collective-permute-start(bf16[512,1024]{1,0:T(8,128)(2,1)S(1)} %constant_dynamic-update-slice_fusion.6.keep_ref), channel_id=1, source_target_pairs={{0,2},{1,3},{2,0},{3,1},{4,6},{5,7},{6,4},{7,5},{8,10},{9,11},{10,... | collective-permute-start | bytes 3145736 | tf_op jit(solution)/shard_map/ppermute | solution.py:791
  119.8 9.6 %collective-permute-start.19 = (bf16[128,2176]{1,0:T(8,128)(2,1)S(1)}, bf16[128,2176]{1,0:T(8,128)(2,1)S(1)}, u32[]{:S(2)}, u32[]{:S(2)}) collective-permute-start(bf16[128,2176]{1,0:T(8,128)(2,1)S(1)} %constant_dynamic-update-slice_fusion.4.refs_0_), channel_id=1, source_target_pairs={{0,4},{1,5},{2,10},{3,11},{4,0},{5,1},{6,14},{7,15},{8,12},{9,13},... | collective-permute-start | bytes 1671176 | tf_op jit(solution)/shard_map/ppermute | solution.py:791
  120.9 8.5 %collective-permute-start.21 = (bf16[128,2176]{1,0:T(8,128)(2,1)S(1)}, bf16[128,2176]{1,0:T(8,128)(2,1)S(1)}, u32[]{:S(2)}, u32[]{:S(2)}) collective-permute-start(bf16[128,2176]{1,0:T(8,128)(2,1)S(1)} %constant_dynamic-update-slice_fusion.4.refs_0_), channel_id=1, source_target_pairs={{0,2},{1,3},{2,0},{3,1},{4,6},{5,7},{6,4},{7,5},{8,10},{9,11},{10,... | collective-permute-start | bytes 1671176 | tf_op jit(solution)/shard_map/ppermute | solution.py:791
  129.4 2.0 %collective-permute-start.22 = (bf16[128,2176]{1,0:T(8,128)(2,1)S(1)}, bf16[128,2176]{1,0:T(8,128)(2,1)S(1)}, u32[]{:S(2)}, u32[]{:S(2)}) collective-permute-start(bf16[128,2176]{1,0:T(8,128)(2,1)S(1)} %collective-permute-done.19.refs_1_), channel_id=1, source_target_pairs={{0,2},{1,3},{2,0},{3,1},{4,6},{5,7},{6,4},{7,5},{8,10},{9,11},{10,... | collective-permute-start | bytes 1671176 | tf_op jit(solution)/shard_map/ppermute | solution.py:791

commit v11 on v10

--- a/solution.py
+++ b/solution.py
@@ -51,13 +51,14 @@
     return pl.BlockSpec((toks, width), lambda i, *_: (i, 0))
 
 
-def call(kernel, name, grid, in_specs, out_specs, out_shape, scratch, info, args, vmem=VMEM_LIMIT):
+def call(kernel, name, grid, in_specs, out_specs, out_shape, scratch, info, args, vmem=VMEM_LIMIT, aliases=()):
     return pl.pallas_call(
         kernel,
         grid_spec=pltpu.PrefetchScalarGridSpec(
             num_scalar_prefetch=1, grid=grid, in_specs=in_specs, out_specs=out_specs, scratch_shapes=scratch
         ),
         out_shape=out_shape,
+        input_output_aliases=dict(aliases),
         compiler_params=pltpu.CompilerParams(vmem_limit_bytes=vmem),
         cost_estimate=pl.CostEstimate(flops=1000, bytes_accessed=1000, transcendentals=0),
         name=name,
@@ -530,7 +531,8 @@
 
 
 def attend_back_kernel(
-    tables, info_ref, qkv_ref, prob_ref, gmix_ref, tok_ref, dwout_ref, vec_ref, *refs
+    tables, info_ref, qkv_ref, prob_ref, gmix_ref, tok_ref, g1_ref, c1_ref, wqkv_ref, dwout_ref, vec_ref,
+    *refs,
 ):
     *sums, grad_ref, dw_keep_ref, dw_send_ref, dqkv_ref, acc_ref, row_ref = refs
     at, last = pl.program_id(0), pl.num_programs(0) - 1
@@ -582,7 +584,19 @@
     @pl.when(at == last)
     def _():
         core, own, other = info_ref[0], info_ref[3], info_ref[4]
-        acc_ref[:, 4 * width :] = row_ref[...].T
+        row_ref[5:6, :] = g1_ref[...]
+        row_ref[6:7, :] = c1_ref[...]
+        wide_row = jnp.concatenate([row_ref[i : i + 1, :] for i in range(3)], axis=1)
+        step = width // 4
+        for r in range(0, width, step):
+            w = wqkv_ref[r : r + step, :].astype(F32)
+            sums = acc_ref[r : r + step, : 3 * width]
+            d_gain = jnp.sum(w * sums, axis=1, keepdims=True)
+            d_bias = jnp.sum(w * wide_row, axis=1, keepdims=True)
+            lane = lax.broadcasted_iota(jnp.int32, (step, LANES), 1)
+            others = row_ref[:, r : r + step].T
+            acc_ref[r : r + step, : 3 * width] = others[:, 5:6] * sums + others[:, 6:7] * wide_row
+            acc_ref[r : r + step, 4 * width :] = jnp.where(lane == 3, d_gain, jnp.where(lane == 4, d_bias, others))
         half = width // 2
         size = width // len(tables[0])
         for place in range(len(tables[0])):
@@ -593,7 +607,7 @@
             dst[to : to + size, :] = acc_ref[rows_at, :].astype(BF)
 
 
-def attend_back(info, tables, qkv, prob, gmix, tokens, dwout, *vecs):
+def attend_back(info, tables, qkv, prob, gmix, tokens, g1, c1, wqkv, dwout, *vecs):
     n, width = tokens.shape
     rows, pairs, slots, _ = prob.shape
     per = TOKS // slots
@@ -606,6 +620,9 @@
             pl.BlockSpec((per, pairs, slots, 2 * slots), lambda i, *_: (i, 0, 0, 0)),
             rows_of(width),
             rows_of(width),
+            whole(1, width),
+            whole(1, width),
+            whole(*wqkv.shape),
             whole(width, width),
         ]
         + [whole(*vec.shape) for vec in vecs],
@@ -617,7 +634,7 @@
             pltpu.VMEM((LANES, width), F32),
         ],
         info,
-        far(qkv, prob, gmix, tokens, dwout, *vecs),
+        far(qkv, prob, gmix, tokens, g1, c1, wqkv, dwout, *vecs),
     )
 
 
@@ -685,93 +702,74 @@
     )
 
 
-def attend_end_kernel(
-    tables, shares, info_ref, *refs
-):
-    quarters, (w_hbm, g1_ref, c1_ref, qkv_hbm, out_hbm), refs = refs[:4], refs[4:9], refs[9:]
-    vec_refs, (qkv_ref, out_ref, col_ref, row_ref, w_ref, sems) = refs[:6], refs[6:]
-    core, own, away = info_ref[0], info_ref[3], info_ref[4]
-    weights = pltpu.make_async_copy(w_hbm, w_ref, sems.at[2 * len(tables[0])])
-    weights.start()
+def attend_end_kernel(tables, which, shares, info_ref, *refs):
+    quarters, refs = refs[: 2 + 2 * which], refs[2 + 2 * which + 2 * which :]
+    qkv_hbm, out_hbm, *refs = refs
+    vec_refs, (qkv_ref, out_ref, *refs, sems) = refs[: 6 * which], refs[6 * which :]
+    core = info_ref[0]
     width = out_ref.shape[1]
     blocks = len(tables[0])
-    size = out_ref.shape[0] // blocks
-    quarter = out_ref.shape[0] // 4
+    quarter = quarters[0].shape[0]
+    size = 4 * quarter // blocks
     spots = []
     for place in range(blocks):
         row = place * size
-        block = block_at(place, tables, core, own if row < 2 * quarter else away)
+        side, half = row // (2 * quarter), row // quarter % 2
+        block = block_at(place, tables, core, info_ref[3 + side])
         at = row % quarter
-        spots.append((quarters[row // quarter], slice(at, at + size), slice(row, row + size), pl.multiple_of(block * size, size)))
+        src = quarters[side + 2 * half * which] if half <= which else None
+        spots.append((half, src, at, side * quarter + at, pl.multiple_of(block * size, size)))
     copies = []
-    for i, (src, rows, here, to) in enumerate(spots):
-        col_ref[pl.ds(to, size), :] = src[rows, 4 * width :].astype(F32)
-        out_ref[here, :] = src[rows, 3 * width : 4 * width].astype(F32)
-        copies.append(pltpu.make_async_copy(out_ref.at[here, :], out_hbm.at[pl.ds(to, size), :], sems.at[i]))
-        copies[-1].start()
-    vec = col_ref[...].T
-    row_ref[...] = vec
-    wide_row = jnp.concatenate([vec[i : i + 1, :] for i in range(3)], axis=1)
-    pair = jnp.concatenate([g1_ref[...], c1_ref[...], jnp.zeros((LANES - 2, width), F32)], axis=0).T
-    col_ref[...] = pair
-    lane = lax.broadcasted_iota(jnp.int32, (size, LANES), 1)
-    for i, (src, rows, here, to) in enumerate(spots):
-        gain_bias = col_ref[pl.ds(to, size), :]
-        sums = src[rows, : 3 * width].astype(F32)
-        qkv_ref[here, :] = gain_bias[:, 0:1] * sums + gain_bias[:, 1:2] * wide_row
-        copies.append(pltpu.make_async_copy(qkv_ref.at[here, :], qkv_hbm.at[pl.ds(to, size), :], sems.at[blocks + i]))
-        copies[-1].start()
-    weights.wait()
-    for src, rows, _, to in spots:
-        here = pl.ds(to, size)
-        sums = src[rows, : 3 * width].astype(F32)
-        w = w_ref[here, :].astype(F32)
-        d_gain = jnp.sum(w * sums, axis=1, keepdims=True)
-        d_bias = jnp.sum(w * wide_row, axis=1, keepdims=True)
-        col_ref[here, :] = jnp.where(lane == 0, d_gain, jnp.where(lane == 1, d_bias, 0.0))
-    both = col_ref[...].T
-    flat = lambda row: row.reshape(row.shape[1])
-    vec_refs[0][...] = flat(both[0:1, :])
-    vec_refs[1][...] = flat(both[1:2, :])
-    for i in range(3):
-        vec_refs[2 + i][...] = flat(vec[SUMS + i : SUMS + i + 1, :])
-    units = vec_refs[5].shape[0]
-    if units >= width:
-        first = SUMS + 8 + info_ref[5] * (units // width)
-        for i in range(units // width):
-            vec_refs[5][i * width : (i + 1) * width] = flat(row_ref[pl.ds(first + i, 1), :])
-    else:
-        row = row_ref[pl.ds(SUMS + 8 + info_ref[5] // shares, 1), :]
-        share = row[:, :units]
-        for i in range(1, shares):
-            share = jnp.where(info_ref[5] % shares == i, row[:, i * units : (i + 1) * units], share)
-        vec_refs[5][...] = flat(share)
+    for half, src, at, row, to in spots:
+        if half != which:
+            continue
+        here, there = pl.ds(row, size), pl.ds(to, size)
+        for ref, hbm, cols in ((qkv_ref, qkv_hbm, slice(0, 3 * width)), (out_ref, out_hbm, slice(3 * width, 4 * width))):
+            ref[row : row + size, :] = src[at : at + size, cols].astype(F32)
+            copies.append(pltpu.make_async_copy(ref.at[here, :], hbm.at[there, :], sems.at[len(copies)]))
+            copies[-1].start()
+    if which:
+        col_ref, row_ref = refs
+        for half, src, at, _, to in spots:
+            col_ref[pl.ds(to, size), :] = src[at : at + size, 4 * width :].astype(F32)
+        vec = col_ref[...].T
+        row_ref[...] = vec
+        flat = lambda row: row.reshape(row.shape[1])
+        for i, at in enumerate((3, 4, SUMS, SUMS + 1, SUMS + 2)):
+            vec_refs[i][...] = flat(vec[at : at + 1, :])
+        units = vec_refs[5].shape[0]
+        if units >= width:
+            first = SUMS + 8 + info_ref[5] * (units // width)
+            for i in range(units // width):
+                vec_refs[5][i * width : (i + 1) * width] = flat(row_ref[pl.ds(first + i, 1), :])
+        else:
+            row = row_ref[pl.ds(SUMS + 8 + info_ref[5] // shares, 1), :]
+            share = row[:, :units]
+            for i in range(1, shares):
+                share = jnp.where(info_ref[5] % shares == i, row[:, i * units : (i + 1) * units], share)
+            vec_refs[5][...] = flat(share)
     for copy in copies:
         copy.wait()
 
 
-def attend_end(info, tables, quarters, w_qkv, g1, c1, units):
-    rows, width = 4 * quarters[0].shape[0], w_qkv.shape[0]
-    blocks = len(tables[0])
+def attend_end(info, tables, quarters, width, units, written=()):
+    rows = 4 * quarters[0].shape[0]
+    which = 1 if written else 0
+    anywhere = pl.BlockSpec(memory_space=pl.ANY)
     return call(
-        functools.partial(attend_end_kernel, tables, max(1, width // units)),
+        functools.partial(attend_end_kernel, tables, which, max(1, width // units)),
         "attend_end",
         (1,),
-        [whole(*quarters[0].shape)] * 4 + [pl.BlockSpec(memory_space=pl.ANY)] + [whole(1, width)] * 2,
-        [pl.BlockSpec(memory_space=pl.ANY)] * 2 + [whole(width)] * 5 + [whole(units)],
+        [whole(*quarters[0].shape)] * len(quarters) + [anywhere] * len(written),
+        [anywhere] * 2 + ([whole(width)] * 5 + [whole(units)]) * which,
         [jax.ShapeDtypeStruct((rows, 3 * width), F32), jax.ShapeDtypeStruct((rows, width), F32)]
-        + [jax.ShapeDtypeStruct((width,), F32)] * 5
-        + [jax.ShapeDtypeStruct((units,), F32)],
-        [
-            pltpu.VMEM((rows, 3 * width), F32),
-            pltpu.VMEM((rows, width), F32),
-            pltpu.VMEM((rows, LANES), F32),
-            pltpu.VMEM((LANES, width), F32),
-            pltpu.VMEM(w_qkv.shape, BF),
-            pltpu.SemaphoreType.DMA((2 * blocks + 1,)),
-        ],
+        + ([jax.ShapeDtypeStruct((width,), F32)] * 5 + [jax.ShapeDtypeStruct((units,), F32)]) * which,
+        [pltpu.VMEM((rows // 2, 3 * width), F32), pltpu.VMEM((rows // 2, width), F32)]
+        + [pltpu.VMEM((rows, LANES), F32), pltpu.VMEM((LANES, width), F32)] * which
+        + [pltpu.SemaphoreType.DMA((len(tables[0]),))],
         info,
-        tuple(quarters) + far(w_qkv, g1, c1),
+        (*quarters, *written),
+        aliases=[(1 + len(quarters) + i, i) for i in range(len(written))],
     )
 
 
@@ -909,7 +907,7 @@
             held = [add(held[j], swap(held[j + mask], mask)) for j in range(mask)]
         ff_keep = held[0]
 
-    dqkv, keep, send = attend_back(info, at_tables(at_in), qkv, prob, gmix, tokens_in, dwout, *vecs)
+    dqkv, keep, send = attend_back(info, at_tables(at_in), qkv, prob, gmix, tokens_in, g1, c1, w_qkv, dwout, *vecs)
     if mixing:
         send, ff_got = after(send, ff_got)
         ff_keep, ff_send = split(info, ff_keep, got, got_own, ff_got)
@@ -935,14 +933,15 @@
             kept, other_kept, *beside = after(kept, other_kept, *beside)
             under_way[other] = other_kept, other_got
         else:
-            kept, got, *beside = after(kept, got, *beside)
+            kept, *beside = after(kept, *beside)
         if len(beside) == 1:
             (grad_tokens,), beside = beside, ()
         elif beside:
             (grad_w_up, grad_w_down), beside = beside, ()
         step, *steps[turn] = steps[turn]
         if step[0] == "last":
-            got, crossed = after(got, crossed)
+            written = attend_end(info, at_tables(at_out), (kept, crossed), width, 2 * units)
+            got, written = after(got, written)
         value = finish(kept, got, step)
         if step[0] == "last":
             under_way[turn] = value, swap(got, core_mask)
@@ -953,9 +952,9 @@
         elif turn == "F":
             beside = ffn_end(info, ff_out_tables, *value)
         else:
-            done = (*value[0], crossed, value[1])
+            done = (value[0][0], crossed, value[0][1], value[1])
     grad_w_qkv, grad_w_out, d_gain1, d_bias1, d_gain2, d_bias2, d_bdown, grad_b_up = attend_end(
-        info, at_tables(at_out), done, w_qkv, g1, c1, 2 * units
+        info, at_tables(at_out), done, width, 2 * units, written
     )
     return (
         block_out, grad_tokens, d_gain1, d_bias1, grad_w_qkv, grad_w_out, d_gain2, d_bias2, grad_w_up, grad_b_up, grad_w_down,

time: 136 us -> 135 us (level)
  waiting for transfers between devices: 45.1 us -> 42.3 us
  Pallas kernels: 60.5 us -> 62.2 us
    ppermute x23, waiting for transfers between devices: 45.1 us -> 42.3 us  [swap(): return lax.ppermute(value, AXES, pairs)]
    pallas_call x8 -> x9, Pallas kernels: 58.6 us -> 60.2 us  [call(): pl.pallas_call(kernel, grid_spec=pltpu.PrefetchScalarGridSpec(num_scalar_...]
  transfers between devices with their start and end apart: 23 -> 23, of which waited for: 15 -> 15; matrix products, arithmetic and copies ran while one was open for 1% -> 1% of each run, Pallas kernels for 39% -> 42%
where the time goes in v11:
time: 135 us
  Pallas kernels  62.2 us (46%)
  waiting for transfers between devices  42.3 us (31%)
  starting transfers between devices  27.8 us (21%)
    pallas_call x9, Pallas kernels, call(): pl.pallas_call(kernel, grid_spec=pltpu.PrefetchScalarGridSpec(num_scalar_...  60.2 us
    ppermute x23, waiting for transfers between devices, swap(): return lax.ppermute(value, AXES, pairs)  42.3 us
    ppermute x23, starting transfers between devices, swap(): return lax.ppermute(value, AXES, pairs)  27.8 us
  transfers between devices with their start and end apart: 23, of which 15 were waited for; matrix products, arithmetic and copies ran while one was open for 1% of the time, Pallas kernels for 42%

profile of v11, /device:TPU:0, one launch (start us, length us, event | category | flops | bytes accessed | tf_op | source)
XLA Modules:
  0.0 134.7 jit_solution(919159814026890729)
XLA Ops:
  0.7 0.1 stack.21.info_ref
  0.8 1.8 %pack.1 = (bf16[528,512]{1,0:T(8,128)(2,1)S(1)}, bf16[512,512]{1,0:T(8,128)(2,1)S(1)}) custom-call(s32[6]{0:T(128)S(1)} %stack.21.info_ref, bf16[512,1024]{1,0:T(8,128)(2,1)} %up_ref.3, bf16[1024]{0:T(1024)(128)(2,1)} %bias_ref.3, bf16[1024,512]{1,0:T(8,128)(2,1)} %down_ref.3), custom_call_target="tpu_custom_call" | custom-call | flops 1000 | bytes 1000 | tf_op jit(solution)/shard_map/pack/pallas_call | solution.py:55
  2.6 3.0 %collective-permute-start = (bf16[528,512]{1,0:T(8,128)(2,1)S(1)}, bf16[528,512]{1,0:T(8,128)(2,1)S(1)}, u32[]{:S(2)}, u32[]{:S(2)}) collective-permute-start(bf16[528,512]{1,0:T(8,128)(2,1)S(1)} %get-tuple-element.103), channel_id=1, source_target_pairs={{0,1},{1,0},{2,3},{3,2},{4,5},{5,4},{6,7},{7,6},{8,9},{9,8},{10,11... | collective-permute-start | bytes 1622024 | tf_op jit(solution)/shard_map/ppermute | solution.py:789
  5.6 0.1 collective-permute-start.1
  5.7 9.0 %attend.1 = (bf16[1024,1536]{1,0:T(8,128)(2,1)}, bf16[8,4,128,256]{3,2,1,0:T(8,128)(2,1)}, bf16[1024,512]{1,0:T(8,128)(2,1)}, f32[1024,512]{1,0:T(8,128)}, bf16[1024,512]{1,0:T(8,128)(2,1)S(1)}) custom-call(s32[6]{0:T(128)S(1)} %stack.21.info_ref, bf16[1024,512]{1,0:T(8,128)(2,1)} %tok_ref.2, f32[1,512]{1,0:T(1,128)} %bitcast.9, f32[1,512]{1,0:T(1,128)} %bitcast.14, ...), custom_call_target="tpu_custom_call" | custom-call | flops 1000 | bytes 1000 | tf_op jit(solution)/shard_map/attend/pallas_call | solution.py:55
  14.7 11.1 %ffn_own.1 = (f32[1024,512]{1,0:T(8,128)S(1)}, f32[1024,512]{1,0:T(8,128)S(1)}, bf16[512,1024]{1,0:T(8,128)(2,1)}, bf16[512,1024]{1,0:T(8,128)(2,1)}, f32[2,512]{1,0:T(2,128)}) custom-call(s32[6]{0:T(128)S(1)} %stack.21.info_ref, bf16[1024,512]{1,0:T(8,128)(2,1)S(1)} %get-tuple-element.96.sec_ref.sec_in, bf16[1024,512]{1,0:T(8,128)(2,1)} %dy_in.1, ...), custom_call_target="tpu_custom_call" | custom-call | flops 1000 | bytes 1000 | tf_op jit(solution)/shard_map/ffn_own/pallas_call | solution.py:55
  25.8 3.3 %collective-permute-done.1.refs_2_ = bf16[512,512]{1,0:T(8,128)(2,1)S(1)} collective-permute-done((bf16[512,512]{1,0:T(8,128)(2,1)S(1)}, bf16[512,512]{1,0:T(8,128)(2,1)S(1)}, u32[]{:S(2)}, u32[]{:S(2)}) %collective-permute-start.1) | collective-permute-done | bytes 524320 | tf_op jit(solution)/shard_map/ppermute | solution.py:789
  29.1 0.5 collective-permute-start.3
  29.7 2.9 %collective-permute-done.3.refs_3_ = bf16[512,512]{1,0:T(8,128)(2,1)S(1)} collective-permute-done((bf16[512,512]{1,0:T(8,128)(2,1)S(1)}, bf16[512,512]{1,0:T(8,128)(2,1)S(1)}, u32[]{:S(2)}, u32[]{:S(2)}) %collective-permute-start.3) | collective-permute-done | bytes 524320 | tf_op jit(solution)/shard_map/ppermute | solution.py:789
  32.6 13.8 %ffn_rest.1 = (bf16[1024,512]{1,0:T(8,128)(2,1)}, f32[1024,512]{1,0:T(8,128)}, bf16[1024,512]{1,0:T(8,128)(2,1)}, f32[8,512]{1,0:T(8,128)}, f32[512,512]{1,0:T(8...) custom-call(s32[6]{0:T(128)S(1)} %stack.21.info_ref, ...), custom_call_target="tpu_custom_call" | custom-call | flops 1000 | bytes 1000 | tf_op jit(solution)/shard_map/ffn_rest/pallas_call | solution.py:55
  46.3 0.2 collective-permute-start.4
  46.5 2.5 %collective-permute-done.4.got_ref = bf16[512,1024]{1,0:T(8,128)(2,1)S(1)} collective-permute-done((bf16[512,1024]{1,0:T(8,128)(2,1)S(1)}, bf16[512,1024]{1,0:T(8,128)(2,1)S(1)}, u32[]{:S(2)}, u32[]{:S(2)}) %collective-permute-start.4) | collective-permute-done | bytes 1048608 | tf_op jit(solution)/shard_map/ppermute | solution.py:789
  49.1 0.8 join.1
  49.9 1.8 %collective-permute-start.6 = (bf16[512,1024]{1,0:T(8,128)(2,1)S(1)}, bf16[512,1024]{1,0:T(8,128)(2,1)S(1)}, u32[]{:S(2)}, u32[]{:S(2)}) collective-permute-start(bf16[512,1024]{1,0:T(8,128)(2,1)S(1)} %join.1), channel_id=1, source_target_pairs={{0,1},{1,0},{2,6},{3,7},{4,5},{5,4},{6,2},{7,3},{8,9},{9,8},{10,14... | collective-permute-start | bytes 3145736 | tf_op jit(solution)/shard_map/ppermute | solution.py:789
  51.7 11.3 %attend_back.1 = (bf16[1024,1536]{1,0:T(8,128)(2,1)S(1)}, bf16[256,2176]{1,0:T(8,128)(2,1)S(1)}, bf16[256,2176]{1,0:T(8,128)(2,1)S(1)}) custom-call(s32[6]{0:T(128)S(1)} %stack.21.info_ref, bf16[1024,1536]{1,0:T(8,128)(2,1)} %get-tuple-element.111.qkv_ref, bf16[8,4,128,256]{3,2,1,0:T(8,128)(2,1)} %get-tuple-element.112.prob_ref, ...), custom_call_target="tpu_custom_call" | custom-call | flops 1000 | bytes 1000 | tf_op jit(solution)/shard_map/attend_back/pallas_call | solution.py:55
  63.0 1.8 %collective-permute-done.6.arrived_ref = bf16[512,1024]{1,0:T(8,128)(2,1)S(1)} collective-permute-done((bf16[512,1024]{1,0:T(8,128)(2,1)S(1)}, bf16[512,1024]{1,0:T(8,128)(2,1)S(1)}, u32[]{:S(2)}, u32[]{:S(2)}) %collective-permute-start.6) | collective-permute-done | bytes 1048608 | tf_op jit(solution)/shard_map/ppermute | solution.py:789
  64.7 1.1 split.1
  65.9 1.8 %collective-permute-start.8 = (bf16[256,1024]{1,0:T(8,128)(2,1)S(1)}, bf16[256,1024]{1,0:T(8,128)(2,1)S(1)}, u32[]{:S(2)}, u32[]{:S(2)}) collective-permute-start(bf16[256,1024]{1,0:T(8,128)(2,1)S(1)} %get-tuple-element.131), channel_id=1, source_target_pairs={{0,4},{1,5},{2,3},{3,2},{4,0},{5,1},{6,7},{7,6},{8,12},{9,13},{10,... | collective-permute-start | bytes 1572872 | tf_op jit(solution)/shard_map/ppermute | solution.py:789
  67.7 0.3 add_convert_fusion
  68.0 0.1 fusion
  68.1 1.6 %collective-permute-start.9 = (bf16[128,2176]{1,0:T(8,128)(2,1)S(1)}, bf16[128,2176]{1,0:T(8,128)(2,1)S(1)}, u32[]{:S(2)}, u32[]{:S(2)}) collective-permute-start(bf16[128,2176]{1,0:T(8,128)(2,1)S(1)} %get-tuple-element.174), channel_id=1, source_target_pairs={{0,4},{1,5},{2,10},{3,11},{4,0},{5,1},{6,14},{7,15},{8,12},{9,13},... | collective-permute-start | bytes 1671176 | tf_op jit(solution)/shard_map/ppermute | solution.py:789
  69.7 5.5 %first_back.1 = f32[1024,512]{1,0:T(8,128)} custom-call(s32[6]{0:T(128)S(1)} %stack.21.info_ref, bf16[1024,1536]{1,0:T(8,128)(2,1)S(1)} %get-tuple-element.126.dqkv_ref, bf16[512,1536]{1,0:T(8,128)(2,1)S(1)} %copy-done.1, bf16[1024,512]{1,0:T(8,128)(2,1)} %tok_ref.2, f32[1024,512]{1,0:T(8,128)} %get-tuple-element.127.gres_ref, f32[1,512]{1,0:T(1,128)} %bitcast.11), custom_call_target="tpu_custom_call" | custom-call | flops 1000 | bytes 1000 | tf_op jit(solution)/shard_map/first_back/pallas_call | solution.py:55
  75.2 0.2 add_convert_fusion.2
  75.5 1.8 %collective-permute-start.10 = (bf16[128,1024]{1,0:T(8,128)(2,1)S(1)}, bf16[128,1024]{1,0:T(8,128)(2,1)S(1)}, u32[]{:S(2)}, u32[]{:S(2)}) collective-permute-start(bf16[128,1024]{1,0:T(8,128)(2,1)S(1)} %get-tuple-element.178), channel_id=1, source_target_pairs={{0,8},{1,9},{2,10},{3,11},{4,12},{5,13},{6,14},{7,15},{8,0},{9,1},... | collective-permute-start | bytes 786440 | tf_op jit(solution)/shard_map/ppermute | solution.py:789
  77.3 5.0 %collective-permute-done.9 = bf16[128,2176]{1,0:T(8,128)(2,1)S(1)} collective-permute-done((bf16[128,2176]{1,0:T(8,128)(2,1)S(1)}, bf16[128,2176]{1,0:T(8,128)(2,1)S(1)}, u32[]{:S(2)}, u32[]{:S(2)}) %collective-permute-start.9) | collective-permute-done | bytes 557088 | tf_op jit(solution)/shard_map/ppermute | solution.py:789
  82.3 0.1 add_convert_fusion.1
  82.5 2.1 %collective-permute-start.11 = (bf16[64,2176]{1,0:T(8,128)(2,1)S(1)}, bf16[64,2176]{1,0:T(8,128)(2,1)S(1)}, u32[]{:S(2)}, u32[]{:S(2)}) collective-permute-start(bf16[64,2176]{1,0:T(8,128)(2,1)S(1)} %get-tuple-element.177), channel_id=1, source_target_pairs={{0,1},{1,0},{2,6},{3,7},{4,5},{5,4},{6,2},{7,3},{8,9},{9,8},{10,14... | collective-permute-start | bytes 835592 | tf_op jit(solution)/shard_map/ppermute | solution.py:789
  84.6 5.9 %collective-permute-done.11 = bf16[64,2176]{1,0:T(8,128)(2,1)S(1)} collective-permute-done((bf16[64,2176]{1,0:T(8,128)(2,1)S(1)}, bf16[64,2176]{1,0:T(8,128)(2,1)S(1)}, u32[]{:S(2)}, u32[]{:S(2)}) %collective-permute-start.11) | collective-permute-done | bytes 278560 | tf_op jit(solution)/shard_map/ppermute | solution.py:789
  90.7 2.1 %collective-permute-start.12 = (bf16[32,2176]{1,0:T(8,128)(2,1)S(1)}, bf16[32,2176]{1,0:T(8,128)(2,1)S(1)}, u32[]{:S(2)}, u32[]{:S(2)}) collective-permute-start(bf16[32,2176]{1,0:T(8,128)(2,1)S(1)} %get-tuple-element.180), channel_id=1, source_target_pairs={{0,8},{1,9},{2,3},{3,2},{4,12},{5,13},{6,7},{7,6},{8,0},{9,1},{10,... | collective-permute-start | bytes 417800 | tf_op jit(solution)/shard_map/ppermute | solution.py:789
  92.8 2.6 %collective-permute-start.13 = (bf16[128,1024]{1,0:T(8,128)(2,1)S(1)}, bf16[128,1024]{1,0:T(8,128)(2,1)S(1)}, u32[]{:S(2)}, u32[]{:S(2)}) collective-permute-start(bf16[128,1024]{1,0:T(8,128)(2,1)S(1)} %add_convert_fusion.5), channel_id=1, source_target_pairs={{0,16},{1,17},{2,18},{3,19},{4,20},{5,21},{6,22},{7,23},{8,24},{9,... | collective-permute-start | bytes 786440 | tf_op jit(solution)/shard_map/ppermute | solution.py:789
  95.4 0.8 collective-permute-done.12
  96.3 3.9 %collective-permute-start.14 = (bf16[32,2176]{1,0:T(8,128)(2,1)S(1)}, bf16[32,2176]{1,0:T(8,128)(2,1)S(1)}, u32[]{:S(2)}, u32[]{:S(2)}) collective-permute-start(bf16[32,2176]{1,0:T(8,128)(2,1)S(1)} %add_convert_fusion.7), channel_id=1, source_target_pairs={{0,16},{1,17},{2,18},{3,19},{4,20},{5,21},{6,22},{7,23},{8,24},{9,... | collective-permute-start | bytes 417800 | tf_op jit(solution)/shard_map/ppermute | solution.py:789
  100.1 3.1 %collective-permute-done.13 = bf16[128,1024]{1,0:T(8,128)(2,1)S(1)} collective-permute-done((bf16[128,1024]{1,0:T(8,128)(2,1)S(1)}, bf16[128,1024]{1,0:T(8,128)(2,1)S(1)}, u32[]{:S(2)}, u32[]{:S(2)}) %collective-permute-start.13) | collective-permute-done | bytes 262176 | tf_op jit(solution)/shard_map/ppermute | solution.py:789
  103.3 1.6 %collective-permute-start.15 = (bf16[128,1024]{1,0:T(8,128)(2,1)S(1)}, bf16[128,1024]{1,0:T(8,128)(2,1)S(1)}, u32[]{:S(2)}, u32[]{:S(2)}) collective-permute-start(bf16[128,1024]{1,0:T(8,128)(2,1)S(1)} %add_convert_fusion.4), channel_id=1, source_target_pairs={{0,4},{1,5},{2,6},{3,7},{4,0},{5,1},{6,2},{7,3},{8,12},{9,13},{10,... | collective-permute-start | bytes 786440 | tf_op jit(solution)/shard_map/ppermute | solution.py:789
  104.9 1.4 %collective-permute-done.14 = bf16[32,2176]{1,0:T(8,128)(2,1)S(1)} collective-permute-done((bf16[32,2176]{1,0:T(8,128)(2,1)S(1)}, bf16[32,2176]{1,0:T(8,128)(2,1)S(1)}, u32[]{:S(2)}, u32[]{:S(2)}) %collective-permute-start.14) | collective-permute-done | bytes 139296 | tf_op jit(solution)/shard_map/ppermute | solution.py:789
  106.4 0.8 collective-permute-start.16
  107.2 2.5 %collective-permute-done.15 = bf16[128,1024]{1,0:T(8,128)(2,1)S(1)} collective-permute-done((bf16[128,1024]{1,0:T(8,128)(2,1)S(1)}, bf16[128,1024]{1,0:T(8,128)(2,1)S(1)}, u32[]{:S(2)}, u32[]{:S(2)}) %collective-permute-start.15) | collective-permute-done | bytes 262176 | tf_op jit(solution)/shard_map/ppermute | solution.py:789
  109.8 2.3 %collective-permute-start.18 = (bf16[256,1024]{1,0:T(8,128)(2,1)S(1)}, bf16[256,1024]{1,0:T(8,128)(2,1)S(1)}, u32[]{:S(2)}, u32[]{:S(2)}) collective-permute-start(bf16[256,1024]{1,0:T(8,128)(2,1)S(1)} %constant_dynamic-update-slice_fusion), channel_id=1, source_target_pairs={{0,8},{1,9},{2,10},{3,11},{4,12},{5,13},{6,14},{7,15},{8,0},{9,1},... | collective-permute-start | bytes 1572872 | tf_op jit(solution)/shard_map/ppermute | solution.py:789
  112.1 1.0 collective-permute-done.16
  113.2 6.5 %collective-permute-done.17 = bf16[64,2176]{1,0:T(8,128)(2,1)S(1)} collective-permute-done((bf16[64,2176]{1,0:T(8,128)(2,1)S(1)}, bf16[64,2176]{1,0:T(8,128)(2,1)S(1)}, u32[]{:S(2)}, u32[]{:S(2)}) %collective-permute-start.17) | collective-permute-done | bytes 278560 | tf_op jit(solution)/shard_map/ppermute | solution.py:789
  119.9 0.5 collective-permute-start.21
  120.4 1.0 collective-permute-start.20
  121.4 1.2 collective-permute-done.19.other_ref
  122.5 3.1 %ffn_end.1 = (f32[512,1024]{1,0:T(8,128)}, f32[1024,512]{1,0:T(8,128)}) custom-call(s32[6]{0:T(128)S(1)} %stack.21.info_ref, bf16[512,1024]{1,0:T(8,128)(2,1)S(1)} %constant_dynamic-update-slice_fusion.6.keep_ref, bf16[512,1024]{1,0:T(8,128)(2,1)S(1)} %collective-permute-done.19.other_ref), custom_call_target="tpu_custom_call" | custom-call | flops 1000 | bytes 1000 | tf_op jit(solution)/shard_map/ffn_end/pallas_call | solution.py:55
  125.6 2.0 %attend_end.2 = (f32[512,1536]{1,0:T(8,128)}, f32[512,512]{1,0:T(8,128)}) custom-call(s32[6]{0:T(128)S(1)} %stack.21.info_ref, bf16[128,2176]{1,0:T(8,128)(2,1)S(1)} %constant_dynamic-update-slice_fusion.4.refs_0_, bf16[128,2176]{1,0:T(8,128)(2,1)S(1)} %collective-permute-done.21.refs_1_), custom_call_target="tpu_custom_call" | custom-call | flops 1000 | bytes 1000 | tf_op jit(solution)/shard_map/attend_end/pallas_call | solution.py:55
  127.6 2.3 %collective-permute-done.20.refs_2_ = bf16[128,2176]{1,0:T(8,128)(2,1)S(1)} collective-permute-done((bf16[128,2176]{1,0:T(8,128)(2,1)S(1)}, bf16[128,2176]{1,0:T(8,128)(2,1)S(1)}, u32[]{:S(2)}, u32[]{:S(2)}) %collective-permute-start.20) | collective-permute-done | bytes 557088 | tf_op jit(solution)/shard_map/ppermute | solution.py:789
  129.9 2.0 %collective-permute-done.22.refs_3_ = bf16[128,2176]{1,0:T(8,128)(2,1)S(1)} collective-permute-done((bf16[128,2176]{1,0:T(8,128)(2,1)S(1)}, bf16[128,2176]{1,0:T(8,128)(2,1)S(1)}, u32[]{:S(2)}, u32[]{:S(2)}) %collective-permute-start.22) | collective-permute-done | bytes 557088 | tf_op jit(solution)/shard_map/ppermute | solution.py:789
  131.9 2.7 %attend_end.3 = (f32[512,1536]{1,0:T(8,128)}, f32[512,512]{1,0:T(8,128)}, f32[512]{0:T(512)}, f32[512]{0:T(512)}, f32[512]{0:T(512)}, /*index=5*/f32[512]{0:T(512)}, f32[512]{0:T(512)}, f32[1024]{0:T(1024)}) custom-call(s32[6]{0:T(128)S(1)} %stack.21.info_ref, ...), custom_call_target="tpu_custom_call", output_to_operand_aliasing={{0}: (5, {}), {1}: (6, {})} | custom-call | flops 1000 | bytes 1000 | tf_op jit(solution)/shard_map/attend_end/pallas_call | solution.py:55
  (40 shorter events, 0.8 us)
Async XLA Ops:
  0.6 5.1 %copy-start = (bf16[512,1536]{1,0:T(8,128)(2,1)S(1)}, bf16[512,1536]{1,0:T(8,128)(2,1)}, u32[]{:S(2)}) copy-start(bf16[512,1536]{1,0:T(8,128)(2,1)} %wqkv_ref.5) | copy-start | bytes 4718596
  0.7 5.1 %copy-start.4 = (bf16[512,512]{1,0:T(8,128)(2,1)S(1)}, bf16[512,512]{1,0:T(8,128)(2,1)}, u32[]{:S(2)}) copy-start(bf16[512,512]{1,0:T(8,128)(2,1)} %wout_ref.3) | copy-start | bytes 1572868
  2.6 12.1 %copy-start.2 = (bf16[512,1024]{1,0:T(8,128)(2,1)S(1)}, bf16[512,1024]{1,0:T(8,128)(2,1)}, u32[]{:S(2)}) copy-start(bf16[512,1024]{1,0:T(8,128)(2,1)} %up_ref.3) | copy-start | bytes 3145732
  2.6 12.1 %copy-start.3 = (bf16[1024,512]{1,0:T(8,128)(2,1)S(1)}, bf16[1024,512]{1,0:T(8,128)(2,1)}, u32[]{:S(2)}) copy-start(bf16[1024,512]{1,0:T(8,128)(2,1)} %down_ref.3) | copy-start | bytes 3145732
  2.6 26.5 %collective-permute-start = (bf16[528,512]{1,0:T(8,128)(2,1)S(1)}, bf16[528,512]{1,0:T(8,128)(2,1)S(1)}, u32[]{:S(2)}, u32[]{:S(2)}) collective-permute-start(bf16[528,512]{1,0:T(8,128)(2,1)S(1)} %get-tuple-element.103), channel_id=1, source_target_pairs={{0,1},{1,0},{2,3},{3,2},{4,5},{5,4},{6,7},{7,6},{8,9},{9,8},{10,11... | collective-permute-start | bytes 1622024 | tf_op jit(solution)/shard_map/ppermute | solution.py:789
  5.6 23.5 %collective-permute-start.1 = (bf16[512,512]{1,0:T(8,128)(2,1)S(1)}, bf16[512,512]{1,0:T(8,128)(2,1)S(1)}, u32[]{:S(2)}, u32[]{:S(2)}) collective-permute-start(bf16[512,512]{1,0:T(8,128)(2,1)S(1)} %get-tuple-element.104), channel_id=1, source_target_pairs={{0,1},{1,0},{2,3},{3,2},{4,5},{5,4},{6,7},{7,6},{8,9},{9,8},{10,11... | collective-permute-start | bytes 1572872 | tf_op jit(solution)/shard_map/ppermute | solution.py:789
  29.1 3.4 %collective-permute-start.2 = (bf16[528,512]{1,0:T(8,128)(2,1)S(1)}, bf16[528,512]{1,0:T(8,128)(2,1)S(1)}, u32[]{:S(2)}, u32[]{:S(2)}) collective-permute-start(bf16[528,512]{1,0:T(8,128)(2,1)S(1)} %collective-permute-done.refs_0_), channel_id=1, source_target_pairs={{0,2},{1,3},{2,0},{3,1},{4,6},{5,7},{6,4},{7,5},{8,10},{9,11},{10,... | collective-permute-start | bytes 1622024 | tf_op jit(solution)/shard_map/ppermute | solution.py:789
  29.1 3.4 %collective-permute-start.3 = (bf16[512,512]{1,0:T(8,128)(2,1)S(1)}, bf16[512,512]{1,0:T(8,128)(2,1)S(1)}, u32[]{:S(2)}, u32[]{:S(2)}) collective-permute-start(bf16[512,512]{1,0:T(8,128)(2,1)S(1)} %collective-permute-done.1.refs_2_), channel_id=1, source_target_pairs={{0,2},{1,3},{2,0},{3,1},{4,6},{5,7},{6,4},{7,5},{8,10},{9,11},{10,... | collective-permute-start | bytes 1572872 | tf_op jit(solution)/shard_map/ppermute | solution.py:789
  29.7 16.9 %collective-permute-start.5 = (bf16[512,1024]{1,0:T(8,128)(2,1)}, bf16[512,1024]{1,0:T(8,128)(2,1)S(1)}, u32[]{:S(2)}, u32[]{:S(2)}) collective-permute-start(bf16[512,1024]{1,0:T(8,128)(2,1)} %get-tuple-element.110), channel_id=1, source_target_pairs={{0,2},{1,3},{2,0},{3,1},{4,6},{5,7},{6,4},{7,5},{8,10},{9,11},{10,... | collective-permute-start | bytes 3145736 | tf_op jit(solution)/shard_map/ppermute | solution.py:789
  46.3 2.7 %collective-permute-start.4 = (bf16[512,1024]{1,0:T(8,128)(2,1)S(1)}, bf16[512,1024]{1,0:T(8,128)(2,1)S(1)}, u32[]{:S(2)}, u32[]{:S(2)}) collective-permute-start(bf16[512,1024]{1,0:T(8,128)(2,1)S(1)} %get-tuple-element.109), channel_id=1, source_target_pairs={{0,2},{1,3},{2,0},{3,1},{4,6},{5,7},{6,4},{7,5},{8,10},{9,11},{10,... | collective-permute-start | bytes 3145736 | tf_op jit(solution)/shard_map/ppermute | solution.py:789
  49.9 14.9 %collective-permute-start.6 = (bf16[512,1024]{1,0:T(8,128)(2,1)S(1)}, bf16[512,1024]{1,0:T(8,128)(2,1)S(1)}, u32[]{:S(2)}, u32[]{:S(2)}) collective-permute-start(bf16[512,1024]{1,0:T(8,128)(2,1)S(1)} %join.1), channel_id=1, source_target_pairs={{0,1},{1,0},{2,6},{3,7},{4,5},{5,4},{6,2},{7,3},{8,9},{9,8},{10,14... | collective-permute-start | bytes 3145736 | tf_op jit(solution)/shard_map/ppermute | solution.py:789
  64.7 3.0 %collective-permute-start.7 = (bf16[256,2176]{1,0:T(8,128)(2,1)S(1)}, bf16[256,2176]{1,0:T(8,128)(2,1)S(1)}, u32[]{:S(2)}, u32[]{:S(2)}) collective-permute-start(bf16[256,2176]{1,0:T(8,128)(2,1)S(1)} %get-tuple-element.125), channel_id=1, source_target_pairs={{0,2},{1,3},{2,0},{3,1},{4,6},{5,7},{6,4},{7,5},{8,10},{9,11},{10,... | collective-permute-start | bytes 3342344 | tf_op jit(solution)/shard_map/ppermute | solution.py:789
  65.9 9.3 %collective-permute-start.8 = (bf16[256,1024]{1,0:T(8,128)(2,1)S(1)}, bf16[256,1024]{1,0:T(8,128)(2,1)S(1)}, u32[]{:S(2)}, u32[]{:S(2)}) collective-permute-start(bf16[256,1024]{1,0:T(8,128)(2,1)S(1)} %get-tuple-element.131), channel_id=1, source_target_pairs={{0,4},{1,5},{2,3},{3,2},{4,0},{5,1},{6,7},{7,6},{8,12},{9,13},{10,... | collective-permute-start | bytes 1572872 | tf_op jit(solution)/shard_map/ppermute | solution.py:789
  67.7 2.0 %copy-start.1 = (bf16[512,1536]{1,0:T(8,128)(2,1)S(1)}, bf16[512,1536]{1,0:T(8,128)(2,1)}, u32[]{:S(2)}) copy-start(bf16[512,1536]{1,0:T(8,128)(2,1)} %wqkv_ref.5) | copy-start | bytes 4718596
  68.1 14.2 %collective-permute-start.9 = (bf16[128,2176]{1,0:T(8,128)(2,1)S(1)}, bf16[128,2176]{1,0:T(8,128)(2,1)S(1)}, u32[]{:S(2)}, u32[]{:S(2)}) collective-permute-start(bf16[128,2176]{1,0:T(8,128)(2,1)S(1)} %get-tuple-element.174), channel_id=1, source_target_pairs={{0,4},{1,5},{2,10},{3,11},{4,0},{5,1},{6,14},{7,15},{8,12},{9,13},... | collective-permute-start | bytes 1671176 | tf_op jit(solution)/shard_map/ppermute | solution.py:789
  75.5 9.1 %collective-permute-start.10 = (bf16[128,1024]{1,0:T(8,128)(2,1)S(1)}, bf16[128,1024]{1,0:T(8,128)(2,1)S(1)}, u32[]{:S(2)}, u32[]{:S(2)}) collective-permute-start(bf16[128,1024]{1,0:T(8,128)(2,1)S(1)} %get-tuple-element.178), channel_id=1, source_target_pairs={{0,8},{1,9},{2,10},{3,11},{4,12},{5,13},{6,14},{7,15},{8,0},{9,1},... | collective-permute-start | bytes 786440 | tf_op jit(solution)/shard_map/ppermute | solution.py:789
  82.5 8.1 %collective-permute-start.11 = (bf16[64,2176]{1,0:T(8,128)(2,1)S(1)}, bf16[64,2176]{1,0:T(8,128)(2,1)S(1)}, u32[]{:S(2)}, u32[]{:S(2)}) collective-permute-start(bf16[64,2176]{1,0:T(8,128)(2,1)S(1)} %get-tuple-element.177), channel_id=1, source_target_pairs={{0,1},{1,0},{2,6},{3,7},{4,5},{5,4},{6,2},{7,3},{8,9},{9,8},{10,14... | collective-permute-start | bytes 835592 | tf_op jit(solution)/shard_map/ppermute | solution.py:789
  90.7 5.5 %collective-permute-start.12 = (bf16[32,2176]{1,0:T(8,128)(2,1)S(1)}, bf16[32,2176]{1,0:T(8,128)(2,1)S(1)}, u32[]{:S(2)}, u32[]{:S(2)}) collective-permute-start(bf16[32,2176]{1,0:T(8,128)(2,1)S(1)} %get-tuple-element.180), channel_id=1, source_target_pairs={{0,8},{1,9},{2,3},{3,2},{4,12},{5,13},{6,7},{7,6},{8,0},{9,1},{10,... | collective-permute-start | bytes 417800 | tf_op jit(solution)/shard_map/ppermute | solution.py:789
  92.8 10.5 %collective-permute-start.13 = (bf16[128,1024]{1,0:T(8,128)(2,1)S(1)}, bf16[128,1024]{1,0:T(8,128)(2,1)S(1)}, u32[]{:S(2)}, u32[]{:S(2)}) collective-permute-start(bf16[128,1024]{1,0:T(8,128)(2,1)S(1)} %add_convert_fusion.5), channel_id=1, source_target_pairs={{0,16},{1,17},{2,18},{3,19},{4,20},{5,21},{6,22},{7,23},{8,24},{9,... | collective-permute-start | bytes 786440 | tf_op jit(solution)/shard_map/ppermute | solution.py:789
  96.3 10.1 %collective-permute-start.14 = (bf16[32,2176]{1,0:T(8,128)(2,1)S(1)}, bf16[32,2176]{1,0:T(8,128)(2,1)S(1)}, u32[]{:S(2)}, u32[]{:S(2)}) collective-permute-start(bf16[32,2176]{1,0:T(8,128)(2,1)S(1)} %add_convert_fusion.7), channel_id=1, source_target_pairs={{0,16},{1,17},{2,18},{3,19},{4,20},{5,21},{6,22},{7,23},{8,24},{9,... | collective-permute-start | bytes 417800 | tf_op jit(solution)/shard_map/ppermute | solution.py:789
  103.3 6.4 %collective-permute-start.15 = (bf16[128,1024]{1,0:T(8,128)(2,1)S(1)}, bf16[128,1024]{1,0:T(8,128)(2,1)S(1)}, u32[]{:S(2)}, u32[]{:S(2)}) collective-permute-start(bf16[128,1024]{1,0:T(8,128)(2,1)S(1)} %add_convert_fusion.4), channel_id=1, source_target_pairs={{0,4},{1,5},{2,6},{3,7},{4,0},{5,1},{6,2},{7,3},{8,12},{9,13},{10,... | collective-permute-start | bytes 786440 | tf_op jit(solution)/shard_map/ppermute | solution.py:789
  106.4 6.7 %collective-permute-start.16 = (bf16[32,2176]{1,0:T(8,128)(2,1)S(1)}, bf16[32,2176]{1,0:T(8,128)(2,1)S(1)}, u32[]{:S(2)}, u32[]{:S(2)}) collective-permute-start(bf16[32,2176]{1,0:T(8,128)(2,1)S(1)} %add_convert_fusion.6), channel_id=1, source_target_pairs={{0,8},{1,9},{2,6},{3,7},{4,12},{5,13},{6,2},{7,3},{8,0},{9,1},{10,... | collective-permute-start | bytes 417800 | tf_op jit(solution)/shard_map/ppermute | solution.py:789
  109.8 10.0 %collective-permute-start.18 = (bf16[256,1024]{1,0:T(8,128)(2,1)S(1)}, bf16[256,1024]{1,0:T(8,128)(2,1)S(1)}, u32[]{:S(2)}, u32[]{:S(2)}) collective-permute-start(bf16[256,1024]{1,0:T(8,128)(2,1)S(1)} %constant_dynamic-update-slice_fusion), channel_id=1, source_target_pairs={{0,8},{1,9},{2,10},{3,11},{4,12},{5,13},{6,14},{7,15},{8,0},{9,1},... | collective-permute-start | bytes 1572872 | tf_op jit(solution)/shard_map/ppermute | solution.py:789
  113.1 6.6 %collective-permute-start.17 = (bf16[64,2176]{1,0:T(8,128)(2,1)S(1)}, bf16[64,2176]{1,0:T(8,128)(2,1)S(1)}, u32[]{:S(2)}, u32[]{:S(2)}) collective-permute-start(bf16[64,2176]{1,0:T(8,128)(2,1)S(1)} %constant_dynamic-update-slice_fusion.2), channel_id=1, source_target_pairs={{0,1},{1,0},{2,3},{3,2},{4,5},{5,4},{6,7},{7,6},{8,9},{9,8},{10,11... | collective-permute-start | bytes 835592 | tf_op jit(solution)/shard_map/ppermute | solution.py:789
  119.8 2.7 %collective-permute-start.19 = (bf16[512,1024]{1,0:T(8,128)(2,1)S(1)}, bf16[512,1024]{1,0:T(8,128)(2,1)S(1)}, u32[]{:S(2)}, u32[]{:S(2)}) collective-permute-start(bf16[512,1024]{1,0:T(8,128)(2,1)S(1)} %constant_dynamic-update-slice_fusion.6.keep_ref), channel_id=1, source_target_pairs={{0,2},{1,3},{2,0},{3,1},{4,6},{5,7},{6,4},{7,5},{8,10},{9,11},{10,... | collective-permute-start | bytes 3145736 | tf_op jit(solution)/shard_map/ppermute | solution.py:789
  119.9 5.7 %collective-permute-start.21 = (bf16[128,2176]{1,0:T(8,128)(2,1)S(1)}, bf16[128,2176]{1,0:T(8,128)(2,1)S(1)}, u32[]{:S(2)}, u32[]{:S(2)}) collective-permute-start(bf16[128,2176]{1,0:T(8,128)(2,1)S(1)} %constant_dynamic-update-slice_fusion.4.refs_0_), channel_id=1, source_target_pairs={{0,2},{1,3},{2,0},{3,1},{4,6},{5,7},{6,4},{7,5},{8,10},{9,11},{10,... | collective-permute-start | bytes 1671176 | tf_op jit(solution)/shard_map/ppermute | solution.py:789
  120.4 9.5 %collective-permute-start.20 = (bf16[128,2176]{1,0:T(8,128)(2,1)S(1)}, bf16[128,2176]{1,0:T(8,128)(2,1)S(1)}, u32[]{:S(2)}, u32[]{:S(2)}) collective-permute-start(bf16[128,2176]{1,0:T(8,128)(2,1)S(1)} %constant_dynamic-update-slice_fusion.4.refs_0_), channel_id=1, source_target_pairs={{0,4},{1,5},{2,10},{3,11},{4,0},{5,1},{6,14},{7,15},{8,12},{9,13},... | collective-permute-start | bytes 1671176 | tf_op jit(solution)/shard_map/ppermute | solution.py:789
  129.9 2.0 %collective-permute-start.22 = (bf16[128,2176]{1,0:T(8,128)(2,1)S(1)}, bf16[128,2176]{1,0:T(8,128)(2,1)S(1)}, u32[]{:S(2)}, u32[]{:S(2)}) collective-permute-start(bf16[128,2176]{1,0:T(8,128)(2,1)S(1)} %collective-permute-done.20.refs_2_), channel_id=1, source_target_pairs={{0,2},{1,3},{2,0},{3,1},{4,6},{5,7},{6,4},{7,5},{8,10},{9,11},{10,... | collective-permute-start | bytes 1671176 | tf_op jit(solution)/shard_map/ppermute | solution.py:789

commit v12 on v11

--- a/solution.py
+++ b/solution.py
@@ -366,15 +366,23 @@
     for t in range(n // toks):
         rows = slice(t * toks, (t + 1) * toks)
         sec = sec_ref[rows, :]
-        pre = mm(sec, up_ref[...]) + bias_ref[...].astype(F32)[:1]
+        every = up_ref.shape[1]
+        parts_of = [slice(c * every // 2, (c + 1) * every // 2) for c in range(2)]
+        pres = [mm(sec, up_ref[:, c]) + bias_ref[:, c].astype(F32)[:1] for c in parts_of]
         if t == 0:
             arrived(second)
         dy = dy_ref[rows, :]
-        dhid = mm_nt(dy, down_ref[...])
-        hid, slope = gelu_pair(pre)
-        hid = hid.astype(BF)
-        dpre = (dhid * slope).astype(BF)
-        more = (mm(sec.T, dpre), mm(dy.T, hid), jnp.sum(dpre.astype(F32), axis=0, keepdims=True))
+        dhids = [mm_nt(dy, down_ref[c, :]) for c in parts_of]
+        hids, dpres, grads_up, grads_down = [], [], [], []
+        sec_t, dy_t = sec.T, dy.T
+        for pre, dhid in zip(pres, dhids):
+            hid, slope = gelu_pair(pre)
+            hids.append(hid.astype(BF))
+            dpres.append((dhid * slope).astype(BF))
+            grads_up.append(mm(sec_t, dpres[-1]))
+            grads_down.append(mm(dy_t, hids[-1]))
+        hid, dpre = jnp.concatenate(hids, axis=1), jnp.concatenate(dpres, axis=1)
+        more = (jnp.concatenate(grads_up, axis=1), jnp.concatenate(grads_down, axis=1), jnp.sum(dpre.astype(F32), axis=0, keepdims=True))
         if t:
             more = (grad_up + more[0], grad_down + more[1], sums + more[2])
         grad_up, grad_down, sums = more
@@ -872,10 +880,11 @@
     out_part, dsec_part, own_keep, own_send, bias_own = ffn_own(
         info, ff_in_tables, mixing, second, cotangent, w_up, b_up, w_down
     )
-    own_send, fetched = after(own_send, fetched)
-    chunks = []
-    for up, down in fetched[1:]:
-        chunks += [(up, down), (swap(up, core_mask), swap(down, core_mask))]
+    ups, downs = [u for u, _ in fetched[1:]], [d for _, d in fetched[1:]]
+    own_send, ups = after(own_send, ups)
+    away_ups = [swap(u, core_mask) for u in ups]
+    away_downs = [swap(d, core_mask) for d in downs]
+    chunks = [pair for here in zip(zip(ups, downs), zip(away_ups, away_downs)) for pair in here]
     rest = ffn_rest(
         info, ff_in_tables, mixing, second, cotangent, out_part, dsec_part, residual, mixed, row(b_down), g2, w_out, own_keep,
         chunks,

time: 135 us -> 134 us (level)
  no operation moved by 1% of the time
where the time goes in v12:
time: 134 us
  Pallas kernels  61.8 us (46%)
  waiting for transfers between devices  41.5 us (31%)
  starting transfers between devices  27.8 us (21%)
    pallas_call x9, Pallas kernels, call(): pl.pallas_call(kernel, grid_spec=pltpu.PrefetchScalarGridSpec(num_scalar_...  59.9 us
    ppermute x23, waiting for transfers between devices, swap(): return lax.ppermute(value, AXES, pairs)  41.5 us
    ppermute x23, starting transfers between devices, swap(): return lax.ppermute(value, AXES, pairs)  27.8 us
  transfers between devices with their start and end apart: 23, of which 15 were waited for; matrix products, arithmetic and copies ran while one was open for 1% of the time, Pallas kernels for 42%

profile of v12, /device:TPU:0, one launch (start us, length us, event | category | flops | bytes accessed | tf_op | source)
XLA Modules:
  0.0 133.6 jit_solution(9550923307359445717)
XLA Ops:
  0.7 0.1 stack.21.info_ref
  0.8 1.8 %pack.1 = (bf16[528,512]{1,0:T(8,128)(2,1)S(1)}, bf16[512,512]{1,0:T(8,128)(2,1)S(1)}) custom-call(s32[6]{0:T(128)S(1)} %stack.21.info_ref, bf16[512,1024]{1,0:T(8,128)(2,1)} %up_ref.3, bf16[1024]{0:T(1024)(128)(2,1)} %bias_ref.3, bf16[1024,512]{1,0:T(8,128)(2,1)} %down_ref.3), custom_call_target="tpu_custom_call" | custom-call | flops 1000 | bytes 1000 | tf_op jit(solution)/shard_map/pack/pallas_call | solution.py:55
  2.6 3.0 %collective-permute-start = (bf16[528,512]{1,0:T(8,128)(2,1)S(1)}, bf16[528,512]{1,0:T(8,128)(2,1)S(1)}, u32[]{:S(2)}, u32[]{:S(2)}) collective-permute-start(bf16[528,512]{1,0:T(8,128)(2,1)S(1)} %get-tuple-element.102), channel_id=1, source_target_pairs={{0,1},{1,0},{2,3},{3,2},{4,5},{5,4},{6,7},{7,6},{8,9},{9,8},{10,11... | collective-permute-start | bytes 1622024 | tf_op jit(solution)/shard_map/ppermute | solution.py:797
  5.6 0.1 collective-permute-start.2
  5.7 9.0 %attend.1 = (bf16[1024,1536]{1,0:T(8,128)(2,1)}, bf16[8,4,128,256]{3,2,1,0:T(8,128)(2,1)}, bf16[1024,512]{1,0:T(8,128)(2,1)}, f32[1024,512]{1,0:T(8,128)}, bf16[1024,512]{1,0:T(8,128)(2,1)S(1)}) custom-call(s32[6]{0:T(128)S(1)} %stack.21.info_ref, bf16[1024,512]{1,0:T(8,128)(2,1)} %tok_ref.2, f32[1,512]{1,0:T(1,128)} %bitcast.9, f32[1,512]{1,0:T(1,128)} %bitcast.14, ...), custom_call_target="tpu_custom_call" | custom-call | flops 1000 | bytes 1000 | tf_op jit(solution)/shard_map/attend/pallas_call | solution.py:55
  14.7 11.1 %ffn_own.1 = (f32[1024,512]{1,0:T(8,128)S(1)}, f32[1024,512]{1,0:T(8,128)S(1)}, bf16[512,1024]{1,0:T(8,128)(2,1)}, bf16[512,1024]{1,0:T(8,128)(2,1)}, f32[2,512]{1,0:T(2,128)}) custom-call(s32[6]{0:T(128)S(1)} %stack.21.info_ref, bf16[1024,512]{1,0:T(8,128)(2,1)S(1)} %get-tuple-element.95.sec_ref.sec_in, bf16[1024,512]{1,0:T(8,128)(2,1)} %dy_in.1, ...), custom_call_target="tpu_custom_call" | custom-call | flops 1000 | bytes 1000 | tf_op jit(solution)/shard_map/ffn_own/pallas_call | solution.py:55
  25.9 3.3 %collective-permute-done.2.refs_2_ = bf16[512,512]{1,0:T(8,128)(2,1)S(1)} collective-permute-done((bf16[512,512]{1,0:T(8,128)(2,1)S(1)}, bf16[512,512]{1,0:T(8,128)(2,1)S(1)}, u32[]{:S(2)}, u32[]{:S(2)}) %collective-permute-start.2) | collective-permute-done | bytes 524320 | tf_op jit(solution)/shard_map/ppermute | solution.py:797
  29.1 0.5 collective-permute-start.5
  29.6 2.1 %collective-permute-done.3.refs_3_ = bf16[512,512]{1,0:T(8,128)(2,1)S(1)} collective-permute-done((bf16[512,512]{1,0:T(8,128)(2,1)S(1)}, bf16[512,512]{1,0:T(8,128)(2,1)S(1)}, u32[]{:S(2)}, u32[]{:S(2)}) %collective-permute-start.3) | collective-permute-done | bytes 524320 | tf_op jit(solution)/shard_map/ppermute | solution.py:797
  31.8 13.4 %ffn_rest.1 = (bf16[1024,512]{1,0:T(8,128)(2,1)}, f32[1024,512]{1,0:T(8,128)}, bf16[1024,512]{1,0:T(8,128)(2,1)}, f32[8,512]{1,0:T(8,128)}, f32[512,512]{1,0:T(8...) custom-call(s32[6]{0:T(128)S(1)} %stack.21.info_ref, ...), custom_call_target="tpu_custom_call" | custom-call | flops 1000 | bytes 1000 | tf_op jit(solution)/shard_map/ffn_rest/pallas_call | solution.py:55
  45.2 0.2 collective-permute-start.4
  45.4 2.5 %collective-permute-done.4.got_ref = bf16[512,1024]{1,0:T(8,128)(2,1)S(1)} collective-permute-done((bf16[512,1024]{1,0:T(8,128)(2,1)S(1)}, bf16[512,1024]{1,0:T(8,128)(2,1)S(1)}, u32[]{:S(2)}, u32[]{:S(2)}) %collective-permute-start.4) | collective-permute-done | bytes 1048608 | tf_op jit(solution)/shard_map/ppermute | solution.py:797
  47.9 0.8 join.1
  48.7 1.8 %collective-permute-start.6 = (bf16[512,1024]{1,0:T(8,128)(2,1)S(1)}, bf16[512,1024]{1,0:T(8,128)(2,1)S(1)}, u32[]{:S(2)}, u32[]{:S(2)}) collective-permute-start(bf16[512,1024]{1,0:T(8,128)(2,1)S(1)} %join.1), channel_id=1, source_target_pairs={{0,1},{1,0},{2,6},{3,7},{4,5},{5,4},{6,2},{7,3},{8,9},{9,8},{10,14... | collective-permute-start | bytes 3145736 | tf_op jit(solution)/shard_map/ppermute | solution.py:797
  50.5 11.3 %attend_back.1 = (bf16[1024,1536]{1,0:T(8,128)(2,1)S(1)}, bf16[256,2176]{1,0:T(8,128)(2,1)S(1)}, bf16[256,2176]{1,0:T(8,128)(2,1)S(1)}) custom-call(s32[6]{0:T(128)S(1)} %stack.21.info_ref, bf16[1024,1536]{1,0:T(8,128)(2,1)} %get-tuple-element.109.qkv_ref, bf16[8,4,128,256]{3,2,1,0:T(8,128)(2,1)} %get-tuple-element.110.prob_ref, ...), custom_call_target="tpu_custom_call" | custom-call | flops 1000 | bytes 1000 | tf_op jit(solution)/shard_map/attend_back/pallas_call | solution.py:55
  61.8 1.8 %collective-permute-done.6.arrived_ref = bf16[512,1024]{1,0:T(8,128)(2,1)S(1)} collective-permute-done((bf16[512,1024]{1,0:T(8,128)(2,1)S(1)}, bf16[512,1024]{1,0:T(8,128)(2,1)S(1)}, u32[]{:S(2)}, u32[]{:S(2)}) %collective-permute-start.6) | collective-permute-done | bytes 1048608 | tf_op jit(solution)/shard_map/ppermute | solution.py:797
  63.6 1.1 split.1
  64.7 1.8 %collective-permute-start.8 = (bf16[256,1024]{1,0:T(8,128)(2,1)S(1)}, bf16[256,1024]{1,0:T(8,128)(2,1)S(1)}, u32[]{:S(2)}, u32[]{:S(2)}) collective-permute-start(bf16[256,1024]{1,0:T(8,128)(2,1)S(1)} %get-tuple-element.129), channel_id=1, source_target_pairs={{0,4},{1,5},{2,3},{3,2},{4,0},{5,1},{6,7},{7,6},{8,12},{9,13},{10,... | collective-permute-start | bytes 1572872 | tf_op jit(solution)/shard_map/ppermute | solution.py:797
  66.6 0.3 add_convert_fusion
  66.8 0.1 fusion
  66.9 1.6 %collective-permute-start.9 = (bf16[128,2176]{1,0:T(8,128)(2,1)S(1)}, bf16[128,2176]{1,0:T(8,128)(2,1)S(1)}, u32[]{:S(2)}, u32[]{:S(2)}) collective-permute-start(bf16[128,2176]{1,0:T(8,128)(2,1)S(1)} %get-tuple-element.172), channel_id=1, source_target_pairs={{0,4},{1,5},{2,10},{3,11},{4,0},{5,1},{6,14},{7,15},{8,12},{9,13},... | collective-permute-start | bytes 1671176 | tf_op jit(solution)/shard_map/ppermute | solution.py:797
  68.5 5.5 %first_back.1 = f32[1024,512]{1,0:T(8,128)} custom-call(s32[6]{0:T(128)S(1)} %stack.21.info_ref, bf16[1024,1536]{1,0:T(8,128)(2,1)S(1)} %get-tuple-element.124.dqkv_ref, bf16[512,1536]{1,0:T(8,128)(2,1)S(1)} %copy-done.1, bf16[1024,512]{1,0:T(8,128)(2,1)} %tok_ref.2, f32[1024,512]{1,0:T(8,128)} %get-tuple-element.125.gres_ref, f32[1,512]{1,0:T(1,128)} %bitcast.11), custom_call_target="tpu_custom_call" | custom-call | flops 1000 | bytes 1000 | tf_op jit(solution)/shard_map/first_back/pallas_call | solution.py:55
  74.1 0.2 add_convert_fusion.2
  74.3 1.8 %collective-permute-start.10 = (bf16[128,1024]{1,0:T(8,128)(2,1)S(1)}, bf16[128,1024]{1,0:T(8,128)(2,1)S(1)}, u32[]{:S(2)}, u32[]{:S(2)}) collective-permute-start(bf16[128,1024]{1,0:T(8,128)(2,1)S(1)} %get-tuple-element.176), channel_id=1, source_target_pairs={{0,8},{1,9},{2,10},{3,11},{4,12},{5,13},{6,14},{7,15},{8,0},{9,1},... | collective-permute-start | bytes 786440 | tf_op jit(solution)/shard_map/ppermute | solution.py:797
  76.1 5.0 %collective-permute-done.9 = bf16[128,2176]{1,0:T(8,128)(2,1)S(1)} collective-permute-done((bf16[128,2176]{1,0:T(8,128)(2,1)S(1)}, bf16[128,2176]{1,0:T(8,128)(2,1)S(1)}, u32[]{:S(2)}, u32[]{:S(2)}) %collective-permute-start.9) | collective-permute-done | bytes 557088 | tf_op jit(solution)/shard_map/ppermute | solution.py:797
  81.1 0.1 add_convert_fusion.1
  81.3 2.1 %collective-permute-start.11 = (bf16[64,2176]{1,0:T(8,128)(2,1)S(1)}, bf16[64,2176]{1,0:T(8,128)(2,1)S(1)}, u32[]{:S(2)}, u32[]{:S(2)}) collective-permute-start(bf16[64,2176]{1,0:T(8,128)(2,1)S(1)} %get-tuple-element.175), channel_id=1, source_target_pairs={{0,1},{1,0},{2,6},{3,7},{4,5},{5,4},{6,2},{7,3},{8,9},{9,8},{10,14... | collective-permute-start | bytes 835592 | tf_op jit(solution)/shard_map/ppermute | solution.py:797
  83.5 5.9 %collective-permute-done.11 = bf16[64,2176]{1,0:T(8,128)(2,1)S(1)} collective-permute-done((bf16[64,2176]{1,0:T(8,128)(2,1)S(1)}, bf16[64,2176]{1,0:T(8,128)(2,1)S(1)}, u32[]{:S(2)}, u32[]{:S(2)}) %collective-permute-start.11) | collective-permute-done | bytes 278560 | tf_op jit(solution)/shard_map/ppermute | solution.py:797
  89.5 2.1 %collective-permute-start.12 = (bf16[32,2176]{1,0:T(8,128)(2,1)S(1)}, bf16[32,2176]{1,0:T(8,128)(2,1)S(1)}, u32[]{:S(2)}, u32[]{:S(2)}) collective-permute-start(bf16[32,2176]{1,0:T(8,128)(2,1)S(1)} %get-tuple-element.178), channel_id=1, source_target_pairs={{0,8},{1,9},{2,3},{3,2},{4,12},{5,13},{6,7},{7,6},{8,0},{9,1},{10,... | collective-permute-start | bytes 417800 | tf_op jit(solution)/shard_map/ppermute | solution.py:797
  91.7 2.6 %collective-permute-start.13 = (bf16[128,1024]{1,0:T(8,128)(2,1)S(1)}, bf16[128,1024]{1,0:T(8,128)(2,1)S(1)}, u32[]{:S(2)}, u32[]{:S(2)}) collective-permute-start(bf16[128,1024]{1,0:T(8,128)(2,1)S(1)} %add_convert_fusion.5), channel_id=1, source_target_pairs={{0,16},{1,17},{2,18},{3,19},{4,20},{5,21},{6,22},{7,23},{8,24},{9,... | collective-permute-start | bytes 786440 | tf_op jit(solution)/shard_map/ppermute | solution.py:797
  94.2 0.8 collective-permute-done.12
  95.1 3.9 %collective-permute-start.14 = (bf16[32,2176]{1,0:T(8,128)(2,1)S(1)}, bf16[32,2176]{1,0:T(8,128)(2,1)S(1)}, u32[]{:S(2)}, u32[]{:S(2)}) collective-permute-start(bf16[32,2176]{1,0:T(8,128)(2,1)S(1)} %add_convert_fusion.7), channel_id=1, source_target_pairs={{0,16},{1,17},{2,18},{3,19},{4,20},{5,21},{6,22},{7,23},{8,24},{9,... | collective-permute-start | bytes 417800 | tf_op jit(solution)/shard_map/ppermute | solution.py:797
  99.0 3.1 %collective-permute-done.13 = bf16[128,1024]{1,0:T(8,128)(2,1)S(1)} collective-permute-done((bf16[128,1024]{1,0:T(8,128)(2,1)S(1)}, bf16[128,1024]{1,0:T(8,128)(2,1)S(1)}, u32[]{:S(2)}, u32[]{:S(2)}) %collective-permute-start.13) | collective-permute-done | bytes 262176 | tf_op jit(solution)/shard_map/ppermute | solution.py:797
  102.2 1.6 %collective-permute-start.15 = (bf16[128,1024]{1,0:T(8,128)(2,1)S(1)}, bf16[128,1024]{1,0:T(8,128)(2,1)S(1)}, u32[]{:S(2)}, u32[]{:S(2)}) collective-permute-start(bf16[128,1024]{1,0:T(8,128)(2,1)S(1)} %add_convert_fusion.4), channel_id=1, source_target_pairs={{0,4},{1,5},{2,6},{3,7},{4,0},{5,1},{6,2},{7,3},{8,12},{9,13},{10,... | collective-permute-start | bytes 786440 | tf_op jit(solution)/shard_map/ppermute | solution.py:797
  103.8 1.4 %collective-permute-done.14 = bf16[32,2176]{1,0:T(8,128)(2,1)S(1)} collective-permute-done((bf16[32,2176]{1,0:T(8,128)(2,1)S(1)}, bf16[32,2176]{1,0:T(8,128)(2,1)S(1)}, u32[]{:S(2)}, u32[]{:S(2)}) %collective-permute-start.14) | collective-permute-done | bytes 139296 | tf_op jit(solution)/shard_map/ppermute | solution.py:797
  105.2 0.8 collective-permute-start.16
  106.1 2.5 %collective-permute-done.15 = bf16[128,1024]{1,0:T(8,128)(2,1)S(1)} collective-permute-done((bf16[128,1024]{1,0:T(8,128)(2,1)S(1)}, bf16[128,1024]{1,0:T(8,128)(2,1)S(1)}, u32[]{:S(2)}, u32[]{:S(2)}) %collective-permute-start.15) | collective-permute-done | bytes 262176 | tf_op jit(solution)/shard_map/ppermute | solution.py:797
  108.6 2.3 %collective-permute-start.18 = (bf16[256,1024]{1,0:T(8,128)(2,1)S(1)}, bf16[256,1024]{1,0:T(8,128)(2,1)S(1)}, u32[]{:S(2)}, u32[]{:S(2)}) collective-permute-start(bf16[256,1024]{1,0:T(8,128)(2,1)S(1)} %constant_dynamic-update-slice_fusion), channel_id=1, source_target_pairs={{0,8},{1,9},{2,10},{3,11},{4,12},{5,13},{6,14},{7,15},{8,0},{9,1},... | collective-permute-start | bytes 1572872 | tf_op jit(solution)/shard_map/ppermute | solution.py:797
  110.9 1.0 collective-permute-done.16
  112.0 6.5 %collective-permute-done.17 = bf16[64,2176]{1,0:T(8,128)(2,1)S(1)} collective-permute-done((bf16[64,2176]{1,0:T(8,128)(2,1)S(1)}, bf16[64,2176]{1,0:T(8,128)(2,1)S(1)}, u32[]{:S(2)}, u32[]{:S(2)}) %collective-permute-start.17) | collective-permute-done | bytes 278560 | tf_op jit(solution)/shard_map/ppermute | solution.py:797
  118.7 0.5 collective-permute-start.21
  119.2 1.0 collective-permute-start.20
  120.2 1.2 collective-permute-done.19.other_ref
  121.4 3.1 %ffn_end.1 = (f32[512,1024]{1,0:T(8,128)}, f32[1024,512]{1,0:T(8,128)}) custom-call(s32[6]{0:T(128)S(1)} %stack.21.info_ref, bf16[512,1024]{1,0:T(8,128)(2,1)S(1)} %constant_dynamic-update-slice_fusion.6.keep_ref, bf16[512,1024]{1,0:T(8,128)(2,1)S(1)} %collective-permute-done.19.other_ref), custom_call_target="tpu_custom_call" | custom-call | flops 1000 | bytes 1000 | tf_op jit(solution)/shard_map/ffn_end/pallas_call | solution.py:55
  124.4 2.0 %attend_end.2 = (f32[512,1536]{1,0:T(8,128)}, f32[512,512]{1,0:T(8,128)}) custom-call(s32[6]{0:T(128)S(1)} %stack.21.info_ref, bf16[128,2176]{1,0:T(8,128)(2,1)S(1)} %constant_dynamic-update-slice_fusion.4.refs_0_, bf16[128,2176]{1,0:T(8,128)(2,1)S(1)} %collective-permute-done.21.refs_1_), custom_call_target="tpu_custom_call" | custom-call | flops 1000 | bytes 1000 | tf_op jit(solution)/shard_map/attend_end/pallas_call | solution.py:55
  126.4 2.3 %collective-permute-done.20.refs_2_ = bf16[128,2176]{1,0:T(8,128)(2,1)S(1)} collective-permute-done((bf16[128,2176]{1,0:T(8,128)(2,1)S(1)}, bf16[128,2176]{1,0:T(8,128)(2,1)S(1)}, u32[]{:S(2)}, u32[]{:S(2)}) %collective-permute-start.20) | collective-permute-done | bytes 557088 | tf_op jit(solution)/shard_map/ppermute | solution.py:797
  128.8 2.0 %collective-permute-done.22.refs_3_ = bf16[128,2176]{1,0:T(8,128)(2,1)S(1)} collective-permute-done((bf16[128,2176]{1,0:T(8,128)(2,1)S(1)}, bf16[128,2176]{1,0:T(8,128)(2,1)S(1)}, u32[]{:S(2)}, u32[]{:S(2)}) %collective-permute-start.22) | collective-permute-done | bytes 557088 | tf_op jit(solution)/shard_map/ppermute | solution.py:797
  130.7 2.7 %attend_end.3 = (f32[512,1536]{1,0:T(8,128)}, f32[512,512]{1,0:T(8,128)}, f32[512]{0:T(512)}, f32[512]{0:T(512)}, f32[512]{0:T(512)}, /*index=5*/f32[512]{0:T(512)}, f32[512]{0:T(512)}, f32[1024]{0:T(1024)}) custom-call(s32[6]{0:T(128)S(1)} %stack.21.info_ref, ...), custom_call_target="tpu_custom_call", output_to_operand_aliasing={{0}: (5, {}), {1}: (6, {})} | custom-call | flops 1000 | bytes 1000 | tf_op jit(solution)/shard_map/attend_end/pallas_call | solution.py:55
  (40 shorter events, 0.8 us)
Async XLA Ops:
  0.6 5.1 %copy-start = (bf16[512,1536]{1,0:T(8,128)(2,1)S(1)}, bf16[512,1536]{1,0:T(8,128)(2,1)}, u32[]{:S(2)}) copy-start(bf16[512,1536]{1,0:T(8,128)(2,1)} %wqkv_ref.5) | copy-start | bytes 4718596
  0.7 5.1 %copy-start.4 = (bf16[512,512]{1,0:T(8,128)(2,1)S(1)}, bf16[512,512]{1,0:T(8,128)(2,1)}, u32[]{:S(2)}) copy-start(bf16[512,512]{1,0:T(8,128)(2,1)} %wout_ref.3) | copy-start | bytes 1572868
  2.6 12.1 %copy-start.2 = (bf16[512,1024]{1,0:T(8,128)(2,1)S(1)}, bf16[512,1024]{1,0:T(8,128)(2,1)}, u32[]{:S(2)}) copy-start(bf16[512,1024]{1,0:T(8,128)(2,1)} %up_ref.3) | copy-start | bytes 3145732
  2.6 12.1 %copy-start.3 = (bf16[1024,512]{1,0:T(8,128)(2,1)S(1)}, bf16[1024,512]{1,0:T(8,128)(2,1)}, u32[]{:S(2)}) copy-start(bf16[1024,512]{1,0:T(8,128)(2,1)} %down_ref.3) | copy-start | bytes 3145732
  2.6 23.2 %collective-permute-start = (bf16[528,512]{1,0:T(8,128)(2,1)S(1)}, bf16[528,512]{1,0:T(8,128)(2,1)S(1)}, u32[]{:S(2)}, u32[]{:S(2)}) collective-permute-start(bf16[528,512]{1,0:T(8,128)(2,1)S(1)} %get-tuple-element.102), channel_id=1, source_target_pairs={{0,1},{1,0},{2,3},{3,2},{4,5},{5,4},{6,7},{7,6},{8,9},{9,8},{10,11... | collective-permute-start | bytes 1622024 | tf_op jit(solution)/shard_map/ppermute | solution.py:797
  5.6 23.5 %collective-permute-start.2 = (bf16[512,512]{1,0:T(8,128)(2,1)S(1)}, bf16[512,512]{1,0:T(8,128)(2,1)S(1)}, u32[]{:S(2)}, u32[]{:S(2)}) collective-permute-start(bf16[512,512]{1,0:T(8,128)(2,1)S(1)} %get-tuple-element.104), channel_id=1, source_target_pairs={{0,1},{1,0},{2,3},{3,2},{4,5},{5,4},{6,7},{7,6},{8,9},{9,8},{10,11... | collective-permute-start | bytes 1572872 | tf_op jit(solution)/shard_map/ppermute | solution.py:797
  25.8 5.9 %collective-permute-start.1 = (bf16[528,512]{1,0:T(8,128)(2,1)S(1)}, bf16[528,512]{1,0:T(8,128)(2,1)S(1)}, u32[]{:S(2)}, u32[]{:S(2)}) collective-permute-start(bf16[528,512]{1,0:T(8,128)(2,1)S(1)} %collective-permute-done.refs_0_), channel_id=1, source_target_pairs={{0,2},{1,3},{2,0},{3,1},{4,6},{5,7},{6,4},{7,5},{8,10},{9,11},{10,... | collective-permute-start | bytes 1622024 | tf_op jit(solution)/shard_map/ppermute | solution.py:797
  29.1 2.6 %collective-permute-start.3 = (bf16[512,512]{1,0:T(8,128)(2,1)S(1)}, bf16[512,512]{1,0:T(8,128)(2,1)S(1)}, u32[]{:S(2)}, u32[]{:S(2)}) collective-permute-start(bf16[512,512]{1,0:T(8,128)(2,1)S(1)} %collective-permute-done.2.refs_2_), channel_id=1, source_target_pairs={{0,2},{1,3},{2,0},{3,1},{4,6},{5,7},{6,4},{7,5},{8,10},{9,11},{10,... | collective-permute-start | bytes 1572872 | tf_op jit(solution)/shard_map/ppermute | solution.py:797
  29.1 16.2 %collective-permute-start.5 = (bf16[512,1024]{1,0:T(8,128)(2,1)}, bf16[512,1024]{1,0:T(8,128)(2,1)S(1)}, u32[]{:S(2)}, u32[]{:S(2)}) collective-permute-start(bf16[512,1024]{1,0:T(8,128)(2,1)} %get-tuple-element.108), channel_id=1, source_target_pairs={{0,2},{1,3},{2,0},{3,1},{4,6},{5,7},{6,4},{7,5},{8,10},{9,11},{10,... | collective-permute-start | bytes 3145736 | tf_op jit(solution)/shard_map/ppermute | solution.py:797
  45.2 2.7 %collective-permute-start.4 = (bf16[512,1024]{1,0:T(8,128)(2,1)S(1)}, bf16[512,1024]{1,0:T(8,128)(2,1)S(1)}, u32[]{:S(2)}, u32[]{:S(2)}) collective-permute-start(bf16[512,1024]{1,0:T(8,128)(2,1)S(1)} %get-tuple-element.107), channel_id=1, source_target_pairs={{0,2},{1,3},{2,0},{3,1},{4,6},{5,7},{6,4},{7,5},{8,10},{9,11},{10,... | collective-permute-start | bytes 3145736 | tf_op jit(solution)/shard_map/ppermute | solution.py:797
  48.7 14.9 %collective-permute-start.6 = (bf16[512,1024]{1,0:T(8,128)(2,1)S(1)}, bf16[512,1024]{1,0:T(8,128)(2,1)S(1)}, u32[]{:S(2)}, u32[]{:S(2)}) collective-permute-start(bf16[512,1024]{1,0:T(8,128)(2,1)S(1)} %join.1), channel_id=1, source_target_pairs={{0,1},{1,0},{2,6},{3,7},{4,5},{5,4},{6,2},{7,3},{8,9},{9,8},{10,14... | collective-permute-start | bytes 3145736 | tf_op jit(solution)/shard_map/ppermute | solution.py:797
  63.6 3.0 %collective-permute-start.7 = (bf16[256,2176]{1,0:T(8,128)(2,1)S(1)}, bf16[256,2176]{1,0:T(8,128)(2,1)S(1)}, u32[]{:S(2)}, u32[]{:S(2)}) collective-permute-start(bf16[256,2176]{1,0:T(8,128)(2,1)S(1)} %get-tuple-element.123), channel_id=1, source_target_pairs={{0,2},{1,3},{2,0},{3,1},{4,6},{5,7},{6,4},{7,5},{8,10},{9,11},{10,... | collective-permute-start | bytes 3342344 | tf_op jit(solution)/shard_map/ppermute | solution.py:797
  64.7 9.3 %collective-permute-start.8 = (bf16[256,1024]{1,0:T(8,128)(2,1)S(1)}, bf16[256,1024]{1,0:T(8,128)(2,1)S(1)}, u32[]{:S(2)}, u32[]{:S(2)}) collective-permute-start(bf16[256,1024]{1,0:T(8,128)(2,1)S(1)} %get-tuple-element.129), channel_id=1, source_target_pairs={{0,4},{1,5},{2,3},{3,2},{4,0},{5,1},{6,7},{7,6},{8,12},{9,13},{10,... | collective-permute-start | bytes 1572872 | tf_op jit(solution)/shard_map/ppermute | solution.py:797
  66.6 2.0 %copy-start.1 = (bf16[512,1536]{1,0:T(8,128)(2,1)S(1)}, bf16[512,1536]{1,0:T(8,128)(2,1)}, u32[]{:S(2)}) copy-start(bf16[512,1536]{1,0:T(8,128)(2,1)} %wqkv_ref.5) | copy-start | bytes 4718596
  66.9 14.2 %collective-permute-start.9 = (bf16[128,2176]{1,0:T(8,128)(2,1)S(1)}, bf16[128,2176]{1,0:T(8,128)(2,1)S(1)}, u32[]{:S(2)}, u32[]{:S(2)}) collective-permute-start(bf16[128,2176]{1,0:T(8,128)(2,1)S(1)} %get-tuple-element.172), channel_id=1, source_target_pairs={{0,4},{1,5},{2,10},{3,11},{4,0},{5,1},{6,14},{7,15},{8,12},{9,13},... | collective-permute-start | bytes 1671176 | tf_op jit(solution)/shard_map/ppermute | solution.py:797
  74.3 9.1 %collective-permute-start.10 = (bf16[128,1024]{1,0:T(8,128)(2,1)S(1)}, bf16[128,1024]{1,0:T(8,128)(2,1)S(1)}, u32[]{:S(2)}, u32[]{:S(2)}) collective-permute-start(bf16[128,1024]{1,0:T(8,128)(2,1)S(1)} %get-tuple-element.176), channel_id=1, source_target_pairs={{0,8},{1,9},{2,10},{3,11},{4,12},{5,13},{6,14},{7,15},{8,0},{9,1},... | collective-permute-start | bytes 786440 | tf_op jit(solution)/shard_map/ppermute | solution.py:797
  81.3 8.1 %collective-permute-start.11 = (bf16[64,2176]{1,0:T(8,128)(2,1)S(1)}, bf16[64,2176]{1,0:T(8,128)(2,1)S(1)}, u32[]{:S(2)}, u32[]{:S(2)}) collective-permute-start(bf16[64,2176]{1,0:T(8,128)(2,1)S(1)} %get-tuple-element.175), channel_id=1, source_target_pairs={{0,1},{1,0},{2,6},{3,7},{4,5},{5,4},{6,2},{7,3},{8,9},{9,8},{10,14... | collective-permute-start | bytes 835592 | tf_op jit(solution)/shard_map/ppermute | solution.py:797
  89.5 5.5 %collective-permute-start.12 = (bf16[32,2176]{1,0:T(8,128)(2,1)S(1)}, bf16[32,2176]{1,0:T(8,128)(2,1)S(1)}, u32[]{:S(2)}, u32[]{:S(2)}) collective-permute-start(bf16[32,2176]{1,0:T(8,128)(2,1)S(1)} %get-tuple-element.178), channel_id=1, source_target_pairs={{0,8},{1,9},{2,3},{3,2},{4,12},{5,13},{6,7},{7,6},{8,0},{9,1},{10,... | collective-permute-start | bytes 417800 | tf_op jit(solution)/shard_map/ppermute | solution.py:797
  91.7 10.4 %collective-permute-start.13 = (bf16[128,1024]{1,0:T(8,128)(2,1)S(1)}, bf16[128,1024]{1,0:T(8,128)(2,1)S(1)}, u32[]{:S(2)}, u32[]{:S(2)}) collective-permute-start(bf16[128,1024]{1,0:T(8,128)(2,1)S(1)} %add_convert_fusion.5), channel_id=1, source_target_pairs={{0,16},{1,17},{2,18},{3,19},{4,20},{5,21},{6,22},{7,23},{8,24},{9,... | collective-permute-start | bytes 786440 | tf_op jit(solution)/shard_map/ppermute | solution.py:797
  95.1 10.1 %collective-permute-start.14 = (bf16[32,2176]{1,0:T(8,128)(2,1)S(1)}, bf16[32,2176]{1,0:T(8,128)(2,1)S(1)}, u32[]{:S(2)}, u32[]{:S(2)}) collective-permute-start(bf16[32,2176]{1,0:T(8,128)(2,1)S(1)} %add_convert_fusion.7), channel_id=1, source_target_pairs={{0,16},{1,17},{2,18},{3,19},{4,20},{5,21},{6,22},{7,23},{8,24},{9,... | collective-permute-start | bytes 417800 | tf_op jit(solution)/shard_map/ppermute | solution.py:797
  102.2 6.4 %collective-permute-start.15 = (bf16[128,1024]{1,0:T(8,128)(2,1)S(1)}, bf16[128,1024]{1,0:T(8,128)(2,1)S(1)}, u32[]{:S(2)}, u32[]{:S(2)}) collective-permute-start(bf16[128,1024]{1,0:T(8,128)(2,1)S(1)} %add_convert_fusion.4), channel_id=1, source_target_pairs={{0,4},{1,5},{2,6},{3,7},{4,0},{5,1},{6,2},{7,3},{8,12},{9,13},{10,... | collective-permute-start | bytes 786440 | tf_op jit(solution)/shard_map/ppermute | solution.py:797
  105.2 6.7 %collective-permute-start.16 = (bf16[32,2176]{1,0:T(8,128)(2,1)S(1)}, bf16[32,2176]{1,0:T(8,128)(2,1)S(1)}, u32[]{:S(2)}, u32[]{:S(2)}) collective-permute-start(bf16[32,2176]{1,0:T(8,128)(2,1)S(1)} %add_convert_fusion.6), channel_id=1, source_target_pairs={{0,8},{1,9},{2,6},{3,7},{4,12},{5,13},{6,2},{7,3},{8,0},{9,1},{10,... | collective-permute-start | bytes 417800 | tf_op jit(solution)/shard_map/ppermute | solution.py:797
  108.6 10.0 %collective-permute-start.18 = (bf16[256,1024]{1,0:T(8,128)(2,1)S(1)}, bf16[256,1024]{1,0:T(8,128)(2,1)S(1)}, u32[]{:S(2)}, u32[]{:S(2)}) collective-permute-start(bf16[256,1024]{1,0:T(8,128)(2,1)S(1)} %constant_dynamic-update-slice_fusion), channel_id=1, source_target_pairs={{0,8},{1,9},{2,10},{3,11},{4,12},{5,13},{6,14},{7,15},{8,0},{9,1},... | collective-permute-start | bytes 1572872 | tf_op jit(solution)/shard_map/ppermute | solution.py:797
  111.9 6.6 %collective-permute-start.17 = (bf16[64,2176]{1,0:T(8,128)(2,1)S(1)}, bf16[64,2176]{1,0:T(8,128)(2,1)S(1)}, u32[]{:S(2)}, u32[]{:S(2)}) collective-permute-start(bf16[64,2176]{1,0:T(8,128)(2,1)S(1)} %constant_dynamic-update-slice_fusion.2), channel_id=1, source_target_pairs={{0,1},{1,0},{2,3},{3,2},{4,5},{5,4},{6,7},{7,6},{8,9},{9,8},{10,11... | collective-permute-start | bytes 835592 | tf_op jit(solution)/shard_map/ppermute | solution.py:797
  118.7 2.7 %collective-permute-start.19 = (bf16[512,1024]{1,0:T(8,128)(2,1)S(1)}, bf16[512,1024]{1,0:T(8,128)(2,1)S(1)}, u32[]{:S(2)}, u32[]{:S(2)}) collective-permute-start(bf16[512,1024]{1,0:T(8,128)(2,1)S(1)} %constant_dynamic-update-slice_fusion.6.keep_ref), channel_id=1, source_target_pairs={{0,2},{1,3},{2,0},{3,1},{4,6},{5,7},{6,4},{7,5},{8,10},{9,11},{10,... | collective-permute-start | bytes 3145736 | tf_op jit(solution)/shard_map/ppermute | solution.py:797
  118.7 5.7 %collective-permute-start.21 = (bf16[128,2176]{1,0:T(8,128)(2,1)S(1)}, bf16[128,2176]{1,0:T(8,128)(2,1)S(1)}, u32[]{:S(2)}, u32[]{:S(2)}) collective-permute-start(bf16[128,2176]{1,0:T(8,128)(2,1)S(1)} %constant_dynamic-update-slice_fusion.4.refs_0_), channel_id=1, source_target_pairs={{0,2},{1,3},{2,0},{3,1},{4,6},{5,7},{6,4},{7,5},{8,10},{9,11},{10,... | collective-permute-start | bytes 1671176 | tf_op jit(solution)/shard_map/ppermute | solution.py:797
  119.2 9.5 %collective-permute-start.20 = (bf16[128,2176]{1,0:T(8,128)(2,1)S(1)}, bf16[128,2176]{1,0:T(8,128)(2,1)S(1)}, u32[]{:S(2)}, u32[]{:S(2)}) collective-permute-start(bf16[128,2176]{1,0:T(8,128)(2,1)S(1)} %constant_dynamic-update-slice_fusion.4.refs_0_), channel_id=1, source_target_pairs={{0,4},{1,5},{2,10},{3,11},{4,0},{5,1},{6,14},{7,15},{8,12},{9,13},... | collective-permute-start | bytes 1671176 | tf_op jit(solution)/shard_map/ppermute | solution.py:797
  128.8 2.0 %collective-permute-start.22 = (bf16[128,2176]{1,0:T(8,128)(2,1)S(1)}, bf16[128,2176]{1,0:T(8,128)(2,1)S(1)}, u32[]{:S(2)}, u32[]{:S(2)}) collective-permute-start(bf16[128,2176]{1,0:T(8,128)(2,1)S(1)} %collective-permute-done.20.refs_2_), channel_id=1, source_target_pairs={{0,2},{1,3},{2,0},{3,1},{4,6},{5,7},{6,4},{7,5},{8,10},{9,11},{10,... | collective-permute-start | bytes 1671176 | tf_op jit(solution)/shard_map/ppermute | solution.py:797

commit v13 on v12

--- a/solution.py
+++ b/solution.py
@@ -739,7 +739,8 @@
     if which:
         col_ref, row_ref = refs
         for half, src, at, _, to in spots:
-            col_ref[pl.ds(to, size), :] = src[at : at + size, 4 * width :].astype(F32)
+            cols = slice(4 * width, None) if half else slice(None)
+            col_ref[pl.ds(to, size), :] = src[at : at + size, cols].astype(F32)
         vec = col_ref[...].T
         row_ref[...] = vec
         flat = lambda row: row.reshape(row.shape[1])
@@ -768,7 +769,9 @@
         functools.partial(attend_end_kernel, tables, which, max(1, width // units)),
         "attend_end",
         (1,),
-        [whole(*quarters[0].shape)] * len(quarters) + [anywhere] * len(written),
+        [pl.BlockSpec((rows // 4, LANES), lambda *_: (0, 4 * width // LANES))] * (2 * which)
+        + [whole(*quarters[0].shape)] * 2
+        + [anywhere] * len(written),
         [anywhere] * 2 + ([whole(width)] * 5 + [whole(units)]) * which,
         [jax.ShapeDtypeStruct((rows, 3 * width), F32), jax.ShapeDtypeStruct((rows, width), F32)]
         + ([jax.ShapeDtypeStruct((width,), F32)] * 5 + [jax.ShapeDtypeStruct((units,), F32)]) * which,
@@ -933,10 +936,12 @@
         first = start(ff_keep, steps["F"][0])
     turns = turns or "".join(a + f for a, f in itertools.zip_longest("A" * len(steps["A"]), "F" * len(steps["F"]), fillvalue=""))
     under_way = {"A": start(keep, steps["A"][0]), "F": first}
-    done, beside = (), (grad_tokens,)
-    for turn in turns:
+    done, beside = (), ()
+    for at_turn, turn in enumerate(turns):
         other = "A" if turn == "F" else "F"
         kept, got = under_way.pop(turn)
+        if at_turn == 1:
+            beside = (grad_tokens,)
         if other in under_way:
             other_kept, other_got = under_way[other]
             kept, other_kept, *beside = after(kept, other_kept, *beside)

time: 134 us -> 134 us (level)
  no operation moved by 1% of the time
where the time goes in v13:
time: 134 us
  Pallas kernels  61.8 us (46%)
  waiting for transfers between devices  41.5 us (31%)
  starting transfers between devices  27.8 us (21%)
    pallas_call x9, Pallas kernels, call(): pl.pallas_call(kernel, grid_spec=pltpu.PrefetchScalarGridSpec(num_scalar_...  59.9 us
    ppermute x23, waiting for transfers between devices, swap(): return lax.ppermute(value, AXES, pairs)  41.5 us
    ppermute x23, starting transfers between devices, swap(): return lax.ppermute(value, AXES, pairs)  27.8 us
  transfers between devices with their start and end apart: 23, of which 15 were waited for; matrix products, arithmetic and copies ran while one was open for 1% of the time, Pallas kernels for 42%

profile of v13, /device:TPU:0, one launch (start us, length us, event | category | flops | bytes accessed | tf_op | source)
XLA Modules:
  0.0 133.6 jit_solution(4267928163497754093)
XLA Ops:
  0.7 0.1 stack.21.info_ref
  0.8 1.8 %pack.1 = (bf16[528,512]{1,0:T(8,128)(2,1)S(1)}, bf16[512,512]{1,0:T(8,128)(2,1)S(1)}) custom-call(s32[6]{0:T(128)S(1)} %stack.21.info_ref, bf16[512,1024]{1,0:T(8,128)(2,1)} %up_ref.3, bf16[1024]{0:T(1024)(128)(2,1)} %bias_ref.3, bf16[1024,512]{1,0:T(8,128)(2,1)} %down_ref.3), custom_call_target="tpu_custom_call" | custom-call | flops 1000 | bytes 1000 | tf_op jit(solution)/shard_map/pack/pallas_call | solution.py:55
  2.6 3.0 %collective-permute-start = (bf16[528,512]{1,0:T(8,128)(2,1)S(1)}, bf16[528,512]{1,0:T(8,128)(2,1)S(1)}, u32[]{:S(2)}, u32[]{:S(2)}) collective-permute-start(bf16[528,512]{1,0:T(8,128)(2,1)S(1)} %get-tuple-element.102), channel_id=1, source_target_pairs={{0,1},{1,0},{2,3},{3,2},{4,5},{5,4},{6,7},{7,6},{8,9},{9,8},{10,11... | collective-permute-start | bytes 1622024 | tf_op jit(solution)/shard_map/ppermute | solution.py:800
  5.6 0.1 collective-permute-start.2
  5.7 9.0 %attend.1 = (bf16[1024,1536]{1,0:T(8,128)(2,1)}, bf16[8,4,128,256]{3,2,1,0:T(8,128)(2,1)}, bf16[1024,512]{1,0:T(8,128)(2,1)}, f32[1024,512]{1,0:T(8,128)}, bf16[1024,512]{1,0:T(8,128)(2,1)S(1)}) custom-call(s32[6]{0:T(128)S(1)} %stack.21.info_ref, bf16[1024,512]{1,0:T(8,128)(2,1)} %tok_ref.2, f32[1,512]{1,0:T(1,128)} %bitcast.9, f32[1,512]{1,0:T(1,128)} %bitcast.14, ...), custom_call_target="tpu_custom_call" | custom-call | flops 1000 | bytes 1000 | tf_op jit(solution)/shard_map/attend/pallas_call | solution.py:55
  14.7 11.1 %ffn_own.1 = (f32[1024,512]{1,0:T(8,128)S(1)}, f32[1024,512]{1,0:T(8,128)S(1)}, bf16[512,1024]{1,0:T(8,128)(2,1)}, bf16[512,1024]{1,0:T(8,128)(2,1)}, f32[2,512]{1,0:T(2,128)}) custom-call(s32[6]{0:T(128)S(1)} %stack.21.info_ref, bf16[1024,512]{1,0:T(8,128)(2,1)S(1)} %get-tuple-element.95.sec_ref.sec_in, bf16[1024,512]{1,0:T(8,128)(2,1)} %dy_in.1, ...), custom_call_target="tpu_custom_call" | custom-call | flops 1000 | bytes 1000 | tf_op jit(solution)/shard_map/ffn_own/pallas_call | solution.py:55
  25.9 3.3 %collective-permute-done.2.refs_2_ = bf16[512,512]{1,0:T(8,128)(2,1)S(1)} collective-permute-done((bf16[512,512]{1,0:T(8,128)(2,1)S(1)}, bf16[512,512]{1,0:T(8,128)(2,1)S(1)}, u32[]{:S(2)}, u32[]{:S(2)}) %collective-permute-start.2) | collective-permute-done | bytes 524320 | tf_op jit(solution)/shard_map/ppermute | solution.py:800
  29.1 0.5 collective-permute-start.5
  29.6 2.1 %collective-permute-done.3.refs_3_ = bf16[512,512]{1,0:T(8,128)(2,1)S(1)} collective-permute-done((bf16[512,512]{1,0:T(8,128)(2,1)S(1)}, bf16[512,512]{1,0:T(8,128)(2,1)S(1)}, u32[]{:S(2)}, u32[]{:S(2)}) %collective-permute-start.3) | collective-permute-done | bytes 524320 | tf_op jit(solution)/shard_map/ppermute | solution.py:800
  31.8 13.4 %ffn_rest.1 = (bf16[1024,512]{1,0:T(8,128)(2,1)}, f32[1024,512]{1,0:T(8,128)}, bf16[1024,512]{1,0:T(8,128)(2,1)}, f32[8,512]{1,0:T(8,128)}, f32[512,512]{1,0:T(8...) custom-call(s32[6]{0:T(128)S(1)} %stack.21.info_ref, ...), custom_call_target="tpu_custom_call" | custom-call | flops 1000 | bytes 1000 | tf_op jit(solution)/shard_map/ffn_rest/pallas_call | solution.py:55
  45.2 0.2 collective-permute-start.4
  45.4 2.5 %collective-permute-done.4.got_ref = bf16[512,1024]{1,0:T(8,128)(2,1)S(1)} collective-permute-done((bf16[512,1024]{1,0:T(8,128)(2,1)S(1)}, bf16[512,1024]{1,0:T(8,128)(2,1)S(1)}, u32[]{:S(2)}, u32[]{:S(2)}) %collective-permute-start.4) | collective-permute-done | bytes 1048608 | tf_op jit(solution)/shard_map/ppermute | solution.py:800
  47.9 0.8 join.1
  48.7 1.8 %collective-permute-start.6 = (bf16[512,1024]{1,0:T(8,128)(2,1)S(1)}, bf16[512,1024]{1,0:T(8,128)(2,1)S(1)}, u32[]{:S(2)}, u32[]{:S(2)}) collective-permute-start(bf16[512,1024]{1,0:T(8,128)(2,1)S(1)} %join.1), channel_id=1, source_target_pairs={{0,1},{1,0},{2,6},{3,7},{4,5},{5,4},{6,2},{7,3},{8,9},{9,8},{10,14... | collective-permute-start | bytes 3145736 | tf_op jit(solution)/shard_map/ppermute | solution.py:800
  50.5 11.3 %attend_back.1 = (bf16[1024,1536]{1,0:T(8,128)(2,1)S(1)}, bf16[256,2176]{1,0:T(8,128)(2,1)S(1)}, bf16[256,2176]{1,0:T(8,128)(2,1)S(1)}) custom-call(s32[6]{0:T(128)S(1)} %stack.21.info_ref, bf16[1024,1536]{1,0:T(8,128)(2,1)} %get-tuple-element.109.qkv_ref, bf16[8,4,128,256]{3,2,1,0:T(8,128)(2,1)} %get-tuple-element.110.prob_ref, ...), custom_call_target="tpu_custom_call" | custom-call | flops 1000 | bytes 1000 | tf_op jit(solution)/shard_map/attend_back/pallas_call | solution.py:55
  61.8 1.8 %collective-permute-done.6.arrived_ref = bf16[512,1024]{1,0:T(8,128)(2,1)S(1)} collective-permute-done((bf16[512,1024]{1,0:T(8,128)(2,1)S(1)}, bf16[512,1024]{1,0:T(8,128)(2,1)S(1)}, u32[]{:S(2)}, u32[]{:S(2)}) %collective-permute-start.6) | collective-permute-done | bytes 1048608 | tf_op jit(solution)/shard_map/ppermute | solution.py:800
  63.6 1.1 split.1
  64.7 1.8 %collective-permute-start.8 = (bf16[256,1024]{1,0:T(8,128)(2,1)S(1)}, bf16[256,1024]{1,0:T(8,128)(2,1)S(1)}, u32[]{:S(2)}, u32[]{:S(2)}) collective-permute-start(bf16[256,1024]{1,0:T(8,128)(2,1)S(1)} %get-tuple-element.126), channel_id=1, source_target_pairs={{0,4},{1,5},{2,3},{3,2},{4,0},{5,1},{6,7},{7,6},{8,12},{9,13},{10,... | collective-permute-start | bytes 1572872 | tf_op jit(solution)/shard_map/ppermute | solution.py:800
  66.6 0.3 add_convert_fusion
  66.8 0.1 fusion
  66.9 1.6 %collective-permute-start.9 = (bf16[128,2176]{1,0:T(8,128)(2,1)S(1)}, bf16[128,2176]{1,0:T(8,128)(2,1)S(1)}, u32[]{:S(2)}, u32[]{:S(2)}) collective-permute-start(bf16[128,2176]{1,0:T(8,128)(2,1)S(1)} %get-tuple-element.172), channel_id=1, source_target_pairs={{0,4},{1,5},{2,10},{3,11},{4,0},{5,1},{6,14},{7,15},{8,12},{9,13},... | collective-permute-start | bytes 1671176 | tf_op jit(solution)/shard_map/ppermute | solution.py:800
  68.5 5.5 %first_back.1 = f32[1024,512]{1,0:T(8,128)} custom-call(s32[6]{0:T(128)S(1)} %stack.21.info_ref, bf16[1024,1536]{1,0:T(8,128)(2,1)S(1)} %get-tuple-element.127.dqkv_ref, bf16[512,1536]{1,0:T(8,128)(2,1)S(1)} %copy-done.1, bf16[1024,512]{1,0:T(8,128)(2,1)} %tok_ref.2, f32[1024,512]{1,0:T(8,128)} %get-tuple-element.128.gres_ref, f32[1,512]{1,0:T(1,128)} %bitcast.11), custom_call_target="tpu_custom_call" | custom-call | flops 1000 | bytes 1000 | tf_op jit(solution)/shard_map/first_back/pallas_call | solution.py:55
  74.1 0.2 add_convert_fusion.2
  74.3 1.8 %collective-permute-start.10 = (bf16[128,1024]{1,0:T(8,128)(2,1)S(1)}, bf16[128,1024]{1,0:T(8,128)(2,1)S(1)}, u32[]{:S(2)}, u32[]{:S(2)}) collective-permute-start(bf16[128,1024]{1,0:T(8,128)(2,1)S(1)} %get-tuple-element.176), channel_id=1, source_target_pairs={{0,8},{1,9},{2,10},{3,11},{4,12},{5,13},{6,14},{7,15},{8,0},{9,1},... | collective-permute-start | bytes 786440 | tf_op jit(solution)/shard_map/ppermute | solution.py:800
  76.1 5.0 %collective-permute-done.9 = bf16[128,2176]{1,0:T(8,128)(2,1)S(1)} collective-permute-done((bf16[128,2176]{1,0:T(8,128)(2,1)S(1)}, bf16[128,2176]{1,0:T(8,128)(2,1)S(1)}, u32[]{:S(2)}, u32[]{:S(2)}) %collective-permute-start.9) | collective-permute-done | bytes 557088 | tf_op jit(solution)/shard_map/ppermute | solution.py:800
  81.1 0.1 add_convert_fusion.1
  81.3 2.1 %collective-permute-start.11 = (bf16[64,2176]{1,0:T(8,128)(2,1)S(1)}, bf16[64,2176]{1,0:T(8,128)(2,1)S(1)}, u32[]{:S(2)}, u32[]{:S(2)}) collective-permute-start(bf16[64,2176]{1,0:T(8,128)(2,1)S(1)} %get-tuple-element.175), channel_id=1, source_target_pairs={{0,1},{1,0},{2,6},{3,7},{4,5},{5,4},{6,2},{7,3},{8,9},{9,8},{10,14... | collective-permute-start | bytes 835592 | tf_op jit(solution)/shard_map/ppermute | solution.py:800
  83.5 5.9 %collective-permute-done.11 = bf16[64,2176]{1,0:T(8,128)(2,1)S(1)} collective-permute-done((bf16[64,2176]{1,0:T(8,128)(2,1)S(1)}, bf16[64,2176]{1,0:T(8,128)(2,1)S(1)}, u32[]{:S(2)}, u32[]{:S(2)}) %collective-permute-start.11) | collective-permute-done | bytes 278560 | tf_op jit(solution)/shard_map/ppermute | solution.py:800
  89.5 2.1 %collective-permute-start.12 = (bf16[32,2176]{1,0:T(8,128)(2,1)S(1)}, bf16[32,2176]{1,0:T(8,128)(2,1)S(1)}, u32[]{:S(2)}, u32[]{:S(2)}) collective-permute-start(bf16[32,2176]{1,0:T(8,128)(2,1)S(1)} %get-tuple-element.178), channel_id=1, source_target_pairs={{0,8},{1,9},{2,3},{3,2},{4,12},{5,13},{6,7},{7,6},{8,0},{9,1},{10,... | collective-permute-start | bytes 417800 | tf_op jit(solution)/shard_map/ppermute | solution.py:800
  91.7 2.6 %collective-permute-start.13 = (bf16[128,1024]{1,0:T(8,128)(2,1)S(1)}, bf16[128,1024]{1,0:T(8,128)(2,1)S(1)}, u32[]{:S(2)}, u32[]{:S(2)}) collective-permute-start(bf16[128,1024]{1,0:T(8,128)(2,1)S(1)} %add_convert_fusion.5), channel_id=1, source_target_pairs={{0,16},{1,17},{2,18},{3,19},{4,20},{5,21},{6,22},{7,23},{8,24},{9,... | collective-permute-start | bytes 786440 | tf_op jit(solution)/shard_map/ppermute | solution.py:800
  94.2 0.8 collective-permute-done.12
  95.1 3.9 %collective-permute-start.14 = (bf16[32,2176]{1,0:T(8,128)(2,1)S(1)}, bf16[32,2176]{1,0:T(8,128)(2,1)S(1)}, u32[]{:S(2)}, u32[]{:S(2)}) collective-permute-start(bf16[32,2176]{1,0:T(8,128)(2,1)S(1)} %add_convert_fusion.7), channel_id=1, source_target_pairs={{0,16},{1,17},{2,18},{3,19},{4,20},{5,21},{6,22},{7,23},{8,24},{9,... | collective-permute-start | bytes 417800 | tf_op jit(solution)/shard_map/ppermute | solution.py:800
  99.0 3.1 %collective-permute-done.13 = bf16[128,1024]{1,0:T(8,128)(2,1)S(1)} collective-permute-done((bf16[128,1024]{1,0:T(8,128)(2,1)S(1)}, bf16[128,1024]{1,0:T(8,128)(2,1)S(1)}, u32[]{:S(2)}, u32[]{:S(2)}) %collective-permute-start.13) | collective-permute-done | bytes 262176 | tf_op jit(solution)/shard_map/ppermute | solution.py:800
  102.2 1.6 %collective-permute-start.15 = (bf16[128,1024]{1,0:T(8,128)(2,1)S(1)}, bf16[128,1024]{1,0:T(8,128)(2,1)S(1)}, u32[]{:S(2)}, u32[]{:S(2)}) collective-permute-start(bf16[128,1024]{1,0:T(8,128)(2,1)S(1)} %add_convert_fusion.4), channel_id=1, source_target_pairs={{0,4},{1,5},{2,6},{3,7},{4,0},{5,1},{6,2},{7,3},{8,12},{9,13},{10,... | collective-permute-start | bytes 786440 | tf_op jit(solution)/shard_map/ppermute | solution.py:800
  103.8 1.4 %collective-permute-done.14 = bf16[32,2176]{1,0:T(8,128)(2,1)S(1)} collective-permute-done((bf16[32,2176]{1,0:T(8,128)(2,1)S(1)}, bf16[32,2176]{1,0:T(8,128)(2,1)S(1)}, u32[]{:S(2)}, u32[]{:S(2)}) %collective-permute-start.14) | collective-permute-done | bytes 139296 | tf_op jit(solution)/shard_map/ppermute | solution.py:800
  105.2 0.8 collective-permute-start.16
  106.1 2.5 %collective-permute-done.15 = bf16[128,1024]{1,0:T(8,128)(2,1)S(1)} collective-permute-done((bf16[128,1024]{1,0:T(8,128)(2,1)S(1)}, bf16[128,1024]{1,0:T(8,128)(2,1)S(1)}, u32[]{:S(2)}, u32[]{:S(2)}) %collective-permute-start.15) | collective-permute-done | bytes 262176 | tf_op jit(solution)/shard_map/ppermute | solution.py:800
  108.6 2.3 %collective-permute-start.18 = (bf16[256,1024]{1,0:T(8,128)(2,1)S(1)}, bf16[256,1024]{1,0:T(8,128)(2,1)S(1)}, u32[]{:S(2)}, u32[]{:S(2)}) collective-permute-start(bf16[256,1024]{1,0:T(8,128)(2,1)S(1)} %constant_dynamic-update-slice_fusion), channel_id=1, source_target_pairs={{0,8},{1,9},{2,10},{3,11},{4,12},{5,13},{6,14},{7,15},{8,0},{9,1},... | collective-permute-start | bytes 1572872 | tf_op jit(solution)/shard_map/ppermute | solution.py:800
  110.9 1.0 collective-permute-done.16
  112.0 6.5 %collective-permute-done.17 = bf16[64,2176]{1,0:T(8,128)(2,1)S(1)} collective-permute-done((bf16[64,2176]{1,0:T(8,128)(2,1)S(1)}, bf16[64,2176]{1,0:T(8,128)(2,1)S(1)}, u32[]{:S(2)}, u32[]{:S(2)}) %collective-permute-start.17) | collective-permute-done | bytes 278560 | tf_op jit(solution)/shard_map/ppermute | solution.py:800
  118.7 0.5 collective-permute-start.21
  119.2 1.0 collective-permute-start.20
  120.2 1.2 collective-permute-done.19.other_ref
  121.4 3.1 %ffn_end.1 = (f32[512,1024]{1,0:T(8,128)}, f32[1024,512]{1,0:T(8,128)}) custom-call(s32[6]{0:T(128)S(1)} %stack.21.info_ref, bf16[512,1024]{1,0:T(8,128)(2,1)S(1)} %constant_dynamic-update-slice_fusion.6.keep_ref, bf16[512,1024]{1,0:T(8,128)(2,1)S(1)} %collective-permute-done.19.other_ref), custom_call_target="tpu_custom_call" | custom-call | flops 1000 | bytes 1000 | tf_op jit(solution)/shard_map/ffn_end/pallas_call | solution.py:55
  124.4 2.0 %attend_end.2 = (f32[512,1536]{1,0:T(8,128)}, f32[512,512]{1,0:T(8,128)}) custom-call(s32[6]{0:T(128)S(1)} %stack.21.info_ref, bf16[128,2176]{1,0:T(8,128)(2,1)S(1)} %constant_dynamic-update-slice_fusion.4.refs_0_, bf16[128,2176]{1,0:T(8,128)(2,1)S(1)} %collective-permute-done.21.refs_1_), custom_call_target="tpu_custom_call" | custom-call | flops 1000 | bytes 1000 | tf_op jit(solution)/shard_map/attend_end/pallas_call | solution.py:55
  126.4 2.3 %collective-permute-done.20.refs_2_ = bf16[128,2176]{1,0:T(8,128)(2,1)S(1)} collective-permute-done((bf16[128,2176]{1,0:T(8,128)(2,1)S(1)}, bf16[128,2176]{1,0:T(8,128)(2,1)S(1)}, u32[]{:S(2)}, u32[]{:S(2)}) %collective-permute-start.20) | collective-permute-done | bytes 557088 | tf_op jit(solution)/shard_map/ppermute | solution.py:800
  128.8 2.0 %collective-permute-done.22.refs_3_ = bf16[128,2176]{1,0:T(8,128)(2,1)S(1)} collective-permute-done((bf16[128,2176]{1,0:T(8,128)(2,1)S(1)}, bf16[128,2176]{1,0:T(8,128)(2,1)S(1)}, u32[]{:S(2)}, u32[]{:S(2)}) %collective-permute-start.22) | collective-permute-done | bytes 557088 | tf_op jit(solution)/shard_map/ppermute | solution.py:800
  130.7 2.7 %attend_end.3 = (f32[512,1536]{1,0:T(8,128)}, f32[512,512]{1,0:T(8,128)}, f32[512]{0:T(512)}, f32[512]{0:T(512)}, f32[512]{0:T(512)}, /*index=5*/f32[512]{0:T(512)}, f32[512]{0:T(512)}, f32[1024]{0:T(1024)}) custom-call(s32[6]{0:T(128)S(1)} %stack.21.info_ref, ...), custom_call_target="tpu_custom_call", output_to_operand_aliasing={{0}: (5, {}), {1}: (6, {})} | custom-call | flops 1000 | bytes 1000 | tf_op jit(solution)/shard_map/attend_end/pallas_call | solution.py:55
  (40 shorter events, 0.8 us)
Async XLA Ops:
  0.6 5.1 %copy-start = (bf16[512,1536]{1,0:T(8,128)(2,1)S(1)}, bf16[512,1536]{1,0:T(8,128)(2,1)}, u32[]{:S(2)}) copy-start(bf16[512,1536]{1,0:T(8,128)(2,1)} %wqkv_ref.5) | copy-start | bytes 4718596
  0.7 5.1 %copy-start.4 = (bf16[512,512]{1,0:T(8,128)(2,1)S(1)}, bf16[512,512]{1,0:T(8,128)(2,1)}, u32[]{:S(2)}) copy-start(bf16[512,512]{1,0:T(8,128)(2,1)} %wout_ref.3) | copy-start | bytes 1572868
  2.6 12.1 %copy-start.2 = (bf16[512,1024]{1,0:T(8,128)(2,1)S(1)}, bf16[512,1024]{1,0:T(8,128)(2,1)}, u32[]{:S(2)}) copy-start(bf16[512,1024]{1,0:T(8,128)(2,1)} %up_ref.3) | copy-start | bytes 3145732
  2.6 12.1 %copy-start.3 = (bf16[1024,512]{1,0:T(8,128)(2,1)S(1)}, bf16[1024,512]{1,0:T(8,128)(2,1)}, u32[]{:S(2)}) copy-start(bf16[1024,512]{1,0:T(8,128)(2,1)} %down_ref.3) | copy-start | bytes 3145732
  2.6 23.2 %collective-permute-start = (bf16[528,512]{1,0:T(8,128)(2,1)S(1)}, bf16[528,512]{1,0:T(8,128)(2,1)S(1)}, u32[]{:S(2)}, u32[]{:S(2)}) collective-permute-start(bf16[528,512]{1,0:T(8,128)(2,1)S(1)} %get-tuple-element.102), channel_id=1, source_target_pairs={{0,1},{1,0},{2,3},{3,2},{4,5},{5,4},{6,7},{7,6},{8,9},{9,8},{10,11... | collective-permute-start | bytes 1622024 | tf_op jit(solution)/shard_map/ppermute | solution.py:800
  5.6 23.5 %collective-permute-start.2 = (bf16[512,512]{1,0:T(8,128)(2,1)S(1)}, bf16[512,512]{1,0:T(8,128)(2,1)S(1)}, u32[]{:S(2)}, u32[]{:S(2)}) collective-permute-start(bf16[512,512]{1,0:T(8,128)(2,1)S(1)} %get-tuple-element.104), channel_id=1, source_target_pairs={{0,1},{1,0},{2,3},{3,2},{4,5},{5,4},{6,7},{7,6},{8,9},{9,8},{10,11... | collective-permute-start | bytes 1572872 | tf_op jit(solution)/shard_map/ppermute | solution.py:800
  25.8 5.9 %collective-permute-start.1 = (bf16[528,512]{1,0:T(8,128)(2,1)S(1)}, bf16[528,512]{1,0:T(8,128)(2,1)S(1)}, u32[]{:S(2)}, u32[]{:S(2)}) collective-permute-start(bf16[528,512]{1,0:T(8,128)(2,1)S(1)} %collective-permute-done.refs_0_), channel_id=1, source_target_pairs={{0,2},{1,3},{2,0},{3,1},{4,6},{5,7},{6,4},{7,5},{8,10},{9,11},{10,... | collective-permute-start | bytes 1622024 | tf_op jit(solution)/shard_map/ppermute | solution.py:800
  29.1 2.6 %collective-permute-start.3 = (bf16[512,512]{1,0:T(8,128)(2,1)S(1)}, bf16[512,512]{1,0:T(8,128)(2,1)S(1)}, u32[]{:S(2)}, u32[]{:S(2)}) collective-permute-start(bf16[512,512]{1,0:T(8,128)(2,1)S(1)} %collective-permute-done.2.refs_2_), channel_id=1, source_target_pairs={{0,2},{1,3},{2,0},{3,1},{4,6},{5,7},{6,4},{7,5},{8,10},{9,11},{10,... | collective-permute-start | bytes 1572872 | tf_op jit(solution)/shard_map/ppermute | solution.py:800
  29.1 16.2 %collective-permute-start.5 = (bf16[512,1024]{1,0:T(8,128)(2,1)}, bf16[512,1024]{1,0:T(8,128)(2,1)S(1)}, u32[]{:S(2)}, u32[]{:S(2)}) collective-permute-start(bf16[512,1024]{1,0:T(8,128)(2,1)} %get-tuple-element.108), channel_id=1, source_target_pairs={{0,2},{1,3},{2,0},{3,1},{4,6},{5,7},{6,4},{7,5},{8,10},{9,11},{10,... | collective-permute-start | bytes 3145736 | tf_op jit(solution)/shard_map/ppermute | solution.py:800
  45.2 2.7 %collective-permute-start.4 = (bf16[512,1024]{1,0:T(8,128)(2,1)S(1)}, bf16[512,1024]{1,0:T(8,128)(2,1)S(1)}, u32[]{:S(2)}, u32[]{:S(2)}) collective-permute-start(bf16[512,1024]{1,0:T(8,128)(2,1)S(1)} %get-tuple-element.107), channel_id=1, source_target_pairs={{0,2},{1,3},{2,0},{3,1},{4,6},{5,7},{6,4},{7,5},{8,10},{9,11},{10,... | collective-permute-start | bytes 3145736 | tf_op jit(solution)/shard_map/ppermute | solution.py:800
  48.7 14.9 %collective-permute-start.6 = (bf16[512,1024]{1,0:T(8,128)(2,1)S(1)}, bf16[512,1024]{1,0:T(8,128)(2,1)S(1)}, u32[]{:S(2)}, u32[]{:S(2)}) collective-permute-start(bf16[512,1024]{1,0:T(8,128)(2,1)S(1)} %join.1), channel_id=1, source_target_pairs={{0,1},{1,0},{2,6},{3,7},{4,5},{5,4},{6,2},{7,3},{8,9},{9,8},{10,14... | collective-permute-start | bytes 3145736 | tf_op jit(solution)/shard_map/ppermute | solution.py:800
  63.6 3.0 %collective-permute-start.7 = (bf16[256,2176]{1,0:T(8,128)(2,1)S(1)}, bf16[256,2176]{1,0:T(8,128)(2,1)S(1)}, u32[]{:S(2)}, u32[]{:S(2)}) collective-permute-start(bf16[256,2176]{1,0:T(8,128)(2,1)S(1)} %get-tuple-element.123), channel_id=1, source_target_pairs={{0,2},{1,3},{2,0},{3,1},{4,6},{5,7},{6,4},{7,5},{8,10},{9,11},{10,... | collective-permute-start | bytes 3342344 | tf_op jit(solution)/shard_map/ppermute | solution.py:800
  64.7 9.3 %collective-permute-start.8 = (bf16[256,1024]{1,0:T(8,128)(2,1)S(1)}, bf16[256,1024]{1,0:T(8,128)(2,1)S(1)}, u32[]{:S(2)}, u32[]{:S(2)}) collective-permute-start(bf16[256,1024]{1,0:T(8,128)(2,1)S(1)} %get-tuple-element.126), channel_id=1, source_target_pairs={{0,4},{1,5},{2,3},{3,2},{4,0},{5,1},{6,7},{7,6},{8,12},{9,13},{10,... | collective-permute-start | bytes 1572872 | tf_op jit(solution)/shard_map/ppermute | solution.py:800
  66.6 2.0 %copy-start.1 = (bf16[512,1536]{1,0:T(8,128)(2,1)S(1)}, bf16[512,1536]{1,0:T(8,128)(2,1)}, u32[]{:S(2)}) copy-start(bf16[512,1536]{1,0:T(8,128)(2,1)} %wqkv_ref.5) | copy-start | bytes 4718596
  66.9 14.2 %collective-permute-start.9 = (bf16[128,2176]{1,0:T(8,128)(2,1)S(1)}, bf16[128,2176]{1,0:T(8,128)(2,1)S(1)}, u32[]{:S(2)}, u32[]{:S(2)}) collective-permute-start(bf16[128,2176]{1,0:T(8,128)(2,1)S(1)} %get-tuple-element.172), channel_id=1, source_target_pairs={{0,4},{1,5},{2,10},{3,11},{4,0},{5,1},{6,14},{7,15},{8,12},{9,13},... | collective-permute-start | bytes 1671176 | tf_op jit(solution)/shard_map/ppermute | solution.py:800
  74.3 9.1 %collective-permute-start.10 = (bf16[128,1024]{1,0:T(8,128)(2,1)S(1)}, bf16[128,1024]{1,0:T(8,128)(2,1)S(1)}, u32[]{:S(2)}, u32[]{:S(2)}) collective-permute-start(bf16[128,1024]{1,0:T(8,128)(2,1)S(1)} %get-tuple-element.176), channel_id=1, source_target_pairs={{0,8},{1,9},{2,10},{3,11},{4,12},{5,13},{6,14},{7,15},{8,0},{9,1},... | collective-permute-start | bytes 786440 | tf_op jit(solution)/shard_map/ppermute | solution.py:800
  81.3 8.1 %collective-permute-start.11 = (bf16[64,2176]{1,0:T(8,128)(2,1)S(1)}, bf16[64,2176]{1,0:T(8,128)(2,1)S(1)}, u32[]{:S(2)}, u32[]{:S(2)}) collective-permute-start(bf16[64,2176]{1,0:T(8,128)(2,1)S(1)} %get-tuple-element.175), channel_id=1, source_target_pairs={{0,1},{1,0},{2,6},{3,7},{4,5},{5,4},{6,2},{7,3},{8,9},{9,8},{10,14... | collective-permute-start | bytes 835592 | tf_op jit(solution)/shard_map/ppermute | solution.py:800
  89.5 5.5 %collective-permute-start.12 = (bf16[32,2176]{1,0:T(8,128)(2,1)S(1)}, bf16[32,2176]{1,0:T(8,128)(2,1)S(1)}, u32[]{:S(2)}, u32[]{:S(2)}) collective-permute-start(bf16[32,2176]{1,0:T(8,128)(2,1)S(1)} %get-tuple-element.178), channel_id=1, source_target_pairs={{0,8},{1,9},{2,3},{3,2},{4,12},{5,13},{6,7},{7,6},{8,0},{9,1},{10,... | collective-permute-start | bytes 417800 | tf_op jit(solution)/shard_map/ppermute | solution.py:800
  91.7 10.4 %collective-permute-start.13 = (bf16[128,1024]{1,0:T(8,128)(2,1)S(1)}, bf16[128,1024]{1,0:T(8,128)(2,1)S(1)}, u32[]{:S(2)}, u32[]{:S(2)}) collective-permute-start(bf16[128,1024]{1,0:T(8,128)(2,1)S(1)} %add_convert_fusion.5), channel_id=1, source_target_pairs={{0,16},{1,17},{2,18},{3,19},{4,20},{5,21},{6,22},{7,23},{8,24},{9,... | collective-permute-start | bytes 786440 | tf_op jit(solution)/shard_map/ppermute | solution.py:800
  95.1 10.1 %collective-permute-start.14 = (bf16[32,2176]{1,0:T(8,128)(2,1)S(1)}, bf16[32,2176]{1,0:T(8,128)(2,1)S(1)}, u32[]{:S(2)}, u32[]{:S(2)}) collective-permute-start(bf16[32,2176]{1,0:T(8,128)(2,1)S(1)} %add_convert_fusion.7), channel_id=1, source_target_pairs={{0,16},{1,17},{2,18},{3,19},{4,20},{5,21},{6,22},{7,23},{8,24},{9,... | collective-permute-start | bytes 417800 | tf_op jit(solution)/shard_map/ppermute | solution.py:800
  102.2 6.4 %collective-permute-start.15 = (bf16[128,1024]{1,0:T(8,128)(2,1)S(1)}, bf16[128,1024]{1,0:T(8,128)(2,1)S(1)}, u32[]{:S(2)}, u32[]{:S(2)}) collective-permute-start(bf16[128,1024]{1,0:T(8,128)(2,1)S(1)} %add_convert_fusion.4), channel_id=1, source_target_pairs={{0,4},{1,5},{2,6},{3,7},{4,0},{5,1},{6,2},{7,3},{8,12},{9,13},{10,... | collective-permute-start | bytes 786440 | tf_op jit(solution)/shard_map/ppermute | solution.py:800
  105.2 6.7 %collective-permute-start.16 = (bf16[32,2176]{1,0:T(8,128)(2,1)S(1)}, bf16[32,2176]{1,0:T(8,128)(2,1)S(1)}, u32[]{:S(2)}, u32[]{:S(2)}) collective-permute-start(bf16[32,2176]{1,0:T(8,128)(2,1)S(1)} %add_convert_fusion.6), channel_id=1, source_target_pairs={{0,8},{1,9},{2,6},{3,7},{4,12},{5,13},{6,2},{7,3},{8,0},{9,1},{10,... | collective-permute-start | bytes 417800 | tf_op jit(solution)/shard_map/ppermute | solution.py:800
  108.6 10.0 %collective-permute-start.18 = (bf16[256,1024]{1,0:T(8,128)(2,1)S(1)}, bf16[256,1024]{1,0:T(8,128)(2,1)S(1)}, u32[]{:S(2)}, u32[]{:S(2)}) collective-permute-start(bf16[256,1024]{1,0:T(8,128)(2,1)S(1)} %constant_dynamic-update-slice_fusion), channel_id=1, source_target_pairs={{0,8},{1,9},{2,10},{3,11},{4,12},{5,13},{6,14},{7,15},{8,0},{9,1},... | collective-permute-start | bytes 1572872 | tf_op jit(solution)/shard_map/ppermute | solution.py:800
  111.9 6.6 %collective-permute-start.17 = (bf16[64,2176]{1,0:T(8,128)(2,1)S(1)}, bf16[64,2176]{1,0:T(8,128)(2,1)S(1)}, u32[]{:S(2)}, u32[]{:S(2)}) collective-permute-start(bf16[64,2176]{1,0:T(8,128)(2,1)S(1)} %constant_dynamic-update-slice_fusion.2), channel_id=1, source_target_pairs={{0,1},{1,0},{2,3},{3,2},{4,5},{5,4},{6,7},{7,6},{8,9},{9,8},{10,11... | collective-permute-start | bytes 835592 | tf_op jit(solution)/shard_map/ppermute | solution.py:800
  118.7 2.7 %collective-permute-start.19 = (bf16[512,1024]{1,0:T(8,128)(2,1)S(1)}, bf16[512,1024]{1,0:T(8,128)(2,1)S(1)}, u32[]{:S(2)}, u32[]{:S(2)}) collective-permute-start(bf16[512,1024]{1,0:T(8,128)(2,1)S(1)} %constant_dynamic-update-slice_fusion.6.keep_ref), channel_id=1, source_target_pairs={{0,2},{1,3},{2,0},{3,1},{4,6},{5,7},{6,4},{7,5},{8,10},{9,11},{10,... | collective-permute-start | bytes 3145736 | tf_op jit(solution)/shard_map/ppermute | solution.py:800
  118.7 5.7 %collective-permute-start.21 = (bf16[128,2176]{1,0:T(8,128)(2,1)S(1)}, bf16[128,2176]{1,0:T(8,128)(2,1)S(1)}, u32[]{:S(2)}, u32[]{:S(2)}) collective-permute-start(bf16[128,2176]{1,0:T(8,128)(2,1)S(1)} %constant_dynamic-update-slice_fusion.4.refs_0_), channel_id=1, source_target_pairs={{0,2},{1,3},{2,0},{3,1},{4,6},{5,7},{6,4},{7,5},{8,10},{9,11},{10,... | collective-permute-start | bytes 1671176 | tf_op jit(solution)/shard_map/ppermute | solution.py:800
  119.2 9.5 %collective-permute-start.20 = (bf16[128,2176]{1,0:T(8,128)(2,1)S(1)}, bf16[128,2176]{1,0:T(8,128)(2,1)S(1)}, u32[]{:S(2)}, u32[]{:S(2)}) collective-permute-start(bf16[128,2176]{1,0:T(8,128)(2,1)S(1)} %constant_dynamic-update-slice_fusion.4.refs_0_), channel_id=1, source_target_pairs={{0,4},{1,5},{2,10},{3,11},{4,0},{5,1},{6,14},{7,15},{8,12},{9,13},... | collective-permute-start | bytes 1671176 | tf_op jit(solution)/shard_map/ppermute | solution.py:800
  128.8 2.0 %collective-permute-start.22 = (bf16[128,2176]{1,0:T(8,128)(2,1)S(1)}, bf16[128,2176]{1,0:T(8,128)(2,1)S(1)}, u32[]{:S(2)}, u32[]{:S(2)}) collective-permute-start(bf16[128,2176]{1,0:T(8,128)(2,1)S(1)} %collective-permute-done.20.refs_2_), channel_id=1, source_target_pairs={{0,2},{1,3},{2,0},{3,1},{4,6},{5,7},{6,4},{7,5},{8,10},{9,11},{10,... | collective-permute-start | bytes 1671176 | tf_op jit(solution)/shard_map/ppermute | solution.py:800

commit v14 on v12

--- a/solution.py
+++ b/solution.py
@@ -301,12 +301,12 @@
 
 
 def ffn_rest_kernel(
-    tables, count, mixing, info_ref, sec_in, dy_in, out_in, dsec_in, res_in, mixed_in, mine_ref, bdown_ref, g2_ref, wout_ref, *refs
+    tables, count, mixing, info_ref, sec_in, dy_in, out_in, dsec_in, res_in, mine_ref, bdown_ref, g2_ref, wout_ref, *refs
 ):
     ups, downs = refs[:count], refs[count : 2 * count]
-    block_out, gres_out, gmix_out, vec_ref, dwout_ref, bias_out = refs[2 * count : 2 * count + 6]
+    block_out, gres_out, gmix_out, branch_out, vec_ref, bias_out = refs[2 * count : 2 * count + 6]
     grads, refs = refs[2 * count + 6 : 3 * count + 6 + mixing], refs[3 * count + 6 + mixing :]
-    sec_ref, dy_ref, out_ref, dsec_ref, res_ref, mixed_ref, branch_ref, up_ref, bias_ref, down_ref, laid_ref, sems = refs
+    sec_ref, dy_ref, out_ref, dsec_ref, res_ref, branch_ref, up_ref, bias_ref, down_ref, laid_ref, sems = refs
     n, width = sec_ref.shape
     units = down_ref.shape[0] // count
     core = info_ref[0]
@@ -342,7 +342,7 @@
         *[(ups[i].at[pl.ds(width, TILE), :], bias_ref.at[:, cols[i]]) for i in range(count)],
     )
     second = move((dy_in, dy_ref), *[(downs[i], down_ref.at[cols[i], :]) for i in range(count)])
-    third = move((out_in, out_ref), (dsec_in, dsec_ref), (res_in, res_ref), (mixed_in, mixed_ref))
+    third = move((out_in, out_ref), (dsec_in, dsec_ref), (res_in, res_ref))
     if mixing:
         keep_ref, send_ref, away_ref = grads
         own_start, own_wait = by_core(
@@ -428,16 +428,16 @@
             branch_ref[rows, :] = gres.astype(BF)
             gone += move((dy_ref.at[span, :], block_out.at[span, :]), (out_ref.at[span, :], gres_out.at[span, :]))
     vec_ref[3:, :] = jnp.zeros((vec_ref.shape[0] - 3, width), F32)
+    gone += move((branch_ref, branch_out))
     sec_ref[...] = mm_nt(branch_ref[...], wout_ref[...]).astype(BF)
     gone += move((sec_ref, gmix_out))
-    dwout_ref[...] = mm_tn(mixed_ref[...], branch_ref[...])
     arrived(gone)
     if mixing:
         own_wait()
         chunk_wait()
 
 
-def ffn_rest(info, tables, mixing, second, dy, out_part, dsec_part, residual, mixed, bdown, g2, wout, mine, chunks):
+def ffn_rest(info, tables, mixing, second, dy, out_part, dsec_part, residual, bdown, g2, wout, mine, chunks):
     n, width = second.shape
     count = len(chunks)
     units = chunks[0][0].shape[1]
@@ -446,14 +446,14 @@
         functools.partial(ffn_rest_kernel, tables, count, mixing),
         "ffn_rest",
         (1,),
-        [anywhere] * 7 + [whole(1, width)] * 2 + [whole(width, width)] + [anywhere] * (2 * count),
-        [anywhere] * 3 + [whole(8, width), whole(width, width), whole(count, units)] + [anywhere] * (count + mixing),
+        [anywhere] * 6 + [whole(1, width)] * 2 + [whole(width, width)] + [anywhere] * (2 * count),
+        [anywhere] * 4 + [whole(8, width), whole(count, units)] + [anywhere] * (count + mixing),
         [
             jax.ShapeDtypeStruct((n, width), BF),
             pltpu.HBM((n, width), F32),
             pltpu.HBM((n, width), BF),
+            pltpu.HBM((n, width), BF),
             pltpu.HBM((8, width), F32),
-            pltpu.HBM((width, width), F32),
             pltpu.HBM((count, units), F32),
         ]
         + [jax.ShapeDtypeStruct((width, 2 * units), BF)] * (count + mixing),
@@ -463,7 +463,6 @@
             pltpu.VMEM((n, width), F32),
             pltpu.VMEM((n, width), F32),
             pltpu.VMEM((n, width), F32),
-            pltpu.VMEM((n, width), BF),
             pltpu.VMEM((n, width), BF),
             pltpu.VMEM((width, count * units), BF),
             pltpu.VMEM((TILE, count * units), BF),
@@ -475,7 +474,7 @@
         near(second)
         + far(dy)
         + near(out_part, dsec_part)
-        + far(residual, mixed, mine, bdown, g2)
+        + far(residual, mine, bdown, g2)
         + (wout,)
         + tuple(c[0] for c in chunks)
         + tuple(c[1] for c in chunks),
@@ -539,7 +538,7 @@
 
 
 def attend_back_kernel(
-    tables, info_ref, qkv_ref, prob_ref, gmix_ref, tok_ref, g1_ref, c1_ref, wqkv_ref, dwout_ref, vec_ref,
+    tables, info_ref, qkv_ref, prob_ref, gmix_ref, tok_ref, mixed_ref, branch_ref, g1_ref, c1_ref, wqkv_ref, vec_ref,
     *refs,
 ):
     *sums, grad_ref, dw_keep_ref, dw_send_ref, dqkv_ref, acc_ref, row_ref = refs
@@ -549,8 +548,7 @@
 
     @pl.when(at == 0)
     def _():
-        acc_ref[:, : 3 * width] = jnp.zeros((width, 3 * width), F32)
-        acc_ref[:, 3 * width : 4 * width] = dwout_ref[...]
+        acc_ref[:, : 4 * width] = jnp.zeros((width, 4 * width), F32)
         row_ref[...] = jnp.zeros_like(row_ref)
         row_ref[SUMS : SUMS + vec_ref.shape[0], :] = vec_ref[...]
         if sums:
@@ -584,6 +582,7 @@
         dqkv_ref[place(r, p, 0)] = mm_tn(stacked, by_head(k * scale)).astype(BF)
     unit, _ = unit_parts(tok_ref[...].astype(F32))
     acc_ref[:, : 3 * width] += mm_tn(unit.astype(BF), dqkv_ref[...])
+    acc_ref[:, 3 * width : 4 * width] += mm_tn(mixed_ref[...], branch_ref[...])
     grad_ref[...] = dqkv_ref[...]
     for i in range(3):
         part = dqkv_ref[:, i * width : (i + 1) * width].astype(F32)
@@ -615,7 +614,7 @@
             dst[to : to + size, :] = acc_ref[rows_at, :].astype(BF)
 
 
-def attend_back(info, tables, qkv, prob, gmix, tokens, g1, c1, wqkv, dwout, *vecs):
+def attend_back(info, tables, qkv, prob, gmix, tokens, mixed, branch, g1, c1, wqkv, *vecs):
     n, width = tokens.shape
     rows, pairs, slots, _ = prob.shape
     per = TOKS // slots
@@ -628,10 +627,11 @@
             pl.BlockSpec((per, pairs, slots, 2 * slots), lambda i, *_: (i, 0, 0, 0)),
             rows_of(width),
             rows_of(width),
+            rows_of(width),
+            rows_of(width),
             whole(1, width),
             whole(1, width),
             whole(*wqkv.shape),
-            whole(width, width),
         ]
         + [whole(*vec.shape) for vec in vecs],
         [rows_of(3 * width)] + [whole(width // 2, 4 * width + LANES)] * 2,
@@ -642,7 +642,7 @@
             pltpu.VMEM((LANES, width), F32),
         ],
         info,
-        far(qkv, prob, gmix, tokens, g1, c1, wqkv, dwout, *vecs),
+        far(qkv, prob, gmix, tokens, mixed, branch, g1, c1, wqkv, *vecs),
     )
 
 
@@ -886,10 +886,10 @@
     away_downs = [swap(d, core_mask) for d in downs]
     chunks = [pair for here in zip(zip(ups, downs), zip(away_ups, away_downs)) for pair in here]
     rest = ffn_rest(
-        info, ff_in_tables, mixing, second, cotangent, out_part, dsec_part, residual, mixed, row(b_down), g2, w_out, own_keep,
+        info, ff_in_tables, mixing, second, cotangent, out_part, dsec_part, residual, row(b_down), g2, w_out, own_keep,
         chunks,
     )
-    block_out, gres, gmix, vec, dwout, bias_rest = rest[:6]
+    block_out, gres, gmix, branch, vec, bias_rest = rest[:6]
     grads = rest[6:]
 
     if narrow == 2 and units == width:
@@ -916,7 +916,7 @@
             held = [add(held[j], swap(held[j + mask], mask)) for j in range(mask)]
         ff_keep = held[0]
 
-    dqkv, keep, send = attend_back(info, at_tables(at_in), qkv, prob, gmix, tokens_in, g1, c1, w_qkv, dwout, *vecs)
+    dqkv, keep, send = attend_back(info, at_tables(at_in), qkv, prob, gmix, tokens_in, mixed, branch, g1, c1, w_qkv, *vecs)
     if mixing:
         send, ff_got = after(send, ff_got)
         ff_keep, ff_send = split(info, ff_keep, got, got_own, ff_got)

time: 134 us -> 134 us (level)
  transfers between devices with their start and end apart: 23 -> 23, of which waited for: 15 -> 15; matrix products, arithmetic and copies ran while one was open for 1% -> 1% of each run, Pallas kernels for 42% -> 43%
where the time goes in v14:
time: 134 us; the launch traced here: 133 us
  Pallas kernels  62.3 us (46%)
  waiting for transfers between devices  40.8 us (30%)
  starting transfers between devices  27.9 us (21%)
    pallas_call x9, Pallas kernels, call(): pl.pallas_call(kernel, grid_spec=pltpu.PrefetchScalarGridSpec(num_scalar_...  60.3 us
    ppermute x23, waiting for transfers between devices, swap(): return lax.ppermute(value, AXES, pairs)  40.8 us
    ppermute x23, starting transfers between devices, swap(): return lax.ppermute(value, AXES, pairs)  27.9 us
  transfers between devices with their start and end apart: 23, of which 15 were waited for; matrix products, arithmetic and copies ran while one was open for 1% of the time, Pallas kernels for 43%

profile of v14, /device:TPU:0, one launch (start us, length us, event | category | flops | bytes accessed | tf_op | source)
XLA Modules:
  0.0 133.3 jit_solution(9666557768477084141)
XLA Ops:
  0.7 0.1 stack.21.info_ref
  0.8 1.8 %pack.1 = (bf16[528,512]{1,0:T(8,128)(2,1)S(1)}, bf16[512,512]{1,0:T(8,128)(2,1)S(1)}) custom-call(s32[6]{0:T(128)S(1)} %stack.21.info_ref, bf16[512,1024]{1,0:T(8,128)(2,1)} %up_ref.3, bf16[1024]{0:T(1024)(128)(2,1)} %bias_ref.3, bf16[1024,512]{1,0:T(8,128)(2,1)} %down_ref.3), custom_call_target="tpu_custom_call" | custom-call | flops 1000 | bytes 1000 | tf_op jit(solution)/shard_map/pack/pallas_call | solution.py:55
  2.6 3.0 %collective-permute-start = (bf16[528,512]{1,0:T(8,128)(2,1)S(1)}, bf16[528,512]{1,0:T(8,128)(2,1)S(1)}, u32[]{:S(2)}, u32[]{:S(2)}) collective-permute-start(bf16[528,512]{1,0:T(8,128)(2,1)S(1)} %get-tuple-element.101), channel_id=1, source_target_pairs={{0,1},{1,0},{2,3},{3,2},{4,5},{5,4},{6,7},{7,6},{8,9},{9,8},{10,11... | collective-permute-start | bytes 1622024 | tf_op jit(solution)/shard_map/ppermute | solution.py:797
  5.6 0.1 collective-permute-start.2
  5.7 9.0 %attend.1 = (bf16[1024,1536]{1,0:T(8,128)(2,1)}, bf16[8,4,128,256]{3,2,1,0:T(8,128)(2,1)}, bf16[1024,512]{1,0:T(8,128)(2,1)}, f32[1024,512]{1,0:T(8,128)}, bf16[1024,512]{1,0:T(8,128)(2,1)S(1)}) custom-call(s32[6]{0:T(128)S(1)} %stack.21.info_ref, bf16[1024,512]{1,0:T(8,128)(2,1)} %tok_ref.2, f32[1,512]{1,0:T(1,128)} %bitcast.9, f32[1,512]{1,0:T(1,128)} %bitcast.12, ...), custom_call_target="tpu_custom_call" | custom-call | flops 1000 | bytes 1000 | tf_op jit(solution)/shard_map/attend/pallas_call | solution.py:55
  14.7 11.1 %ffn_own.1 = (f32[1024,512]{1,0:T(8,128)S(1)}, f32[1024,512]{1,0:T(8,128)S(1)}, bf16[512,1024]{1,0:T(8,128)(2,1)}, bf16[512,1024]{1,0:T(8,128)(2,1)}, f32[2,512]{1,0:T(2,128)}) custom-call(s32[6]{0:T(128)S(1)} %stack.21.info_ref, bf16[1024,512]{1,0:T(8,128)(2,1)S(1)} %get-tuple-element.95.sec_ref.sec_in, bf16[1024,512]{1,0:T(8,128)(2,1)} %dy_in.1, ...), custom_call_target="tpu_custom_call" | custom-call | flops 1000 | bytes 1000 | tf_op jit(solution)/shard_map/ffn_own/pallas_call | solution.py:55
  25.9 3.3 %collective-permute-done.2.refs_2_ = bf16[512,512]{1,0:T(8,128)(2,1)S(1)} collective-permute-done((bf16[512,512]{1,0:T(8,128)(2,1)S(1)}, bf16[512,512]{1,0:T(8,128)(2,1)S(1)}, u32[]{:S(2)}, u32[]{:S(2)}) %collective-permute-start.2) | collective-permute-done | bytes 524320 | tf_op jit(solution)/shard_map/ppermute | solution.py:797
  29.1 0.5 collective-permute-start.5
  29.6 2.1 %collective-permute-done.3.refs_3_ = bf16[512,512]{1,0:T(8,128)(2,1)S(1)} collective-permute-done((bf16[512,512]{1,0:T(8,128)(2,1)S(1)}, bf16[512,512]{1,0:T(8,128)(2,1)S(1)}, u32[]{:S(2)}, u32[]{:S(2)}) %collective-permute-start.3) | collective-permute-done | bytes 524320 | tf_op jit(solution)/shard_map/ppermute | solution.py:797
  31.8 13.2 %ffn_rest.1 = (bf16[1024,512]{1,0:T(8,128)(2,1)}, f32[1024,512]{1,0:T(8,128)}, bf16[1024,512]{1,0:T(8,128)(2,1)}, bf16[1024,512]{1,0:T(8,128)(2,1)}, f32[8,512]{...) custom-call(s32[6]{0:T(128)S(1)} %stack.21.info_ref, ...), custom_call_target="tpu_custom_call" | custom-call | flops 1000 | bytes 1000 | tf_op jit(solution)/shard_map/ffn_rest/pallas_call | solution.py:55
  44.9 0.2 collective-permute-start.4
  45.1 2.5 %collective-permute-done.4.got_ref = bf16[512,1024]{1,0:T(8,128)(2,1)S(1)} collective-permute-done((bf16[512,1024]{1,0:T(8,128)(2,1)S(1)}, bf16[512,1024]{1,0:T(8,128)(2,1)S(1)}, u32[]{:S(2)}, u32[]{:S(2)}) %collective-permute-start.4) | collective-permute-done | bytes 1048608 | tf_op jit(solution)/shard_map/ppermute | solution.py:797
  47.7 0.8 join.1
  48.5 1.8 %collective-permute-start.6 = (bf16[512,1024]{1,0:T(8,128)(2,1)S(1)}, bf16[512,1024]{1,0:T(8,128)(2,1)S(1)}, u32[]{:S(2)}, u32[]{:S(2)}) collective-permute-start(bf16[512,1024]{1,0:T(8,128)(2,1)S(1)} %join.1), channel_id=1, source_target_pairs={{0,1},{1,0},{2,6},{3,7},{4,5},{5,4},{6,2},{7,3},{8,9},{9,8},{10,14... | collective-permute-start | bytes 3145736 | tf_op jit(solution)/shard_map/ppermute | solution.py:797
  50.3 12.0 %attend_back.1 = (bf16[1024,1536]{1,0:T(8,128)(2,1)S(1)}, bf16[256,2176]{1,0:T(8,128)(2,1)S(1)}, bf16[256,2176]{1,0:T(8,128)(2,1)S(1)}) custom-call(s32[6]{0:T(128)S(1)} %stack.21.info_ref, bf16[1024,1536]{1,0:T(8,128)(2,1)} %get-tuple-element.108.qkv_ref, bf16[8,4,128,256]{3,2,1,0:T(8,128)(2,1)} %get-tuple-element.109.prob_ref, ...), custom_call_target="tpu_custom_call" | custom-call | flops 1000 | bytes 1000 | tf_op jit(solution)/shard_map/attend_back/pallas_call | solution.py:55
  62.3 1.1 collective-permute-done.6.arrived_ref
  63.3 1.1 split.1
  64.5 1.8 %collective-permute-start.8 = (bf16[256,1024]{1,0:T(8,128)(2,1)S(1)}, bf16[256,1024]{1,0:T(8,128)(2,1)S(1)}, u32[]{:S(2)}, u32[]{:S(2)}) collective-permute-start(bf16[256,1024]{1,0:T(8,128)(2,1)S(1)} %get-tuple-element.129), channel_id=1, source_target_pairs={{0,4},{1,5},{2,3},{3,2},{4,0},{5,1},{6,7},{7,6},{8,12},{9,13},{10,... | collective-permute-start | bytes 1572872 | tf_op jit(solution)/shard_map/ppermute | solution.py:797
  66.3 0.3 add_convert_fusion
  66.6 0.1 fusion
  66.7 1.6 %collective-permute-start.9 = (bf16[128,2176]{1,0:T(8,128)(2,1)S(1)}, bf16[128,2176]{1,0:T(8,128)(2,1)S(1)}, u32[]{:S(2)}, u32[]{:S(2)}) collective-permute-start(bf16[128,2176]{1,0:T(8,128)(2,1)S(1)} %get-tuple-element.172), channel_id=1, source_target_pairs={{0,4},{1,5},{2,10},{3,11},{4,0},{5,1},{6,14},{7,15},{8,12},{9,13},... | collective-permute-start | bytes 1671176 | tf_op jit(solution)/shard_map/ppermute | solution.py:797
  68.3 5.5 %first_back.1 = f32[1024,512]{1,0:T(8,128)} custom-call(s32[6]{0:T(128)S(1)} %stack.21.info_ref, bf16[1024,1536]{1,0:T(8,128)(2,1)S(1)} %get-tuple-element.124.dqkv_ref, bf16[512,1536]{1,0:T(8,128)(2,1)S(1)} %copy-done.1, bf16[1024,512]{1,0:T(8,128)(2,1)} %tok_ref.2, f32[1024,512]{1,0:T(8,128)} %get-tuple-element.125.gres_ref, f32[1,512]{1,0:T(1,128)} %bitcast.11), custom_call_target="tpu_custom_call" | custom-call | flops 1000 | bytes 1000 | tf_op jit(solution)/shard_map/first_back/pallas_call | solution.py:55
  73.8 0.2 add_convert_fusion.2
  74.1 1.8 %collective-permute-start.10 = (bf16[128,1024]{1,0:T(8,128)(2,1)S(1)}, bf16[128,1024]{1,0:T(8,128)(2,1)S(1)}, u32[]{:S(2)}, u32[]{:S(2)}) collective-permute-start(bf16[128,1024]{1,0:T(8,128)(2,1)S(1)} %get-tuple-element.176), channel_id=1, source_target_pairs={{0,8},{1,9},{2,10},{3,11},{4,12},{5,13},{6,14},{7,15},{8,0},{9,1},... | collective-permute-start | bytes 786440 | tf_op jit(solution)/shard_map/ppermute | solution.py:797
  75.9 5.0 %collective-permute-done.9 = bf16[128,2176]{1,0:T(8,128)(2,1)S(1)} collective-permute-done((bf16[128,2176]{1,0:T(8,128)(2,1)S(1)}, bf16[128,2176]{1,0:T(8,128)(2,1)S(1)}, u32[]{:S(2)}, u32[]{:S(2)}) %collective-permute-start.9) | collective-permute-done | bytes 557088 | tf_op jit(solution)/shard_map/ppermute | solution.py:797
  80.9 0.1 add_convert_fusion.1
  81.1 2.1 %collective-permute-start.11 = (bf16[64,2176]{1,0:T(8,128)(2,1)S(1)}, bf16[64,2176]{1,0:T(8,128)(2,1)S(1)}, u32[]{:S(2)}, u32[]{:S(2)}) collective-permute-start(bf16[64,2176]{1,0:T(8,128)(2,1)S(1)} %get-tuple-element.175), channel_id=1, source_target_pairs={{0,1},{1,0},{2,6},{3,7},{4,5},{5,4},{6,2},{7,3},{8,9},{9,8},{10,14... | collective-permute-start | bytes 835592 | tf_op jit(solution)/shard_map/ppermute | solution.py:797
  83.2 5.9 %collective-permute-done.11 = bf16[64,2176]{1,0:T(8,128)(2,1)S(1)} collective-permute-done((bf16[64,2176]{1,0:T(8,128)(2,1)S(1)}, bf16[64,2176]{1,0:T(8,128)(2,1)S(1)}, u32[]{:S(2)}, u32[]{:S(2)}) %collective-permute-start.11) | collective-permute-done | bytes 278560 | tf_op jit(solution)/shard_map/ppermute | solution.py:797
  89.3 2.1 %collective-permute-start.12 = (bf16[32,2176]{1,0:T(8,128)(2,1)S(1)}, bf16[32,2176]{1,0:T(8,128)(2,1)S(1)}, u32[]{:S(2)}, u32[]{:S(2)}) collective-permute-start(bf16[32,2176]{1,0:T(8,128)(2,1)S(1)} %get-tuple-element.178), channel_id=1, source_target_pairs={{0,8},{1,9},{2,3},{3,2},{4,12},{5,13},{6,7},{7,6},{8,0},{9,1},{10,... | collective-permute-start | bytes 417800 | tf_op jit(solution)/shard_map/ppermute | solution.py:797
  91.4 2.6 %collective-permute-start.13 = (bf16[128,1024]{1,0:T(8,128)(2,1)S(1)}, bf16[128,1024]{1,0:T(8,128)(2,1)S(1)}, u32[]{:S(2)}, u32[]{:S(2)}) collective-permute-start(bf16[128,1024]{1,0:T(8,128)(2,1)S(1)} %add_convert_fusion.5), channel_id=1, source_target_pairs={{0,16},{1,17},{2,18},{3,19},{4,20},{5,21},{6,22},{7,23},{8,24},{9,... | collective-permute-start | bytes 786440 | tf_op jit(solution)/shard_map/ppermute | solution.py:797
  94.0 0.8 collective-permute-done.12
  94.9 3.9 %collective-permute-start.14 = (bf16[32,2176]{1,0:T(8,128)(2,1)S(1)}, bf16[32,2176]{1,0:T(8,128)(2,1)S(1)}, u32[]{:S(2)}, u32[]{:S(2)}) collective-permute-start(bf16[32,2176]{1,0:T(8,128)(2,1)S(1)} %add_convert_fusion.7), channel_id=1, source_target_pairs={{0,16},{1,17},{2,18},{3,19},{4,20},{5,21},{6,22},{7,23},{8,24},{9,... | collective-permute-start | bytes 417800 | tf_op jit(solution)/shard_map/ppermute | solution.py:797
  98.7 3.1 %collective-permute-done.13 = bf16[128,1024]{1,0:T(8,128)(2,1)S(1)} collective-permute-done((bf16[128,1024]{1,0:T(8,128)(2,1)S(1)}, bf16[128,1024]{1,0:T(8,128)(2,1)S(1)}, u32[]{:S(2)}, u32[]{:S(2)}) %collective-permute-start.13) | collective-permute-done | bytes 262176 | tf_op jit(solution)/shard_map/ppermute | solution.py:797
  101.9 1.6 %collective-permute-start.15 = (bf16[128,1024]{1,0:T(8,128)(2,1)S(1)}, bf16[128,1024]{1,0:T(8,128)(2,1)S(1)}, u32[]{:S(2)}, u32[]{:S(2)}) collective-permute-start(bf16[128,1024]{1,0:T(8,128)(2,1)S(1)} %add_convert_fusion.4), channel_id=1, source_target_pairs={{0,4},{1,5},{2,6},{3,7},{4,0},{5,1},{6,2},{7,3},{8,12},{9,13},{10,... | collective-permute-start | bytes 786440 | tf_op jit(solution)/shard_map/ppermute | solution.py:797
  103.5 1.4 %collective-permute-done.14 = bf16[32,2176]{1,0:T(8,128)(2,1)S(1)} collective-permute-done((bf16[32,2176]{1,0:T(8,128)(2,1)S(1)}, bf16[32,2176]{1,0:T(8,128)(2,1)S(1)}, u32[]{:S(2)}, u32[]{:S(2)}) %collective-permute-start.14) | collective-permute-done | bytes 139296 | tf_op jit(solution)/shard_map/ppermute | solution.py:797
  105.0 0.8 collective-permute-start.16
  105.8 2.5 %collective-permute-done.15 = bf16[128,1024]{1,0:T(8,128)(2,1)S(1)} collective-permute-done((bf16[128,1024]{1,0:T(8,128)(2,1)S(1)}, bf16[128,1024]{1,0:T(8,128)(2,1)S(1)}, u32[]{:S(2)}, u32[]{:S(2)}) %collective-permute-start.15) | collective-permute-done | bytes 262176 | tf_op jit(solution)/shard_map/ppermute | solution.py:797
  108.4 2.3 %collective-permute-start.18 = (bf16[256,1024]{1,0:T(8,128)(2,1)S(1)}, bf16[256,1024]{1,0:T(8,128)(2,1)S(1)}, u32[]{:S(2)}, u32[]{:S(2)}) collective-permute-start(bf16[256,1024]{1,0:T(8,128)(2,1)S(1)} %constant_dynamic-update-slice_fusion), channel_id=1, source_target_pairs={{0,8},{1,9},{2,10},{3,11},{4,12},{5,13},{6,14},{7,15},{8,0},{9,1},... | collective-permute-start | bytes 1572872 | tf_op jit(solution)/shard_map/ppermute | solution.py:797
  110.7 1.0 collective-permute-done.16
  111.8 6.5 %collective-permute-done.17 = bf16[64,2176]{1,0:T(8,128)(2,1)S(1)} collective-permute-done((bf16[64,2176]{1,0:T(8,128)(2,1)S(1)}, bf16[64,2176]{1,0:T(8,128)(2,1)S(1)}, u32[]{:S(2)}, u32[]{:S(2)}) %collective-permute-start.17) | collective-permute-done | bytes 278560 | tf_op jit(solution)/shard_map/ppermute | solution.py:797
  118.5 0.5 collective-permute-start.21
  119.0 1.0 collective-permute-start.20
  120.0 1.2 collective-permute-done.19.other_ref
  121.1 3.1 %ffn_end.1 = (f32[512,1024]{1,0:T(8,128)}, f32[1024,512]{1,0:T(8,128)}) custom-call(s32[6]{0:T(128)S(1)} %stack.21.info_ref, bf16[512,1024]{1,0:T(8,128)(2,1)S(1)} %constant_dynamic-update-slice_fusion.6.keep_ref, bf16[512,1024]{1,0:T(8,128)(2,1)S(1)} %collective-permute-done.19.other_ref), custom_call_target="tpu_custom_call" | custom-call | flops 1000 | bytes 1000 | tf_op jit(solution)/shard_map/ffn_end/pallas_call | solution.py:55
  124.2 2.0 %attend_end.2 = (f32[512,1536]{1,0:T(8,128)}, f32[512,512]{1,0:T(8,128)}) custom-call(s32[6]{0:T(128)S(1)} %stack.21.info_ref, bf16[128,2176]{1,0:T(8,128)(2,1)S(1)} %constant_dynamic-update-slice_fusion.4.refs_0_, bf16[128,2176]{1,0:T(8,128)(2,1)S(1)} %collective-permute-done.21.refs_1_), custom_call_target="tpu_custom_call" | custom-call | flops 1000 | bytes 1000 | tf_op jit(solution)/shard_map/attend_end/pallas_call | solution.py:55
  126.2 2.3 %collective-permute-done.20.refs_2_ = bf16[128,2176]{1,0:T(8,128)(2,1)S(1)} collective-permute-done((bf16[128,2176]{1,0:T(8,128)(2,1)S(1)}, bf16[128,2176]{1,0:T(8,128)(2,1)S(1)}, u32[]{:S(2)}, u32[]{:S(2)}) %collective-permute-start.20) | collective-permute-done | bytes 557088 | tf_op jit(solution)/shard_map/ppermute | solution.py:797
  128.5 2.0 %collective-permute-done.22.refs_3_ = bf16[128,2176]{1,0:T(8,128)(2,1)S(1)} collective-permute-done((bf16[128,2176]{1,0:T(8,128)(2,1)S(1)}, bf16[128,2176]{1,0:T(8,128)(2,1)S(1)}, u32[]{:S(2)}, u32[]{:S(2)}) %collective-permute-start.22) | collective-permute-done | bytes 557088 | tf_op jit(solution)/shard_map/ppermute | solution.py:797
  130.5 2.7 %attend_end.3 = (f32[512,1536]{1,0:T(8,128)}, f32[512,512]{1,0:T(8,128)}, f32[512]{0:T(512)}, f32[512]{0:T(512)}, f32[512]{0:T(512)}, /*index=5*/f32[512]{0:T(512)}, f32[512]{0:T(512)}, f32[1024]{0:T(1024)}) custom-call(s32[6]{0:T(128)S(1)} %stack.21.info_ref, ...), custom_call_target="tpu_custom_call", output_to_operand_aliasing={{0}: (5, {}), {1}: (6, {})} | custom-call | flops 1000 | bytes 1000 | tf_op jit(solution)/shard_map/attend_end/pallas_call | solution.py:55
  (40 shorter events, 0.8 us)
Async XLA Ops:
  0.6 5.1 %copy-start = (bf16[512,1536]{1,0:T(8,128)(2,1)S(1)}, bf16[512,1536]{1,0:T(8,128)(2,1)}, u32[]{:S(2)}) copy-start(bf16[512,1536]{1,0:T(8,128)(2,1)} %wqkv_ref.5) | copy-start | bytes 4718596
  0.7 5.1 %copy-start.4 = (bf16[512,512]{1,0:T(8,128)(2,1)S(1)}, bf16[512,512]{1,0:T(8,128)(2,1)}, u32[]{:S(2)}) copy-start(bf16[512,512]{1,0:T(8,128)(2,1)} %wout_ref.3) | copy-start | bytes 1572868
  2.6 12.1 %copy-start.2 = (bf16[512,1024]{1,0:T(8,128)(2,1)S(1)}, bf16[512,1024]{1,0:T(8,128)(2,1)}, u32[]{:S(2)}) copy-start(bf16[512,1024]{1,0:T(8,128)(2,1)} %up_ref.3) | copy-start | bytes 3145732
  2.6 12.1 %copy-start.3 = (bf16[1024,512]{1,0:T(8,128)(2,1)S(1)}, bf16[1024,512]{1,0:T(8,128)(2,1)}, u32[]{:S(2)}) copy-start(bf16[1024,512]{1,0:T(8,128)(2,1)} %down_ref.3) | copy-start | bytes 3145732
  2.6 23.2 %collective-permute-start = (bf16[528,512]{1,0:T(8,128)(2,1)S(1)}, bf16[528,512]{1,0:T(8,128)(2,1)S(1)}, u32[]{:S(2)}, u32[]{:S(2)}) collective-permute-start(bf16[528,512]{1,0:T(8,128)(2,1)S(1)} %get-tuple-element.101), channel_id=1, source_target_pairs={{0,1},{1,0},{2,3},{3,2},{4,5},{5,4},{6,7},{7,6},{8,9},{9,8},{10,11... | collective-permute-start | bytes 1622024 | tf_op jit(solution)/shard_map/ppermute | solution.py:797
  5.6 23.5 %collective-permute-start.2 = (bf16[512,512]{1,0:T(8,128)(2,1)S(1)}, bf16[512,512]{1,0:T(8,128)(2,1)S(1)}, u32[]{:S(2)}, u32[]{:S(2)}) collective-permute-start(bf16[512,512]{1,0:T(8,128)(2,1)S(1)} %get-tuple-element.103), channel_id=1, source_target_pairs={{0,1},{1,0},{2,3},{3,2},{4,5},{5,4},{6,7},{7,6},{8,9},{9,8},{10,11... | collective-permute-start | bytes 1572872 | tf_op jit(solution)/shard_map/ppermute | solution.py:797
  25.8 5.9 %collective-permute-start.1 = (bf16[528,512]{1,0:T(8,128)(2,1)S(1)}, bf16[528,512]{1,0:T(8,128)(2,1)S(1)}, u32[]{:S(2)}, u32[]{:S(2)}) collective-permute-start(bf16[528,512]{1,0:T(8,128)(2,1)S(1)} %collective-permute-done.refs_0_), channel_id=1, source_target_pairs={{0,2},{1,3},{2,0},{3,1},{4,6},{5,7},{6,4},{7,5},{8,10},{9,11},{10,... | collective-permute-start | bytes 1622024 | tf_op jit(solution)/shard_map/ppermute | solution.py:797
  29.1 2.6 %collective-permute-start.3 = (bf16[512,512]{1,0:T(8,128)(2,1)S(1)}, bf16[512,512]{1,0:T(8,128)(2,1)S(1)}, u32[]{:S(2)}, u32[]{:S(2)}) collective-permute-start(bf16[512,512]{1,0:T(8,128)(2,1)S(1)} %collective-permute-done.2.refs_2_), channel_id=1, source_target_pairs={{0,2},{1,3},{2,0},{3,1},{4,6},{5,7},{6,4},{7,5},{8,10},{9,11},{10,... | collective-permute-start | bytes 1572872 | tf_op jit(solution)/shard_map/ppermute | solution.py:797
  29.1 16.0 %collective-permute-start.5 = (bf16[512,1024]{1,0:T(8,128)(2,1)}, bf16[512,1024]{1,0:T(8,128)(2,1)S(1)}, u32[]{:S(2)}, u32[]{:S(2)}) collective-permute-start(bf16[512,1024]{1,0:T(8,128)(2,1)} %get-tuple-element.107), channel_id=1, source_target_pairs={{0,2},{1,3},{2,0},{3,1},{4,6},{5,7},{6,4},{7,5},{8,10},{9,11},{10,... | collective-permute-start | bytes 3145736 | tf_op jit(solution)/shard_map/ppermute | solution.py:797
  44.9 2.7 %collective-permute-start.4 = (bf16[512,1024]{1,0:T(8,128)(2,1)S(1)}, bf16[512,1024]{1,0:T(8,128)(2,1)S(1)}, u32[]{:S(2)}, u32[]{:S(2)}) collective-permute-start(bf16[512,1024]{1,0:T(8,128)(2,1)S(1)} %get-tuple-element.106), channel_id=1, source_target_pairs={{0,2},{1,3},{2,0},{3,1},{4,6},{5,7},{6,4},{7,5},{8,10},{9,11},{10,... | collective-permute-start | bytes 3145736 | tf_op jit(solution)/shard_map/ppermute | solution.py:797
  48.5 14.9 %collective-permute-start.6 = (bf16[512,1024]{1,0:T(8,128)(2,1)S(1)}, bf16[512,1024]{1,0:T(8,128)(2,1)S(1)}, u32[]{:S(2)}, u32[]{:S(2)}) collective-permute-start(bf16[512,1024]{1,0:T(8,128)(2,1)S(1)} %join.1), channel_id=1, source_target_pairs={{0,1},{1,0},{2,6},{3,7},{4,5},{5,4},{6,2},{7,3},{8,9},{9,8},{10,14... | collective-permute-start | bytes 3145736 | tf_op jit(solution)/shard_map/ppermute | solution.py:797
  63.3 3.0 %collective-permute-start.7 = (bf16[256,2176]{1,0:T(8,128)(2,1)S(1)}, bf16[256,2176]{1,0:T(8,128)(2,1)S(1)}, u32[]{:S(2)}, u32[]{:S(2)}) collective-permute-start(bf16[256,2176]{1,0:T(8,128)(2,1)S(1)} %get-tuple-element.123), channel_id=1, source_target_pairs={{0,2},{1,3},{2,0},{3,1},{4,6},{5,7},{6,4},{7,5},{8,10},{9,11},{10,... | collective-permute-start | bytes 3342344 | tf_op jit(solution)/shard_map/ppermute | solution.py:797
  64.5 9.3 %collective-permute-start.8 = (bf16[256,1024]{1,0:T(8,128)(2,1)S(1)}, bf16[256,1024]{1,0:T(8,128)(2,1)S(1)}, u32[]{:S(2)}, u32[]{:S(2)}) collective-permute-start(bf16[256,1024]{1,0:T(8,128)(2,1)S(1)} %get-tuple-element.129), channel_id=1, source_target_pairs={{0,4},{1,5},{2,3},{3,2},{4,0},{5,1},{6,7},{7,6},{8,12},{9,13},{10,... | collective-permute-start | bytes 1572872 | tf_op jit(solution)/shard_map/ppermute | solution.py:797
  66.3 2.0 %copy-start.1 = (bf16[512,1536]{1,0:T(8,128)(2,1)S(1)}, bf16[512,1536]{1,0:T(8,128)(2,1)}, u32[]{:S(2)}) copy-start(bf16[512,1536]{1,0:T(8,128)(2,1)} %wqkv_ref.5) | copy-start | bytes 4718596
  66.7 14.2 %collective-permute-start.9 = (bf16[128,2176]{1,0:T(8,128)(2,1)S(1)}, bf16[128,2176]{1,0:T(8,128)(2,1)S(1)}, u32[]{:S(2)}, u32[]{:S(2)}) collective-permute-start(bf16[128,2176]{1,0:T(8,128)(2,1)S(1)} %get-tuple-element.172), channel_id=1, source_target_pairs={{0,4},{1,5},{2,10},{3,11},{4,0},{5,1},{6,14},{7,15},{8,12},{9,13},... | collective-permute-start | bytes 1671176 | tf_op jit(solution)/shard_map/ppermute | solution.py:797
  74.1 9.1 %collective-permute-start.10 = (bf16[128,1024]{1,0:T(8,128)(2,1)S(1)}, bf16[128,1024]{1,0:T(8,128)(2,1)S(1)}, u32[]{:S(2)}, u32[]{:S(2)}) collective-permute-start(bf16[128,1024]{1,0:T(8,128)(2,1)S(1)} %get-tuple-element.176), channel_id=1, source_target_pairs={{0,8},{1,9},{2,10},{3,11},{4,12},{5,13},{6,14},{7,15},{8,0},{9,1},... | collective-permute-start | bytes 786440 | tf_op jit(solution)/shard_map/ppermute | solution.py:797
  81.1 8.1 %collective-permute-start.11 = (bf16[64,2176]{1,0:T(8,128)(2,1)S(1)}, bf16[64,2176]{1,0:T(8,128)(2,1)S(1)}, u32[]{:S(2)}, u32[]{:S(2)}) collective-permute-start(bf16[64,2176]{1,0:T(8,128)(2,1)S(1)} %get-tuple-element.175), channel_id=1, source_target_pairs={{0,1},{1,0},{2,6},{3,7},{4,5},{5,4},{6,2},{7,3},{8,9},{9,8},{10,14... | collective-permute-start | bytes 835592 | tf_op jit(solution)/shard_map/ppermute | solution.py:797
  89.3 5.5 %collective-permute-start.12 = (bf16[32,2176]{1,0:T(8,128)(2,1)S(1)}, bf16[32,2176]{1,0:T(8,128)(2,1)S(1)}, u32[]{:S(2)}, u32[]{:S(2)}) collective-permute-start(bf16[32,2176]{1,0:T(8,128)(2,1)S(1)} %get-tuple-element.178), channel_id=1, source_target_pairs={{0,8},{1,9},{2,3},{3,2},{4,12},{5,13},{6,7},{7,6},{8,0},{9,1},{10,... | collective-permute-start | bytes 417800 | tf_op jit(solution)/shard_map/ppermute | solution.py:797
  91.4 10.5 %collective-permute-start.13 = (bf16[128,1024]{1,0:T(8,128)(2,1)S(1)}, bf16[128,1024]{1,0:T(8,128)(2,1)S(1)}, u32[]{:S(2)}, u32[]{:S(2)}) collective-permute-start(bf16[128,1024]{1,0:T(8,128)(2,1)S(1)} %add_convert_fusion.5), channel_id=1, source_target_pairs={{0,16},{1,17},{2,18},{3,19},{4,20},{5,21},{6,22},{7,23},{8,24},{9,... | collective-permute-start | bytes 786440 | tf_op jit(solution)/shard_map/ppermute | solution.py:797
  94.9 10.1 %collective-permute-start.14 = (bf16[32,2176]{1,0:T(8,128)(2,1)S(1)}, bf16[32,2176]{1,0:T(8,128)(2,1)S(1)}, u32[]{:S(2)}, u32[]{:S(2)}) collective-permute-start(bf16[32,2176]{1,0:T(8,128)(2,1)S(1)} %add_convert_fusion.7), channel_id=1, source_target_pairs={{0,16},{1,17},{2,18},{3,19},{4,20},{5,21},{6,22},{7,23},{8,24},{9,... | collective-permute-start | bytes 417800 | tf_op jit(solution)/shard_map/ppermute | solution.py:797
  101.9 6.4 %collective-permute-start.15 = (bf16[128,1024]{1,0:T(8,128)(2,1)S(1)}, bf16[128,1024]{1,0:T(8,128)(2,1)S(1)}, u32[]{:S(2)}, u32[]{:S(2)}) collective-permute-start(bf16[128,1024]{1,0:T(8,128)(2,1)S(1)} %add_convert_fusion.4), channel_id=1, source_target_pairs={{0,4},{1,5},{2,6},{3,7},{4,0},{5,1},{6,2},{7,3},{8,12},{9,13},{10,... | collective-permute-start | bytes 786440 | tf_op jit(solution)/shard_map/ppermute | solution.py:797
  105.0 6.7 %collective-permute-start.16 = (bf16[32,2176]{1,0:T(8,128)(2,1)S(1)}, bf16[32,2176]{1,0:T(8,128)(2,1)S(1)}, u32[]{:S(2)}, u32[]{:S(2)}) collective-permute-start(bf16[32,2176]{1,0:T(8,128)(2,1)S(1)} %add_convert_fusion.6), channel_id=1, source_target_pairs={{0,8},{1,9},{2,6},{3,7},{4,12},{5,13},{6,2},{7,3},{8,0},{9,1},{10,... | collective-permute-start | bytes 417800 | tf_op jit(solution)/shard_map/ppermute | solution.py:797
  108.4 10.0 %collective-permute-start.18 = (bf16[256,1024]{1,0:T(8,128)(2,1)S(1)}, bf16[256,1024]{1,0:T(8,128)(2,1)S(1)}, u32[]{:S(2)}, u32[]{:S(2)}) collective-permute-start(bf16[256,1024]{1,0:T(8,128)(2,1)S(1)} %constant_dynamic-update-slice_fusion), channel_id=1, source_target_pairs={{0,8},{1,9},{2,10},{3,11},{4,12},{5,13},{6,14},{7,15},{8,0},{9,1},... | collective-permute-start | bytes 1572872 | tf_op jit(solution)/shard_map/ppermute | solution.py:797
  111.7 6.6 %collective-permute-start.17 = (bf16[64,2176]{1,0:T(8,128)(2,1)S(1)}, bf16[64,2176]{1,0:T(8,128)(2,1)S(1)}, u32[]{:S(2)}, u32[]{:S(2)}) collective-permute-start(bf16[64,2176]{1,0:T(8,128)(2,1)S(1)} %constant_dynamic-update-slice_fusion.2), channel_id=1, source_target_pairs={{0,1},{1,0},{2,3},{3,2},{4,5},{5,4},{6,7},{7,6},{8,9},{9,8},{10,11... | collective-permute-start | bytes 835592 | tf_op jit(solution)/shard_map/ppermute | solution.py:797
  118.4 2.7 %collective-permute-start.19 = (bf16[512,1024]{1,0:T(8,128)(2,1)S(1)}, bf16[512,1024]{1,0:T(8,128)(2,1)S(1)}, u32[]{:S(2)}, u32[]{:S(2)}) collective-permute-start(bf16[512,1024]{1,0:T(8,128)(2,1)S(1)} %constant_dynamic-update-slice_fusion.6.keep_ref), channel_id=1, source_target_pairs={{0,2},{1,3},{2,0},{3,1},{4,6},{5,7},{6,4},{7,5},{8,10},{9,11},{10,... | collective-permute-start | bytes 3145736 | tf_op jit(solution)/shard_map/ppermute | solution.py:797
  118.5 5.7 %collective-permute-start.21 = (bf16[128,2176]{1,0:T(8,128)(2,1)S(1)}, bf16[128,2176]{1,0:T(8,128)(2,1)S(1)}, u32[]{:S(2)}, u32[]{:S(2)}) collective-permute-start(bf16[128,2176]{1,0:T(8,128)(2,1)S(1)} %constant_dynamic-update-slice_fusion.4.refs_0_), channel_id=1, source_target_pairs={{0,2},{1,3},{2,0},{3,1},{4,6},{5,7},{6,4},{7,5},{8,10},{9,11},{10,... | collective-permute-start | bytes 1671176 | tf_op jit(solution)/shard_map/ppermute | solution.py:797
  119.0 9.5 %collective-permute-start.20 = (bf16[128,2176]{1,0:T(8,128)(2,1)S(1)}, bf16[128,2176]{1,0:T(8,128)(2,1)S(1)}, u32[]{:S(2)}, u32[]{:S(2)}) collective-permute-start(bf16[128,2176]{1,0:T(8,128)(2,1)S(1)} %constant_dynamic-update-slice_fusion.4.refs_0_), channel_id=1, source_target_pairs={{0,4},{1,5},{2,10},{3,11},{4,0},{5,1},{6,14},{7,15},{8,12},{9,13},... | collective-permute-start | bytes 1671176 | tf_op jit(solution)/shard_map/ppermute | solution.py:797
  128.5 2.0 %collective-permute-start.22 = (bf16[128,2176]{1,0:T(8,128)(2,1)S(1)}, bf16[128,2176]{1,0:T(8,128)(2,1)S(1)}, u32[]{:S(2)}, u32[]{:S(2)}) collective-permute-start(bf16[128,2176]{1,0:T(8,128)(2,1)S(1)} %collective-permute-done.20.refs_2_), channel_id=1, source_target_pairs={{0,2},{1,3},{2,0},{3,1},{4,6},{5,7},{6,4},{7,5},{8,10},{9,11},{10,... | collective-permute-start | bytes 1671176 | tf_op jit(solution)/shard_map/ppermute | solution.py:797

commit v15 on v14

--- a/solution.py
+++ b/solution.py
@@ -406,7 +406,7 @@
         gone = move(*[(laid_ref.at[i], grads[i]) for i in range(count)])
 
     arrived(third)
-    step = min(TOKS // 2, toks)
+    step = min(64, toks)
     for t, (hid, dpre) in enumerate(parts):
         out_all, dsec_all = mm(hid, down_ref[...]), mm_nt(dpre, up_ref[...])
         for r in range(0, toks, step):
@@ -468,7 +468,7 @@
             pltpu.VMEM((TILE, count * units), BF),
             pltpu.VMEM((count * units, width), BF),
             pltpu.VMEM((count, width, 2 * units), BF),
-            pltpu.SemaphoreType.DMA((24 + 4 * count,)),
+            pltpu.SemaphoreType.DMA((24 + 4 * count + n // 32,)),
         ],
         info,
         near(second)

time: 134 us -> 134 us (level)
  no operation moved by 1% of the time
where the time goes in v15:
time: 134 us
  Pallas kernels  62.6 us (47%)
  waiting for transfers between devices  40.8 us (30%)
  starting transfers between devices  27.9 us (21%)
    pallas_call x9, Pallas kernels, call(): pl.pallas_call(kernel, grid_spec=pltpu.PrefetchScalarGridSpec(num_scalar_...  60.6 us
    ppermute x23, waiting for transfers between devices, swap(): return lax.ppermute(value, AXES, pairs)  40.8 us
    ppermute x23, starting transfers between devices, swap(): return lax.ppermute(value, AXES, pairs)  27.9 us
  transfers between devices with their start and end apart: 23, of which 15 were waited for; matrix products, arithmetic and copies ran while one was open for 1% of the time, Pallas kernels for 43%

profile of v15, /device:TPU:0, one launch (start us, length us, event | category | flops | bytes accessed | tf_op | source)
XLA Modules:
  0.0 133.6 jit_solution(10334030752530314928)
XLA Ops:
  0.7 0.1 stack.21.info_ref
  0.8 1.8 %pack.1 = (bf16[528,512]{1,0:T(8,128)(2,1)S(1)}, bf16[512,512]{1,0:T(8,128)(2,1)S(1)}) custom-call(s32[6]{0:T(128)S(1)} %stack.21.info_ref, bf16[512,1024]{1,0:T(8,128)(2,1)} %up_ref.3, bf16[1024]{0:T(1024)(128)(2,1)} %bias_ref.3, bf16[1024,512]{1,0:T(8,128)(2,1)} %down_ref.3), custom_call_target="tpu_custom_call" | custom-call | flops 1000 | bytes 1000 | tf_op jit(solution)/shard_map/pack/pallas_call | solution.py:55
  2.6 3.0 %collective-permute-start = (bf16[528,512]{1,0:T(8,128)(2,1)S(1)}, bf16[528,512]{1,0:T(8,128)(2,1)S(1)}, u32[]{:S(2)}, u32[]{:S(2)}) collective-permute-start(bf16[528,512]{1,0:T(8,128)(2,1)S(1)} %get-tuple-element.101), channel_id=1, source_target_pairs={{0,1},{1,0},{2,3},{3,2},{4,5},{5,4},{6,7},{7,6},{8,9},{9,8},{10,11... | collective-permute-start | bytes 1622024 | tf_op jit(solution)/shard_map/ppermute | solution.py:797
  5.6 0.1 collective-permute-start.2
  5.7 9.0 %attend.1 = (bf16[1024,1536]{1,0:T(8,128)(2,1)}, bf16[8,4,128,256]{3,2,1,0:T(8,128)(2,1)}, bf16[1024,512]{1,0:T(8,128)(2,1)}, f32[1024,512]{1,0:T(8,128)}, bf16[1024,512]{1,0:T(8,128)(2,1)S(1)}) custom-call(s32[6]{0:T(128)S(1)} %stack.21.info_ref, bf16[1024,512]{1,0:T(8,128)(2,1)} %tok_ref.2, f32[1,512]{1,0:T(1,128)} %bitcast.9, f32[1,512]{1,0:T(1,128)} %bitcast.12, ...), custom_call_target="tpu_custom_call" | custom-call | flops 1000 | bytes 1000 | tf_op jit(solution)/shard_map/attend/pallas_call | solution.py:55
  14.7 11.1 %ffn_own.1 = (f32[1024,512]{1,0:T(8,128)S(1)}, f32[1024,512]{1,0:T(8,128)S(1)}, bf16[512,1024]{1,0:T(8,128)(2,1)}, bf16[512,1024]{1,0:T(8,128)(2,1)}, f32[2,512]{1,0:T(2,128)}) custom-call(s32[6]{0:T(128)S(1)} %stack.21.info_ref, bf16[1024,512]{1,0:T(8,128)(2,1)S(1)} %get-tuple-element.95.sec_ref.sec_in, bf16[1024,512]{1,0:T(8,128)(2,1)} %dy_in.1, ...), custom_call_target="tpu_custom_call" | custom-call | flops 1000 | bytes 1000 | tf_op jit(solution)/shard_map/ffn_own/pallas_call | solution.py:55
  25.9 3.3 %collective-permute-done.2.refs_2_ = bf16[512,512]{1,0:T(8,128)(2,1)S(1)} collective-permute-done((bf16[512,512]{1,0:T(8,128)(2,1)S(1)}, bf16[512,512]{1,0:T(8,128)(2,1)S(1)}, u32[]{:S(2)}, u32[]{:S(2)}) %collective-permute-start.2) | collective-permute-done | bytes 524320 | tf_op jit(solution)/shard_map/ppermute | solution.py:797
  29.1 0.5 collective-permute-start.5
  29.6 2.1 %collective-permute-done.3.refs_3_ = bf16[512,512]{1,0:T(8,128)(2,1)S(1)} collective-permute-done((bf16[512,512]{1,0:T(8,128)(2,1)S(1)}, bf16[512,512]{1,0:T(8,128)(2,1)S(1)}, u32[]{:S(2)}, u32[]{:S(2)}) %collective-permute-start.3) | collective-permute-done | bytes 524320 | tf_op jit(solution)/shard_map/ppermute | solution.py:797
  31.8 13.5 %ffn_rest.1 = (bf16[1024,512]{1,0:T(8,128)(2,1)}, f32[1024,512]{1,0:T(8,128)}, bf16[1024,512]{1,0:T(8,128)(2,1)}, bf16[1024,512]{1,0:T(8,128)(2,1)}, f32[8,512]{...) custom-call(s32[6]{0:T(128)S(1)} %stack.21.info_ref, ...), custom_call_target="tpu_custom_call" | custom-call | flops 1000 | bytes 1000 | tf_op jit(solution)/shard_map/ffn_rest/pallas_call | solution.py:55
  45.3 0.2 collective-permute-start.4
  45.5 2.5 %collective-permute-done.4.got_ref = bf16[512,1024]{1,0:T(8,128)(2,1)S(1)} collective-permute-done((bf16[512,1024]{1,0:T(8,128)(2,1)S(1)}, bf16[512,1024]{1,0:T(8,128)(2,1)S(1)}, u32[]{:S(2)}, u32[]{:S(2)}) %collective-permute-start.4) | collective-permute-done | bytes 1048608 | tf_op jit(solution)/shard_map/ppermute | solution.py:797
  48.0 0.8 join.1
  48.8 1.8 %collective-permute-start.6 = (bf16[512,1024]{1,0:T(8,128)(2,1)S(1)}, bf16[512,1024]{1,0:T(8,128)(2,1)S(1)}, u32[]{:S(2)}, u32[]{:S(2)}) collective-permute-start(bf16[512,1024]{1,0:T(8,128)(2,1)S(1)} %join.1), channel_id=1, source_target_pairs={{0,1},{1,0},{2,6},{3,7},{4,5},{5,4},{6,2},{7,3},{8,9},{9,8},{10,14... | collective-permute-start | bytes 3145736 | tf_op jit(solution)/shard_map/ppermute | solution.py:797
  50.6 12.0 %attend_back.1 = (bf16[1024,1536]{1,0:T(8,128)(2,1)S(1)}, bf16[256,2176]{1,0:T(8,128)(2,1)S(1)}, bf16[256,2176]{1,0:T(8,128)(2,1)S(1)}) custom-call(s32[6]{0:T(128)S(1)} %stack.21.info_ref, bf16[1024,1536]{1,0:T(8,128)(2,1)} %get-tuple-element.108.qkv_ref, bf16[8,4,128,256]{3,2,1,0:T(8,128)(2,1)} %get-tuple-element.109.prob_ref, ...), custom_call_target="tpu_custom_call" | custom-call | flops 1000 | bytes 1000 | tf_op jit(solution)/shard_map/attend_back/pallas_call | solution.py:55
  62.6 1.1 collective-permute-done.6.arrived_ref
  63.6 1.1 split.1
  64.8 1.8 %collective-permute-start.8 = (bf16[256,1024]{1,0:T(8,128)(2,1)S(1)}, bf16[256,1024]{1,0:T(8,128)(2,1)S(1)}, u32[]{:S(2)}, u32[]{:S(2)}) collective-permute-start(bf16[256,1024]{1,0:T(8,128)(2,1)S(1)} %get-tuple-element.129), channel_id=1, source_target_pairs={{0,4},{1,5},{2,3},{3,2},{4,0},{5,1},{6,7},{7,6},{8,12},{9,13},{10,... | collective-permute-start | bytes 1572872 | tf_op jit(solution)/shard_map/ppermute | solution.py:797
  66.6 0.3 add_convert_fusion
  66.9 0.1 fusion
  67.0 1.6 %collective-permute-start.9 = (bf16[128,2176]{1,0:T(8,128)(2,1)S(1)}, bf16[128,2176]{1,0:T(8,128)(2,1)S(1)}, u32[]{:S(2)}, u32[]{:S(2)}) collective-permute-start(bf16[128,2176]{1,0:T(8,128)(2,1)S(1)} %get-tuple-element.172), channel_id=1, source_target_pairs={{0,4},{1,5},{2,10},{3,11},{4,0},{5,1},{6,14},{7,15},{8,12},{9,13},... | collective-permute-start | bytes 1671176 | tf_op jit(solution)/shard_map/ppermute | solution.py:797
  68.6 5.5 %first_back.1 = f32[1024,512]{1,0:T(8,128)} custom-call(s32[6]{0:T(128)S(1)} %stack.21.info_ref, bf16[1024,1536]{1,0:T(8,128)(2,1)S(1)} %get-tuple-element.124.dqkv_ref, bf16[512,1536]{1,0:T(8,128)(2,1)S(1)} %copy-done.1, bf16[1024,512]{1,0:T(8,128)(2,1)} %tok_ref.2, f32[1024,512]{1,0:T(8,128)} %get-tuple-element.125.gres_ref, f32[1,512]{1,0:T(1,128)} %bitcast.11), custom_call_target="tpu_custom_call" | custom-call | flops 1000 | bytes 1000 | tf_op jit(solution)/shard_map/first_back/pallas_call | solution.py:55
  74.1 0.2 add_convert_fusion.2
  74.4 1.8 %collective-permute-start.10 = (bf16[128,1024]{1,0:T(8,128)(2,1)S(1)}, bf16[128,1024]{1,0:T(8,128)(2,1)S(1)}, u32[]{:S(2)}, u32[]{:S(2)}) collective-permute-start(bf16[128,1024]{1,0:T(8,128)(2,1)S(1)} %get-tuple-element.176), channel_id=1, source_target_pairs={{0,8},{1,9},{2,10},{3,11},{4,12},{5,13},{6,14},{7,15},{8,0},{9,1},... | collective-permute-start | bytes 786440 | tf_op jit(solution)/shard_map/ppermute | solution.py:797
  76.2 5.0 %collective-permute-done.9 = bf16[128,2176]{1,0:T(8,128)(2,1)S(1)} collective-permute-done((bf16[128,2176]{1,0:T(8,128)(2,1)S(1)}, bf16[128,2176]{1,0:T(8,128)(2,1)S(1)}, u32[]{:S(2)}, u32[]{:S(2)}) %collective-permute-start.9) | collective-permute-done | bytes 557088 | tf_op jit(solution)/shard_map/ppermute | solution.py:797
  81.2 0.1 add_convert_fusion.1
  81.4 2.1 %collective-permute-start.11 = (bf16[64,2176]{1,0:T(8,128)(2,1)S(1)}, bf16[64,2176]{1,0:T(8,128)(2,1)S(1)}, u32[]{:S(2)}, u32[]{:S(2)}) collective-permute-start(bf16[64,2176]{1,0:T(8,128)(2,1)S(1)} %get-tuple-element.175), channel_id=1, source_target_pairs={{0,1},{1,0},{2,6},{3,7},{4,5},{5,4},{6,2},{7,3},{8,9},{9,8},{10,14... | collective-permute-start | bytes 835592 | tf_op jit(solution)/shard_map/ppermute | solution.py:797
  83.5 5.9 %collective-permute-done.11 = bf16[64,2176]{1,0:T(8,128)(2,1)S(1)} collective-permute-done((bf16[64,2176]{1,0:T(8,128)(2,1)S(1)}, bf16[64,2176]{1,0:T(8,128)(2,1)S(1)}, u32[]{:S(2)}, u32[]{:S(2)}) %collective-permute-start.11) | collective-permute-done | bytes 278560 | tf_op jit(solution)/shard_map/ppermute | solution.py:797
  89.6 2.1 %collective-permute-start.12 = (bf16[32,2176]{1,0:T(8,128)(2,1)S(1)}, bf16[32,2176]{1,0:T(8,128)(2,1)S(1)}, u32[]{:S(2)}, u32[]{:S(2)}) collective-permute-start(bf16[32,2176]{1,0:T(8,128)(2,1)S(1)} %get-tuple-element.178), channel_id=1, source_target_pairs={{0,8},{1,9},{2,3},{3,2},{4,12},{5,13},{6,7},{7,6},{8,0},{9,1},{10,... | collective-permute-start | bytes 417800 | tf_op jit(solution)/shard_map/ppermute | solution.py:797
  91.7 2.6 %collective-permute-start.13 = (bf16[128,1024]{1,0:T(8,128)(2,1)S(1)}, bf16[128,1024]{1,0:T(8,128)(2,1)S(1)}, u32[]{:S(2)}, u32[]{:S(2)}) collective-permute-start(bf16[128,1024]{1,0:T(8,128)(2,1)S(1)} %add_convert_fusion.5), channel_id=1, source_target_pairs={{0,16},{1,17},{2,18},{3,19},{4,20},{5,21},{6,22},{7,23},{8,24},{9,... | collective-permute-start | bytes 786440 | tf_op jit(solution)/shard_map/ppermute | solution.py:797
  94.3 0.8 collective-permute-done.12
  95.2 3.9 %collective-permute-start.14 = (bf16[32,2176]{1,0:T(8,128)(2,1)S(1)}, bf16[32,2176]{1,0:T(8,128)(2,1)S(1)}, u32[]{:S(2)}, u32[]{:S(2)}) collective-permute-start(bf16[32,2176]{1,0:T(8,128)(2,1)S(1)} %add_convert_fusion.7), channel_id=1, source_target_pairs={{0,16},{1,17},{2,18},{3,19},{4,20},{5,21},{6,22},{7,23},{8,24},{9,... | collective-permute-start | bytes 417800 | tf_op jit(solution)/shard_map/ppermute | solution.py:797
  99.0 3.1 %collective-permute-done.13 = bf16[128,1024]{1,0:T(8,128)(2,1)S(1)} collective-permute-done((bf16[128,1024]{1,0:T(8,128)(2,1)S(1)}, bf16[128,1024]{1,0:T(8,128)(2,1)S(1)}, u32[]{:S(2)}, u32[]{:S(2)}) %collective-permute-start.13) | collective-permute-done | bytes 262176 | tf_op jit(solution)/shard_map/ppermute | solution.py:797
  102.2 1.6 %collective-permute-start.15 = (bf16[128,1024]{1,0:T(8,128)(2,1)S(1)}, bf16[128,1024]{1,0:T(8,128)(2,1)S(1)}, u32[]{:S(2)}, u32[]{:S(2)}) collective-permute-start(bf16[128,1024]{1,0:T(8,128)(2,1)S(1)} %add_convert_fusion.4), channel_id=1, source_target_pairs={{0,4},{1,5},{2,6},{3,7},{4,0},{5,1},{6,2},{7,3},{8,12},{9,13},{10,... | collective-permute-start | bytes 786440 | tf_op jit(solution)/shard_map/ppermute | solution.py:797
  103.8 1.4 %collective-permute-done.14 = bf16[32,2176]{1,0:T(8,128)(2,1)S(1)} collective-permute-done((bf16[32,2176]{1,0:T(8,128)(2,1)S(1)}, bf16[32,2176]{1,0:T(8,128)(2,1)S(1)}, u32[]{:S(2)}, u32[]{:S(2)}) %collective-permute-start.14) | collective-permute-done | bytes 139296 | tf_op jit(solution)/shard_map/ppermute | solution.py:797
  105.3 0.8 collective-permute-start.16
  106.2 2.5 %collective-permute-done.15 = bf16[128,1024]{1,0:T(8,128)(2,1)S(1)} collective-permute-done((bf16[128,1024]{1,0:T(8,128)(2,1)S(1)}, bf16[128,1024]{1,0:T(8,128)(2,1)S(1)}, u32[]{:S(2)}, u32[]{:S(2)}) %collective-permute-start.15) | collective-permute-done | bytes 262176 | tf_op jit(solution)/shard_map/ppermute | solution.py:797
  108.7 2.3 %collective-permute-start.18 = (bf16[256,1024]{1,0:T(8,128)(2,1)S(1)}, bf16[256,1024]{1,0:T(8,128)(2,1)S(1)}, u32[]{:S(2)}, u32[]{:S(2)}) collective-permute-start(bf16[256,1024]{1,0:T(8,128)(2,1)S(1)} %constant_dynamic-update-slice_fusion), channel_id=1, source_target_pairs={{0,8},{1,9},{2,10},{3,11},{4,12},{5,13},{6,14},{7,15},{8,0},{9,1},... | collective-permute-start | bytes 1572872 | tf_op jit(solution)/shard_map/ppermute | solution.py:797
  111.0 1.0 collective-permute-done.16
  112.1 6.5 %collective-permute-done.17 = bf16[64,2176]{1,0:T(8,128)(2,1)S(1)} collective-permute-done((bf16[64,2176]{1,0:T(8,128)(2,1)S(1)}, bf16[64,2176]{1,0:T(8,128)(2,1)S(1)}, u32[]{:S(2)}, u32[]{:S(2)}) %collective-permute-start.17) | collective-permute-done | bytes 278560 | tf_op jit(solution)/shard_map/ppermute | solution.py:797
  118.8 0.5 collective-permute-start.21
  119.3 1.0 collective-permute-start.20
  120.3 1.2 collective-permute-done.19.other_ref
  121.4 3.1 %ffn_end.1 = (f32[512,1024]{1,0:T(8,128)}, f32[1024,512]{1,0:T(8,128)}) custom-call(s32[6]{0:T(128)S(1)} %stack.21.info_ref, bf16[512,1024]{1,0:T(8,128)(2,1)S(1)} %constant_dynamic-update-slice_fusion.6.keep_ref, bf16[512,1024]{1,0:T(8,128)(2,1)S(1)} %collective-permute-done.19.other_ref), custom_call_target="tpu_custom_call" | custom-call | flops 1000 | bytes 1000 | tf_op jit(solution)/shard_map/ffn_end/pallas_call | solution.py:55
  124.5 2.0 %attend_end.2 = (f32[512,1536]{1,0:T(8,128)}, f32[512,512]{1,0:T(8,128)}) custom-call(s32[6]{0:T(128)S(1)} %stack.21.info_ref, bf16[128,2176]{1,0:T(8,128)(2,1)S(1)} %constant_dynamic-update-slice_fusion.4.refs_0_, bf16[128,2176]{1,0:T(8,128)(2,1)S(1)} %collective-permute-done.21.refs_1_), custom_call_target="tpu_custom_call" | custom-call | flops 1000 | bytes 1000 | tf_op jit(solution)/shard_map/attend_end/pallas_call | solution.py:55
  126.5 2.3 %collective-permute-done.20.refs_2_ = bf16[128,2176]{1,0:T(8,128)(2,1)S(1)} collective-permute-done((bf16[128,2176]{1,0:T(8,128)(2,1)S(1)}, bf16[128,2176]{1,0:T(8,128)(2,1)S(1)}, u32[]{:S(2)}, u32[]{:S(2)}) %collective-permute-start.20) | collective-permute-done | bytes 557088 | tf_op jit(solution)/shard_map/ppermute | solution.py:797
  128.8 2.0 %collective-permute-done.22.refs_3_ = bf16[128,2176]{1,0:T(8,128)(2,1)S(1)} collective-permute-done((bf16[128,2176]{1,0:T(8,128)(2,1)S(1)}, bf16[128,2176]{1,0:T(8,128)(2,1)S(1)}, u32[]{:S(2)}, u32[]{:S(2)}) %collective-permute-start.22) | collective-permute-done | bytes 557088 | tf_op jit(solution)/shard_map/ppermute | solution.py:797
  130.8 2.7 %attend_end.3 = (f32[512,1536]{1,0:T(8,128)}, f32[512,512]{1,0:T(8,128)}, f32[512]{0:T(512)}, f32[512]{0:T(512)}, f32[512]{0:T(512)}, /*index=5*/f32[512]{0:T(512)}, f32[512]{0:T(512)}, f32[1024]{0:T(1024)}) custom-call(s32[6]{0:T(128)S(1)} %stack.21.info_ref, ...), custom_call_target="tpu_custom_call", output_to_operand_aliasing={{0}: (5, {}), {1}: (6, {})} | custom-call | flops 1000 | bytes 1000 | tf_op jit(solution)/shard_map/attend_end/pallas_call | solution.py:55
  (40 shorter events, 0.8 us)
Async XLA Ops:
  0.6 5.1 %copy-start = (bf16[512,1536]{1,0:T(8,128)(2,1)S(1)}, bf16[512,1536]{1,0:T(8,128)(2,1)}, u32[]{:S(2)}) copy-start(bf16[512,1536]{1,0:T(8,128)(2,1)} %wqkv_ref.5) | copy-start | bytes 4718596
  0.7 5.1 %copy-start.4 = (bf16[512,512]{1,0:T(8,128)(2,1)S(1)}, bf16[512,512]{1,0:T(8,128)(2,1)}, u32[]{:S(2)}) copy-start(bf16[512,512]{1,0:T(8,128)(2,1)} %wout_ref.3) | copy-start | bytes 1572868
  2.6 12.1 %copy-start.2 = (bf16[512,1024]{1,0:T(8,128)(2,1)S(1)}, bf16[512,1024]{1,0:T(8,128)(2,1)}, u32[]{:S(2)}) copy-start(bf16[512,1024]{1,0:T(8,128)(2,1)} %up_ref.3) | copy-start | bytes 3145732
  2.6 12.1 %copy-start.3 = (bf16[1024,512]{1,0:T(8,128)(2,1)S(1)}, bf16[1024,512]{1,0:T(8,128)(2,1)}, u32[]{:S(2)}) copy-start(bf16[1024,512]{1,0:T(8,128)(2,1)} %down_ref.3) | copy-start | bytes 3145732
  2.6 23.2 %collective-permute-start = (bf16[528,512]{1,0:T(8,128)(2,1)S(1)}, bf16[528,512]{1,0:T(8,128)(2,1)S(1)}, u32[]{:S(2)}, u32[]{:S(2)}) collective-permute-start(bf16[528,512]{1,0:T(8,128)(2,1)S(1)} %get-tuple-element.101), channel_id=1, source_target_pairs={{0,1},{1,0},{2,3},{3,2},{4,5},{5,4},{6,7},{7,6},{8,9},{9,8},{10,11... | collective-permute-start | bytes 1622024 | tf_op jit(solution)/shard_map/ppermute | solution.py:797
  5.6 23.5 %collective-permute-start.2 = (bf16[512,512]{1,0:T(8,128)(2,1)S(1)}, bf16[512,512]{1,0:T(8,128)(2,1)S(1)}, u32[]{:S(2)}, u32[]{:S(2)}) collective-permute-start(bf16[512,512]{1,0:T(8,128)(2,1)S(1)} %get-tuple-element.103), channel_id=1, source_target_pairs={{0,1},{1,0},{2,3},{3,2},{4,5},{5,4},{6,7},{7,6},{8,9},{9,8},{10,11... | collective-permute-start | bytes 1572872 | tf_op jit(solution)/shard_map/ppermute | solution.py:797
  25.8 5.9 %collective-permute-start.1 = (bf16[528,512]{1,0:T(8,128)(2,1)S(1)}, bf16[528,512]{1,0:T(8,128)(2,1)S(1)}, u32[]{:S(2)}, u32[]{:S(2)}) collective-permute-start(bf16[528,512]{1,0:T(8,128)(2,1)S(1)} %collective-permute-done.refs_0_), channel_id=1, source_target_pairs={{0,2},{1,3},{2,0},{3,1},{4,6},{5,7},{6,4},{7,5},{8,10},{9,11},{10,... | collective-permute-start | bytes 1622024 | tf_op jit(solution)/shard_map/ppermute | solution.py:797
  29.1 2.6 %collective-permute-start.3 = (bf16[512,512]{1,0:T(8,128)(2,1)S(1)}, bf16[512,512]{1,0:T(8,128)(2,1)S(1)}, u32[]{:S(2)}, u32[]{:S(2)}) collective-permute-start(bf16[512,512]{1,0:T(8,128)(2,1)S(1)} %collective-permute-done.2.refs_2_), channel_id=1, source_target_pairs={{0,2},{1,3},{2,0},{3,1},{4,6},{5,7},{6,4},{7,5},{8,10},{9,11},{10,... | collective-permute-start | bytes 1572872 | tf_op jit(solution)/shard_map/ppermute | solution.py:797
  29.1 16.3 %collective-permute-start.5 = (bf16[512,1024]{1,0:T(8,128)(2,1)}, bf16[512,1024]{1,0:T(8,128)(2,1)S(1)}, u32[]{:S(2)}, u32[]{:S(2)}) collective-permute-start(bf16[512,1024]{1,0:T(8,128)(2,1)} %get-tuple-element.107), channel_id=1, source_target_pairs={{0,2},{1,3},{2,0},{3,1},{4,6},{5,7},{6,4},{7,5},{8,10},{9,11},{10,... | collective-permute-start | bytes 3145736 | tf_op jit(solution)/shard_map/ppermute | solution.py:797
  45.3 2.7 %collective-permute-start.4 = (bf16[512,1024]{1,0:T(8,128)(2,1)S(1)}, bf16[512,1024]{1,0:T(8,128)(2,1)S(1)}, u32[]{:S(2)}, u32[]{:S(2)}) collective-permute-start(bf16[512,1024]{1,0:T(8,128)(2,1)S(1)} %get-tuple-element.106), channel_id=1, source_target_pairs={{0,2},{1,3},{2,0},{3,1},{4,6},{5,7},{6,4},{7,5},{8,10},{9,11},{10,... | collective-permute-start | bytes 3145736 | tf_op jit(solution)/shard_map/ppermute | solution.py:797
  48.8 14.9 %collective-permute-start.6 = (bf16[512,1024]{1,0:T(8,128)(2,1)S(1)}, bf16[512,1024]{1,0:T(8,128)(2,1)S(1)}, u32[]{:S(2)}, u32[]{:S(2)}) collective-permute-start(bf16[512,1024]{1,0:T(8,128)(2,1)S(1)} %join.1), channel_id=1, source_target_pairs={{0,1},{1,0},{2,6},{3,7},{4,5},{5,4},{6,2},{7,3},{8,9},{9,8},{10,14... | collective-permute-start | bytes 3145736 | tf_op jit(solution)/shard_map/ppermute | solution.py:797
  63.6 3.0 %collective-permute-start.7 = (bf16[256,2176]{1,0:T(8,128)(2,1)S(1)}, bf16[256,2176]{1,0:T(8,128)(2,1)S(1)}, u32[]{:S(2)}, u32[]{:S(2)}) collective-permute-start(bf16[256,2176]{1,0:T(8,128)(2,1)S(1)} %get-tuple-element.123), channel_id=1, source_target_pairs={{0,2},{1,3},{2,0},{3,1},{4,6},{5,7},{6,4},{7,5},{8,10},{9,11},{10,... | collective-permute-start | bytes 3342344 | tf_op jit(solution)/shard_map/ppermute | solution.py:797
  64.8 9.3 %collective-permute-start.8 = (bf16[256,1024]{1,0:T(8,128)(2,1)S(1)}, bf16[256,1024]{1,0:T(8,128)(2,1)S(1)}, u32[]{:S(2)}, u32[]{:S(2)}) collective-permute-start(bf16[256,1024]{1,0:T(8,128)(2,1)S(1)} %get-tuple-element.129), channel_id=1, source_target_pairs={{0,4},{1,5},{2,3},{3,2},{4,0},{5,1},{6,7},{7,6},{8,12},{9,13},{10,... | collective-permute-start | bytes 1572872 | tf_op jit(solution)/shard_map/ppermute | solution.py:797
  66.6 2.0 %copy-start.1 = (bf16[512,1536]{1,0:T(8,128)(2,1)S(1)}, bf16[512,1536]{1,0:T(8,128)(2,1)}, u32[]{:S(2)}) copy-start(bf16[512,1536]{1,0:T(8,128)(2,1)} %wqkv_ref.5) | copy-start | bytes 4718596
  67.0 14.2 %collective-permute-start.9 = (bf16[128,2176]{1,0:T(8,128)(2,1)S(1)}, bf16[128,2176]{1,0:T(8,128)(2,1)S(1)}, u32[]{:S(2)}, u32[]{:S(2)}) collective-permute-start(bf16[128,2176]{1,0:T(8,128)(2,1)S(1)} %get-tuple-element.172), channel_id=1, source_target_pairs={{0,4},{1,5},{2,10},{3,11},{4,0},{5,1},{6,14},{7,15},{8,12},{9,13},... | collective-permute-start | bytes 1671176 | tf_op jit(solution)/shard_map/ppermute | solution.py:797
  74.4 9.1 %collective-permute-start.10 = (bf16[128,1024]{1,0:T(8,128)(2,1)S(1)}, bf16[128,1024]{1,0:T(8,128)(2,1)S(1)}, u32[]{:S(2)}, u32[]{:S(2)}) collective-permute-start(bf16[128,1024]{1,0:T(8,128)(2,1)S(1)} %get-tuple-element.176), channel_id=1, source_target_pairs={{0,8},{1,9},{2,10},{3,11},{4,12},{5,13},{6,14},{7,15},{8,0},{9,1},... | collective-permute-start | bytes 786440 | tf_op jit(solution)/shard_map/ppermute | solution.py:797
  81.4 8.1 %collective-permute-start.11 = (bf16[64,2176]{1,0:T(8,128)(2,1)S(1)}, bf16[64,2176]{1,0:T(8,128)(2,1)S(1)}, u32[]{:S(2)}, u32[]{:S(2)}) collective-permute-start(bf16[64,2176]{1,0:T(8,128)(2,1)S(1)} %get-tuple-element.175), channel_id=1, source_target_pairs={{0,1},{1,0},{2,6},{3,7},{4,5},{5,4},{6,2},{7,3},{8,9},{9,8},{10,14... | collective-permute-start | bytes 835592 | tf_op jit(solution)/shard_map/ppermute | solution.py:797
  89.6 5.5 %collective-permute-start.12 = (bf16[32,2176]{1,0:T(8,128)(2,1)S(1)}, bf16[32,2176]{1,0:T(8,128)(2,1)S(1)}, u32[]{:S(2)}, u32[]{:S(2)}) collective-permute-start(bf16[32,2176]{1,0:T(8,128)(2,1)S(1)} %get-tuple-element.178), channel_id=1, source_target_pairs={{0,8},{1,9},{2,3},{3,2},{4,12},{5,13},{6,7},{7,6},{8,0},{9,1},{10,... | collective-permute-start | bytes 417800 | tf_op jit(solution)/shard_map/ppermute | solution.py:797
  91.7 10.5 %collective-permute-start.13 = (bf16[128,1024]{1,0:T(8,128)(2,1)S(1)}, bf16[128,1024]{1,0:T(8,128)(2,1)S(1)}, u32[]{:S(2)}, u32[]{:S(2)}) collective-permute-start(bf16[128,1024]{1,0:T(8,128)(2,1)S(1)} %add_convert_fusion.5), channel_id=1, source_target_pairs={{0,16},{1,17},{2,18},{3,19},{4,20},{5,21},{6,22},{7,23},{8,24},{9,... | collective-permute-start | bytes 786440 | tf_op jit(solution)/shard_map/ppermute | solution.py:797
  95.2 10.1 %collective-permute-start.14 = (bf16[32,2176]{1,0:T(8,128)(2,1)S(1)}, bf16[32,2176]{1,0:T(8,128)(2,1)S(1)}, u32[]{:S(2)}, u32[]{:S(2)}) collective-permute-start(bf16[32,2176]{1,0:T(8,128)(2,1)S(1)} %add_convert_fusion.7), channel_id=1, source_target_pairs={{0,16},{1,17},{2,18},{3,19},{4,20},{5,21},{6,22},{7,23},{8,24},{9,... | collective-permute-start | bytes 417800 | tf_op jit(solution)/shard_map/ppermute | solution.py:797
  102.2 6.4 %collective-permute-start.15 = (bf16[128,1024]{1,0:T(8,128)(2,1)S(1)}, bf16[128,1024]{1,0:T(8,128)(2,1)S(1)}, u32[]{:S(2)}, u32[]{:S(2)}) collective-permute-start(bf16[128,1024]{1,0:T(8,128)(2,1)S(1)} %add_convert_fusion.4), channel_id=1, source_target_pairs={{0,4},{1,5},{2,6},{3,7},{4,0},{5,1},{6,2},{7,3},{8,12},{9,13},{10,... | collective-permute-start | bytes 786440 | tf_op jit(solution)/shard_map/ppermute | solution.py:797
  105.3 6.7 %collective-permute-start.16 = (bf16[32,2176]{1,0:T(8,128)(2,1)S(1)}, bf16[32,2176]{1,0:T(8,128)(2,1)S(1)}, u32[]{:S(2)}, u32[]{:S(2)}) collective-permute-start(bf16[32,2176]{1,0:T(8,128)(2,1)S(1)} %add_convert_fusion.6), channel_id=1, source_target_pairs={{0,8},{1,9},{2,6},{3,7},{4,12},{5,13},{6,2},{7,3},{8,0},{9,1},{10,... | collective-permute-start | bytes 417800 | tf_op jit(solution)/shard_map/ppermute | solution.py:797
  108.7 10.0 %collective-permute-start.18 = (bf16[256,1024]{1,0:T(8,128)(2,1)S(1)}, bf16[256,1024]{1,0:T(8,128)(2,1)S(1)}, u32[]{:S(2)}, u32[]{:S(2)}) collective-permute-start(bf16[256,1024]{1,0:T(8,128)(2,1)S(1)} %constant_dynamic-update-slice_fusion), channel_id=1, source_target_pairs={{0,8},{1,9},{2,10},{3,11},{4,12},{5,13},{6,14},{7,15},{8,0},{9,1},... | collective-permute-start | bytes 1572872 | tf_op jit(solution)/shard_map/ppermute | solution.py:797
  112.0 6.6 %collective-permute-start.17 = (bf16[64,2176]{1,0:T(8,128)(2,1)S(1)}, bf16[64,2176]{1,0:T(8,128)(2,1)S(1)}, u32[]{:S(2)}, u32[]{:S(2)}) collective-permute-start(bf16[64,2176]{1,0:T(8,128)(2,1)S(1)} %constant_dynamic-update-slice_fusion.2), channel_id=1, source_target_pairs={{0,1},{1,0},{2,3},{3,2},{4,5},{5,4},{6,7},{7,6},{8,9},{9,8},{10,11... | collective-permute-start | bytes 835592 | tf_op jit(solution)/shard_map/ppermute | solution.py:797
  118.7 2.7 %collective-permute-start.19 = (bf16[512,1024]{1,0:T(8,128)(2,1)S(1)}, bf16[512,1024]{1,0:T(8,128)(2,1)S(1)}, u32[]{:S(2)}, u32[]{:S(2)}) collective-permute-start(bf16[512,1024]{1,0:T(8,128)(2,1)S(1)} %constant_dynamic-update-slice_fusion.6.keep_ref), channel_id=1, source_target_pairs={{0,2},{1,3},{2,0},{3,1},{4,6},{5,7},{6,4},{7,5},{8,10},{9,11},{10,... | collective-permute-start | bytes 3145736 | tf_op jit(solution)/shard_map/ppermute | solution.py:797
  118.8 5.7 %collective-permute-start.21 = (bf16[128,2176]{1,0:T(8,128)(2,1)S(1)}, bf16[128,2176]{1,0:T(8,128)(2,1)S(1)}, u32[]{:S(2)}, u32[]{:S(2)}) collective-permute-start(bf16[128,2176]{1,0:T(8,128)(2,1)S(1)} %constant_dynamic-update-slice_fusion.4.refs_0_), channel_id=1, source_target_pairs={{0,2},{1,3},{2,0},{3,1},{4,6},{5,7},{6,4},{7,5},{8,10},{9,11},{10,... | collective-permute-start | bytes 1671176 | tf_op jit(solution)/shard_map/ppermute | solution.py:797
  119.3 9.5 %collective-permute-start.20 = (bf16[128,2176]{1,0:T(8,128)(2,1)S(1)}, bf16[128,2176]{1,0:T(8,128)(2,1)S(1)}, u32[]{:S(2)}, u32[]{:S(2)}) collective-permute-start(bf16[128,2176]{1,0:T(8,128)(2,1)S(1)} %constant_dynamic-update-slice_fusion.4.refs_0_), channel_id=1, source_target_pairs={{0,4},{1,5},{2,10},{3,11},{4,0},{5,1},{6,14},{7,15},{8,12},{9,13},... | collective-permute-start | bytes 1671176 | tf_op jit(solution)/shard_map/ppermute | solution.py:797
  128.8 2.0 %collective-permute-start.22 = (bf16[128,2176]{1,0:T(8,128)(2,1)S(1)}, bf16[128,2176]{1,0:T(8,128)(2,1)S(1)}, u32[]{:S(2)}, u32[]{:S(2)}) collective-permute-start(bf16[128,2176]{1,0:T(8,128)(2,1)S(1)} %collective-permute-done.20.refs_2_), channel_id=1, source_target_pairs={{0,2},{1,3},{2,0},{3,1},{4,6},{5,7},{6,4},{7,5},{8,10},{9,11},{10,... | collective-permute-start | bytes 1671176 | tf_op jit(solution)/shard_map/ppermute | solution.py:797
